TPU v7x, 32 devices: a whole 2x2x4 slice. The times are simulated.
32 devices in a mesh: rows: 4 (over z), wide: 8 (over y, x, core).
Axes of the slice: x: 2, y: 2, z: 4, core: 2. Of those that a mesh axis runs over, the one named last changes fastest.
Arguments:
- tokens: bfloat16 [4, 1536, 2048], P('rows', 'wide'), may hold values from -6 to 6
- segments: int32 [4, 1536], P('rows', 'wide'), may hold values from 0 to 6, as said below
- w_qkv: bfloat16 [2048, 6144], P(('rows', 'wide')), may hold values from -0.125 to 0.125
- b_qkv: bfloat16 [6144], P(('rows', 'wide')), may hold values from -4 to 4
- w_out: bfloat16 [2048, 2048], P(('rows', 'wide')), may hold values from -0.75 to 0.75
- ln1_gain: bfloat16 [2048], P(('rows', 'wide')), may hold values from 0.5 to 1.5
- ln1_bias: bfloat16 [2048], P(('rows', 'wide')), may hold values from -4 to 4
- ln2_gain: bfloat16 [2048], P(('rows', 'wide')), may hold values from 0.5 to 1.5
- ln2_bias: bfloat16 [2048], P(('rows', 'wide')), may hold values from -4 to 4
- w_gate: bfloat16 [2048, 5632], P('rows', 'wide'), may hold values from -0.125 to 0.125
- w_up: bfloat16 [2048, 5632], P('rows', 'wide'), may hold values from -0.125 to 0.125
- w_down: bfloat16 [2048, 5632], P('rows', 'wide'), may hold values from -0.078125 to 0.078125
- out_grad: bfloat16 [4, 1536, 2048], P('rows', 'wide'), may hold values from -6 to 6
Outputs:
- mixed: bfloat16 [4, 1536, 2048], P('rows', 'wide')
- grad_tokens: float32 [4, 1536, 2048], P('rows', 'wide')
- grad_w_qkv: float32 [2048, 6144], P(('rows', 'wide'))
- grad_b_qkv: float32 [6144], P(('rows', 'wide'))
- grad_w_out: float32 [2048, 2048], P(('rows', 'wide'))
- grad_ln1_gain: float32 [2048], P(('rows', 'wide'))
- grad_ln1_bias: float32 [2048], P(('rows', 'wide'))
- grad_ln2_gain: float32 [2048], P(('rows', 'wide'))
- grad_ln2_bias: float32 [2048], P(('rows', 'wide'))
- grad_w_gate: float32 [2048, 5632], P('rows', 'wide')
- grad_w_up: float32 [2048, 5632], P('rows', 'wide')
- grad_w_down: float32 [2048, 5632], P('rows', 'wide')
Inputs may be any that keep to these rules, and one draw needn't show every extreme that they name: `segments`: each row holds documents 0 to 6 in order, none empty; documents 0 to 2 end within the row's first 192 tokens and document 6 starts within its last 192, so document 3 runs from the first device of wide to the last.
All inputs are finite; a program needn't handle non-finite values.
Results may differ from a plain program's by a relative error of at most 0.015.
Values may be sent and summed in bfloat16 or wider, within the bound.
No kernel may reach another device: no remote copies, remote signals or barrier semaphores. Data moves between devices by JAX's collectives and lax.ppermute only.
A program may use at most 320 MiB of HBM per device.

v0:
```python
import math

import jax
import jax.numpy as jnp
from jax import lax
from jax.sharding import PartitionSpec as P

HEADS = 32
HEAD_DIM = 64
ROT = 16


epsilon = 1e-05
neg_large = -1e30


def layer_norm(values, gain, shift):
    centre = jnp.mean(values, axis=-1, keepdims=True)
    centred = values - centre
    spread = jnp.mean(centred * centred, axis=-1, keepdims=True)
    return centred * lax.rsqrt(spread + epsilon) * gain + shift


def rotary(values, places):
    half_rot = ROT // 2
    freqs = 10000.0 ** (-2.0 * jnp.arange(half_rot, dtype=jnp.float32) / ROT)
    angles = places.astype(jnp.float32)[:, None] * freqs[None, :]
    cosine = jnp.cos(angles)[:, None, :]
    sine = jnp.sin(angles)[:, None, :]
    first_half = values[..., :half_rot]
    second_half = values[..., half_rot:ROT]
    remainder = values[..., ROT:]
    return jnp.concatenate(
        [
            first_half * cosine - second_half * sine,
            second_half * cosine + first_half * sine,
            remainder,
        ],
        axis=-1,
    )


def split_heads(flat):
    return flat.reshape(flat.shape[0], HEADS, HEAD_DIM)


def block_scores(queries, keys, score_scale):
    return (
        jnp.einsum("qhd,khd->hqk", queries, keys, preferred_element_type=jnp.float32) * score_scale
    )


def visible_pairs(query_place, query_segs, key_place, key_segs):
    return (query_segs[:, None] == key_segs[None, :]) & (key_place[None, :] <= query_place[:, None])


def probs_from(scores, visible, log_total):
    return jnp.where(
        visible, jnp.exp(jnp.where(visible, scores - log_total[..., None], neg_large)), 0.0
    )


def score_grads(attn_probs, grad_probs, visible, delta):
    return jnp.where(visible, attn_probs * (grad_probs - delta[..., None]), 0.0).astype(
        jnp.bfloat16
    )


def contract_rows(left, right):
    return lax.dot_general(
        left, right, (((0,), (0,)), ((), ())), preferred_element_type=jnp.float32
    )


def contract_cols(left, right):
    return lax.dot_general(
        left, right, (((1,), (1,)), ((), ())), preferred_element_type=jnp.float32
    )


def swiglu(gate_in, up_in):
    return jax.nn.silu(gate_in) * up_in


def shards(
    tokens,
    segments,
    w_qkv,
    b_qkv,
    w_out,
    ln1_gain,
    ln1_bias,
    ln2_gain,
    ln2_bias,
    w_gate,
    w_up,
    w_down,
    out_grad,
):
    local_rows = tokens.shape[1]
    model_width = tokens.shape[2]
    row_len = local_rows * lax.axis_size("wide")
    block_rows = math.gcd(row_len, 512)
    blocks = row_len // block_rows
    score_scale = HEAD_DIM ** (-0.5)
    numbers = jnp.arange(blocks, dtype=jnp.int32)
    first_row = lax.axis_index("wide") * local_rows
    row_segs = lax.all_gather(segments, "wide", axis=1, tiled=True)[0]
    own_segs = segments[0]
    own_place = first_row + jnp.arange(local_rows, dtype=jnp.int32)
    row_place = jnp.arange(row_len, dtype=jnp.int32)
    doc_first = jnp.sum((row_segs[None, :] < own_segs[:, None]).astype(jnp.int32), axis=1)
    positions = own_place - doc_first
    w_qkv_all, b_qkv_all, w_out_all, gain_one, shift_one, gain_two, shift_two = (
        lax.all_gather(w_qkv, ("rows", "wide"), axis=0, tiled=True),
        lax.all_gather(b_qkv, ("rows", "wide"), axis=0, tiled=True),
        lax.all_gather(w_out, ("rows", "wide"), axis=0, tiled=True),
        lax.all_gather(ln1_gain, ("rows", "wide"), axis=0, tiled=True),
        lax.all_gather(ln1_bias, ("rows", "wide"), axis=0, tiled=True),
        lax.all_gather(ln2_gain, ("rows", "wide"), axis=0, tiled=True),
        lax.all_gather(ln2_bias, ("rows", "wide"), axis=0, tiled=True),
    )
    inputs = tokens[0].astype(jnp.float32)
    norm_one, norm_one_back = jax.vjp(
        layer_norm, inputs, gain_one.astype(jnp.float32), shift_one.astype(jnp.float32)
    )
    act_one = norm_one.astype(jnp.bfloat16)
    projected = jnp.dot(act_one, w_qkv_all, preferred_element_type=jnp.float32) + b_qkv_all.astype(
        jnp.float32
    )

    def turn(values):
        return rotary(values, positions)

    query_rot, query_back = jax.vjp(turn, split_heads(projected[:, :model_width]))
    key_rot, key_back = jax.vjp(turn, split_heads(projected[:, model_width : 2 * model_width]))
    query_low = query_rot.astype(jnp.bfloat16)
    key_low = key_rot.astype(jnp.bfloat16).reshape(local_rows, model_width)
    value_low = projected[:, 2 * model_width :].astype(jnp.bfloat16)
    key_row, value_row = (
        lax.all_gather(key_low, "wide", axis=0, tiled=True),
        lax.all_gather(value_low, "wide", axis=0, tiled=True),
    )

    def key_block(number):
        offset = number * block_rows
        keys_blk = split_heads(lax.dynamic_slice_in_dim(key_row, offset, block_rows, 0))
        values_blk = split_heads(lax.dynamic_slice_in_dim(value_row, offset, block_rows, 0))
        key_place = lax.dynamic_slice_in_dim(row_place, offset, block_rows, 0)
        key_segs = lax.dynamic_slice_in_dim(row_segs, offset, block_rows, 0)
        visible = visible_pairs(own_place, own_segs, key_place, key_segs)[None]
        return (keys_blk, values_blk, visible)

    def stat_step(state, number):
        running_max, running_sum = state
        keys_blk, values_blk, visible = key_block(number)
        scores = jnp.where(visible, block_scores(query_low, keys_blk, score_scale), neg_large)
        new_max = jnp.maximum(running_max, jnp.max(scores, axis=-1))
        terms = jnp.where(visible, jnp.exp(scores - new_max[..., None]), 0.0)
        return (
            (new_max, running_sum * jnp.exp(running_max - new_max) + jnp.sum(terms, axis=-1)),
            None,
        )

    start_max = jnp.full((HEADS, local_rows), neg_large, jnp.float32)
    start_sum = jnp.zeros((HEADS, local_rows), jnp.float32)
    (peak, denom), ignored = lax.scan(stat_step, (start_max, start_sum), numbers)
    log_total = peak + jnp.log(denom)

    def probs_of(number):
        keys_blk, values_blk, visible = key_block(number)
        attn_probs = probs_from(block_scores(query_low, keys_blk, score_scale), visible, log_total)
        return (keys_blk, values_blk, visible, attn_probs)

    def out_step(totals, number):
        keys_blk, values_blk, visible, attn_probs = probs_of(number)
        return (
            totals
            + jnp.einsum(
                "hqk,khd->qhd",
                attn_probs.astype(jnp.bfloat16),
                values_blk,
                preferred_element_type=jnp.float32,
            ),
            None,
        )

    head_zeros = jnp.zeros((local_rows, HEADS, HEAD_DIM), jnp.float32)
    attended, ignored = lax.scan(out_step, head_zeros, numbers)
    attn_low = attended.reshape(local_rows, model_width).astype(jnp.bfloat16)
    middle = inputs + jnp.dot(attn_low, w_out_all, preferred_element_type=jnp.float32)
    norm_two, norm_two_back = jax.vjp(
        layer_norm, middle, gain_two.astype(jnp.float32), shift_two.astype(jnp.float32)
    )
    act_two = norm_two.astype(jnp.bfloat16)
    gate_slab, up_slab, down_slab = (
        lax.all_gather(w_gate, "rows", axis=0, tiled=True),
        lax.all_gather(w_up, "rows", axis=0, tiled=True),
        lax.all_gather(w_down, "rows", axis=0, tiled=True),
    )
    row_act = lax.all_gather(act_two, "wide", axis=0, tiled=True)
    gate = jnp.dot(row_act, gate_slab, preferred_element_type=jnp.float32)
    upper = jnp.dot(row_act, up_slab, preferred_element_type=jnp.float32)
    hidden_full, swiglu_back = jax.vjp(swiglu, gate, upper)
    hidden = hidden_full.astype(jnp.bfloat16)
    mixed = lax.psum_scatter(
        contract_cols(hidden, down_slab).astype(jnp.bfloat16),
        "wide",
        scatter_dimension=0,
        tiled=True,
    ).astype(jnp.float32)
    result = (middle + mixed).astype(jnp.bfloat16)[None]
    grad_low = out_grad[0]
    row_grad = lax.all_gather(grad_low, "wide", axis=0, tiled=True)
    grad_down = contract_rows(row_grad, hidden)
    grad_hidden = jnp.dot(row_grad, down_slab, preferred_element_type=jnp.float32)
    grad_gate_full, grad_up_full = swiglu_back(grad_hidden)
    grad_gate_low = grad_gate_full.astype(jnp.bfloat16)
    grad_up_low = grad_up_full.astype(jnp.bfloat16)
    grad_gate = contract_rows(row_act, grad_gate_low)
    grad_up = contract_rows(row_act, grad_up_low)
    grad_act_two = lax.psum_scatter(
        (contract_cols(grad_gate_low, gate_slab) + contract_cols(grad_up_low, up_slab)).astype(
            jnp.bfloat16
        ),
        "wide",
        scatter_dimension=0,
        tiled=True,
    ).astype(jnp.float32)
    grad_middle_norm, grad_gain_two, grad_shift_two = norm_two_back(grad_act_two)
    grad_middle = grad_low.astype(jnp.float32) + grad_middle_norm
    branch_low = grad_middle.astype(jnp.bfloat16)
    grad_w_out = contract_rows(attn_low, branch_low)
    grad_attended = split_heads(contract_cols(branch_low, w_out_all).astype(jnp.bfloat16))

    def delta_step(totals, number):
        keys_blk, values_blk, visible, attn_probs = probs_of(number)
        grad_probs = jnp.einsum(
            "qhd,khd->hqk", grad_attended, values_blk, preferred_element_type=jnp.float32
        )
        return (totals + jnp.sum(attn_probs * grad_probs, axis=-1), None)

    delta, ignored = lax.scan(delta_step, start_sum, numbers)

    def grad_step(totals, number):
        keys_blk, values_blk, visible, attn_probs = probs_of(number)
        grad_probs = jnp.einsum(
            "qhd,khd->hqk", grad_attended, values_blk, preferred_element_type=jnp.float32
        )
        grad_scores = score_grads(attn_probs, grad_probs, visible, delta)
        totals = (
            totals
            + jnp.einsum("hqk,khd->qhd", grad_scores, keys_blk, preferred_element_type=jnp.float32)
            * score_scale
        )
        grad_keys_blk = (
            jnp.einsum("hqk,qhd->khd", grad_scores, query_low, preferred_element_type=jnp.float32)
            * score_scale
        )
        grad_values_blk = jnp.einsum(
            "hqk,qhd->khd",
            attn_probs.astype(jnp.bfloat16),
            grad_attended,
            preferred_element_type=jnp.float32,
        )
        return (
            totals,
            (
                grad_keys_blk.reshape(block_rows, model_width),
                grad_values_blk.reshape(block_rows, model_width),
            ),
        )

    grad_query, (key_parts, value_parts) = lax.scan(grad_step, head_zeros, numbers)
    grad_keys, grad_values = (
        lax.psum_scatter(
            key_parts.reshape(row_len, model_width).astype(jnp.bfloat16),
            "wide",
            scatter_dimension=0,
            tiled=True,
        ).astype(jnp.float32),
        lax.psum_scatter(
            value_parts.reshape(row_len, model_width).astype(jnp.bfloat16),
            "wide",
            scatter_dimension=0,
            tiled=True,
        ).astype(jnp.float32),
    )
    grad_query_raw = query_back(grad_query)[0]
    grad_key_raw = key_back(split_heads(grad_keys))[0]
    grad_proj = jnp.concatenate(
        [
            grad_query_raw.reshape(local_rows, model_width),
            grad_key_raw.reshape(local_rows, model_width),
            grad_values,
        ],
        axis=1,
    ).astype(jnp.bfloat16)
    grad_w_qkv = contract_rows(act_one, grad_proj)
    grad_b_qkv = jnp.sum(grad_proj, axis=0, dtype=jnp.float32)
    grad_act_one = contract_cols(grad_proj, w_qkv_all)
    grad_input_norm, grad_gain_one, grad_shift_one = norm_one_back(grad_act_one)
    grad_tokens = (grad_middle + grad_input_norm)[None]
    sums = (
        lax.psum_scatter(grad_w_qkv, ("rows", "wide"), scatter_dimension=0, tiled=True),
        lax.psum_scatter(grad_b_qkv, ("rows", "wide"), scatter_dimension=0, tiled=True),
        lax.psum_scatter(grad_w_out, ("rows", "wide"), scatter_dimension=0, tiled=True),
        lax.psum_scatter(grad_gain_one, ("rows", "wide"), scatter_dimension=0, tiled=True),
        lax.psum_scatter(grad_shift_one, ("rows", "wide"), scatter_dimension=0, tiled=True),
        lax.psum_scatter(grad_gain_two, ("rows", "wide"), scatter_dimension=0, tiled=True),
        lax.psum_scatter(grad_shift_two, ("rows", "wide"), scatter_dimension=0, tiled=True),
    )
    mlp_sums = (
        lax.psum_scatter(
            grad_gate.astype(jnp.bfloat16), "rows", scatter_dimension=0, tiled=True
        ).astype(jnp.float32),
        lax.psum_scatter(
            grad_up.astype(jnp.bfloat16), "rows", scatter_dimension=0, tiled=True
        ).astype(jnp.float32),
        lax.psum_scatter(
            grad_down.astype(jnp.bfloat16), "rows", scatter_dimension=0, tiled=True
        ).astype(jnp.float32),
    )
    return (
        result,
        grad_tokens,
        sums[0],
        sums[1],
        sums[2],
        sums[3],
        sums[4],
        sums[5],
        sums[6],
        mlp_sums[0],
        mlp_sums[1],
        mlp_sums[2],
    )


def solution(mesh):
    in_specs = (
        P("rows", "wide", None),
        P("rows", "wide"),
        P(("rows", "wide"), None),
        P(("rows", "wide")),
        P(("rows", "wide"), None),
        P(("rows", "wide")),
        P(("rows", "wide")),
        P(("rows", "wide")),
        P(("rows", "wide")),
        P("rows", "wide"),
        P("rows", "wide"),
        P("rows", "wide"),
        P("rows", "wide", None),
    )
    out_specs = (
        P("rows", "wide", None),
        P("rows", "wide", None),
        P(("rows", "wide"), None),
        P(("rows", "wide")),
        P(("rows", "wide"), None),
        P(("rows", "wide")),
        P(("rows", "wide")),
        P(("rows", "wide")),
        P(("rows", "wide")),
        P("rows", "wide"),
        P("rows", "wide"),
        P("rows", "wide"),
    )
    return jax.shard_map(shards, mesh=mesh, in_specs=in_specs, out_specs=out_specs, check_vma=False)
```

profile of v0, /device:TPU:0, one launch (start us, length us, event | category | flops | bytes accessed | tf_op | source)
XLA Modules:
  0.0 1911.5 jit_solution(6351771319849504466)
XLA Ops:
  13.4 43.4 %all-reduce.18 = (bf16[6144]{0:T(1024)(128)(2,1)S(1)}, bf16[2048]{0:T(1024)(128)(2,1)S(1)}, bf16[2048]{0:T(1024)(128)(2,1)S(1)}, bf16[2048]{0:T(1024)(128)(2,1)S(1)}, bf16[2048]{0:T(1024)(128)(2,1)S(1)}) all-reduce(bf16[6144]{0:T(1024)(128)(2,1)S(1)} %dynamic-update-slice.2, ...), channel_id=1, replica_groups=mesh['rows'=4,'wide'=8] {'rows','wide'}, use_global_device_ids=true, to_apply=%add.8 | all-reduce | flops 14336 | bytes 57344
  58.5 8.5 all-reduce.9
  70.3 99.7 %all-gather.11.cloned.1.call-done = bf16[2048,6144]{1,0:T(8,128)(2,1)} async-done(((bf16[64,6144]{1,0:T(8,128)(2,1)}), bf16[2048,6144]{1,0:T(8,128)(2,1)}) %all-gather.11.cloned.1.call-update) | async-done | bytes 25165840 | tf_op jit(solution)/shard_map/all_gather | solution.py:115
  170.0 10.9 convolution_add_fusion
  198.3 38.1 %all-gather.15.cloned.1.call-done = bf16[1536,2048]{1,0:T(8,128)(2,1)} async-done(((bf16[192,2048]{1,0:T(8,128)(2,1)}), bf16[1536,2048]{1,0:T(8,128)(2,1)}) %all-gather.15.cloned.1.call-update) | async-done | bytes 6291472 | tf_op jit(solution)/shard_map/all_gather | solution.py:141
  236.4 8.7 copy.73
  245.1 30.6 %while.50 = (s32[]{:T(128)}, f32[32,192]{1,0:T(8,128)S(1)}, f32[32,192]{1,0:T(8,128)S(1)}, s32[1,192]{1,0:T(1,128)S(1)}, s32[3]{0:T(128)S(1)}, /*index=5*/s32[15...) while((s32[]{:T(128)}, f32[32,192]{1,0:T(8,128)S(1)}, ...), condition=%wide.region_6.7_spmd.clone, body=%wide.region_3.6_spmd.clone.sunk | while | flops 428144832 | bytes 32872928 | solution.py:167
  251.4 4.0 select_reduce_fusion.2
  261.5 4.0 select_reduce_fusion.2
  275.7 8.7 all-gather.13.cloned.1.call-done
  284.4 8.5 copy.72
  292.9 40.5 %while.51 = (s32[]{:T(128)}, f32[192,32,64]{0,2,1:T(8,128)}, s32[3]{0:T(128)S(1)}, bf16[1536,2048]{0,1:T(8,128)(2,1)}, s32[1,192]{1,0:T(1,128)S(1)}, /*index=5*/...) while((s32[]{:T(128)}, f32[192,32,64]{0,2,1:T(8,128)}, ...), condition=%wide.region_8.9_spmd.clone, body=%wide.region_7.8_spmd.clone.sunk | while | flops 822116544 | bytes 16751081 | solution.py:189
  294.5 4.0 constant_dynamic-slice_fusion.13
  298.5 7.8 bitcast_add_fusion.4
  311.7 8.2 bitcast_add_fusion.4
  325.3 8.2 bitcast_add_fusion.4
  336.4 28.3 %all-gather.17.cloned.1.call-done = bf16[2048,2048]{1,0:T(8,128)(2,1)} async-done(((bf16[64,2048]{1,0:T(8,128)(2,1)}), bf16[2048,2048]{1,0:T(8,128)(2,1)}) %all-gather.17.cloned.1.call-update) | async-done | bytes 8388624 | tf_op jit(solution)/shard_map/all_gather | solution.py:117
  364.7 5.6 fusion.79
  374.5 49.4 %all-gather.23.cloned.1.call-done = bf16[2048,704]{0,1:T(8,128)(2,1)} async-done(((bf16[512,704]{0,1:T(8,128)(2,1)}), bf16[2048,704]{0,1:T(8,128)(2,1)}) %all-gather.23.cloned.1.call-update) | async-done | bytes 2883600 | tf_op jit(solution)/shard_map/all_gather | solution.py:198
  423.9 46.6 %all-gather.19.cloned.1.call-done = bf16[1536,2048]{1,0:T(8,128)(2,1)} async-done(((bf16[192,2048]{1,0:T(8,128)(2,1)}), bf16[1536,2048]{1,0:T(8,128)(2,1)}) %all-gather.19.cloned.1.call-update) | async-done | bytes 6291472 | tf_op jit(solution)/shard_map/all_gather | solution.py:201
  470.5 10.3 fusion.83
  480.8 50.4 %all-gather.21.cloned.1.call-done = bf16[2048,704]{0,1:T(8,128)(2,1)} async-done(((bf16[512,704]{0,1:T(8,128)(2,1)}), bf16[2048,704]{0,1:T(8,128)(2,1)}) %all-gather.21.cloned.1.call-update) | async-done | bytes 2883600 | tf_op jit(solution)/shard_map/all_gather | solution.py:197
  531.2 10.3 fusion.82
  541.6 49.1 %all-gather.25.cloned.1.call-done = bf16[2048,704]{0,1:T(8,128)(2,1)} async-done(((bf16[512,704]{0,1:T(8,128)(2,1)}), bf16[2048,704]{0,1:T(8,128)(2,1)}) %all-gather.25.cloned.1.call-update) | async-done | bytes 2883600 | tf_op jit(solution)/shard_map/all_gather | solution.py:199
  590.7 46.2 %all-gather.27.cloned.1.call-done = bf16[1,1536,2048]{2,1,0:T(8,128)(2,1)} async-done(((bf16[1,192,2048]{2,1,0:T(8,128)(2,1)}), bf16[1,1536,2048]{2,1,0:T(8,128)(2,1)}) %all-gather.27.cloned.1.call-update) | async-done | bytes 6291472 | tf_op jit(solution)/shard_map/all_gather | solution.py:214
  636.9 14.9 multiply_convert_fusion
  651.8 5.1 fusion.84
  656.9 8.7 add_convert_fusion
  665.7 9.2 convolution_convert_fusion
  675.1 52.4 %reduce-scatter.12.cloned.1.call-done = bf16[192,2048]{1,0:T(8,128)(2,1)} async-done(((bf16[1536,2048]{1,0:T(8,128)(2,1)}), bf16[192,2048]{1,0:T(8,128)(2,1)}) %reduce-scatter.12.cloned.1.call-update) | async-done | bytes 786448 | tf_op jit(solution)/shard_map/reduce_scatter | solution.py:222
  729.9 63.1 %reduce-scatter.10.cloned.1.call-done = bf16[192,2048]{1,0:T(8,128)(2,1)} async-done(((bf16[1536,2048]{1,0:T(8,128)(2,1)}), bf16[192,2048]{1,0:T(8,128)(2,1)}) %reduce-scatter.10.cloned.1.call-update) | async-done | bytes 786448 | tf_op jit(solution)/shard_map/reduce_scatter | solution.py:206
  798.2 6.3 convolution_convert_fusion.3
  805.8 36.7 %while.52 = (s32[]{:T(128)}, f32[32,192]{1,0:T(8,128)S(1)}, s32[1,192]{1,0:T(1,128)S(1)}, s32[3]{0:T(128)S(1)}, s32[1536]{0:T(1024)S(1)}, /*index=5*/s32[1536]{0...) while((s32[]{:T(128)}, f32[32,192]{1,0:T(8,128)S(1)}, ...), condition=%wide.region_17.18_spmd.clone, body=%wide.region_15.17_spmd.clone.sunk | while | flops 824481984 | bytes 39655920 | solution.py:243
  811.7 6.3 fusion.168
  823.9 6.3 fusion.168
  836.2 6.3 fusion.168
  842.5 132.8 %while.53 = (s32[]{:T(128)}, f32[192,32,64]{0,2,1:T(8,128)}, bf16[3,512,2048]{2,1,0:T(8,128)(2,1)}, bf16[3,512,2048]{2,1,0:T(8,128)(2,1)}, s32[3]{0:T(128)S(1)},...) while((s32[]{:T(128)}, f32[192,32,64]{0,2,1:T(8,128)}, ...), condition=%wide.region_19.20_spmd.clone, body=%wide.region_18.19_spmd.clone.sunk | while | flops 2057732352 | bytes 149281328 | solution.py:274
  849.8 4.5 copy-done
  854.3 6.1 fusion.181
  860.4 8.6 fusion.180
  892.8 4.5 copy-done
  897.3 6.1 fusion.181
  903.4 8.6 fusion.180
  912.0 5.0 bitcast_add_fusion.5
  926.6 4.0 constant_dynamic-update-slice_fusion.3
  937.5 4.5 copy-done
  942.0 6.1 fusion.181
  948.1 8.6 fusion.180
  956.7 5.0 bitcast_add_fusion.5
  971.3 4.1 constant_dynamic-update-slice_fusion.3
  977.0 8.7 fusion.48
  987.6 9.5 convolution_convert_fusion.1
  998.7 9.6 convolution_convert_fusion.2
  1009.7 8.1 fusion.85
  1020.5 16.7 reduce-scatter.14.cloned.1.call-done
  1043.8 58.9 %reduce-scatter.16.cloned.1.call-done = bf16[192,2048]{1,0:T(8,128)(2,1)} async-done(((bf16[1536,2048]{1,0:T(8,128)(2,1)}), bf16[192,2048]{1,0:T(8,128)(2,1)}) %reduce-scatter.16.cloned.1.call-update) | async-done | bytes 786448 | tf_op jit(solution)/shard_map/reduce_scatter | solution.py:282
  1102.8 21.3 %fusion.71 = f32[2048,6144]{1,0:T(8,128)} fusion(bf16[1,192,2048]{2,1,0:T(8,128)(2,1)S(1)} %copy-done.3, f32[2048]{0:T(1024)S(1)} %copy-done.18, f32[2048]{0:T(1024)S(1)} %copy-done.16, f32[192]{0:T(256)S(1)} %copy-done.26, f32[192]{0:T(256)S(1)} %copy-done.24, bf16[192,2048]{1,0:T(8,128)(2,1)} %reduce-scatter.16.cloned.1.call-done, ...), kind=kOutput, calls=%fused_computation.142 | convolution fusion | flops 4841275392 | bytes 53495296 | tf_op jit(solution)/shard_map/dot_general | solution.py:70
  1124.1 37.0 %reduce-scatter.26.cloned.1.call-done = bf16[512,704]{0,1:T(8,128)(2,1)} async-done(((bf16[2048,704]{0,1:T(8,128)(2,1)}), bf16[512,704]{0,1:T(8,128)(2,1)}) %reduce-scatter.26.cloned.1.call-update) | async-done | bytes 720912 | tf_op jit(solution)/shard_map/reduce_scatter | solution.py:320
  1163.5 55.8 %reduce-scatter.24.cloned.1.call-done = bf16[512,704]{0,1:T(8,128)(2,1)} async-done(((bf16[2048,704]{0,1:T(8,128)(2,1)}), bf16[512,704]{0,1:T(8,128)(2,1)}) %reduce-scatter.24.cloned.1.call-update) | async-done | bytes 720912 | tf_op jit(solution)/shard_map/reduce_scatter | solution.py:317
  1221.8 55.8 %reduce-scatter.22.cloned.1.call-done = bf16[512,704]{0,1:T(8,128)(2,1)} async-done(((bf16[2048,704]{0,1:T(8,128)(2,1)}), bf16[512,704]{0,1:T(8,128)(2,1)}) %reduce-scatter.22.cloned.1.call-update) | async-done | bytes 720912 | tf_op jit(solution)/shard_map/reduce_scatter | solution.py:314
  1280.4 14.2 fusion.76
  1297.0 44.3 %all-reduce.17 = (f32[6144]{0:T(1024)S(1)}, f32[2048]{0:T(1024)S(1)}, f32[2048]{0:T(1024)S(1)}, f32[2048]{0:T(1024)S(1)}, f32[2048]{0:T(1024)S(1)}) all-reduce(f32[6144]{0:T(1024)S(1)} %convert_reduce_fusion, f32[2048]{0:T(1024)S(1)} %get-tuple-element.610, ...), channel_id=8, replica_groups=mesh['rows'=4,'wide'=8] {'rows','wide'}, use_global_device_ids=true, to_apply=%region_26.27.clone | all-reduce | flops 14336 | bytes 114688
  1347.6 116.8 %reduce-scatter.20.cloned.1.call-done = f32[64,2048]{1,0:T(8,128)} async-done(((f32[2048,2048]{1,0:T(8,128)}), f32[64,2048]{1,0:T(8,128)}) %reduce-scatter.20.cloned.1.call-update) | async-done | bytes 524304 | tf_op jit(solution)/shard_map/reduce_scatter | solution.py:307
  1464.4 440.1 %reduce-scatter.18.cloned.1.call-done = f32[64,6144]{1,0:T(8,128)} async-done(((f32[2048,6144]{1,0:T(8,128)}), f32[64,6144]{1,0:T(8,128)}) %reduce-scatter.18.cloned.1.call-update) | async-done | bytes 1572880 | tf_op jit(solution)/shard_map/reduce_scatter | solution.py:305
  (305 shorter events, 176.9 us)
Async XLA Ops:
  7.2 62.1 %copy-start.1 = (bf16[1,192,2048]{2,1,0:T(8,128)(2,1)S(1)}, bf16[1,192,2048]{2,1,0:T(8,128)(2,1)}, u32[]{:S(2)}) copy-start(bf16[1,192,2048]{2,1,0:T(8,128)(2,1)} %param.21) | copy-start | bytes 2359300
  7.2 162.8 %all-gather.11.cloned.1.call-start = ((), (), s32[]{:S(2)}) async-start(), calls=%async_computation.9 | async-start | bytes 25952256 | tf_op jit(solution)/shard_map/all_gather | solution.py:115
  7.9 228.5 %all-gather.15.cloned.1.call-start = ((), (), s32[]{:S(2)}) async-start(), calls=%async_computation.11 | async-start | bytes 7077888 | tf_op jit(solution)/shard_map/all_gather | solution.py:141
  56.9 124.0 %copy-start.15 = (f32[2048]{0:T(1024)}, f32[2048]{0:T(1024)S(1)}, u32[]{:S(2)}) copy-start(f32[2048]{0:T(1024)S(1)} %convert_element_type.134) | copy-start | bytes 24580
  56.9 124.0 %copy-start.17 = (f32[2048]{0:T(1024)}, f32[2048]{0:T(1024)S(1)}, u32[]{:S(2)}) copy-start(f32[2048]{0:T(1024)S(1)} %convert_element_type.135) | copy-start | bytes 24580
  69.2 111.7 %copy-start.23 = (f32[192]{0:T(256)}, f32[192]{0:T(256)S(1)}, u32[]{:S(2)}) copy-start(f32[192]{0:T(256)S(1)} %broadcast_multiply_fusion.1) | copy-start | bytes 2308
  69.6 0.5 copy-start.31
  70.1 110.8 %copy-start.25 = (f32[192]{0:T(256)}, f32[192]{0:T(256)S(1)}, u32[]{:S(2)}) copy-start(f32[192]{0:T(256)S(1)} %fusion.69) | copy-start | bytes 2308
  70.3 119.4 %copy-start.19 = (f32[192,8]{0,1:T(8,128)}, f32[192,8]{0,1:T(8,128)S(1)}, u32[]{:S(2)}) copy-start(f32[192,8]{0,1:T(8,128)S(1)} %get-tuple-element.751) | copy-start | bytes 18436
  70.3 119.4 %copy-start.21 = (f32[192,8]{0,1:T(8,128)}, f32[192,8]{0,1:T(8,128)S(1)}, u32[]{:S(2)}) copy-start(f32[192,8]{0,1:T(8,128)S(1)} %get-tuple-element.752) | copy-start | bytes 18436
  181.0 2.6 copy-start.10
  192.5 91.9 %all-gather.13.cloned.1.call-start = ((), (), s32[]{:S(2)}) async-start(), calls=%async_computation.10 | async-start | bytes 7077888 | tf_op jit(solution)/shard_map/all_gather | solution.py:142
  195.0 169.7 %all-gather.17.cloned.1.call-start = ((), (), s32[]{:S(2)}) async-start(), calls=%async_computation.12 | async-start | bytes 8650752 | tf_op jit(solution)/shard_map/all_gather | solution.py:117
  195.6 228.3 %all-gather.23.cloned.1.call-start = ((), (), s32[]{:S(2)}) async-start(), calls=%async_computation.15 | async-start | bytes 3604480 | tf_op jit(solution)/shard_map/all_gather | solution.py:198
  196.2 274.3 %all-gather.19.cloned.1.call-start = ((), (), s32[]{:S(2)}) async-start(), calls=%async_computation.13 | async-start | bytes 7077888 | tf_op jit(solution)/shard_map/all_gather | solution.py:201
  198.3 46.8 %copy-start.14 = (s32[1,192]{1,0:T(1,128)S(1)}, s32[1,192]{1,0:T(1,128)}, u32[]{:S(2)}) copy-start(s32[1,192]{1,0:T(1,128)} %param.22) | copy-start | bytes 2308
  333.5 31.3 %copy-start.2 = (bf16[1,192,2048]{2,1,0:T(8,128)(2,1)S(1)}, bf16[1,192,2048]{2,1,0:T(8,128)(2,1)}, u32[]{:S(2)}) copy-start(bf16[1,192,2048]{2,1,0:T(8,128)(2,1)} %param.21) | copy-start | bytes 2359300
  372.0 159.3 %all-gather.21.cloned.1.call-start = ((), (), s32[]{:S(2)}) async-start(), calls=%async_computation.14 | async-start | bytes 3604480 | tf_op jit(solution)/shard_map/all_gather | solution.py:197
  372.7 218.0 %all-gather.25.cloned.1.call-start = ((), (), s32[]{:S(2)}) async-start(), calls=%async_computation.16 | async-start | bytes 3604480 | tf_op jit(solution)/shard_map/all_gather | solution.py:199
  373.5 263.4 %all-gather.27.cloned.1.call-start = ((), (), s32[]{:S(2)}) async-start(), calls=%async_computation.26 | async-start | bytes 7077888 | tf_op jit(solution)/shard_map/all_gather | solution.py:214
  374.2 353.3 %reduce-scatter.12.cloned.1.call-start = ((), (), s32[]{:S(2)}) async-start(), calls=%async_computation.18 | async-start | bytes 7077888 | tf_op jit(solution)/shard_map/reduce_scatter | solution.py:222
  636.9 14.9 copy-start.34
  651.8 5.1 copy-start.35
  651.8 5.1 copy-start.33
  665.6 127.4 %reduce-scatter.10.cloned.1.call-start = ((), (), s32[]{:S(2)}) async-start(), calls=%async_computation.17 | async-start | bytes 7077888 | tf_op jit(solution)/shard_map/reduce_scatter | solution.py:206
  674.8 362.4 %reduce-scatter.14.cloned.1.call-start = ((), (), s32[]{:S(2)}) async-start(), calls=%async_computation.19 | async-start | bytes 7077888 | tf_op jit(solution)/shard_map/reduce_scatter | solution.py:276
  729.9 67.1 %copy-start.7 = (bf16[1,192,2048]{2,1,0:T(8,128)(2,1)S(1)}, bf16[1,192,2048]{2,1,0:T(8,128)(2,1)}, u32[]{:S(2)}) copy-start(bf16[1,192,2048]{2,1,0:T(8,128)(2,1)} %param.33) | copy-start | bytes 2359300
  795.9 1.1 copy-start.4
  795.9 8.6 copy-start.29
  797.3 0.9 copy-start.11
  849.8 4.5 copy-start
  892.8 4.5 copy-start
  937.5 4.5 copy-start
  975.3 127.4 %reduce-scatter.16.cloned.1.call-start = ((), (), s32[]{:S(2)}) async-start(), calls=%async_computation.20 | async-start | bytes 7077888 | tf_op jit(solution)/shard_map/reduce_scatter | solution.py:282
  975.4 1.6 copy-start.38
  976.1 185.0 %reduce-scatter.26.cloned.1.call-start = ((), (), s32[]{:S(2)}) async-start(), calls=%async_computation.25 | async-start | bytes 3604480 | tf_op jit(solution)/shard_map/reduce_scatter | solution.py:320
  985.7 1.9 copy-start.37
  985.7 233.6 %reduce-scatter.24.cloned.1.call-start = ((), (), s32[]{:S(2)}) async-start(), calls=%async_computation.24 | async-start | bytes 3604480 | tf_op jit(solution)/shard_map/reduce_scatter | solution.py:317
  997.1 1.6 copy-start.36
  997.1 280.5 %reduce-scatter.22.cloned.1.call-start = ((), (), s32[]{:S(2)}) async-start(), calls=%async_computation.23 | async-start | bytes 3604480 | tf_op jit(solution)/shard_map/reduce_scatter | solution.py:314
  1008.3 1.2 copy-start.6
  1008.3 1.4 copy-start.12
  1008.3 456.1 %reduce-scatter.20.cloned.1.call-start = ((), (), s32[]{:S(2)}) async-start(), calls=%async_computation.22 | async-start | bytes 17301504 | tf_op jit(solution)/shard_map/reduce_scatter | solution.py:307
  1017.8 886.6 %reduce-scatter.18.cloned.1.call-start = ((), (), s32[]{:S(2)}) async-start(), calls=%async_computation.21 | async-start | bytes 51904512 | tf_op jit(solution)/shard_map/reduce_scatter | solution.py:305
  1038.7 0.7 copy-start.20
  1038.7 0.7 copy-start.22
  1038.7 1.9 copy-start.9
  1041.8 60.9 %copy-start.3 = (bf16[1,192,2048]{2,1,0:T(8,128)(2,1)S(1)}, bf16[1,192,2048]{2,1,0:T(8,128)(2,1)}, u32[]{:S(2)}) copy-start(bf16[1,192,2048]{2,1,0:T(8,128)(2,1)} %param.21) | copy-start | bytes 2359300
  1041.8 60.9 %copy-start.16 = (f32[2048]{0:T(1024)S(1)}, f32[2048]{0:T(1024)}, u32[]{:S(2)}) copy-start(f32[2048]{0:T(1024)} %copy-done.15) | copy-start | bytes 24580
  1041.8 60.9 %copy-start.18 = (f32[2048]{0:T(1024)S(1)}, f32[2048]{0:T(1024)}, u32[]{:S(2)}) copy-start(f32[2048]{0:T(1024)} %copy-done.17) | copy-start | bytes 24580
  1041.8 60.9 %copy-start.24 = (f32[192]{0:T(256)S(1)}, f32[192]{0:T(256)}, u32[]{:S(2)}) copy-start(f32[192]{0:T(256)} %copy-done.23) | copy-start | bytes 2308
  1041.8 60.9 %copy-start.26 = (f32[192]{0:T(256)S(1)}, f32[192]{0:T(256)}, u32[]{:S(2)}) copy-start(f32[192]{0:T(256)} %copy-done.25) | copy-start | bytes 2308
  1163.5 116.5 %copy-start.13 = (bf16[192,2048]{1,0:T(8,128)(2,1)S(1)}, bf16[192,2048]{1,0:T(8,128)(2,1)}, u32[]{:S(2)}) copy-start(bf16[192,2048]{1,0:T(8,128)(2,1)} %reduce-scatter.16.cloned.1.call-done) | copy-start | bytes 2359300
  1280.4 14.3 copy-start.32
  1294.6 2.4 copy-start.27
  1294.6 2.4 copy-start.28
  1294.6 49.7 %copy-start.5 = (f32[192,2048]{1,0:T(8,128)S(1)}, f32[192,2048]{1,0:T(8,128)}, u32[]{:S(2)}) copy-start(f32[192,2048]{1,0:T(8,128)} %copy-done.4) | copy-start | bytes 4718596
  1294.6 49.7 %copy-start.8 = (bf16[1,192,2048]{2,1,0:T(8,128)(2,1)S(1)}, bf16[1,192,2048]{2,1,0:T(8,128)(2,1)}, u32[]{:S(2)}) copy-start(bf16[1,192,2048]{2,1,0:T(8,128)(2,1)} %param.33) | copy-start | bytes 2359300
  1294.6 49.7 %copy-start.30 = (f32[192]{0:T(256)S(1)}, f32[192]{0:T(256)}, u32[]{:S(2)}) copy-start(f32[192]{0:T(256)} %copy-done.29) | copy-start | bytes 2308
Sparse Core Ops, SparseCore 0:
  10.9 159.0 all-gather.10
  192.6 43.6 all-gather.14
  238.9 45.5 all-gather.12
  287.1 77.5 all-gather.16
  366.1 57.7 all-gather.22
  426.2 44.2 all-gather.18
  472.1 59.1 all-gather.20
  532.8 57.8 all-gather.24
  592.6 44.2 all-gather.26
  665.7 61.7 reduce-scatter.11
  731.3 61.7 reduce-scatter.9
  975.5 61.7 reduce-scatter.13
  1041.0 61.7 reduce-scatter.15
  1104.9 56.1 reduce-scatter.25
  1163.3 56.0 reduce-scatter.23
  1221.5 56.0 reduce-scatter.21
  1280.3 184.0 reduce-scatter.19
  1471.2 433.1 reduce-scatter.17
where the time goes:
time: 1920 us; the launch traced here: 1910 us
  waiting for transfers between devices  1320 us (69%)
  matrix products  280 us (15%)
  local copies, waits for them, and re-layouts  147 us (8%)
  blocking collectives  96.2 us (5%)
  other arithmetic  44.1 us (2%)
    reduce_scatter x1, waiting for transfers between devices, shards(): lax.psum_scatter(grad_w_qkv, ('rows', 'wide'), scatter_dimension=0, tiled...  440 us
    reduce_scatter x1, waiting for transfers between devices, shards(): lax.psum_scatter(grad_w_out, ('rows', 'wide'), scatter_dimension=0, tiled...  117 us
    all_gather x1, waiting for transfers between devices, shards(): lax.all_gather(w_qkv, ('rows', 'wide'), axis=0, tiled=True)  99.7 us
    unnamed x2, blocking collectives  87.8 us
    reduce_scatter x1, waiting for transfers between devices, shards(): lax.psum_scatter(contract_cols(hidden, down_slab).astype(jnp.bfloat16), '...  63.1 us
    reduce_scatter x1, waiting for transfers between devices, shards(): lax.psum_scatter(value_parts.reshape(row_len, model_width).astype(jnp.bfl...  58.9 us
    dot_general x5, matrix products, contract_rows(): lax.dot_general(left, right, (((0,), (0,)), ((), ())), preferred_element_...  57.1 us
    reduce_scatter x1, waiting for transfers between devices, shards(): lax.psum_scatter(grad_gate.astype(jnp.bfloat16), 'rows', scatter_dimensio...  55.8 us
  transfers between devices with their start and end apart: 18, of which 18 were waited for; matrix products, arithmetic and copies ran while one was open for 12% of the time, Pallas kernels for 0%

commit v1 on v0

v1 whole, which is shorter than its diff:
```python
import functools
import math

import jax
import jax.numpy as jnp
from jax import lax
from jax.experimental import pallas as pl
from jax.experimental.pallas import tpu as pltpu
from jax.sharding import PartitionSpec as P

HEADS = 32
HEAD_DIM = 64
ROT = 16
PAIR = 2 * HEAD_DIM

epsilon = 1e-05
neg_large = -1e30
BF = jnp.bfloat16
F32 = jnp.float32
ALL = ("rows", "wide")
NT = (((1,), (1,)), ((), ()))
TN = (((0,), (0,)), ((), ()))


def dot(left, right, dims=(((1,), (0,)), ((), ()))):
    return lax.dot_general(left, right, dims, preferred_element_type=F32)


def swap(x, bit, axis="wide"):
    return lax.ppermute(x, axis, [(i, i ^ bit) for i in range(lax.axis_size(axis))])


def upper_bits():
    return [1 << k for k in range(1, lax.axis_size("wide").bit_length() - 1)]


def gather_plane(x):
    bits = upper_bits()
    if len(bits) == 2:
        half = x.shape[0] // 2
        one, two = bits
        top, low = x[:half], x[half:]
        top_two, low_one = swap(top, two), swap(low, one)
        low_two, top_one = swap(low, two), swap(top, one)
        top_both, low_both = swap(top_two, one), swap(low_one, two)
        own = jnp.concatenate(
            [top, low, top_one, low_one, top_two, low_two, top_both, low_both]
        )
    else:
        own = x
        for bit in bits:
            own = jnp.concatenate([own, swap(own, bit)])
    return own, swap(own, 1)


def add_low(left, right):
    return (left.astype(F32) + right.astype(F32)).astype(BF)


def scatter_plane(own, other):
    bits = upper_bits()
    got = swap(other, 1)
    total = add_low(own, got)
    if len(bits) == 2:
        one, two = bits
        half = total.shape[0] // 8

        def part(m, h):
            return total[(2 * m + h) * half : (2 * m + h + 1) * half]

        far_top, far_low = swap(part(3, 0), one), swap(part(3, 1), two)
        top_one, low_two = swap(part(1, 0), one), swap(part(2, 1), two)
        top_two = swap(add_low(part(2, 0), far_top), two)
        low_one = swap(add_low(part(1, 1), far_low), one)
        return jnp.concatenate(
            [
                part(0, 0).astype(F32) + top_one.astype(F32) + top_two.astype(F32),
                part(0, 1).astype(F32) + low_one.astype(F32) + low_two.astype(F32),
            ]
        )
    for bit in reversed(bits[1:]):
        half = total.shape[0] // 2
        total = add_low(total[:half], swap(total[half:], bit))
    half = total.shape[0] // 2
    return total[:half].astype(F32) + swap(total[half:], bits[0]).astype(F32)


def to_relative(x):
    count = lax.axis_size("wide")
    me = lax.axis_index("wide")
    blocks = x.reshape(count, x.shape[0] // count, x.shape[1])

    def pick(first):
        return jnp.concatenate(
            [
                lax.dynamic_index_in_dim(blocks, me ^ m, 0, keepdims=False)
                for m in range(first, count, 2)
            ]
        )

    return pick(0), pick(1)


def to_absolute(own, other):
    count = lax.axis_size("wide")
    me = lax.axis_index("wide")
    half = count // 2
    blocks = jnp.concatenate([own, other]).reshape(count, -1, own.shape[1])
    pieces = []
    for place in range(count):
        m = me ^ place
        pieces.append(
            lax.dynamic_index_in_dim(blocks, (m & 1) * half + (m >> 1), 0, keepdims=False)
        )
    return jnp.concatenate(pieces)


def scatter_small(x):
    count_rows, count_wide = lax.axis_size("rows"), lax.axis_size("wide")
    me_rows, me_wide = lax.axis_index("rows"), lax.axis_index("wide")
    width = x.shape[1]
    x = x.reshape(count_rows, count_wide * width)
    size = count_rows // 2
    while size >= 1:
        side = (me_rows // size) % 2
        halves = x.reshape(2, -1, x.shape[1])
        keep = lax.dynamic_index_in_dim(halves, side, 0, keepdims=False)
        give = lax.dynamic_index_in_dim(halves, 1 - side, 0, keepdims=False)
        x = keep + swap(give, size, "rows")
        size //= 2
    x = x.reshape(count_wide, width)
    size = count_wide // 2
    while size >= 1:
        side = (me_wide // size) % 2
        halves = x.reshape(2, -1, x.shape[1])
        keep = lax.dynamic_index_in_dim(halves, side, 0, keepdims=False)
        give = lax.dynamic_index_in_dim(halves, 1 - side, 0, keepdims=False)
        x = keep + swap(give, size, "wide")
        size //= 2
    return x.reshape(width)


def turn_lanes(x, cosine, ahead, behind):
    half_rot = ROT // 2
    lanes = x.shape[-1]
    return (
        x * cosine
        + pltpu.roll(x, lanes - half_rot, 1) * ahead
        + pltpu.roll(x, half_rot, 1) * behind
    )


def project_kernel(
    order, own_ref, other_ref, gain, shift, weight, bias, cosine, ahead, behind, act, q, k, v
):
    count = pl.num_programs(0)
    step = pl.program_id(0)
    width = q.shape[1]

    def work(x_ref):
        x = x_ref[...].astype(F32)
        centred = x - jnp.mean(x, axis=1, keepdims=True)
        spread = jnp.mean(centred * centred, axis=1, keepdims=True)
        normed = (centred * lax.rsqrt(spread + epsilon) * gain[...] + shift[...]).astype(BF)
        act[...] = normed
        projected = dot(normed, weight[...]) + bias[...]
        for at in range(0, width, PAIR):
            angles = (cosine[...], ahead[...], behind[...])
            q[:, at : at + PAIR] = turn_lanes(projected[:, at : at + PAIR], *angles).astype(BF)
            k[:, at : at + PAIR] = turn_lanes(
                projected[:, width + at : width + at + PAIR], *angles
            ).astype(BF)
        v[...] = projected[:, 2 * width :].astype(BF)

    @pl.when(step < count // 2)
    def _():
        work(own_ref)

    @pl.when(step >= count // 2)
    def _():
        work(other_ref)


def project(own, other, gain, shift, weight, bias, tables):
    count = lax.axis_size("wide")
    half = count // 2
    rows = own.shape[0] // half
    depth, columns = weight.shape
    width = columns // 3
    total = rows * count
    me = lax.axis_index("wide")
    order = jnp.stack([me ^ m for m in list(range(0, count, 2)) + list(range(1, count, 2))])

    def whole(i, order):
        return (0, 0)

    def placed(i, order):
        return (order[i], 0)

    vec = pl.BlockSpec((1, depth), whole)
    table = pl.BlockSpec((rows, PAIR), placed)
    out = pl.BlockSpec((rows, width), placed)
    return pl.pallas_call(
        project_kernel,
        grid_spec=pltpu.PrefetchScalarGridSpec(
            num_scalar_prefetch=1,
            grid=(count,),
            in_specs=[
                pl.BlockSpec((rows, depth), lambda i, order: (jnp.minimum(i, half - 1), 0)),
                pl.BlockSpec((rows, depth), lambda i, order: (jnp.maximum(i - half, 0), 0)),
                vec,
                vec,
                pl.BlockSpec((depth, columns), whole),
                pl.BlockSpec((1, columns), whole),
                table,
                table,
                table,
            ],
            out_specs=[pl.BlockSpec((rows, depth), placed), out, out, out],
        ),
        out_shape=[
            jax.ShapeDtypeStruct((total, depth), BF),
            jax.ShapeDtypeStruct((total, width), BF),
            jax.ShapeDtypeStruct((total, width), BF),
            jax.ShapeDtypeStruct((total, width), BF),
        ],
        cost_estimate=pl.CostEstimate(
            flops=2 * total * depth * columns,
            bytes_accessed=2 * (2 * total * depth + total * columns + depth * columns),
            transcendentals=0,
        ),
        compiler_params=pltpu.CompilerParams(
            dimension_semantics=("arbitrary",), vmem_limit_bytes=48 * 2**20
        ),
        name="project",
    )(order, own, other, gain, shift, weight, bias, *tables)


def head_mask(head, shape):
    lane = lax.broadcasted_iota(jnp.int32, shape, 1)
    return (lane // HEAD_DIM) == head


def attend_kernel(first, q_ref, k_ref, v_ref, o_ref, log_ref, v_turned):
    block = q_ref.shape[0]
    at = pl.program_id(1)
    scale = HEAD_DIM ** (-0.5)

    @pl.when(at == 0)
    def _():
        v_turned[...] = v_ref[...].astype(F32).T.astype(BF)

    q = q_ref[...] * jnp.asarray(scale, BF)
    queries = [jnp.where(head_mask(h, q.shape), q, jnp.zeros_like(q)) for h in range(2)]
    own_first = first[...]
    own_place = at * block + lax.broadcasted_iota(jnp.int32, (1, block), 1)

    def step(number, state):
        keys = k_ref[pl.ds(number * block, block), :]
        values = v_turned[:, pl.ds(number * block, block)]
        place = number * block + lax.broadcasted_iota(jnp.int32, (block, block), 0)
        visible = (place >= own_first) & (place <= own_place)
        out = []
        for h in range(2):
            peak, total, mix = state[h]
            scores = jnp.where(visible, dot(keys, queries[h], NT), neg_large)
            new_peak = jnp.maximum(peak, jnp.max(scores, axis=0, keepdims=True))
            terms = jnp.where(visible, jnp.exp(scores - new_peak), 0.0)
            decay = jnp.exp(peak - new_peak)
            out.append(
                (
                    new_peak,
                    total * decay + jnp.sum(terms, axis=0, keepdims=True),
                    mix * decay
                    + dot(values[h * HEAD_DIM : (h + 1) * HEAD_DIM], terms.astype(BF)),
                )
            )
        return tuple(out)

    start = (
        jnp.full((1, block), neg_large, F32),
        jnp.zeros((1, block), F32),
        jnp.zeros((HEAD_DIM, block), F32),
    )
    state = lax.fori_loop(0, at + 1, step, (start, start))
    mixes = []
    for h in range(2):
        peak, total, mix = state[h]
        mixes.append(mix / total)
        log_ref[0, h : h + 1, :] = peak + jnp.log(total)
    o_ref[...] = jnp.concatenate(mixes, axis=0).T.astype(BF)


def attend(first, q, k, v):
    total, width = q.shape
    pairs = width // PAIR
    block = math.gcd(total, 256)
    return pl.pallas_call(
        attend_kernel,
        grid=(pairs, total // block),
        in_specs=[
            pl.BlockSpec((1, block), lambda p, i: (0, i)),
            pl.BlockSpec((block, PAIR), lambda p, i: (i, p)),
            pl.BlockSpec((total, PAIR), lambda p, i: (0, p)),
            pl.BlockSpec((total, PAIR), lambda p, i: (0, p)),
        ],
        out_specs=[
            pl.BlockSpec((block, PAIR), lambda p, i: (i, p)),
            pl.BlockSpec((1, 2, block), lambda p, i: (p, 0, i)),
        ],
        out_shape=[
            jax.ShapeDtypeStruct((total, width), BF),
            jax.ShapeDtypeStruct((pairs, 2, total), F32),
        ],
        scratch_shapes=[pltpu.VMEM((PAIR, total), BF)],
        cost_estimate=pl.CostEstimate(
            flops=8 * total * total * width,
            bytes_accessed=8 * total * width,
            transcendentals=total * total * width // PAIR,
        ),
        compiler_params=pltpu.CompilerParams(
            dimension_semantics=("arbitrary", "arbitrary"), vmem_limit_bytes=32 * 2**20
        ),
        name="attend",
    )(first, q, k, v)


def attend_back_kernel(
    first, q_ref, k_ref, v_ref, o_ref, g_ref, log_ref, cosine, ahead, behind,
    gq_ref, gk_ref, gv_ref, k_turned, delta, sum_q,
):
    total = q_ref.shape[0]
    block = k_ref.shape[0]
    at = pl.program_id(1)
    last = pl.num_programs(1)
    scale = HEAD_DIM ** (-0.5)
    k = k_ref[...]
    k_turned[...] = k.astype(F32).T.astype(BF)

    @pl.when(at == 0)
    def _():
        sum_q[...] = jnp.zeros_like(sum_q)

        def fill(number, carry):
            spot = pl.ds(number * block, block)
            both = (g_ref[spot, :].astype(F32) * o_ref[spot, :].astype(F32)).T
            for h in range(2):
                delta[h : h + 1, spot] = jnp.sum(
                    both[h * HEAD_DIM : (h + 1) * HEAD_DIM], axis=0, keepdims=True
                )
            return carry

        lax.fori_loop(0, last, fill, 0)

    v = v_ref[...]
    place = at * block + lax.broadcasted_iota(jnp.int32, (block, block), 0)

    def step(number, state):
        sum_k, sum_v = state
        spot = pl.ds(number * block, block)
        q = q_ref[spot, :] * jnp.asarray(scale, BF)
        g = g_ref[spot, :]
        own_place = number * block + lax.broadcasted_iota(jnp.int32, (1, block), 1)
        visible = (place >= first[:, spot]) & (place <= own_place)
        for h in range(2):
            mask = head_mask(h, q.shape)
            q_head = jnp.where(mask, q, jnp.zeros_like(q))
            g_head = jnp.where(mask, g, jnp.zeros_like(g))
            scores = dot(k, q_head, NT)
            probs = jnp.where(
                visible,
                jnp.exp(jnp.where(visible, scores - log_ref[0, h : h + 1, spot], neg_large)),
                0.0,
            )
            slopes = dot(v, g_head, NT)
            low = (probs * (slopes - delta[h : h + 1, spot])).astype(BF)
            sum_v = sum_v + dot(probs.astype(BF), g_head)
            sum_k = sum_k + dot(low, q_head)
            span = slice(h * HEAD_DIM, (h + 1) * HEAD_DIM)
            sum_q[span, spot] += dot(k_turned[span, :], low)
        return (sum_k, sum_v)

    zeros = jnp.zeros((block, PAIR), F32)
    sum_k, sum_v = lax.fori_loop(at, last, step, (zeros, zeros))
    gv_ref[...] = sum_v.astype(BF)
    mine = pl.ds(at * block, block)
    gk_ref[...] = turn_lanes(sum_k, cosine[mine, :], -ahead[mine, :], -behind[mine, :]).astype(BF)

    @pl.when(at == last - 1)
    def _():
        def finish(number, carry):
            spot = pl.ds(number * block, block)
            gq_ref[spot, :] = turn_lanes(
                sum_q[:, spot].T * scale, cosine[spot, :], -ahead[spot, :], -behind[spot, :]
            ).astype(BF)
            return carry

        lax.fori_loop(0, last, finish, 0)


def attend_back(first, q, k, v, o, g, logs, tables):
    total, width = q.shape
    pairs = width // PAIR
    block = math.gcd(total, 256)
    whole = pl.BlockSpec((total, PAIR), lambda p, i: (0, p))
    part = pl.BlockSpec((block, PAIR), lambda p, i: (i, p))
    table = pl.BlockSpec((total, PAIR), lambda p, i: (0, 0))
    shape = jax.ShapeDtypeStruct((total, width), BF)
    return pl.pallas_call(
        attend_back_kernel,
        grid=(pairs, total // block),
        in_specs=[
            pl.BlockSpec((1, total), lambda p, i: (0, 0)),
            whole,
            part,
            part,
            whole,
            whole,
            pl.BlockSpec((1, 2, total), lambda p, i: (p, 0, 0)),
            table,
            table,
            table,
        ],
        out_specs=[whole, part, part],
        out_shape=[shape, shape, shape],
        scratch_shapes=[
            pltpu.VMEM((PAIR, block), BF),
            pltpu.VMEM((2, total), F32),
            pltpu.VMEM((PAIR, total), F32),
        ],
        cost_estimate=pl.CostEstimate(
            flops=20 * total * total * width,
            bytes_accessed=16 * total * width,
            transcendentals=total * total * width // PAIR,
        ),
        compiler_params=pltpu.CompilerParams(
            dimension_semantics=("arbitrary", "arbitrary"), vmem_limit_bytes=48 * 2**20
        ),
        name="attend_back",
    )(first, q, k, v, o, g, logs, *tables)


def norm_parts(values):
    centred = values - jnp.mean(values, axis=-1, keepdims=True)
    spread = jnp.mean(centred * centred, axis=-1, keepdims=True)
    rate = lax.rsqrt(spread + epsilon)
    return centred * rate, rate


def norm_back(incoming, unit, rate, gain):
    scaled = incoming * gain
    return (
        rate
        * (
            scaled
            - jnp.mean(scaled, axis=-1, keepdims=True)
            - unit * jnp.mean(scaled * unit, axis=-1, keepdims=True)
        ),
        jnp.sum(incoming * unit, axis=0),
        jnp.sum(incoming, axis=0),
    )


def shards(
    tokens,
    segments,
    w_qkv,
    b_qkv,
    w_out,
    ln1_gain,
    ln1_bias,
    ln2_gain,
    ln2_bias,
    w_gate,
    w_up,
    w_down,
    out_grad,
):
    rows_n, wide_n = lax.axis_size("rows"), lax.axis_size("wide")
    me_row, me = lax.axis_index("rows"), lax.axis_index("wide")
    devices = rows_n * wide_n
    local = tokens.shape[1]
    width = tokens.shape[2]
    row_len = local * wide_n
    per = HEADS // wide_n
    span = per * HEAD_DIM
    slab = width // devices
    bias_slab = 3 * width // devices

    packed = jnp.concatenate(
        [b_qkv, ln1_gain, ln1_bias, ln2_gain, ln2_bias, segments[0].astype(BF)]
    )
    small = lax.all_gather(lax.all_gather(packed, "rows"), "wide")
    flat = small.transpose(1, 0, 2)

    def vector(start, size):
        return flat[:, :, start : start + size].reshape(1, devices * size).astype(F32)

    bias = vector(0, bias_slab)
    gain_one = vector(bias_slab, slab)
    shift_one = vector(bias_slab + slab, slab)
    gain_two = vector(bias_slab + 2 * slab, slab)
    shift_two = vector(bias_slab + 3 * slab, slab)
    row_segs = lax.dynamic_index_in_dim(small, me_row, 1, keepdims=False)[
        :, bias_slab + 4 * slab :
    ].reshape(row_len)
    own_bias = lax.dynamic_index_in_dim(
        bias.reshape(3, per, wide_n, HEAD_DIM), me, 2, keepdims=False
    ).reshape(1, 3 * span)

    doc_first = jnp.sum((row_segs[:, None] < row_segs[None, :]).astype(jnp.int32), axis=0)
    positions = jnp.arange(row_len, dtype=jnp.int32) - doc_first
    freqs = 10000.0 ** (-2.0 * jnp.arange(ROT // 2, dtype=F32) / ROT)
    lane = jnp.arange(PAIR) % HEAD_DIM
    lane_freqs = jnp.where(lane < ROT, jnp.tile(freqs, PAIR // (ROT // 2)), 0.0)
    angles = positions.astype(F32)[:, None] * lane_freqs[None, :]
    sine = jnp.sin(angles)
    half_rot = ROT // 2
    tables = (
        jnp.cos(angles),
        jnp.where(lane < half_rot, -sine, 0.0),
        jnp.where((lane >= half_rot) & (lane < ROT), sine, 0.0),
    )
    first = doc_first.reshape(1, row_len)

    fast_out = slab == HEAD_DIM and per == rows_n
    if fast_out:
        w_out_own = lax.all_gather(w_out, "rows", axis=0, tiled=True)
    else:
        w_out_own = lax.dynamic_index_in_dim(
            lax.all_gather(w_out, ALL, axis=0, tiled=True).reshape(
                per, wide_n, HEAD_DIM, width
            ),
            me,
            1,
            keepdims=False,
        ).reshape(span, width)
    by_head = w_qkv.reshape(slab, 3 * per, wide_n, HEAD_DIM).transpose(2, 0, 1, 3)
    w_qkv_part = lax.all_to_all(
        by_head.reshape(wide_n * slab, 3 * span), "wide", 0, 0, tiled=True
    )
    w_qkv_own = lax.all_gather(w_qkv_part, "rows", axis=0, tiled=True)
    gate_slab, up_slab, down_slab = (
        lax.all_gather(w_gate, "rows", axis=0, tiled=True),
        lax.all_gather(w_up, "rows", axis=0, tiled=True),
        lax.all_gather(w_down, "rows", axis=0, tiled=True),
    )

    own, other = gather_plane(tokens[0])
    act_one, q, k, v = project(
        own, other, gain_one, shift_one, w_qkv_own, own_bias, tables
    )
    attn_low, logs = attend(first, q, k, v)
    attn_own, attn_other = to_relative(attn_low)
    inputs = tokens[0].astype(F32)
    middle = inputs + scatter_plane(
        dot(attn_own, w_out_own).astype(BF), dot(attn_other, w_out_own).astype(BF)
    )
    unit_two, rate_two = norm_parts(middle)
    act_two = (unit_two * gain_two + shift_two).astype(BF)
    row_act = jnp.concatenate(gather_plane(act_two))
    grad_low = out_grad[0]
    row_grad = jnp.concatenate(gather_plane(grad_low))
    middle_row = row_act.shape[0] // 2

    gate = dot(row_act, gate_slab)
    upper = dot(row_act, up_slab)
    sig = jax.nn.sigmoid(gate)
    silu = gate * sig
    hidden = (silu * upper).astype(BF)
    mixed_part = dot(hidden, down_slab, NT).astype(BF)
    mixed = scatter_plane(mixed_part[:middle_row], mixed_part[middle_row:])
    result = (middle + mixed).astype(BF)[None]

    grad_down = dot(row_grad, hidden, TN)
    grad_hidden = dot(row_grad, down_slab)
    grad_gate_low = (grad_hidden * upper * sig * (1.0 + gate * (1.0 - sig))).astype(BF)
    grad_up_low = (grad_hidden * silu).astype(BF)
    grad_gate = dot(row_act, grad_gate_low, TN)
    grad_up = dot(row_act, grad_up_low, TN)
    act_part = (
        dot(grad_gate_low, gate_slab, NT) + dot(grad_up_low, up_slab, NT)
    ).astype(BF)
    grad_act_two = scatter_plane(act_part[:middle_row], act_part[middle_row:])
    grad_norm, grad_gain_two, grad_shift_two = norm_back(
        grad_act_two, unit_two, rate_two, gain_two
    )
    grad_middle = grad_low.astype(F32) + grad_norm
    branch_own, branch_other = gather_plane(grad_middle.astype(BF))
    branch = jnp.concatenate([branch_own, branch_other])
    grad_w_out = dot(jnp.concatenate([attn_own, attn_other]), branch, TN)
    grad_attn = to_absolute(
        dot(branch_own, w_out_own, NT).astype(BF), dot(branch_other, w_out_own, NT).astype(BF)
    )
    grad_q, grad_k, grad_v = attend_back(first, q, k, v, attn_low, grad_attn, logs, tables)
    grad_proj = jnp.concatenate([grad_q, grad_k, grad_v], axis=1)
    grad_w_qkv = dot(act_one, grad_proj, TN)
    grad_bias = jnp.sum(grad_proj, axis=0, dtype=F32)
    proj_own, proj_other = to_relative(grad_proj)
    grad_act_one = scatter_plane(
        dot(proj_own, w_qkv_own, NT).astype(BF), dot(proj_other, w_qkv_own, NT).astype(BF)
    )
    unit_one, rate_one = norm_parts(inputs)
    grad_input, grad_gain_one, grad_shift_one = norm_back(
        grad_act_one, unit_one, rate_one, gain_one
    )
    grad_tokens = (grad_middle + grad_input)[None]

    def sum_rows(x):
        return lax.psum_scatter(x.astype(BF), "rows", scatter_dimension=0, tiled=True)

    out_down = sum_rows(grad_down).astype(F32)
    out_gate = sum_rows(grad_gate).astype(F32)
    out_up = sum_rows(grad_up).astype(F32)
    if fast_out:
        out_w_out = sum_rows(grad_w_out).astype(F32)
    else:
        spread_out = lax.dynamic_update_index_in_dim(
            jnp.zeros((per, wide_n, HEAD_DIM, width), BF),
            grad_w_out.astype(BF).reshape(per, HEAD_DIM, width),
            me,
            1,
        )
        out_w_out = lax.psum_scatter(
            spread_out.reshape(width, width), ALL, scatter_dimension=0, tiled=True
        ).astype(F32)
    part_qkv = lax.all_to_all(sum_rows(grad_w_qkv), "wide", 0, 0, tiled=True)
    out_qkv = (
        part_qkv.reshape(wide_n, slab, 3 * per, HEAD_DIM)
        .transpose(1, 2, 0, 3)
        .reshape(slab, 3 * width)
        .astype(F32)
    )
    full_bias = lax.dynamic_update_index_in_dim(
        jnp.zeros((3, per, wide_n, HEAD_DIM), F32),
        grad_bias.reshape(3, per, HEAD_DIM),
        me,
        2,
    )
    sums = scatter_small(
        jnp.concatenate(
            [
                full_bias.reshape(devices, bias_slab),
                grad_gain_one.reshape(devices, slab),
                grad_shift_one.reshape(devices, slab),
                grad_gain_two.reshape(devices, slab),
                grad_shift_two.reshape(devices, slab),
            ],
            axis=1,
        )
    )
    out_bias = sums[:bias_slab]
    small_outs = [
        sums[bias_slab + i * slab : bias_slab + (i + 1) * slab] for i in range(4)
    ]
    return (
        result,
        grad_tokens,
        out_qkv,
        out_bias,
        out_w_out,
        *small_outs,
        out_gate,
        out_up,
        out_down,
    )


def solution(mesh):
    by_token = P("rows", "wide", None)
    by_both = P(("rows", "wide"), None)
    vector = P(("rows", "wide"))
    by_slab = P("rows", "wide")
    in_specs = (
        by_token, P("rows", "wide"), by_both, vector, by_both, vector, vector, vector, vector,
        by_slab, by_slab, by_slab, by_token,
    )
    out_specs = (
        by_token, by_token, by_both, vector, by_both, vector, vector, vector, vector,
        by_slab, by_slab, by_slab,
    )
    return jax.shard_map(shards, mesh=mesh, in_specs=in_specs, out_specs=out_specs, check_vma=False)
```

time: 1920 us -> 652 us (0.34)
  waiting for transfers between devices: 1320 us -> 164 us
  matrix products: 280 us -> 120 us
  Pallas kernels: 0 us -> 87.2 us
  starting transfers between devices: 1.28 us -> 62.7 us
  blocking collectives: 96.2 us -> 41.4 us
  local copies, waits for them, and re-layouts: 147 us -> 97.3 us
    reduce_scatter x9 -> x5, waiting for transfers between devices: 897 us -> 0.05 us  [sum_rows(): lax.psum_scatter(x.astype(BF), 'rows', scatter_dimension=0, tiled=True)]
    all_gather x6 -> x2, waiting for transfers between devices: 268 us -> 5.5 us  [the longest x1 5.5 us: shards(): w_qkv_own = lax.all_gather(w_qkv_part, 'rows', axis=0, tiled=True)]
    dot_general x42 -> x17, matrix products: 280 us -> 120 us  [dot(): return lax.dot_general(left, right, dims, preferred_element_type=F32)]
    ppermute x0 -> x61, waiting for transfers between devices: none -> 125 us  [swap(): lax.ppermute(x, axis, [(i, i ^ bit) for i in range(lax.axis_size(axis))])]
    unnamed x2 -> x0, blocking collectives: 87.8 us -> none
    pallas_call x0 -> x3, Pallas kernels: none -> 87.2 us  [the longest x1 38.5 us: attend_back(): pl.pallas_call(attend_back_kernel, grid=(pairs, total // block), in_specs...]
    ppermute x0 -> x61, starting transfers between devices: none -> 56.4 us  [swap(): lax.ppermute(x, axis, [(i, i ^ bit) for i in range(lax.axis_size(axis))])]
    all_gather x1, waiting for transfers between devices: 50.4 us -> 0.01 us  [shards(): lax.all_gather(w_gate, 'rows', axis=0, tiled=True)]
  transfers between devices with their start and end apart: 18 -> 72, of which waited for: 18 -> 32; matrix products, arithmetic and copies ran while one was open for 12% -> 34% of each run, Pallas kernels for 0% -> 13%
where the time goes in v1:
time: 652 us; the launch traced here: 646 us
  waiting for transfers between devices  164 us (25%)
  matrix products  120 us (18%)
  local copies, waits for them, and re-layouts  97.3 us (15%)
  Pallas kernels  87.2 us (13%)
  starting transfers between devices  62.7 us (10%)
  other arithmetic  58.3 us (9%)
  blocking collectives  41.4 us (6%)
  between operations  15.6 us (2%)
    ppermute x61, waiting for transfers between devices, swap(): lax.ppermute(x, axis, [(i, i ^ bit) for i in range(lax.axis_size(axis))])  125 us
    dot_general x17, matrix products, dot(): return lax.dot_general(left, right, dims, preferred_element_type=F32)  120 us
    ppermute x61, starting transfers between devices, swap(): lax.ppermute(x, axis, [(i, i ^ bit) for i in range(lax.axis_size(axis))])  56.4 us
    unnamed x179, local copies, waits for them, and re-layouts  42.1 us
    pallas_call x1, Pallas kernels, attend_back(): pl.pallas_call(attend_back_kernel, grid=(pairs, total // block), in_specs...  38.5 us
    pallas_call x1, Pallas kernels, attend(): pl.pallas_call(attend_kernel, grid=(pairs, total // block), in_specs=[pl....  33.8 us
    all_gather x1, waiting for transfers between devices, shards(): lax.all_gather(w_down, 'rows', axis=0, tiled=True)  26.7 us
    all_gather x2, blocking collectives, shards(): small = lax.all_gather(lax.all_gather(packed, 'rows'), 'wide')  23.6 us
  transfers between devices with their start and end apart: 72, of which 32 were waited for; matrix products, arithmetic and copies ran while one was open for 34% of the time, Pallas kernels for 13%

profile of v1, /device:TPU:0, one launch (start us, length us, event | category | flops | bytes accessed | tf_op | source)
XLA Modules:
  0.0 646.5 jit_solution(6380984944545718331)
XLA Ops:
  7.2 3.4 reshape.439
  14.4 17.8 %all_to_all.21 = bf16[8,64,768]{2,1,0:T(8,128)(2,1)} all-to-all(bf16[8,64,768]{2,1,0:T(8,128)(2,1)} %all_to_all.14), channel_id=1, replica_groups=mesh['rows'=4,'wide'=8] {'wide'}, dimensions={0} | all-to-all | bytes 1572864 | tf_op jit(solution)/shard_map/all_to_all | solution.py:539
  38.3 6.8 %collective-permute-done.2 = bf16[96,2048]{1,0:T(8,128)(2,1)S(1)} collective-permute-done((bf16[96,2048]{1,0:T(8,128)(2,1)S(1)}, bf16[96,2048]{1,0:T(8,128)(2,1)S(1)}, u32[]{:S(2)}, u32[]{:S(2)}) %collective-permute-start.2) | collective-permute-done | bytes 393248 | tf_op jit(solution)/shard_map/ppermute | solution.py:30
  46.6 6.4 collective-permute-done.1
  56.6 2.9 collective-permute-done.4
  61.8 13.9 %all-gather.2 = bf16[4,1,640]{2,1,0:T(2,128)(2,1)S(1)} all-gather(bf16[1,1,640]{2,1,0:T(2,128)(2,1)S(1)} %reshape.459), channel_id=2, replica_groups=mesh['rows'=4,'wide'=8] {'rows'}, dimensions={0}, use_global_device_ids=true | all-gather | bytes 6400 | tf_op jit(solution)/shard_map/all_gather | solution.py:493
  75.7 9.7 %all-gather.3 = bf16[8,4,640]{2,1,0:T(4,128)(2,1)S(1)} all-gather(bf16[1,4,640]{2,1,0:T(4,128)(2,1)S(1)} %bitcast.230), channel_id=3, replica_groups=mesh['rows'=4,'wide'=8] {'wide'}, dimensions={0}, use_global_device_ids=true | all-gather | bytes 46080 | tf_op jit(solution)/shard_map/all_gather | solution.py:493
  86.8 2.9 fusion.36
  90.3 5.5 all-gather.10.cloned.1.call-done.weight
  95.8 14.9 %project.1 = (bf16[1536,2048]{1,0:T(8,128)(2,1)}, bf16[1536,256]{1,0:T(8,128)(2,1)S(1)}, bf16[1536,256]{1,0:T(8,128)(2,1)S(1)}, bf16[1536,256]{1,0:T(8,128)(2,1)S(1)}) custom-call(s32[8]{0:T(128)S(1)} %stack.35.order, bf16[768,2048]{1,0:T(8,128)(2,1)} %constant_dynamic-update-slice_fusion.own_ref, bf16[768,2048]{1,0:T(8,128)(2,1)} %collective-permute-done.6.other_ref, ...), custom_call_target="tpu_custom_call" | custom-call | flops 4831838208 | bytes 18087936 | tf_op jit(solution)/shard_map/project/pallas_call | solution.py:203
  110.7 33.8 %attend.1 = (bf16[1536,256]{1,0:T(8,128)(2,1)S(1)}, f32[2,2,1536]{2,1,0:T(2,128)S(1)}) custom-call(s32[1,1536]{1,0:T(1,128)S(1)} %reshape.438.first, bf16[1536,256]{1,0:T(8,128)(2,1)S(1)} %get-tuple-element.21.q_ref, bf16[1536,256]{1,0:T(8,128)(2,1)S(1)} %get-tuple-element.22.k_ref, bf16[1536,256]{1,0:T(8,128)(2,1)S(1)} %get-tuple-element.23.v_ref), custom_call_target="tpu_custom_call" | custom-call | flops 4831838208 | bytes 3145728 | tf_op jit(solution)/shard_map/attend/pallas_call | solution.py:298
  149.9 4.2 convolution_convert_fusion.3
  161.7 2.9 add_convert_fusion.4
  166.4 2.5 collective-permute-done.30
  172.7 11.3 %collective-permute-done.9 = bf16[96,2048]{1,0:T(8,128)(2,1)S(1)} collective-permute-done((bf16[96,2048]{1,0:T(8,128)(2,1)S(1)}, bf16[96,2048]{1,0:T(8,128)(2,1)S(1)}, u32[]{:S(2)}, u32[]{:S(2)}) %collective-permute-start.9) | collective-permute-done | bytes 393248 | tf_op jit(solution)/shard_map/ppermute | solution.py:30
  191.4 9.1 %collective-permute-done.8 = bf16[96,2048]{1,0:T(8,128)(2,1)S(1)} collective-permute-done((bf16[96,2048]{1,0:T(8,128)(2,1)S(1)}, bf16[96,2048]{1,0:T(8,128)(2,1)S(1)}, u32[]{:S(2)}, u32[]{:S(2)}) %collective-permute-start.8) | collective-permute-done | bytes 393248 | tf_op jit(solution)/shard_map/ppermute | solution.py:30
  206.4 6.3 collective-permute-done.13
  222.4 7.1 %collective-permute-done.16 = bf16[96,2048]{1,0:T(8,128)(2,1)S(1)} collective-permute-done((bf16[96,2048]{1,0:T(8,128)(2,1)S(1)}, bf16[96,2048]{1,0:T(8,128)(2,1)S(1)}, u32[]{:S(2)}, u32[]{:S(2)}) %collective-permute-start.16) | collective-permute-done | bytes 393248 | tf_op jit(solution)/shard_map/ppermute | solution.py:30
  230.1 6.4 collective-permute-done.15
  245.3 4.0 constant_dynamic-update-slice_fusion.31
  251.2 4.1 constant_dynamic-update-slice_fusion.15
  255.4 10.4 %fusion.79 = f32[1536,704]{0,1:T(8,128)} fusion(bf16[1536,2048]{1,0:T(8,128)(2,1)} %constant_dynamic-update-slice_fusion.15, bf16[2048,704]{0,1:T(8,128)(2,1)} %all-gather.14.cloned.1.call-done), kind=kOutput, calls=%fused_computation.270 | convolution fusion | flops 4429185024 | bytes 13500416 | tf_op jit(solution)/shard_map/dot_general | solution.py:26
  265.7 10.4 %fusion.80 = f32[1536,704]{0,1:T(8,128)} fusion(bf16[1536,2048]{1,0:T(8,128)(2,1)} %constant_dynamic-update-slice_fusion.15, bf16[2048,704]{0,1:T(8,128)(2,1)} %all-gather.16.cloned.1.call-done), kind=kOutput, calls=%fused_computation.271 | convolution fusion | flops 4429185024 | bytes 13500416 | tf_op jit(solution)/shard_map/dot_general | solution.py:26
  276.1 26.7 %all-gather.18.cloned.1.call-done = bf16[2048,704]{0,1:T(8,128)(2,1)} async-done(((bf16[512,704]{0,1:T(8,128)(2,1)}), bf16[2048,704]{0,1:T(8,128)(2,1)}) %all-gather.18.cloned.1.call-update) | async-done | bytes 2883600 | tf_op jit(solution)/shard_map/all_gather | solution.py:546
  302.9 12.7 %multiply_convert_fusion = (bf16[1536,704]{0,1:T(8,128)(2,1)S(1)}, bf16[1536,704]{0,1:T(8,128)(2,1)S(1)}, bf16[1536,704]{0,1:T(8,128)(2,1)S(1)}) fusion(f32[1536,704]{0,1:T(8,128)} %fusion.79, f32[1536,704]{0,1:T(8,128)} %fusion.80, bf16[1536,2048]{1,0:T(8,128)(2,1)} %constant_dynamic-update-slice_fusion.31, bf16[2048,704]{0,1:T(8,128)(2,1)} %all-gather.18.cloned.1.call-done), kind=kOutput, calls=%fused_computation.8 | convolution fusion | flops 4445405184 | bytes 24313856 | tf_op jit(solution)/shard_map/dot_general | solution.py:26
  315.6 8.2 %fusion.81 = f32[1536,2048]{1,0:T(8,128)} fusion(bf16[1536,704]{0,1:T(8,128)(2,1)S(1)} %get-tuple-element.67, bf16[2048,704]{0,1:T(8,128)(2,1)S(1)} %copy-done.57), kind=kOutput, calls=%fused_computation.272 | convolution fusion | flops 4429185024 | bytes 17629184 | tf_op jit(solution)/shard_map/dot_general | solution.py:26
  323.9 8.5 %add_convert_fusion = bf16[1536,2048]{1,0:T(8,128)(2,1)S(1)} fusion(f32[1536,2048]{1,0:T(8,128)} %fusion.81, bf16[1536,704]{0,1:T(8,128)(2,1)S(1)} %get-tuple-element.66, bf16[2048,704]{0,1:T(8,128)(2,1)S(1)} %copy-done.58), kind=kOutput, calls=%fused_computation | convolution fusion | flops 4435476480 | bytes 23920640 | tf_op jit(solution)/shard_map/dot_general | solution.py:26
  335.9 6.0 convolution_convert_fusion.6
  342.0 4.2 add_convert_fusion.2
  350.6 8.4 %collective-permute-done.37 = bf16[96,2048]{1,0:T(8,128)(2,1)S(1)} collective-permute-done((bf16[96,2048]{1,0:T(8,128)(2,1)S(1)}, bf16[96,2048]{1,0:T(8,128)(2,1)S(1)}, u32[]{:S(2)}, u32[]{:S(2)}) %collective-permute-start.37) | collective-permute-done | bytes 393248 | tf_op jit(solution)/shard_map/ppermute | solution.py:30
  361.2 5.8 collective-permute-done.36
  367.1 4.2 collective-permute-done.38
  374.6 9.0 %convolution_convert_fusion.8 = bf16[2048,704]{0,1:T(8,128)(2,1)} fusion(bf16[1536,704]{0,1:T(8,128)(2,1)S(1)} %copy-done.61, bf16[1536,2048]{1,0:T(8,128)(2,1)} %constant_dynamic-update-slice_fusion.15), kind=kOutput, calls=%fused_computation.20 | convolution fusion | flops 4430626816 | bytes 11337728 | tf_op jit(solution)/shard_map/dot_general | solution.py:26
  386.1 2.7 multiply_reduce_fusion
  395.6 7.0 %collective-permute-done.44 = bf16[96,2048]{1,0:T(8,128)(2,1)S(1)} collective-permute-done((bf16[96,2048]{1,0:T(8,128)(2,1)S(1)}, bf16[96,2048]{1,0:T(8,128)(2,1)S(1)}, u32[]{:S(2)}, u32[]{:S(2)}) %collective-permute-start.44) | collective-permute-done | bytes 393248 | tf_op jit(solution)/shard_map/ppermute | solution.py:30
  404.7 7.4 %collective-permute-done.42 = bf16[96,2048]{1,0:T(8,128)(2,1)S(1)} collective-permute-done((bf16[96,2048]{1,0:T(8,128)(2,1)S(1)}, bf16[96,2048]{1,0:T(8,128)(2,1)S(1)}, u32[]{:S(2)}, u32[]{:S(2)}) %collective-permute-start.42) | collective-permute-done | bytes 393248 | tf_op jit(solution)/shard_map/ppermute | solution.py:30
  418.3 7.4 %convolution_convert_fusion = bf16[1536,2048]{1,0:T(8,128)(2,1)S(1)} fusion(bf16[1536,704]{0,1:T(8,128)(2,1)} %copy-done.64, bf16[2048,704]{0,1:T(8,128)(2,1)} %all-gather.18.cloned.1.call-done), kind=kOutput, calls=%fused_computation.2 | convolution fusion | flops 4432330752 | bytes 11337728 | tf_op jit(solution)/shard_map/dot_general | solution.py:26
  430.2 8.7 %convolution_convert_fusion.7 = bf16[2048,704]{0,1:T(8,128)(2,1)} fusion(bf16[1536,704]{0,1:T(8,128)(2,1)S(1)} %copy-done.63, bf16[1536,2048]{1,0:T(8,128)(2,1)} %constant_dynamic-update-slice_fusion.15), kind=kOutput, calls=%fused_computation.19 | convolution fusion | flops 4430626816 | bytes 11337728 | tf_op jit(solution)/shard_map/dot_general | solution.py:26
  439.2 2.9 convolution_convert_fusion.11
  442.1 2.9 convolution_convert_fusion.10
  446.7 38.5 %attend_back.1 = (bf16[1536,256]{1,0:T(8,128)(2,1)S(1)}, bf16[1536,256]{1,0:T(8,128)(2,1)S(1)}, bf16[1536,256]{1,0:T(8,128)(2,1)S(1)}) custom-call(s32[1,1536]{1,0:T(1,128)S(1)} %reshape.438.first, bf16[1536,256]{1,0:T(8,128)(2,1)S(1)} %get-tuple-element.21.q_ref, bf16[1536,256]{1,0:T(8,128)(2,1)S(1)} %copy-done.4, bf16[1536,256]{1,0:T(8,128)(2,1)S(1)} %copy-done.6, ...), custom_call_target="tpu_custom_call" | custom-call | flops 12079595520 | bytes 6291456 | tf_op jit(solution)/shard_map/attend_back/pallas_call | solution.py:409
  487.7 4.1 convolution_convert_fusion.1
  492.0 4.2 add_convert_fusion.3
  499.9 4.0 constant_dynamic-update-slice_fusion.66
  503.9 5.9 convolution_convert_fusion.9
  510.3 5.9 add_convert_fusion.1
  519.7 9.6 %convolution_convert_fusion.5 = bf16[2048,768]{1,0:T(8,128)(2,1)} fusion(bf16[1536,2048]{1,0:T(8,128)(2,1)} %get-tuple-element.29, bf16[1536,768]{1,0:T(8,128)(2,1)S(1)} %constant_dynamic-update-slice_fusion.55), kind=kOutput, calls=%fused_computation.17 | convolution fusion | flops 4833411072 | bytes 11796480 | tf_op jit(solution)/shard_map/dot_general | solution.py:26
  535.4 4.6 collective-permute-done.50
  544.6 6.9 %collective-permute-done.52 = bf16[96,2048]{1,0:T(8,128)(2,1)S(1)} collective-permute-done((bf16[96,2048]{1,0:T(8,128)(2,1)S(1)}, bf16[96,2048]{1,0:T(8,128)(2,1)S(1)}, u32[]{:S(2)}, u32[]{:S(2)}) %collective-permute-start.52) | collective-permute-done | bytes 393248 | tf_op jit(solution)/shard_map/ppermute | solution.py:30
  553.1 3.0 fusion.69
  557.3 2.6 collective-permute-done.24
  560.0 2.6 add_bitcast_fusion.1
  569.0 5.8 collective-permute-done.55
  578.9 2.5 fusion.8
  589.3 3.1 collective-permute-done.56
  593.3 2.4 fusion.17
  595.7 2.4 convert_element_type.451
  598.2 2.6 convert_element_type.447
  600.8 2.4 convert_element_type.449
  612.7 4.4 all-to-all-start.1
  617.2 4.2 fusion.10
  622.6 7.1 %all-to-all-done.1 = bf16[8,64,768]{2,1,0:T(8,128)(2,1)} async-done(((bf16[8,64,768]{2,1,0:T(8,128)(2,1)}), bf16[8,64,768]{2,1,0:T(8,128)(2,1)}, u32[]{:S(2)}, u32[]{:S(2)}) %all-to-all-start.1) | async-done | bytes 786464 | tf_op jit(solution)/shard_map/all_to_all | solution.py:627
  629.7 3.8 reshape.456
  633.5 4.0 copy.60
  (408 shorter events, 164.7 us)
Async XLA Ops:
  7.2 88.6 %all-gather.10.cloned.1.call-start = ((), (), s32[]{:S(2)}) async-start(), calls=%async_computation.7 | async-start | bytes 3932160 | tf_op jit(solution)/shard_map/all_gather | solution.py:542
  32.3 117.6 %all-gather.12.cloned.1.call-start = ((), (), s32[]{:S(2)}) async-start(), calls=%async_computation.8 | async-start | bytes 1310720 | tf_op jit(solution)/shard_map/all_gather | solution.py:528
  32.4 21.1 %collective-permute-start = (bf16[96,2048]{1,0:T(8,128)(2,1)S(1)}, bf16[96,2048]{1,0:T(8,128)(2,1)S(1)}, u32[]{:S(2)}, u32[]{:S(2)}) collective-permute-start(bf16[96,2048]{1,0:T(8,128)(2,1)S(1)} %get-tuple-element.111), channel_id=1, source_target_pairs={{0,2},{1,3},{2,0},{3,1},{4,6},{5,7},{6,4},{7,5},{8,10},{9,11},{10,... | collective-permute-start | bytes 1179656 | tf_op jit(solution)/shard_map/ppermute | solution.py:30
  33.0 12.0 %collective-permute-start.2 = (bf16[96,2048]{1,0:T(8,128)(2,1)S(1)}, bf16[96,2048]{1,0:T(8,128)(2,1)S(1)}, u32[]{:S(2)}, u32[]{:S(2)}) collective-permute-start(bf16[96,2048]{1,0:T(8,128)(2,1)S(1)} %get-tuple-element.111), channel_id=1, source_target_pairs={{0,4},{1,5},{2,6},{3,7},{4,0},{5,1},{6,2},{7,3},{8,12},{9,13},{10,... | collective-permute-start | bytes 1179656 | tf_op jit(solution)/shard_map/ppermute | solution.py:30
  33.6 19.4 %collective-permute-start.1 = (bf16[96,2048]{1,0:T(8,128)(2,1)S(1)}, bf16[96,2048]{1,0:T(8,128)(2,1)S(1)}, u32[]{:S(2)}, u32[]{:S(2)}) collective-permute-start(bf16[96,2048]{1,0:T(8,128)(2,1)S(1)} %get-tuple-element.110), channel_id=1, source_target_pairs={{0,2},{1,3},{2,0},{3,1},{4,6},{5,7},{6,4},{7,5},{8,10},{9,11},{10,... | collective-permute-start | bytes 1179656 | tf_op jit(solution)/shard_map/ppermute | solution.py:30
  35.1 20.8 %collective-permute-start.3 = (bf16[96,2048]{1,0:T(8,128)(2,1)S(1)}, bf16[96,2048]{1,0:T(8,128)(2,1)S(1)}, u32[]{:S(2)}, u32[]{:S(2)}) collective-permute-start(bf16[96,2048]{1,0:T(8,128)(2,1)S(1)} %get-tuple-element.110), channel_id=1, source_target_pairs={{0,4},{1,5},{2,6},{3,7},{4,0},{5,1},{6,2},{7,3},{8,12},{9,13},{10,... | collective-permute-start | bytes 1179656 | tf_op jit(solution)/shard_map/ppermute | solution.py:30
  36.6 218.8 %all-gather.14.cloned.1.call-start = ((), (), s32[]{:S(2)}) async-start(), calls=%async_computation.9 | async-start | bytes 3604480 | tf_op jit(solution)/shard_map/all_gather | solution.py:544
  45.1 14.4 %collective-permute-start.4 = (bf16[96,2048]{1,0:T(8,128)(2,1)S(1)}, bf16[96,2048]{1,0:T(8,128)(2,1)S(1)}, u32[]{:S(2)}, u32[]{:S(2)}) collective-permute-start(bf16[96,2048]{1,0:T(8,128)(2,1)S(1)} %collective-permute-done.2), channel_id=1, source_target_pairs={{0,2},{1,3},{2,0},{3,1},{4,6},{5,7},{6,4},{7,5},{8,10},{9,11},{10,... | collective-permute-start | bytes 1179656 | tf_op jit(solution)/shard_map/ppermute | solution.py:30
  61.6 28.7 %collective-permute-start.6 = (bf16[768,2048]{1,0:T(8,128)(2,1)}, bf16[768,2048]{1,0:T(8,128)(2,1)}, u32[]{:S(2)}, u32[]{:S(2)}) collective-permute-start(bf16[768,2048]{1,0:T(8,128)(2,1)} %constant_dynamic-update-slice_fusion.own_ref), channel_id=1, source_target_pairs={{0,1},{1,0},{2,3},{3,2},{4,5},{5,4},{6,7},{7,6},{8,9},{9,8},{10,11... | collective-permute-start | bytes 9437192 | tf_op jit(solution)/shard_map/ppermute | solution.py:30
  61.6 204.2 %all-gather.16.cloned.1.call-start = ((), (), s32[]{:S(2)}) async-start(), calls=%async_computation.10 | async-start | bytes 3604480 | tf_op jit(solution)/shard_map/all_gather | solution.py:545
  155.1 14.3 %collective-permute-start.28 = (bf16[96,2048]{1,0:T(8,128)(2,1)}, bf16[96,2048]{1,0:T(8,128)(2,1)}, u32[]{:S(2)}, u32[]{:S(2)}) collective-permute-start(bf16[96,2048]{1,0:T(8,128)(2,1)} %get-tuple-element.107), channel_id=1, source_target_pairs={{0,2},{1,3},{2,0},{3,1},{4,6},{5,7},{6,4},{7,5},{8,10},{9,11},{10,... | collective-permute-start | bytes 1179656 | tf_op jit(solution)/shard_map/ppermute | solution.py:30
  156.6 12.3 %collective-permute-start.30 = (bf16[96,2048]{1,0:T(8,128)(2,1)}, bf16[96,2048]{1,0:T(8,128)(2,1)}, u32[]{:S(2)}, u32[]{:S(2)}) collective-permute-start(bf16[96,2048]{1,0:T(8,128)(2,1)} %get-tuple-element.107), channel_id=1, source_target_pairs={{0,4},{1,5},{2,6},{3,7},{4,0},{5,1},{6,2},{7,3},{8,12},{9,13},{10,... | collective-permute-start | bytes 1179656 | tf_op jit(solution)/shard_map/ppermute | solution.py:30
  158.0 27.6 %collective-permute-start.29 = (bf16[96,2048]{1,0:T(8,128)(2,1)}, bf16[96,2048]{1,0:T(8,128)(2,1)}, u32[]{:S(2)}, u32[]{:S(2)}) collective-permute-start(bf16[96,2048]{1,0:T(8,128)(2,1)} %get-tuple-element.106), channel_id=1, source_target_pairs={{0,2},{1,3},{2,0},{3,1},{4,6},{5,7},{6,4},{7,5},{8,10},{9,11},{10,... | collective-permute-start | bytes 1179656 | tf_op jit(solution)/shard_map/ppermute | solution.py:30
  158.6 45.2 %collective-permute-start.31 = (bf16[96,2048]{1,0:T(8,128)(2,1)}, bf16[96,2048]{1,0:T(8,128)(2,1)}, u32[]{:S(2)}, u32[]{:S(2)}) collective-permute-start(bf16[96,2048]{1,0:T(8,128)(2,1)} %get-tuple-element.106), channel_id=1, source_target_pairs={{0,4},{1,5},{2,6},{3,7},{4,0},{5,1},{6,2},{7,3},{8,12},{9,13},{10,... | collective-permute-start | bytes 1179656 | tf_op jit(solution)/shard_map/ppermute | solution.py:30
  159.1 143.7 %all-gather.18.cloned.1.call-start = ((), (), s32[]{:S(2)}) async-start(), calls=%async_computation.11 | async-start | bytes 3604480 | tf_op jit(solution)/shard_map/all_gather | solution.py:546
  164.8 19.2 %collective-permute-start.9 = (bf16[96,2048]{1,0:T(8,128)(2,1)S(1)}, bf16[96,2048]{1,0:T(8,128)(2,1)S(1)}, u32[]{:S(2)}, u32[]{:S(2)}) collective-permute-start(bf16[96,2048]{1,0:T(8,128)(2,1)S(1)} %get-tuple-element.90), channel_id=1, source_target_pairs={{0,2},{1,3},{2,0},{3,1},{4,6},{5,7},{6,4},{7,5},{8,10},{9,11},{10,... | collective-permute-start | bytes 1179656 | tf_op jit(solution)/shard_map/ppermute | solution.py:30
  168.8 36.8 %collective-permute-start.32 = (bf16[96,2048]{1,0:T(8,128)(2,1)}, bf16[96,2048]{1,0:T(8,128)(2,1)S(1)}, u32[]{:S(2)}, u32[]{:S(2)}) collective-permute-start(bf16[96,2048]{1,0:T(8,128)(2,1)} %collective-permute-done.30), channel_id=1, source_target_pairs={{0,2},{1,3},{2,0},{3,1},{4,6},{5,7},{6,4},{7,5},{8,10},{9,11},{10,... | collective-permute-start | bytes 1179656 | tf_op jit(solution)/shard_map/ppermute | solution.py:30
  171.2 19.7 %collective-permute-start.11 = (bf16[96,2048]{1,0:T(8,128)(2,1)S(1)}, bf16[96,2048]{1,0:T(8,128)(2,1)S(1)}, u32[]{:S(2)}, u32[]{:S(2)}) collective-permute-start(bf16[96,2048]{1,0:T(8,128)(2,1)S(1)} %get-tuple-element.89), channel_id=1, source_target_pairs={{0,4},{1,5},{2,6},{3,7},{4,0},{5,1},{6,2},{7,3},{8,12},{9,13},{10,... | collective-permute-start | bytes 1179656 | tf_op jit(solution)/shard_map/ppermute | solution.py:30
  184.0 16.5 %collective-permute-start.8 = (bf16[96,2048]{1,0:T(8,128)(2,1)S(1)}, bf16[96,2048]{1,0:T(8,128)(2,1)S(1)}, u32[]{:S(2)}, u32[]{:S(2)}) collective-permute-start(bf16[96,2048]{1,0:T(8,128)(2,1)S(1)} %get-tuple-element.87), channel_id=1, source_target_pairs={{0,2},{1,3},{2,0},{3,1},{4,6},{5,7},{6,4},{7,5},{8,10},{9,11},{10,... | collective-permute-start | bytes 1179656 | tf_op jit(solution)/shard_map/ppermute | solution.py:30
  185.6 16.4 %collective-permute-start.10 = (bf16[96,2048]{1,0:T(8,128)(2,1)S(1)}, bf16[96,2048]{1,0:T(8,128)(2,1)S(1)}, u32[]{:S(2)}, u32[]{:S(2)}) collective-permute-start(bf16[96,2048]{1,0:T(8,128)(2,1)S(1)} %add_convert_fusion.13), channel_id=1, source_target_pairs={{0,4},{1,5},{2,6},{3,7},{4,0},{5,1},{6,2},{7,3},{8,12},{9,13},{10,... | collective-permute-start | bytes 1179656 | tf_op jit(solution)/shard_map/ppermute | solution.py:30
  190.8 28.4 %collective-permute-start.33 = (bf16[96,2048]{1,0:T(8,128)(2,1)}, bf16[96,2048]{1,0:T(8,128)(2,1)S(1)}, u32[]{:S(2)}, u32[]{:S(2)}) collective-permute-start(bf16[96,2048]{1,0:T(8,128)(2,1)} %collective-permute-done.29), channel_id=1, source_target_pairs={{0,4},{1,5},{2,6},{3,7},{4,0},{5,1},{6,2},{7,3},{8,12},{9,13},{10,... | collective-permute-start | bytes 1179656 | tf_op jit(solution)/shard_map/ppermute | solution.py:30
  200.5 12.3 %collective-permute-start.13 = (bf16[96,2048]{1,0:T(8,128)(2,1)S(1)}, bf16[96,2048]{1,0:T(8,128)(2,1)S(1)}, u32[]{:S(2)}, u32[]{:S(2)}) collective-permute-start(bf16[96,2048]{1,0:T(8,128)(2,1)S(1)} %get-tuple-element.88), channel_id=1, source_target_pairs={{0,4},{1,5},{2,6},{3,7},{4,0},{5,1},{6,2},{7,3},{8,12},{9,13},{10,... | collective-permute-start | bytes 1179656 | tf_op jit(solution)/shard_map/ppermute | solution.py:30
  202.3 10.6 %collective-permute-start.12 = (bf16[96,2048]{1,0:T(8,128)(2,1)S(1)}, bf16[96,2048]{1,0:T(8,128)(2,1)S(1)}, u32[]{:S(2)}, u32[]{:S(2)}) collective-permute-start(bf16[96,2048]{1,0:T(8,128)(2,1)S(1)} %get-tuple-element.86), channel_id=1, source_target_pairs={{0,2},{1,3},{2,0},{3,1},{4,6},{5,7},{6,4},{7,5},{8,10},{9,11},{10,... | collective-permute-start | bytes 1179656 | tf_op jit(solution)/shard_map/ppermute | solution.py:30
  215.9 21.8 %collective-permute-start.14 = (bf16[96,2048]{1,0:T(8,128)(2,1)S(1)}, bf16[96,2048]{1,0:T(8,128)(2,1)S(1)}, u32[]{:S(2)}, u32[]{:S(2)}) collective-permute-start(bf16[96,2048]{1,0:T(8,128)(2,1)S(1)} %get-tuple-element.109), channel_id=1, source_target_pairs={{0,2},{1,3},{2,0},{3,1},{4,6},{5,7},{6,4},{7,5},{8,10},{9,11},{10,... | collective-permute-start | bytes 1179656 | tf_op jit(solution)/shard_map/ppermute | solution.py:30
  217.4 12.1 %collective-permute-start.16 = (bf16[96,2048]{1,0:T(8,128)(2,1)S(1)}, bf16[96,2048]{1,0:T(8,128)(2,1)S(1)}, u32[]{:S(2)}, u32[]{:S(2)}) collective-permute-start(bf16[96,2048]{1,0:T(8,128)(2,1)S(1)} %get-tuple-element.109), channel_id=1, source_target_pairs={{0,4},{1,5},{2,6},{3,7},{4,0},{5,1},{6,2},{7,3},{8,12},{9,13},{10,... | collective-permute-start | bytes 1179656 | tf_op jit(solution)/shard_map/ppermute | solution.py:30
  218.0 18.5 %collective-permute-start.15 = (bf16[96,2048]{1,0:T(8,128)(2,1)S(1)}, bf16[96,2048]{1,0:T(8,128)(2,1)S(1)}, u32[]{:S(2)}, u32[]{:S(2)}) collective-permute-start(bf16[96,2048]{1,0:T(8,128)(2,1)S(1)} %get-tuple-element.108), channel_id=1, source_target_pairs={{0,2},{1,3},{2,0},{3,1},{4,6},{5,7},{6,4},{7,5},{8,10},{9,11},{10,... | collective-permute-start | bytes 1179656 | tf_op jit(solution)/shard_map/ppermute | solution.py:30
  220.1 25.2 %collective-permute-start.34 = (bf16[768,2048]{1,0:T(8,128)(2,1)}, bf16[768,2048]{1,0:T(8,128)(2,1)}, u32[]{:S(2)}, u32[]{:S(2)}) collective-permute-start(bf16[768,2048]{1,0:T(8,128)(2,1)} %get-tuple-element.124), channel_id=1, source_target_pairs={{0,1},{1,0},{2,3},{3,2},{4,5},{5,4},{6,7},{7,6},{8,9},{9,8},{10,11... | collective-permute-start | bytes 9437192 | tf_op jit(solution)/shard_map/ppermute | solution.py:30
  220.1 20.5 %collective-permute-start.17 = (bf16[96,2048]{1,0:T(8,128)(2,1)S(1)}, bf16[96,2048]{1,0:T(8,128)(2,1)S(1)}, u32[]{:S(2)}, u32[]{:S(2)}) collective-permute-start(bf16[96,2048]{1,0:T(8,128)(2,1)S(1)} %get-tuple-element.108), channel_id=1, source_target_pairs={{0,4},{1,5},{2,6},{3,7},{4,0},{5,1},{6,2},{7,3},{8,12},{9,13},{10,... | collective-permute-start | bytes 1179656 | tf_op jit(solution)/shard_map/ppermute | solution.py:30
  229.5 13.1 %collective-permute-start.18 = (bf16[96,2048]{1,0:T(8,128)(2,1)S(1)}, bf16[96,2048]{1,0:T(8,128)(2,1)S(1)}, u32[]{:S(2)}, u32[]{:S(2)}) collective-permute-start(bf16[96,2048]{1,0:T(8,128)(2,1)S(1)} %collective-permute-done.16), channel_id=1, source_target_pairs={{0,2},{1,3},{2,0},{3,1},{4,6},{5,7},{6,4},{7,5},{8,10},{9,11},{10,... | collective-permute-start | bytes 1179656 | tf_op jit(solution)/shard_map/ppermute | solution.py:30
  245.3 350.5 %reduce-scatter.14.cloned.1.call-start = ((), (), s32[]{:S(2)}) async-start(), calls=%async_computation.16 | async-start | bytes 3604480 | tf_op jit(solution)/shard_map/reduce_scatter | solution.py:610
  341.9 256.3 %reduce-scatter.10.cloned.1.call-start = ((), (), s32[]{:S(2)}) async-start(), calls=%async_computation.14 | async-start | bytes 3604480 | tf_op jit(solution)/shard_map/reduce_scatter | solution.py:610
  347.1 11.9 %collective-permute-start.37 = (bf16[96,2048]{1,0:T(8,128)(2,1)S(1)}, bf16[96,2048]{1,0:T(8,128)(2,1)S(1)}, u32[]{:S(2)}, u32[]{:S(2)}) collective-permute-start(bf16[96,2048]{1,0:T(8,128)(2,1)S(1)} %get-tuple-element.78), channel_id=1, source_target_pairs={{0,2},{1,3},{2,0},{3,1},{4,6},{5,7},{6,4},{7,5},{8,10},{9,11},{10,... | collective-permute-start | bytes 1179656 | tf_op jit(solution)/shard_map/ppermute | solution.py:30
  348.6 18.5 %collective-permute-start.36 = (bf16[96,2048]{1,0:T(8,128)(2,1)S(1)}, bf16[96,2048]{1,0:T(8,128)(2,1)S(1)}, u32[]{:S(2)}, u32[]{:S(2)}) collective-permute-start(bf16[96,2048]{1,0:T(8,128)(2,1)S(1)} %get-tuple-element.75), channel_id=1, source_target_pairs={{0,2},{1,3},{2,0},{3,1},{4,6},{5,7},{6,4},{7,5},{8,10},{9,11},{10,... | collective-permute-start | bytes 1179656 | tf_op jit(solution)/shard_map/ppermute | solution.py:30
  349.2 17.9 %collective-permute-start.39 = (bf16[96,2048]{1,0:T(8,128)(2,1)S(1)}, bf16[96,2048]{1,0:T(8,128)(2,1)S(1)}, u32[]{:S(2)}, u32[]{:S(2)}) collective-permute-start(bf16[96,2048]{1,0:T(8,128)(2,1)S(1)} %get-tuple-element.77), channel_id=1, source_target_pairs={{0,4},{1,5},{2,6},{3,7},{4,0},{5,1},{6,2},{7,3},{8,12},{9,13},{10,... | collective-permute-start | bytes 1179656 | tf_op jit(solution)/shard_map/ppermute | solution.py:30
  359.1 12.1 %collective-permute-start.38 = (bf16[96,2048]{1,0:T(8,128)(2,1)S(1)}, bf16[96,2048]{1,0:T(8,128)(2,1)S(1)}, u32[]{:S(2)}, u32[]{:S(2)}) collective-permute-start(bf16[96,2048]{1,0:T(8,128)(2,1)S(1)} %add_convert_fusion.9), channel_id=1, source_target_pairs={{0,4},{1,5},{2,6},{3,7},{4,0},{5,1},{6,2},{7,3},{8,12},{9,13},{10,... | collective-permute-start | bytes 1179656 | tf_op jit(solution)/shard_map/ppermute | solution.py:30
  360.7 23.2 %collective-permute-start.41 = (bf16[96,2048]{1,0:T(8,128)(2,1)}, bf16[96,2048]{1,0:T(8,128)(2,1)}, u32[]{:S(2)}, u32[]{:S(2)}) collective-permute-start(bf16[96,2048]{1,0:T(8,128)(2,1)} %get-tuple-element.76), channel_id=1, source_target_pairs={{0,4},{1,5},{2,6},{3,7},{4,0},{5,1},{6,2},{7,3},{8,12},{9,13},{10,... | collective-permute-start | bytes 1179656 | tf_op jit(solution)/shard_map/ppermute | solution.py:30
  373.2 10.8 %collective-permute-start.40 = (bf16[96,2048]{1,0:T(8,128)(2,1)}, bf16[96,2048]{1,0:T(8,128)(2,1)}, u32[]{:S(2)}, u32[]{:S(2)}) collective-permute-start(bf16[96,2048]{1,0:T(8,128)(2,1)} %get-tuple-element.74), channel_id=1, source_target_pairs={{0,2},{1,3},{2,0},{3,1},{4,6},{5,7},{6,4},{7,5},{8,10},{9,11},{10,... | collective-permute-start | bytes 1179656 | tf_op jit(solution)/shard_map/ppermute | solution.py:30
  383.6 217.2 %reduce-scatter.12.cloned.1.call-start = ((), (), s32[]{:S(2)}) async-start(), calls=%async_computation.15 | async-start | bytes 3604480 | tf_op jit(solution)/shard_map/reduce_scatter | solution.py:610
  390.5 12.1 %collective-permute-start.44 = (bf16[96,2048]{1,0:T(8,128)(2,1)S(1)}, bf16[96,2048]{1,0:T(8,128)(2,1)S(1)}, u32[]{:S(2)}, u32[]{:S(2)}) collective-permute-start(bf16[96,2048]{1,0:T(8,128)(2,1)S(1)} %get-tuple-element.101), channel_id=1, source_target_pairs={{0,4},{1,5},{2,6},{3,7},{4,0},{5,1},{6,2},{7,3},{8,12},{9,13},{10,... | collective-permute-start | bytes 1179656 | tf_op jit(solution)/shard_map/ppermute | solution.py:30
  392.1 12.1 %collective-permute-start.43 = (bf16[96,2048]{1,0:T(8,128)(2,1)S(1)}, bf16[96,2048]{1,0:T(8,128)(2,1)S(1)}, u32[]{:S(2)}, u32[]{:S(2)}) collective-permute-start(bf16[96,2048]{1,0:T(8,128)(2,1)S(1)} %get-tuple-element.100), channel_id=1, source_target_pairs={{0,2},{1,3},{2,0},{3,1},{4,6},{5,7},{6,4},{7,5},{8,10},{9,11},{10,... | collective-permute-start | bytes 1179656 | tf_op jit(solution)/shard_map/ppermute | solution.py:30
  392.7 19.5 %collective-permute-start.42 = (bf16[96,2048]{1,0:T(8,128)(2,1)S(1)}, bf16[96,2048]{1,0:T(8,128)(2,1)S(1)}, u32[]{:S(2)}, u32[]{:S(2)}) collective-permute-start(bf16[96,2048]{1,0:T(8,128)(2,1)S(1)} %get-tuple-element.101), channel_id=1, source_target_pairs={{0,2},{1,3},{2,0},{3,1},{4,6},{5,7},{6,4},{7,5},{8,10},{9,11},{10,... | collective-permute-start | bytes 1179656 | tf_op jit(solution)/shard_map/ppermute | solution.py:30
  394.1 21.1 %collective-permute-start.45 = (bf16[96,2048]{1,0:T(8,128)(2,1)S(1)}, bf16[96,2048]{1,0:T(8,128)(2,1)S(1)}, u32[]{:S(2)}, u32[]{:S(2)}) collective-permute-start(bf16[96,2048]{1,0:T(8,128)(2,1)S(1)} %get-tuple-element.100), channel_id=1, source_target_pairs={{0,4},{1,5},{2,6},{3,7},{4,0},{5,1},{6,2},{7,3},{8,12},{9,13},{10,... | collective-permute-start | bytes 1179656 | tf_op jit(solution)/shard_map/ppermute | solution.py:30
  402.6 13.7 %collective-permute-start.46 = (bf16[96,2048]{1,0:T(8,128)(2,1)S(1)}, bf16[96,2048]{1,0:T(8,128)(2,1)S(1)}, u32[]{:S(2)}, u32[]{:S(2)}) collective-permute-start(bf16[96,2048]{1,0:T(8,128)(2,1)S(1)} %collective-permute-done.44), channel_id=1, source_target_pairs={{0,2},{1,3},{2,0},{3,1},{4,6},{5,7},{6,4},{7,5},{8,10},{9,11},{10,... | collective-permute-start | bytes 1179656 | tf_op jit(solution)/shard_map/ppermute | solution.py:30
  404.2 13.2 %collective-permute-start.47 = (bf16[96,2048]{1,0:T(8,128)(2,1)S(1)}, bf16[96,2048]{1,0:T(8,128)(2,1)S(1)}, u32[]{:S(2)}, u32[]{:S(2)}) collective-permute-start(bf16[96,2048]{1,0:T(8,128)(2,1)S(1)} %collective-permute-done.43), channel_id=1, source_target_pairs={{0,4},{1,5},{2,6},{3,7},{4,0},{5,1},{6,2},{7,3},{8,12},{9,13},{10,... | collective-permute-start | bytes 1179656 | tf_op jit(solution)/shard_map/ppermute | solution.py:30
  418.3 23.8 %collective-permute-start.48 = (bf16[768,2048]{1,0:T(8,128)(2,1)}, bf16[768,2048]{1,0:T(8,128)(2,1)}, u32[]{:S(2)}, u32[]{:S(2)}) collective-permute-start(bf16[768,2048]{1,0:T(8,128)(2,1)} %get-tuple-element.113), channel_id=1, source_target_pairs={{0,1},{1,0},{2,3},{3,2},{4,5},{5,4},{6,7},{7,6},{8,9},{9,8},{10,11... | collective-permute-start | bytes 9437192 | tf_op jit(solution)/shard_map/ppermute | solution.py:30
  429.6 62.4 %collective-permute-start.21 = (bf16[768,2048]{1,0:T(8,128)(2,1)}, bf16[768,2048]{1,0:T(8,128)(2,1)}, u32[]{:S(2)}, u32[]{:S(2)}) collective-permute-start(bf16[768,2048]{1,0:T(8,128)(2,1)} %slice.277), channel_id=1, source_target_pairs={{0,1},{1,0},{2,3},{3,2},{4,5},{5,4},{6,7},{7,6},{8,9},{9,8},{10,11... | collective-permute-start | bytes 9437192 | tf_op jit(solution)/shard_map/ppermute | solution.py:30
  438.9 164.3 %reduce-scatter.8.cloned.1.call-start = ((), (), s32[]{:S(2)}) async-start(), calls=%async_computation.13 | async-start | bytes 1310720 | tf_op jit(solution)/shard_map/reduce_scatter | solution.py:610
  491.8 18.5 %collective-permute-start.49 = (bf16[768,2048]{1,0:T(8,128)(2,1)}, bf16[768,2048]{1,0:T(8,128)(2,1)}, u32[]{:S(2)}, u32[]{:S(2)}) collective-permute-start(bf16[768,2048]{1,0:T(8,128)(2,1)} %convolution_convert_fusion.1), channel_id=1, source_target_pairs={{0,1},{1,0},{2,3},{3,2},{4,5},{5,4},{6,7},{7,6},{8,9},{9,8},{10,11... | collective-permute-start | bytes 9437192 | tf_op jit(solution)/shard_map/ppermute | solution.py:30
  497.3 36.3 %collective-permute-start.23 = (bf16[96,2048]{1,0:T(8,128)(2,1)}, bf16[96,2048]{1,0:T(8,128)(2,1)}, u32[]{:S(2)}, u32[]{:S(2)}) collective-permute-start(bf16[96,2048]{1,0:T(8,128)(2,1)} %get-tuple-element.84), channel_id=1, source_target_pairs={{0,2},{1,3},{2,0},{3,1},{4,6},{5,7},{6,4},{7,5},{8,10},{9,11},{10,... | collective-permute-start | bytes 1179656 | tf_op jit(solution)/shard_map/ppermute | solution.py:30
  497.9 58.1 %collective-permute-start.22 = (bf16[96,2048]{1,0:T(8,128)(2,1)S(1)}, bf16[96,2048]{1,0:T(8,128)(2,1)S(1)}, u32[]{:S(2)}, u32[]{:S(2)}) collective-permute-start(bf16[96,2048]{1,0:T(8,128)(2,1)S(1)} %get-tuple-element.81), channel_id=1, source_target_pairs={{0,2},{1,3},{2,0},{3,1},{4,6},{5,7},{6,4},{7,5},{8,10},{9,11},{10,... | collective-permute-start | bytes 1179656 | tf_op jit(solution)/shard_map/ppermute | solution.py:30
  499.3 58.0 %collective-permute-start.25 = (bf16[96,2048]{1,0:T(8,128)(2,1)}, bf16[96,2048]{1,0:T(8,128)(2,1)}, u32[]{:S(2)}, u32[]{:S(2)}) collective-permute-start(bf16[96,2048]{1,0:T(8,128)(2,1)} %get-tuple-element.83), channel_id=1, source_target_pairs={{0,4},{1,5},{2,6},{3,7},{4,0},{5,1},{6,2},{7,3},{8,12},{9,13},{10,... | collective-permute-start | bytes 1179656 | tf_op jit(solution)/shard_map/ppermute | solution.py:30
  509.8 102.9 %reduce-scatter.6.cloned.1.call-start = ((), (), s32[]{:S(2)}) async-start(), calls=%async_computation.12 | async-start | bytes 3932160 | tf_op jit(solution)/shard_map/reduce_scatter | solution.py:610
  519.1 11.7 %collective-permute-start.51 = (bf16[96,2048]{1,0:T(8,128)(2,1)}, bf16[96,2048]{1,0:T(8,128)(2,1)}, u32[]{:S(2)}, u32[]{:S(2)}) collective-permute-start(bf16[96,2048]{1,0:T(8,128)(2,1)} %get-tuple-element.73), channel_id=1, source_target_pairs={{0,2},{1,3},{2,0},{3,1},{4,6},{5,7},{6,4},{7,5},{8,10},{9,11},{10,... | collective-permute-start | bytes 1179656 | tf_op jit(solution)/shard_map/ppermute | solution.py:30
  529.3 10.6 %collective-permute-start.50 = (bf16[96,2048]{1,0:T(8,128)(2,1)}, bf16[96,2048]{1,0:T(8,128)(2,1)S(1)}, u32[]{:S(2)}, u32[]{:S(2)}) collective-permute-start(bf16[96,2048]{1,0:T(8,128)(2,1)} %get-tuple-element.70), channel_id=1, source_target_pairs={{0,2},{1,3},{2,0},{3,1},{4,6},{5,7},{6,4},{7,5},{8,10},{9,11},{10,... | collective-permute-start | bytes 1179656 | tf_op jit(solution)/shard_map/ppermute | solution.py:30
  530.8 12.3 %collective-permute-start.53 = (bf16[96,2048]{1,0:T(8,128)(2,1)}, bf16[96,2048]{1,0:T(8,128)(2,1)S(1)}, u32[]{:S(2)}, u32[]{:S(2)}) collective-permute-start(bf16[96,2048]{1,0:T(8,128)(2,1)} %get-tuple-element.72), channel_id=1, source_target_pairs={{0,4},{1,5},{2,6},{3,7},{4,0},{5,1},{6,2},{7,3},{8,12},{9,13},{10,... | collective-permute-start | bytes 1179656 | tf_op jit(solution)/shard_map/ppermute | solution.py:30
  533.6 17.9 %collective-permute-start.52 = (bf16[96,2048]{1,0:T(8,128)(2,1)S(1)}, bf16[96,2048]{1,0:T(8,128)(2,1)S(1)}, u32[]{:S(2)}, u32[]{:S(2)}) collective-permute-start(bf16[96,2048]{1,0:T(8,128)(2,1)S(1)} %add_convert_fusion.7), channel_id=1, source_target_pairs={{0,4},{1,5},{2,6},{3,7},{4,0},{5,1},{6,2},{7,3},{8,12},{9,13},{10,... | collective-permute-start | bytes 1179656 | tf_op jit(solution)/shard_map/ppermute | solution.py:30
  540.0 20.0 %collective-permute-start.24 = (bf16[96,2048]{1,0:T(8,128)(2,1)S(1)}, bf16[96,2048]{1,0:T(8,128)(2,1)S(1)}, u32[]{:S(2)}, u32[]{:S(2)}) collective-permute-start(bf16[96,2048]{1,0:T(8,128)(2,1)S(1)} %add_convert_fusion.11), channel_id=1, source_target_pairs={{0,4},{1,5},{2,6},{3,7},{4,0},{5,1},{6,2},{7,3},{8,12},{9,13},{10,... | collective-permute-start | bytes 1179656 | tf_op jit(solution)/shard_map/ppermute | solution.py:30
  543.1 44.8 %collective-permute-start.27 = (bf16[96,2048]{1,0:T(8,128)(2,1)S(1)}, bf16[96,2048]{1,0:T(8,128)(2,1)}, u32[]{:S(2)}, u32[]{:S(2)}) collective-permute-start(bf16[96,2048]{1,0:T(8,128)(2,1)S(1)} %get-tuple-element.82), channel_id=1, source_target_pairs={{0,4},{1,5},{2,6},{3,7},{4,0},{5,1},{6,2},{7,3},{8,12},{9,13},{10,... | collective-permute-start | bytes 1179656 | tf_op jit(solution)/shard_map/ppermute | solution.py:30
  551.5 23.3 %collective-permute-start.55 = (bf16[96,2048]{1,0:T(8,128)(2,1)}, bf16[96,2048]{1,0:T(8,128)(2,1)}, u32[]{:S(2)}, u32[]{:S(2)}) collective-permute-start(bf16[96,2048]{1,0:T(8,128)(2,1)} %get-tuple-element.71), channel_id=1, source_target_pairs={{0,4},{1,5},{2,6},{3,7},{4,0},{5,1},{6,2},{7,3},{8,12},{9,13},{10,... | collective-permute-start | bytes 1179656 | tf_op jit(solution)/shard_map/ppermute | solution.py:30
  556.8 18.0 %collective-permute-start.54 = (bf16[96,2048]{1,0:T(8,128)(2,1)}, bf16[96,2048]{1,0:T(8,128)(2,1)}, u32[]{:S(2)}, u32[]{:S(2)}) collective-permute-start(bf16[96,2048]{1,0:T(8,128)(2,1)} %get-tuple-element.69), channel_id=1, source_target_pairs={{0,2},{1,3},{2,0},{3,1},{4,6},{5,7},{6,4},{7,5},{8,10},{9,11},{10,... | collective-permute-start | bytes 1179656 | tf_op jit(solution)/shard_map/ppermute | solution.py:30
  562.6 25.3 %collective-permute-start.26 = (bf16[96,2048]{1,0:T(8,128)(2,1)}, bf16[96,2048]{1,0:T(8,128)(2,1)}, u32[]{:S(2)}, u32[]{:S(2)}) collective-permute-start(bf16[96,2048]{1,0:T(8,128)(2,1)} %get-tuple-element.80), channel_id=1, source_target_pairs={{0,2},{1,3},{2,0},{3,1},{4,6},{5,7},{6,4},{7,5},{8,10},{9,11},{10,... | collective-permute-start | bytes 1179656 | tf_op jit(solution)/shard_map/ppermute | solution.py:30
  593.2 11.8 %collective-permute-start.57 = (f32[1,3584]{1,0:T(1,128)S(1)}, f32[1,3584]{1,0:T(1,128)S(1)}, u32[]{:S(2)}, u32[]{:S(2)}) collective-permute-start(f32[1,3584]{1,0:T(1,128)S(1)} %constant_dynamic-slice_fusion.6), channel_id=1, source_target_pairs={{0,8},{8,0},{16,24},{24,16},{1,9},{9,1},{17,25},{25,17},{2,10},{10... | collective-permute-start | bytes 43016 | tf_op jit(solution)/shard_map/ppermute | solution.py:30
  612.6 8.9 %collective-permute-start.60 = (f32[1,448]{1,0:T(1,128)S(1)}, f32[1,448]{1,0:T(1,128)S(1)}, u32[]{:S(2)}, u32[]{:S(2)}) collective-permute-start(f32[1,448]{1,0:T(1,128)S(1)} %constant_dynamic-slice_fusion), channel_id=1, source_target_pairs={{0,1},{1,0},{2,3},{3,2},{4,5},{5,4},{6,7},{7,6},{8,9},{9,8},{10,11... | collective-permute-start | bytes 5384 | tf_op jit(solution)/shard_map/ppermute | solution.py:30
  612.7 17.0 %all-to-all-start.1 = ((bf16[8,64,768]{2,1,0:T(8,128)(2,1)}), bf16[8,64,768]{2,1,0:T(8,128)(2,1)}, u32[]{:S(2)}, u32[]{:S(2)}) async-start(bf16[8,64,768]{2,1,0:T(8,128)(2,1)} %bitcast.225), calls=%async_computation.2 | async-start | bytes 1572864 | tf_op jit(solution)/shard_map/all_to_all | solution.py:627
  (75 other events, 1328.3 us)
Sparse Core Ops, SparseCore 0:
  32.4 63.3 all-gather.9
  97.3 26.5 all-gather.11
  125.5 58.6 all-gather.13
  185.7 57.8 all-gather.15
  245.4 57.4 all-gather.17
  342.1 55.0 reduce-scatter.13
  399.5 56.0 reduce-scatter.9
  457.8 56.0 reduce-scatter.11
  516.8 26.9 reduce-scatter.7
  546.1 59.8 reduce-scatter.5

commit v2 on v1

--- a/solution.py
+++ b/solution.py
@@ -34,55 +34,107 @@
     return [1 << k for k in range(1, lax.axis_size("wide").bit_length() - 1)]
 
 
-def gather_plane(x):
+def gather_first(x):
     bits = upper_bits()
-    if len(bits) == 2:
-        half = x.shape[0] // 2
-        one, two = bits
-        top, low = x[:half], x[half:]
-        top_two, low_one = swap(top, two), swap(low, one)
-        low_two, top_one = swap(low, two), swap(top, one)
-        top_both, low_both = swap(top_two, one), swap(low_one, two)
-        own = jnp.concatenate(
-            [top, low, top_one, low_one, top_two, low_two, top_both, low_both]
-        )
-    else:
+    if len(bits) != 2:
+        return ()
+    one, two = bits
+    half = x.shape[0] // 2
+    top, low = x[:half], x[half:]
+    return swap(top, two), swap(low, one), swap(low, two), swap(top, one)
+
+
+def gather_second(x, got):
+    bits = upper_bits()
+    if len(bits) != 2:
+        return ()
+    one, two = bits
+    return swap(got[0], one), swap(got[1], two)
+
+
+def gather_third(x, got, passed):
+    if not got:
         own = x
-        for bit in bits:
+        for bit in upper_bits():
             own = jnp.concatenate([own, swap(own, bit)])
+        return own
+    half = x.shape[0] // 2
+    top_two, low_one, low_two, top_one = got
+    return jnp.concatenate(
+        [x[:half], x[half:], top_one, low_one, top_two, low_two, passed[0], passed[1]]
+    )
+
+
+def gather_last(x, got, passed):
+    own = gather_third(x, got, passed)
     return own, swap(own, 1)
+
+
+def gather_own(x):
+    got = gather_first(x)
+    return gather_third(x, got, gather_second(x, got))
 
 
 def add_low(left, right):
     return (left.astype(F32) + right.astype(F32)).astype(BF)
 
 
-def scatter_plane(own, other):
+def start_scatter(own, other):
+    return add_low(lax.optimization_barrier(own), swap(other, 1))
+
+
+def block_of(total, m, h):
+    half = total.shape[0] // 8
+    return total[(2 * m + h) * half : (2 * m + h + 1) * half]
+
+
+def scatter_first(total):
     bits = upper_bits()
-    got = swap(other, 1)
-    total = add_low(own, got)
-    if len(bits) == 2:
-        one, two = bits
-        half = total.shape[0] // 8
-
-        def part(m, h):
-            return total[(2 * m + h) * half : (2 * m + h + 1) * half]
-
-        far_top, far_low = swap(part(3, 0), one), swap(part(3, 1), two)
-        top_one, low_two = swap(part(1, 0), one), swap(part(2, 1), two)
-        top_two = swap(add_low(part(2, 0), far_top), two)
-        low_one = swap(add_low(part(1, 1), far_low), one)
+    if len(bits) != 2:
+        return ()
+    one, two = bits
+    return (
+        swap(block_of(total, 3, 0), one),
+        swap(block_of(total, 3, 1), two),
+        swap(block_of(total, 1, 0), one),
+        swap(block_of(total, 2, 1), two),
+    )
+
+
+def scatter_second(total, got):
+    bits = upper_bits()
+    if len(bits) != 2:
+        return ()
+    one, two = bits
+    return (
+        swap(add_low(block_of(total, 2, 0), got[0]), two),
+        swap(add_low(block_of(total, 1, 1), got[1]), one),
+    )
+
+
+def scatter_last(total, got, passed):
+    if got:
         return jnp.concatenate(
             [
-                part(0, 0).astype(F32) + top_one.astype(F32) + top_two.astype(F32),
-                part(0, 1).astype(F32) + low_one.astype(F32) + low_two.astype(F32),
+                block_of(total, 0, h).astype(F32) + got[2 + h].astype(F32) + passed[h].astype(F32)
+                for h in range(2)
             ]
         )
+    bits = upper_bits()
     for bit in reversed(bits[1:]):
         half = total.shape[0] // 2
         total = add_low(total[:half], swap(total[half:], bit))
     half = total.shape[0] // 2
     return total[:half].astype(F32) + swap(total[half:], bits[0]).astype(F32)
+
+
+def scatter_plane(total):
+    got = scatter_first(total)
+    return scatter_last(total, got, scatter_second(total, got))
+
+
+def after(x, *others):
+    return lax.optimization_barrier((x, others))[0]
 
 
 def to_relative(x):
@@ -115,27 +167,16 @@
     return jnp.concatenate(pieces)
 
 
-def scatter_small(x):
-    count_rows, count_wide = lax.axis_size("rows"), lax.axis_size("wide")
-    me_rows, me_wide = lax.axis_index("rows"), lax.axis_index("wide")
+def halve(x, axis):
+    count, me = lax.axis_size(axis), lax.axis_index(axis)
     width = x.shape[1]
-    x = x.reshape(count_rows, count_wide * width)
-    size = count_rows // 2
+    size = count // 2
     while size >= 1:
-        side = (me_rows // size) % 2
-        halves = x.reshape(2, -1, x.shape[1])
+        side = (me // size) % 2
+        halves = x.reshape(2, -1, width)
         keep = lax.dynamic_index_in_dim(halves, side, 0, keepdims=False)
         give = lax.dynamic_index_in_dim(halves, 1 - side, 0, keepdims=False)
-        x = keep + swap(give, size, "rows")
-        size //= 2
-    x = x.reshape(count_wide, width)
-    size = count_wide // 2
-    while size >= 1:
-        side = (me_wide // size) % 2
-        halves = x.reshape(2, -1, x.shape[1])
-        keep = lax.dynamic_index_in_dim(halves, side, 0, keepdims=False)
-        give = lax.dynamic_index_in_dim(halves, 1 - side, 0, keepdims=False)
-        x = keep + swap(give, size, "wide")
+        x = keep + swap(give, size, axis)
         size //= 2
     return x.reshape(width)
 
@@ -151,7 +192,8 @@
 
 
 def project_kernel(
-    order, own_ref, other_ref, gain, shift, weight, bias, cosine, ahead, behind, act, q, k, v
+    order, own_ref, other_ref, gain, shift, weight, bias, cosine, ahead, behind,
+    act, q, k, v, stats,
 ):
     count = pl.num_programs(0)
     step = pl.program_id(0)
@@ -159,9 +201,12 @@
 
     def work(x_ref):
         x = x_ref[...].astype(F32)
-        centred = x - jnp.mean(x, axis=1, keepdims=True)
-        spread = jnp.mean(centred * centred, axis=1, keepdims=True)
-        normed = (centred * lax.rsqrt(spread + epsilon) * gain[...] + shift[...]).astype(BF)
+        centre = jnp.mean(x, axis=1, keepdims=True)
+        centred = x - centre
+        rate = lax.rsqrt(jnp.mean(centred * centred, axis=1, keepdims=True) + epsilon)
+        lane = lax.broadcasted_iota(jnp.int32, stats.shape, 1)
+        stats[...] = jnp.where(lane == 0, centre, rate)
+        normed = (centred * rate * gain[...] + shift[...]).astype(BF)
         act[...] = normed
         projected = dot(normed, weight[...]) + bias[...]
         for at in range(0, width, PAIR):
@@ -216,24 +261,85 @@
                 table,
                 table,
             ],
-            out_specs=[pl.BlockSpec((rows, depth), placed), out, out, out],
+            out_specs=[
+                pl.BlockSpec((rows, depth), placed),
+                out,
+                out,
+                out,
+                pl.BlockSpec((rows, PAIR), lambda i, order: (i, 0)),
+            ],
         ),
         out_shape=[
             jax.ShapeDtypeStruct((total, depth), BF),
             jax.ShapeDtypeStruct((total, width), BF),
             jax.ShapeDtypeStruct((total, width), BF),
             jax.ShapeDtypeStruct((total, width), BF),
+            jax.ShapeDtypeStruct((total, PAIR), F32),
         ],
-        cost_estimate=pl.CostEstimate(
-            flops=2 * total * depth * columns,
-            bytes_accessed=2 * (2 * total * depth + total * columns + depth * columns),
-            transcendentals=0,
-        ),
+        cost_estimate=pl.CostEstimate(flops=17 * 10**9, bytes_accessed=1, transcendentals=0),
         compiler_params=pltpu.CompilerParams(
             dimension_semantics=("arbitrary",), vmem_limit_bytes=48 * 2**20
         ),
         name="project",
     )(order, own, other, gain, shift, weight, bias, *tables)
+
+
+def unproject_kernel(order, g_ref, x_ref, stats, weight, out, gain, shift, bias, held):
+    half = order.shape[0]
+    rows = held.shape[0] // half
+
+    @pl.when(pl.program_id(0) == 0)
+    def _():
+        for i in range(half):
+            start = pl.multiple_of(order[i] * rows, rows)
+            held[i * rows : (i + 1) * rows, :] = g_ref[pl.ds(start, rows), :]
+        bias[...] = jnp.sum(held[...].astype(F32), axis=0, keepdims=True)
+
+    unit = (x_ref[...].astype(F32) - stats[:, 0:1]) * stats[:, 1:2]
+    incoming = dot(held[...], weight[...], NT)
+    out[...] = incoming.astype(BF)
+    gain[...] = jnp.sum(incoming * unit, axis=0, keepdims=True)
+    shift[...] = jnp.sum(incoming, axis=0, keepdims=True)
+
+
+def unproject(grads, x, stats, weight, first):
+    count = lax.axis_size("wide")
+    total = x.shape[0]
+    depth, columns = weight.shape
+    block = math.gcd(depth, 1024)
+    order = jnp.stack([lax.axis_index("wide") ^ m for m in range(first, count, 2)])
+    vec = pl.BlockSpec((1, block), lambda j, order: (0, j))
+    return pl.pallas_call(
+        unproject_kernel,
+        grid_spec=pltpu.PrefetchScalarGridSpec(
+            num_scalar_prefetch=1,
+            grid=(depth // block,),
+            in_specs=[
+                pl.BlockSpec(grads.shape, lambda j, order: (0, 0)),
+                pl.BlockSpec((total, block), lambda j, order: (0, j)),
+                pl.BlockSpec((total, PAIR), lambda j, order: (first, 0)),
+                pl.BlockSpec((block, columns), lambda j, order: (j, 0)),
+            ],
+            out_specs=[
+                pl.BlockSpec((total, block), lambda j, order: (0, j)),
+                vec,
+                vec,
+                pl.BlockSpec((1, columns), lambda j, order: (0, 0)),
+            ],
+            scratch_shapes=[pltpu.VMEM((total, columns), BF)],
+        ),
+        out_shape=[
+            jax.ShapeDtypeStruct((total, depth), BF),
+            jax.ShapeDtypeStruct((1, depth), F32),
+            jax.ShapeDtypeStruct((1, depth), F32),
+            jax.ShapeDtypeStruct((1, columns), F32),
+        ],
+        cost_estimate=pl.CostEstimate(flops=7 * 10**9, bytes_accessed=1, transcendentals=0),
+        compiler_params=pltpu.CompilerParams(
+            dimension_semantics=("arbitrary",), vmem_limit_bytes=48 * 2**20
+        ),
+        name="unproject",
+    )(order, grads, x, stats, weight)
 
 
 def head_mask(head, shape):
@@ -313,11 +419,7 @@
             jax.ShapeDtypeStruct((pairs, 2, total), F32),
         ],
         scratch_shapes=[pltpu.VMEM((PAIR, total), BF)],
-        cost_estimate=pl.CostEstimate(
-            flops=8 * total * total * width,
-            bytes_accessed=8 * total * width,
-            transcendentals=total * total * width // PAIR,
-        ),
+        cost_estimate=pl.CostEstimate(flops=39 * 10**9, bytes_accessed=1, transcendentals=0),
         compiler_params=pltpu.CompilerParams(
             dimension_semantics=("arbitrary", "arbitrary"), vmem_limit_bytes=32 * 2**20
         ),
@@ -428,11 +530,7 @@
             pltpu.VMEM((2, total), F32),
             pltpu.VMEM((PAIR, total), F32),
         ],
-        cost_estimate=pl.CostEstimate(
-            flops=20 * total * total * width,
-            bytes_accessed=16 * total * width,
-            transcendentals=total * total * width // PAIR,
-        ),
+        cost_estimate=pl.CostEstimate(flops=44 * 10**9, bytes_accessed=1, transcendentals=0),
         compiler_params=pltpu.CompilerParams(
             dimension_semantics=("arbitrary", "arbitrary"), vmem_limit_bytes=48 * 2**20
         ),
@@ -440,6 +538,58 @@
     )(first, q, k, v, o, g, logs, *tables)
 
 
+def regroup_kernel(x_ref, o_ref):
+    count, rows, width = o_ref.shape
+    groups = width // HEAD_DIM
+    for w in range(count):
+        for g in range(0, groups, 2):
+            pieces = []
+            for j in (g, g + 1):
+                at = (j * count + w) * HEAD_DIM
+                base = at // PAIR * PAIR
+                pair = x_ref[:, base : base + PAIR].astype(F32)
+                pieces.append(pair[:, at - base : at - base + HEAD_DIM])
+            o_ref[w, :, g * HEAD_DIM : g * HEAD_DIM + PAIR] = jnp.concatenate(
+                pieces, axis=1
+            ).astype(o_ref.dtype)
+
+
+def regroup(x, count):
+    rows, columns = x.shape
+    return pl.pallas_call(
+        regroup_kernel,
+        out_shape=jax.ShapeDtypeStruct((count, rows, columns // count), x.dtype),
+        compiler_params=pltpu.CompilerParams(vmem_limit_bytes=16 * 2**20),
+        name="regroup",
+    )(x)
+
+
+def regroup_back_kernel(x_ref, o_ref):
+    parts, count, rows, width = x_ref.shape
+    for g in range(width // HEAD_DIM):
+        base = g * HEAD_DIM // PAIR * PAIR
+        shift = g * HEAD_DIM - base
+        for w in range(0, count, 2):
+            pieces = []
+            for j in (w, w + 1):
+                total = x_ref[0, j, :, base : base + PAIR].astype(F32)
+                for part in range(1, parts):
+                    total = total + x_ref[part, j, :, base : base + PAIR].astype(F32)
+                pieces.append(total[:, shift : shift + HEAD_DIM])
+            at = (g * count + w) * HEAD_DIM
+            o_ref[:, at : at + PAIR] = jnp.concatenate(pieces, axis=1)
+
+
+def regroup_back(x):
+    parts, count, rows, width = x.shape
+    return pl.pallas_call(
+        regroup_back_kernel,
+        out_shape=jax.ShapeDtypeStruct((rows, count * width), F32),
+        compiler_params=pltpu.CompilerParams(vmem_limit_bytes=16 * 2**20),
+        name="regroup_back",
+    )(x)
+
+
 def norm_parts(values):
     centred = values - jnp.mean(values, axis=-1, keepdims=True)
     spread = jnp.mean(centred * centred, axis=-1, keepdims=True)
@@ -449,15 +599,10 @@
 
 def norm_back(incoming, unit, rate, gain):
     scaled = incoming * gain
-    return (
-        rate
-        * (
-            scaled
-            - jnp.mean(scaled, axis=-1, keepdims=True)
-            - unit * jnp.mean(scaled * unit, axis=-1, keepdims=True)
-        ),
-        jnp.sum(incoming * unit, axis=0),
-        jnp.sum(incoming, axis=0),
+    return rate * (
+        scaled
+        - jnp.mean(scaled, axis=-1, keepdims=True)
+        - unit * jnp.mean(scaled * unit, axis=-1, keepdims=True)
     )
 
 
@@ -487,41 +632,16 @@
     slab = width // devices
     bias_slab = 3 * width // devices
 
-    packed = jnp.concatenate(
-        [b_qkv, ln1_gain, ln1_bias, ln2_gain, ln2_bias, segments[0].astype(BF)]
-    )
-    small = lax.all_gather(lax.all_gather(packed, "rows"), "wide")
-    flat = small.transpose(1, 0, 2)
-
-    def vector(start, size):
-        return flat[:, :, start : start + size].reshape(1, devices * size).astype(F32)
-
-    bias = vector(0, bias_slab)
-    gain_one = vector(bias_slab, slab)
-    shift_one = vector(bias_slab + slab, slab)
-    gain_two = vector(bias_slab + 2 * slab, slab)
-    shift_two = vector(bias_slab + 3 * slab, slab)
-    row_segs = lax.dynamic_index_in_dim(small, me_row, 1, keepdims=False)[
-        :, bias_slab + 4 * slab :
-    ].reshape(row_len)
-    own_bias = lax.dynamic_index_in_dim(
-        bias.reshape(3, per, wide_n, HEAD_DIM), me, 2, keepdims=False
-    ).reshape(1, 3 * span)
-
-    doc_first = jnp.sum((row_segs[:, None] < row_segs[None, :]).astype(jnp.int32), axis=0)
-    positions = jnp.arange(row_len, dtype=jnp.int32) - doc_first
-    freqs = 10000.0 ** (-2.0 * jnp.arange(ROT // 2, dtype=F32) / ROT)
-    lane = jnp.arange(PAIR) % HEAD_DIM
-    lane_freqs = jnp.where(lane < ROT, jnp.tile(freqs, PAIR // (ROT // 2)), 0.0)
-    angles = positions.astype(F32)[:, None] * lane_freqs[None, :]
-    sine = jnp.sin(angles)
-    half_rot = ROT // 2
-    tables = (
-        jnp.cos(angles),
-        jnp.where(lane < half_rot, -sine, 0.0),
-        jnp.where((lane >= half_rot) & (lane < ROT), sine, 0.0),
-    )
-    first = doc_first.reshape(1, row_len)
+    def stage(run, *args):
+        shapes = jax.eval_shape(run, *args)
+
+        def blank(*args):
+            return jax.tree.map(lambda x: jnp.zeros(x.shape, x.dtype), shapes)
+
+        return lax.cond(segments[0, 0] >= 0, run, blank, *args)
+
+    def sum_rows(x, dim):
+        return lax.psum_scatter(x, "rows", scatter_dimension=dim, tiled=True)
 
     fast_out = slab == HEAD_DIM and per == rows_n
     if fast_out:
@@ -535,120 +655,244 @@
             1,
             keepdims=False,
         ).reshape(span, width)
-    by_head = w_qkv.reshape(slab, 3 * per, wide_n, HEAD_DIM).transpose(2, 0, 1, 3)
     w_qkv_part = lax.all_to_all(
-        by_head.reshape(wide_n * slab, 3 * span), "wide", 0, 0, tiled=True
-    )
+        regroup(w_qkv, wide_n), "wide", 0, 0, tiled=True
+    ).reshape(wide_n * slab, 3 * span)
     w_qkv_own = lax.all_gather(w_qkv_part, "rows", axis=0, tiled=True)
-    gate_slab, up_slab, down_slab = (
-        lax.all_gather(w_gate, "rows", axis=0, tiled=True),
-        lax.all_gather(w_up, "rows", axis=0, tiled=True),
-        lax.all_gather(w_down, "rows", axis=0, tiled=True),
-    )
-
-    own, other = gather_plane(tokens[0])
-    act_one, q, k, v = project(
-        own, other, gain_one, shift_one, w_qkv_own, own_bias, tables
-    )
-    attn_low, logs = attend(first, q, k, v)
-    attn_own, attn_other = to_relative(attn_low)
-    inputs = tokens[0].astype(F32)
-    middle = inputs + scatter_plane(
-        dot(attn_own, w_out_own).astype(BF), dot(attn_other, w_out_own).astype(BF)
-    )
-    unit_two, rate_two = norm_parts(middle)
-    act_two = (unit_two * gain_two + shift_two).astype(BF)
-    row_act = jnp.concatenate(gather_plane(act_two))
+    units = w_gate.shape[1]
+    enter_slab = lax.all_gather(
+        jnp.concatenate([w_gate, w_up], axis=1), "rows", axis=0, tiled=True
+    )
+    down_slab = lax.all_gather(w_down, "rows", axis=0, tiled=True)
+
     grad_low = out_grad[0]
-    row_grad = jnp.concatenate(gather_plane(grad_low))
-    middle_row = row_act.shape[0] // 2
-
-    gate = dot(row_act, gate_slab)
-    upper = dot(row_act, up_slab)
-    sig = jax.nn.sigmoid(gate)
-    silu = gate * sig
-    hidden = (silu * upper).astype(BF)
-    mixed_part = dot(hidden, down_slab, NT).astype(BF)
-    mixed = scatter_plane(mixed_part[:middle_row], mixed_part[middle_row:])
-    result = (middle + mixed).astype(BF)[None]
-
-    grad_down = dot(row_grad, hidden, TN)
-    grad_hidden = dot(row_grad, down_slab)
-    grad_gate_low = (grad_hidden * upper * sig * (1.0 + gate * (1.0 - sig))).astype(BF)
-    grad_up_low = (grad_hidden * silu).astype(BF)
-    grad_gate = dot(row_act, grad_gate_low, TN)
-    grad_up = dot(row_act, grad_up_low, TN)
-    act_part = (
-        dot(grad_gate_low, gate_slab, NT) + dot(grad_up_low, up_slab, NT)
+
+    def first_stage(b_qkv, ln1_gain, ln1_bias, ln2_gain, ln2_bias, segs, tokens):
+        packed = jnp.concatenate([b_qkv, ln1_gain, ln1_bias, ln2_gain, ln2_bias, segs])
+        small = lax.all_gather(lax.all_gather(packed, "rows"), "wide")
+        got = gather_first(tokens)
+        own, other = gather_last(
+            tokens, got, gather_second(tokens, after(got, small) if got else got)
+        )
+        flat = small.transpose(1, 0, 2)
+
+        def vector(start, size):
+            return flat[:, :, start : start + size].reshape(1, devices * size).astype(F32)
+
+        row_segs = lax.dynamic_index_in_dim(small, me_row, 1, keepdims=False)[
+            :, bias_slab + 4 * slab :
+        ].reshape(row_len)
+        own_bias = lax.dynamic_index_in_dim(
+            vector(0, bias_slab).reshape(3, per, wide_n, HEAD_DIM), me, 2, keepdims=False
+        ).reshape(1, 3 * span)
+
+        doc_first = jnp.sum((row_segs[:, None] < row_segs[None, :]).astype(jnp.int32), axis=0)
+        positions = jnp.arange(row_len, dtype=jnp.int32) - doc_first
+        freqs = 10000.0 ** (-2.0 * jnp.arange(ROT // 2, dtype=F32) / ROT)
+        lane = jnp.arange(PAIR) % HEAD_DIM
+        lane_freqs = jnp.where(lane < ROT, jnp.tile(freqs, PAIR // (ROT // 2)), 0.0)
+        angles = positions.astype(F32)[:, None] * lane_freqs[None, :]
+        sine = jnp.sin(angles)
+        half_rot = ROT // 2
+        tables = (
+            jnp.cos(angles),
+            jnp.where(lane < half_rot, -sine, 0.0),
+            jnp.where((lane >= half_rot) & (lane < ROT), sine, 0.0),
+        )
+        gains = tuple(vector(bias_slab + i * slab, slab) for i in range(4))
+        return own, other, own_bias, gains, doc_first.reshape(1, row_len), tables
+
+    own, other, own_bias, gains, first, tables = stage(
+        first_stage,
+        after(b_qkv, w_qkv_part),
+        ln1_gain,
+        ln1_bias,
+        ln2_gain,
+        ln2_bias,
+        segments[0].astype(BF),
+        tokens[0],
+    )
+    gain_one, shift_one, gain_two, shift_two = gains
+    grads_got = gather_first(after(grad_low, own))
+
+    act_one, q, k, v, stats = project(
+        after(own, w_out_own), other, gain_one, shift_one, w_qkv_own, own_bias, tables
+    )
+    grads_passed = gather_second(grad_low, grads_got)
+    attn_low, logs = attend(first, after(q, *grads_got), k, v)
+    attn_low = after(attn_low, *grads_passed)
+
+    def middle_stage(attn_low, w_out_own, gain_two, shift_two, tokens, grads):
+        row_grad = jnp.concatenate(gather_last(*grads))
+        attn_halves = to_relative(attn_low)
+        total = start_scatter(*[dot(a, w_out_own).astype(BF) for a in attn_halves])
+        middle = tokens.astype(F32) + scatter_plane(total)
+        unit, rate = norm_parts(middle)
+        act_two = (unit * gain_two + shift_two).astype(BF)
+        return attn_halves, middle, unit, rate, gather_own(act_two), row_grad
+
+    attn_halves, middle, unit_two, rate_two, act_own, row_grad = stage(
+        middle_stage,
+        attn_low,
+        w_out_own,
+        gain_two,
+        shift_two,
+        tokens[0],
+        (grad_low, grads_got, grads_passed),
+    )
+
+    over_first = (((0,), (1,)), ((), ()))
+    over_second = (((1,), (0,)), ((), ()))
+
+    def enter_stage(act_own, enter_slab, row_grad):
+        act_halves = (act_own, swap(act_own, 1))
+        entered = [dot(enter_slab, act, over_first) for act in act_halves]
+        hidden = [(jax.nn.silu(e[:units]) * e[units:]).astype(BF) for e in entered]
+        grad_down = dot(
+            row_grad, jnp.concatenate(hidden, axis=1), (((0,), (1,)), ((), ()))
+        ).astype(BF)
+        return act_halves, entered, hidden, grad_down
+
+    act_halves, entered, hidden, grad_down = stage(enter_stage, act_own, enter_slab, row_grad)
+    sum_down = sum_rows(grad_down, 0)
+
+    def hidden_stage(act_halves, entered, row_grad, enter_slab, down_slab):
+        enter_grads, act_parts = [], []
+        for e, grad in zip(entered, jnp.split(row_grad, 2)):
+            gate, upper = e[:units], e[units:]
+            sig = jax.nn.sigmoid(gate)
+            grad_hidden = dot(down_slab, grad, over_first)
+            enter_grads.append(
+                jnp.concatenate(
+                    [
+                        (grad_hidden * upper * sig * (1.0 + gate * (1.0 - sig))).astype(BF),
+                        (grad_hidden * (gate * sig)).astype(BF),
+                    ]
+                )
+            )
+            act_parts.append(dot(enter_grads[-1], enter_slab, over_first).astype(BF))
+        grad_enter = dot(
+            jnp.concatenate(enter_grads, axis=1), jnp.concatenate(act_halves), over_second
+        ).astype(BF)
+        return start_scatter(*act_parts), grad_enter
+
+    act_sum, grad_enter = stage(
+        hidden_stage, act_halves, entered, row_grad, enter_slab, down_slab
+    )
+    sum_enter = sum_rows(grad_enter, 1)
+
+    def norm_stage(act_sum, unit, rate, gain, grad_low, hidden, down_slab):
+        grad_act_two = scatter_plane(act_sum)
+        grad_norm = norm_back(grad_act_two, unit, rate, gain)
+        return (
+            grad_low.astype(F32) + grad_norm,
+            jnp.sum(grad_act_two * unit, axis=0),
+            jnp.sum(grad_act_two, axis=0),
+            start_scatter(*[dot(h, down_slab, over_first).astype(BF) for h in hidden]),
+        )
+
+    grad_middle, grad_gain_two, grad_shift_two, mixed_sum = stage(
+        norm_stage, act_sum, unit_two, rate_two, gain_two, grad_low, hidden, down_slab
+    )
+
+    branch_own = stage(gather_own, after(grad_middle, sum_down).astype(BF))
+    branch_halves = (branch_own, swap(branch_own, 1))
+    grad_w_out = dot(
+        jnp.concatenate(attn_halves), jnp.concatenate(branch_halves), TN
     ).astype(BF)
-    grad_act_two = scatter_plane(act_part[:middle_row], act_part[middle_row:])
-    grad_norm, grad_gain_two, grad_shift_two = norm_back(
-        grad_act_two, unit_two, rate_two, gain_two
-    )
-    grad_middle = grad_low.astype(F32) + grad_norm
-    branch_own, branch_other = gather_plane(grad_middle.astype(BF))
-    branch = jnp.concatenate([branch_own, branch_other])
-    grad_w_out = dot(jnp.concatenate([attn_own, attn_other]), branch, TN)
-    grad_attn = to_absolute(
-        dot(branch_own, w_out_own, NT).astype(BF), dot(branch_other, w_out_own, NT).astype(BF)
-    )
-    grad_q, grad_k, grad_v = attend_back(first, q, k, v, attn_low, grad_attn, logs, tables)
-    grad_proj = jnp.concatenate([grad_q, grad_k, grad_v], axis=1)
-    grad_w_qkv = dot(act_one, grad_proj, TN)
-    grad_bias = jnp.sum(grad_proj, axis=0, dtype=F32)
-    proj_own, proj_other = to_relative(grad_proj)
-    grad_act_one = scatter_plane(
-        dot(proj_own, w_qkv_own, NT).astype(BF), dot(proj_other, w_qkv_own, NT).astype(BF)
-    )
-    unit_one, rate_one = norm_parts(inputs)
-    grad_input, grad_gain_one, grad_shift_one = norm_back(
-        grad_act_one, unit_one, rate_one, gain_one
-    )
-    grad_tokens = (grad_middle + grad_input)[None]
-
-    def sum_rows(x):
-        return lax.psum_scatter(x.astype(BF), "rows", scatter_dimension=0, tiled=True)
-
-    out_down = sum_rows(grad_down).astype(F32)
-    out_gate = sum_rows(grad_gate).astype(F32)
-    out_up = sum_rows(grad_up).astype(F32)
     if fast_out:
-        out_w_out = sum_rows(grad_w_out).astype(F32)
+        sum_w_out = sum_rows(grad_w_out, 0)
     else:
         spread_out = lax.dynamic_update_index_in_dim(
             jnp.zeros((per, wide_n, HEAD_DIM, width), BF),
-            grad_w_out.astype(BF).reshape(per, HEAD_DIM, width),
+            grad_w_out.reshape(per, HEAD_DIM, width),
             me,
             1,
         )
-        out_w_out = lax.psum_scatter(
+        sum_w_out = lax.psum_scatter(
             spread_out.reshape(width, width), ALL, scatter_dimension=0, tiled=True
-        ).astype(F32)
-    part_qkv = lax.all_to_all(sum_rows(grad_w_qkv), "wide", 0, 0, tiled=True)
-    out_qkv = (
-        part_qkv.reshape(wide_n, slab, 3 * per, HEAD_DIM)
-        .transpose(1, 2, 0, 3)
-        .reshape(slab, 3 * width)
-        .astype(F32)
-    )
-    full_bias = lax.dynamic_update_index_in_dim(
-        jnp.zeros((3, per, wide_n, HEAD_DIM), F32),
-        grad_bias.reshape(3, per, HEAD_DIM),
-        me,
-        2,
-    )
-    sums = scatter_small(
-        jnp.concatenate(
+        )
+
+    def back_stage(branch_halves, w_out_own, first, q, k, v, attn_low, logs, tables, act_one, mixed_sum):
+        grad_attn = to_absolute(*[dot(b, w_out_own, NT).astype(BF) for b in branch_halves])
+        grads = attend_back(first, q, k, v, attn_low, grad_attn, logs, tables)
+        grad_proj = jnp.concatenate(grads, axis=1)
+        return grad_proj, dot(act_one, grad_proj, TN).astype(BF), scatter_first(mixed_sum)
+
+    grad_proj, grad_w_qkv, mixed_got = stage(
+        back_stage,
+        after(branch_halves, grad_w_out),
+        w_out_own,
+        first,
+        q,
+        k,
+        v,
+        attn_low,
+        logs,
+        tables,
+        act_one,
+        mixed_sum,
+    )
+    grad_proj, grad_w_qkv = after((grad_proj, grad_w_qkv), sum_enter)
+    grad_w_qkv = after(grad_w_qkv, sum_w_out)
+    sum_qkv = sum_rows(grad_w_qkv, 0)
+
+    def last_stage(
+        grad_proj, w_qkv_own, own, other, stats, gain, grad_middle, grad_gain_two, grad_shift_two,
+        mixed_sum, mixed_got,
+    ):
+        mixed = scatter_last(mixed_sum, mixed_got, scatter_second(mixed_sum, mixed_got))
+        part_other, *sums_other = unproject(grad_proj, other, stats, w_qkv_own, 1)
+        part_own, *sums_own = unproject(grad_proj, own, stats, w_qkv_own, 0)
+        total = start_scatter(part_own, part_other)
+        grad_gain, grad_shift, grad_bias = (a + b for a, b in zip(sums_own, sums_other))
+        full_bias = lax.dynamic_update_index_in_dim(
+            jnp.zeros((3, per, wide_n, HEAD_DIM), F32),
+            grad_bias.reshape(3, per, HEAD_DIM),
+            me,
+            2,
+        )
+        small = jnp.concatenate(
             [
                 full_bias.reshape(devices, bias_slab),
-                grad_gain_one.reshape(devices, slab),
-                grad_shift_one.reshape(devices, slab),
+                grad_gain.reshape(devices, slab),
+                grad_shift.reshape(devices, slab),
                 grad_gain_two.reshape(devices, slab),
                 grad_shift_two.reshape(devices, slab),
             ],
             axis=1,
         )
-    )
+        small = small.reshape(rows_n, wide_n, -1).transpose(1, 0, 2)
+        sums = halve(small.reshape(wide_n, -1), "wide").reshape(rows_n, -1)
+        rate = stats[:local, 1:2]
+        unit = (own[:local].astype(F32) - stats[:local, 0:1]) * rate
+        return grad_middle + norm_back(scatter_plane(total), unit, rate, gain), sums, mixed
+
+    grad_tokens, sums, mixed = stage(
+        last_stage,
+        after(grad_proj, grad_w_qkv),
+        w_qkv_own,
+        own,
+        other,
+        stats,
+        gain_one,
+        grad_middle,
+        grad_gain_two,
+        grad_shift_two,
+        mixed_sum,
+        mixed_got,
+    )
+    grad_tokens = grad_tokens[None]
+    mixed, sum_down, sum_enter = after((mixed, sum_down, sum_enter), sums)
+    part_qkv = lax.all_to_all(
+        after(sum_qkv, sums).reshape(wide_n, slab, 3 * span), "wide", 0, 0, tiled=True
+    )
+    sums = halve(after(sums, sum_qkv), "rows")
+    result = (middle + mixed).astype(BF)[None]
+    out_down = sum_down.astype(F32)
+    out_gate, out_up = sum_enter[:units].T.astype(F32), sum_enter[units:].T.astype(F32)
+    out_w_out = after(sum_w_out, sums).astype(F32)
+    out_qkv = regroup_back(part_qkv[None])
     out_bias = sums[:bias_slab]
     small_outs = [
         sums[bias_slab + i * slab : bias_slab + (i + 1) * slab] for i in range(4)

time: 652 us -> 597 us (0.916)
  waiting for transfers between devices: 164 us -> 131 us
  local copies, waits for them, and re-layouts: 97.3 us -> 69.3 us
  matrix products: 120 us -> 96.2 us
  Pallas kernels: 87.2 us -> 106 us
  loops' own time: 0 us -> 11.2 us
    unnamed x179 -> x53, local copies, waits for them, and re-layouts: 42.1 us -> 8.76 us
    cond x0 -> x78, local copies, waits for them, and re-layouts: none -> 31.1 us
    all_gather x3 -> x2, waiting for transfers between devices: 26.7 us -> 0.03 us  [the longest x1 0.02 us: shards(): down_slab = lax.all_gather(w_down, 'rows', axis=0, tiled=True)]
    dot_general x17 -> x16, matrix products: 120 us -> 96.2 us  [dot(): return lax.dot_general(left, right, dims, preferred_element_type=F32)]
    pallas_call x0 -> x4, Pallas kernels: none -> 17.1 us  [the longest x2 15.3 us: unproject(): pl.pallas_call(unproject_kernel, grid_spec=pltpu.PrefetchScalarGridSpec(n...]
    another operation x0 -> x8, loops' own time: none -> 11.2 us  [stage(): return lax.cond(segments[0, 0] >= 0, run, blank, *args)]
    reduce_sum x10 -> x6, other arithmetic: 17.5 us -> 6.45 us  [the longest x3 3.21 us: norm_stage(): jnp.sum(grad_act_two, axis=0)]
    convert_element_type x3 -> x0, local copies, waits for them, and re-layouts: 9.74 us -> none  [shards(): out_qkv = part_qkv.reshape(wide_n, slab, 3 * per, HEAD_DIM).transpose(1,...]
  transfers between devices with their start and end apart: 72 -> 70, of which waited for: 32 -> 31; matrix products, arithmetic and copies ran while one was open for 34% -> 37% of each run, Pallas kernels for 13% -> 18%
where the time goes in v2:
time: 597 us; the launch traced here: 588 us
  waiting for transfers between devices  131 us (22%)
  Pallas kernels  106 us (18%)
  matrix products  96.2 us (16%)
  local copies, waits for them, and re-layouts  69.3 us (12%)
  other arithmetic  63 us (11%)
  starting transfers between devices  56.8 us (10%)
  blocking collectives  39.1 us (7%)
  between operations  15.6 us (3%)
  loops' own time  11.2 us (2%)
    ppermute x61, waiting for transfers between devices, swap(): lax.ppermute(x, axis, [(i, i ^ bit) for i in range(lax.axis_size(axis))])  116 us
    dot_general x16, matrix products, dot(): return lax.dot_general(left, right, dims, preferred_element_type=F32)  96.2 us
    ppermute x61, starting transfers between devices, swap(): lax.ppermute(x, axis, [(i, i ^ bit) for i in range(lax.axis_size(axis))])  52.6 us
    pallas_call x1, Pallas kernels, attend_back(): pl.pallas_call(attend_back_kernel, grid=(pairs, total // block), in_specs...  38.6 us
    pallas_call x1, Pallas kernels, attend(): pl.pallas_call(attend_kernel, grid=(pairs, total // block), in_specs=[pl....  34.8 us
    cond x78, local copies, waits for them, and re-layouts  31.1 us
    all_gather x2, blocking collectives, first_stage(): small = lax.all_gather(lax.all_gather(packed, 'rows'), 'wide')  21.4 us
    all_to_all x1, blocking collectives, shards(): lax.all_to_all(regroup(w_qkv, wide_n), 'wide', 0, 0, tiled=True)  17.8 us
  transfers between devices with their start and end apart: 70, of which 31 were waited for; matrix products, arithmetic and copies ran while one was open for 37% of the time, Pallas kernels for 18%

profile of v2, /device:TPU:0, one launch (start us, length us, event | category | flops | bytes accessed | tf_op | source)
XLA Modules:
  0.0 588.4 jit_solution(3614359608384525536)
XLA Ops:
  9.5 17.8 %all_to_all.10 = bf16[8,64,768]{2,1,0:T(8,128)(2,1)} all-to-all(bf16[8,64,768]{2,1,0:T(8,128)(2,1)S(1)} %regroup.1), channel_id=1, replica_groups=mesh['rows'=4,'wide'=8] {'wide'}, dimensions={0} | all-to-all | bytes 1572864 | tf_op jit(solution)/shard_map/all_to_all | solution.py:658
  31.3 51.4 %conditional.8 = (bf16[768,2048]{1,0:T(8,128)(2,1)}, bf16[768,2048]{1,0:T(8,128)(2,1)}, f32[1,768]{1,0:T(1,128)}, f32[1,2048]{1,0:T(1,128)S(1)}, f32[1,2048]{1,0...) conditional(s32[]{:T(128)} %bitcast.43, () %tuple.88, ...), branch_computations={%region_0.0_spmd, %region_1.3_spmd} | conditional | flops 7882702 | bytes 32684408 | solution.py:641
  36.9 3.4 concatenate.60
  40.3 13.3 %all-gather.2 = bf16[4,1,640]{2,1,0:T(2,128)(2,1)S(1)} all-gather(bf16[1,1,640]{2,1,0:T(2,128)(2,1)S(1)} %reshape.245), channel_id=2, replica_groups=mesh['rows'=4,'wide'=8] {'rows'}, dimensions={0}, use_global_device_ids=true | all-gather | bytes 6400 | tf_op jit(solution)/shard_map/cond/branch_1_fun/all_gather | solution.py:672
  53.6 8.1 %all-gather.3 = bf16[8,4,640]{2,1,0:T(4,128)(2,1)S(1)} all-gather(bf16[1,4,640]{2,1,0:T(4,128)(2,1)S(1)} %bitcast.155), channel_id=3, replica_groups=mesh['rows'=4,'wide'=8] {'wide'}, dimensions={0}, use_global_device_ids=true | all-gather | bytes 46080 | tf_op jit(solution)/shard_map/cond/branch_1_fun/all_gather | solution.py:672
  67.9 6.2 %collective-permute-done.10 = bf16[96,2048]{1,0:T(8,128)(2,1)S(1)} collective-permute-done((bf16[96,2048]{1,0:T(8,128)(2,1)S(1)}, bf16[96,2048]{1,0:T(8,128)(2,1)S(1)}, u32[]{:S(2)}, u32[]{:S(2)}) %collective-permute-start.10) | collective-permute-done | bytes 393248 | tf_op jit(solution)/shard_map/cond/branch_1_fun/ppermute | solution.py:30
  79.9 2.9 fusion.31
  90.6 5.4 collective-permute-done.52
  98.1 6.7 %all-gather.11.cloned.1.call-done.weight = bf16[2048,768]{1,0:T(8,128)(2,1)} async-done(((bf16[512,768]{1,0:T(8,128)(2,1)}), bf16[2048,768]{1,0:T(8,128)(2,1)}) %all-gather.11.cloned.1.call-update) | async-done | bytes 3145744 | tf_op jit(solution)/shard_map/all_gather | solution.py:661
  104.9 15.2 %project.1 = (bf16[1536,2048]{1,0:T(8,128)(2,1)}, bf16[1536,256]{1,0:T(8,128)(2,1)S(1)}, bf16[1536,256]{1,0:T(8,128)(2,1)S(1)}, bf16[1536,256]{1,0:T(8,128)(2,1)S(1)}, f32[1536,128]{1,0:T(8,128)}) custom-call(s32[8]{0:T(128)S(1)} %stack.65.order, bf16[768,2048]{1,0:T(8,128)(2,1)} %get-tuple-element.304.own_ref, ...), custom_call_target="tpu_custom_call" | custom-call | flops 16999999488 | bytes 1 | tf_op jit(solution)/shard_map/project/pallas_call | solution.py:248
  120.1 34.8 %attend.1 = (bf16[1536,256]{1,0:T(8,128)(2,1)}, f32[2,2,1536]{2,1,0:T(2,128)}) custom-call(s32[1,1536]{1,0:T(1,128)} %get-tuple-element.302.first, bf16[1536,256]{1,0:T(8,128)(2,1)S(1)} %get-tuple-element.314.q_ref, bf16[1536,256]{1,0:T(8,128)(2,1)S(1)} %get-tuple-element.315.k_ref, bf16[1536,256]{1,0:T(8,128)(2,1)S(1)} %get-tuple-element.316.v_ref), custom_call_target="tpu_custom_call" | custom-call | flops 38999998464 | bytes 1 | tf_op jit(solution)/shard_map/attend/pallas_call | solution.py:404
  155.0 79.5 %conditional.9 = (bf16[768,256]{1,0:T(8,128)(2,1)S(1)}, bf16[768,256]{1,0:T(8,128)(2,1)}, f32[192,2048]{1,0:T(8,128)S(1)}, f32[192,2048]{1,0:T(8,128)S(1)}, f32[...) conditional(s32[]{:T(128)} %bitcast.43, () %tuple.87, (bf16[1536,256]{1,0:T(8,128)(2,1)}, ...), branch_computations={%region_3.4_spmd, %region_4.7_spmd} | conditional | flops 1631453312 | bytes 133717992 | solution.py:641
  173.3 5.5 collective-permute-done.27
  186.9 5.4 collective-permute-done.28
  193.9 6.1 %collective-permute-done.29 = bf16[96,2048]{1,0:T(8,128)(2,1)S(1)} collective-permute-done((bf16[96,2048]{1,0:T(8,128)(2,1)S(1)}, bf16[96,2048]{1,0:T(8,128)(2,1)S(1)}, u32[]{:S(2)}, u32[]{:S(2)}) %collective-permute-start.29) | collective-permute-done | bytes 393248 | tf_op jit(solution)/shard_map/cond/branch_1_fun/ppermute | solution.py:30
  199.9 2.4 collective-permute-done.31
  212.2 5.8 collective-permute-done.34
  220.1 7.8 %collective-permute-done.32 = bf16[96,2048]{1,0:T(8,128)(2,1)S(1)} collective-permute-done((bf16[96,2048]{1,0:T(8,128)(2,1)S(1)}, bf16[96,2048]{1,0:T(8,128)(2,1)S(1)}, u32[]{:S(2)}, u32[]{:S(2)}) %collective-permute-start.32) | collective-permute-done | bytes 393248 | tf_op jit(solution)/shard_map/cond/branch_1_fun/ppermute | solution.py:30
  235.7 49.1 %conditional.10 = (bf16[768,2048]{1,0:T(8,128)(2,1)}, bf16[768,2048]{1,0:T(8,128)(2,1)}, f32[1408,768]{1,0:T(8,128)}, f32[1408,768]{1,0:T(8,128)}, bf16[704,768]...) conditional(s32[]{:T(128)} %bitcast.43, () %tuple.101, (bf16[768,2048]{1,0:T(8,128)(2,1)}, ...), branch_computations={%region_7.8_spmd, %region_8.9_spmd} | conditional | flops 13299810304 | bytes 90570872 | solution.py:641
  245.4 4.2 copy.175
  249.6 8.8 %fusion.59 = f32[1408,768]{1,0:T(8,128)} fusion(bf16[2048,1408]{1,0:T(8,128)(2,1)S(1)} %copy-done.34, bf16[768,2048]{1,0:T(8,128)(2,1)} %get-tuple-element.520), kind=kOutput, calls=%fused_computation.218 | convolution fusion | flops 4429185024 | bytes 13238272 | tf_op jit(solution)/shard_map/cond/branch_1_fun/dot_general | solution.py:26
  258.4 3.9 fusion.2
  262.3 8.7 %fusion.60 = f32[1408,768]{1,0:T(8,128)} fusion(bf16[2048,1408]{1,0:T(8,128)(2,1)S(1)} %copy-done.34, bf16[768,2048]{1,0:T(8,128)(2,1)} %collective-permute-done.39), kind=kOutput, calls=%fused_computation.219 | convolution fusion | flops 4429185024 | bytes 13238272 | tf_op jit(solution)/shard_map/cond/branch_1_fun/dot_general | solution.py:26
  271.0 3.9 fusion.1
  274.9 9.7 %fusion = bf16[2048,704]{0,1:T(8,128)(2,1)} fusion(bf16[1536,2048]{1,0:T(8,128)(2,1)} %get-tuple-element.169, bf16[704,768]{1,0:T(8,128)(2,1)} %fusion.1, bf16[704,768]{1,0:T(8,128)(2,1)} %fusion.2), kind=kOutput, calls=%fused_computation.46 | convolution fusion | flops 4434952192 | bytes 11337728 | tf_op jit(solution)/shard_map/cond/branch_1_fun/dot_general | solution.py:26
  284.8 44.2 %conditional.11 = (bf16[768,2048]{1,0:T(8,128)(2,1)}, bf16[1408,2048]{1,0:T(8,128)(2,1)}) conditional(s32[]{:T(128)} %bitcast.43, () %tuple.100, (bf16[1536,2048]{1,0:T(8,128)(2,1)}, bf16[2048,704]{1,0:T(8,128)(2,1)}, f32[1408,768]{1,0:T(8,128)}, bf16[2048,1408]{1,0:T(8,128)(2,1)}, f32[1408,768]{1,0:T(8,128)}, ...), branch_computations={%region_9.10_spmd, %region_10.11_spmd} | conditional | flops 22210838528 | bytes 124780680 | solution.py:641
  284.9 8.0 %multiply_convert_fusion.1 = (bf16[704,768]{1,0:T(8,128)(2,1)S(1)}, bf16[704,768]{1,0:T(8,128)(2,1)S(1)}) fusion(f32[1408,768]{1,0:T(8,128)} %get-tuple-element.174, bf16[2048,704]{1,0:T(8,128)(2,1)} %get-tuple-element.170, bf16[1536,2048]{1,0:T(8,128)(2,1)} %get-tuple-element.171), kind=kOutput, calls=%fused_computation.80 | convolution fusion | flops 2221621248 | bytes 12779520 | tf_op jit(solution)/shard_map/cond/branch_1_fun/dot_general | solution.py:26
  292.9 7.3 %convolution_convert_fusion.4 = bf16[768,2048]{1,0:T(8,128)(2,1)} fusion(bf16[2048,1408]{1,0:T(8,128)(2,1)S(1)} %copy-done.35, bf16[704,768]{1,0:T(8,128)(2,1)S(1)} %get-tuple-element.402, bf16[704,768]{1,0:T(8,128)(2,1)S(1)} %get-tuple-element.401), kind=kOutput, calls=%fused_computation.67 | convolution fusion | flops 4435083264 | bytes 11075584 | tf_op jit(solution)/shard_map/cond/branch_1_fun/dot_general | solution.py:26
  300.6 6.6 %multiply_convert_fusion.3 = (bf16[704,768]{1,0:T(8,128)(2,1)S(1)}, bf16[704,768]{1,0:T(8,128)(2,1)S(1)}) fusion(f32[1408,768]{1,0:T(8,128)} %get-tuple-element.172, bf16[2048,704]{1,0:T(8,128)(2,1)S(1)} %copy-done.36, bf16[1536,2048]{1,0:T(8,128)(2,1)} %get-tuple-element.171), kind=kOutput, calls=%fused_computation.83 | convolution fusion | flops 2221621248 | bytes 12517376 | tf_op jit(solution)/shard_map/cond/branch_1_fun/dot_general | solution.py:26
  307.2 5.3 convolution_convert_fusion.5
  312.5 13.3 %convolution_convert_fusion.3 = bf16[1408,2048]{1,0:T(8,128)(2,1)} fusion(bf16[768,2048]{1,0:T(8,128)(2,1)} %get-tuple-element.176, bf16[768,2048]{1,0:T(8,128)(2,1)} %get-tuple-element.175, bf16[704,768]{1,0:T(8,128)(2,1)S(1)} %get-tuple-element.402, bf16[704,768]{1,0:T(8,128)(2,1)S(1)} %get-tuple-element.401, bf16[704,768]{1,0:T(8,128)(2,1)} %copy-done.40, ...), kind=kOutput, calls=%fused_computation.55 | convolution fusion | flops 8891138048 | bytes 16384000 | tf_op jit(solution)/shard_map/cond/branch_1_fun/dot_general | solution.py:26
  325.8 3.0 add_convert_fusion.4
  330.2 47.6 %conditional.12 = (f32[192,2048]{1,0:T(8,128)}, f32[2048]{0:T(1024)S(1)}, f32[2048]{0:T(1024)}, bf16[768,2048]{1,0:T(8,128)(2,1)}) conditional(s32[]{:T(128)} %bitcast.43, () %tuple.99, (bf16[192,2048]{1,0:T(8,128)(2,1)S(1)}, f32[192,1]{0,1:T(1,128)}, bf16[768,2048]{1,0:T(8,128)(2,1)}, f32[1,2048]{1,0:T(1,128)S(1)}, f32[192,2048]{1,0:T(8,128)S(1)}, ...), branch_computations={%region_11.12_spmd, %region_12.18_spmd} | conditional | flops 4448448512 | bytes 75373648 | solution.py:641
  332.5 4.2 convolution_convert_fusion.6
  338.7 5.1 collective-permute-done.42
  347.0 4.4 collective-permute-done.41
  351.4 7.2 %collective-permute-done.43 = bf16[96,2048]{1,0:T(8,128)(2,1)S(1)} collective-permute-done((bf16[96,2048]{1,0:T(8,128)(2,1)S(1)}, bf16[96,2048]{1,0:T(8,128)(2,1)S(1)}, u32[]{:S(2)}, u32[]{:S(2)}) %collective-permute-start.43) | collective-permute-done | bytes 393248 | tf_op jit(solution)/shard_map/cond/branch_1_fun/ppermute | solution.py:30
  360.9 4.2 convolution_convert_fusion.7
  366.2 3.5 collective-permute-done.46
  372.2 2.4 multiply_add_fusion
  374.6 3.2 add_convert_fusion.5
  377.8 30.1 %conditional.13 = (bf16[768,2048]{1,0:T(8,128)(2,1)}) conditional(s32[]{:T(128)} %bitcast.43, () %tuple.98, f32[192,2048]{1,0:T(8,128)} %get-tuple-element.335), branch_computations={%region_19.20_spmd, %region_20.21_spmd} | conditional | flops 393215 | bytes 18874616 | solution.py:641
  377.8 2.4 constant_dynamic-update-slice_fusion.28
  384.3 8.0 %collective-permute-done.2 = bf16[96,2048]{1,0:T(8,128)(2,1)S(1)} collective-permute-done((bf16[96,2048]{1,0:T(8,128)(2,1)S(1)}, bf16[96,2048]{1,0:T(8,128)(2,1)S(1)}, u32[]{:S(2)}, u32[]{:S(2)}) %collective-permute-start.2) | collective-permute-done | bytes 393248 | tf_op jit(solution)/shard_map/cond/branch_1_fun/ppermute | solution.py:30
  394.4 7.0 %collective-permute-done = bf16[96,2048]{1,0:T(8,128)(2,1)S(1)} collective-permute-done((bf16[96,2048]{1,0:T(8,128)(2,1)S(1)}, bf16[96,2048]{1,0:T(8,128)(2,1)S(1)}, u32[]{:S(2)}, u32[]{:S(2)}) %collective-permute-start) | collective-permute-done | bytes 393248 | tf_op jit(solution)/shard_map/cond/branch_1_fun/ppermute | solution.py:30
  407.9 5.9 collective-permute-done.58
  415.4 4.9 fusion.39
  420.4 61.9 %conditional.14 = (bf16[1536,768]{1,0:T(8,128)(2,1)}, bf16[2048,768]{0,1:T(8,128)(2,1)}, bf16[96,2048]{1,0:T(8,128)(2,1)}, bf16[96,2048]{1,0:T(8,128)(2,1)}, bf1...) conditional(s32[]{:T(128)} %bitcast.43, () %tuple.97, (bf16[768,2048]{1,0:T(8,128)(2,1)}, ...), branch_computations={%region_21.22_spmd, %region_22.23_spmd} | conditional | flops 50445991936 | bytes 72975448 | solution.py:641
  420.6 2.5 fusion.51
  427.2 3.1 convolution_convert_fusion.10
  432.4 38.6 %attend_back.1 = (bf16[1536,256]{1,0:T(8,128)(2,1)S(1)}, bf16[1536,256]{1,0:T(8,128)(2,1)S(1)}, bf16[1536,256]{1,0:T(8,128)(2,1)S(1)}) custom-call(s32[1,1536]{1,0:T(1,128)} %get-tuple-element.185.first, bf16[1536,256]{1,0:T(8,128)(2,1)} %get-tuple-element.186.q_ref, bf16[1536,256]{1,0:T(8,128)(2,1)} %get-tuple-element.187.k_ref, ...), custom_call_target="tpu_custom_call" | custom-call | flops 44000002048 | bytes 1 | tf_op jit(solution)/shard_map/cond/branch_1_fun/attend_back/pallas_call | solution.py:511
  474.1 8.2 %fusion.30 = bf16[2048,768]{0,1:T(8,128)(2,1)} fusion(bf16[1536,768]{1,0:T(8,128)(2,1)} %constant_dynamic-update-slice_fusion.29, bf16[1536,2048]{1,0:T(8,128)(2,1)S(1)} %bitcast.158), kind=kOutput, calls=%fused_computation.110 | convolution fusion | flops 4833411072 | bytes 11796480 | tf_op jit(solution)/shard_map/cond/branch_1_fun/dot_general | solution.py:26
  484.2 73.9 %conditional.15 = (f32[4,448]{1,0:T(4,128)}, f32[192,2048]{1,0:T(8,128)}, f32[1,192,2048]{2,1,0:T(8,128)}) conditional(s32[]{:T(128)} %bitcast.43, () %tuple.96, (bf16[1536,768]{1,0:T(8,128)(2,1)}, bf16[768,2048]{1,0:T(8,128)(2,1)}, f32[1536,128]{1,0:T(8,128)S(1)}, bf16[2048,768]{1,0:T(8,128)(2,1)}, bf16[768,2048]{1,0:T(8,128)(2,1)}, ...), branch_computations={%region_25.26_spmd, %region_26.29_spmd} | conditional | flops 14020857856 | bytes 78349888 | solution.py:641
  484.3 8.3 %unproject.3 = (bf16[768,2048]{1,0:T(8,128)(2,1)}, f32[1,2048]{1,0:T(1,128)S(1)}, f32[1,2048]{1,0:T(1,128)S(1)}, f32[1,768]{1,0:T(1,128)S(1)}) custom-call(s32[4]{0:T(128)S(1)} %get-tuple-element.431.order, bf16[1536,768]{1,0:T(8,128)(2,1)} %get-tuple-element.202.g_ref, bf16[768,2048]{1,0:T(8,128)(2,1)} %get-tuple-element.207.x_ref, ...), custom_call_target="tpu_custom_call" | custom-call | flops 7000000000 | bytes 1 | tf_op jit(solution)/shard_map/cond/branch_1_fun/unproject/pallas_call | solution.py:312
  492.7 7.0 %unproject.2 = (bf16[768,2048]{1,0:T(8,128)(2,1)S(1)}, f32[1,2048]{1,0:T(1,128)S(1)}, f32[1,2048]{1,0:T(1,128)S(1)}, f32[1,768]{1,0:T(1,128)S(1)}) custom-call(s32[4]{0:T(128)S(1)} %get-tuple-element.430.order, bf16[1536,768]{1,0:T(8,128)(2,1)} %get-tuple-element.202.g_ref, bf16[768,2048]{1,0:T(8,128)(2,1)} %get-tuple-element.203.x_ref, ...), custom_call_target="tpu_custom_call" | custom-call | flops 7000000000 | bytes 1 | tf_op jit(solution)/shard_map/cond/branch_1_fun/unproject/pallas_call | solution.py:312
  502.7 2.5 collective-permute-done.13
  510.6 3.2 add_convert_fusion.8
  521.8 5.9 collective-permute-done.20
  536.1 4.8 collective-permute-done.21
  548.5 3.4 collective-permute-done.24
  554.7 3.4 add_bitcast_fusion
  559.3 3.1 fusion.42
  563.5 3.7 all-to-all-start.1
  572.1 7.6 %all-to-all-done.1 = bf16[8,64,768]{2,1,0:T(8,128)(2,1)S(1)} async-done(((bf16[8,64,768]{2,1,0:T(8,128)(2,1)}), bf16[8,64,768]{2,1,0:T(8,128)(2,1)S(1)}, u32[]{:S(2)}, u32[]{:S(2)}) %all-to-all-start.1) | async-done | bytes 786464 | tf_op jit(solution)/shard_map/all_to_all | solution.py:887
  (365 shorter events, 164.7 us)
Async XLA Ops:
  7.2 91.0 %all-gather.9.cloned.1.call-start = ((), (), s32[]{:S(2)}) async-start(), calls=%async_computation.6 | async-start | bytes 1310720 | tf_op jit(solution)/shard_map/all_gather | solution.py:648
  7.9 97.0 %all-gather.11.cloned.1.call-start = ((), (), s32[]{:S(2)}) async-start(), calls=%async_computation.7 | async-start | bytes 3932160 | tf_op jit(solution)/shard_map/all_gather | solution.py:661
  27.2 207.3 %all-gather.15.cloned.1.call-start = ((), (), s32[]{:S(2)}) async-start(), calls=%async_computation.9 | async-start | bytes 7208960 | tf_op jit(solution)/shard_map/all_gather | solution.py:663
  29.4 255.4 %all-gather.13.cloned.1.call-start = ((), (), s32[]{:S(2)}) async-start(), calls=%async_computation.8 | async-start | bytes 3932160 | tf_op jit(solution)/shard_map/all_gather | solution.py:666
  32.2 30.5 %collective-permute-start.6 = (bf16[96,2048]{1,0:T(8,128)(2,1)}, bf16[96,2048]{1,0:T(8,128)(2,1)S(1)}, u32[]{:S(2)}, u32[]{:S(2)}) collective-permute-start(bf16[96,2048]{1,0:T(8,128)(2,1)} %get-tuple-element.410), channel_id=1, source_target_pairs={{0,2},{1,3},{2,0},{3,1},{4,6},{5,7},{6,4},{7,5},{8,10},{9,11},{10,... | collective-permute-start | bytes 1179656 | tf_op jit(solution)/shard_map/cond/branch_1_fun/ppermute | solution.py:30
  32.7 29.9 %collective-permute-start.7 = (bf16[96,2048]{1,0:T(8,128)(2,1)S(1)}, bf16[96,2048]{1,0:T(8,128)(2,1)S(1)}, u32[]{:S(2)}, u32[]{:S(2)}) collective-permute-start(bf16[96,2048]{1,0:T(8,128)(2,1)S(1)} %get-tuple-element.409), channel_id=1, source_target_pairs={{0,2},{1,3},{2,0},{3,1},{4,6},{5,7},{6,4},{7,5},{8,10},{9,11},{10,... | collective-permute-start | bytes 1179656 | tf_op jit(solution)/shard_map/cond/branch_1_fun/ppermute | solution.py:30
  34.2 28.5 %collective-permute-start.8 = (bf16[96,2048]{1,0:T(8,128)(2,1)}, bf16[96,2048]{1,0:T(8,128)(2,1)S(1)}, u32[]{:S(2)}, u32[]{:S(2)}) collective-permute-start(bf16[96,2048]{1,0:T(8,128)(2,1)} %get-tuple-element.410), channel_id=1, source_target_pairs={{0,4},{1,5},{2,6},{3,7},{4,0},{5,1},{6,2},{7,3},{8,12},{9,13},{10,... | collective-permute-start | bytes 1179656 | tf_op jit(solution)/shard_map/cond/branch_1_fun/ppermute | solution.py:30
  34.8 27.9 %collective-permute-start.9 = (bf16[96,2048]{1,0:T(8,128)(2,1)S(1)}, bf16[96,2048]{1,0:T(8,128)(2,1)S(1)}, u32[]{:S(2)}, u32[]{:S(2)}) collective-permute-start(bf16[96,2048]{1,0:T(8,128)(2,1)S(1)} %get-tuple-element.409), channel_id=1, source_target_pairs={{0,4},{1,5},{2,6},{3,7},{4,0},{5,1},{6,2},{7,3},{8,12},{9,13},{10,... | collective-permute-start | bytes 1179656 | tf_op jit(solution)/shard_map/cond/branch_1_fun/ppermute | solution.py:30
  62.7 11.4 %collective-permute-start.10 = (bf16[96,2048]{1,0:T(8,128)(2,1)S(1)}, bf16[96,2048]{1,0:T(8,128)(2,1)S(1)}, u32[]{:S(2)}, u32[]{:S(2)}) collective-permute-start(bf16[96,2048]{1,0:T(8,128)(2,1)S(1)} %collective-permute-done.8), channel_id=1, source_target_pairs={{0,2},{1,3},{2,0},{3,1},{4,6},{5,7},{6,4},{7,5},{8,10},{9,11},{10,... | collective-permute-start | bytes 1179656 | tf_op jit(solution)/shard_map/cond/branch_1_fun/ppermute | solution.py:30
  64.3 11.1 %collective-permute-start.11 = (bf16[96,2048]{1,0:T(8,128)(2,1)S(1)}, bf16[96,2048]{1,0:T(8,128)(2,1)S(1)}, u32[]{:S(2)}, u32[]{:S(2)}) collective-permute-start(bf16[96,2048]{1,0:T(8,128)(2,1)S(1)} %collective-permute-done.7), channel_id=1, source_target_pairs={{0,4},{1,5},{2,6},{3,7},{4,0},{5,1},{6,2},{7,3},{8,12},{9,13},{10,... | collective-permute-start | bytes 1179656 | tf_op jit(solution)/shard_map/cond/branch_1_fun/ppermute | solution.py:30
  76.1 6.6 %collective-permute-start.12 = (bf16[768,2048]{1,0:T(8,128)(2,1)}, bf16[768,2048]{1,0:T(8,128)(2,1)}, u32[]{:S(2)}, u32[]{:S(2)}) collective-permute-start(bf16[768,2048]{1,0:T(8,128)(2,1)} %constant_dynamic-update-slice_fusion.32), channel_id=1, source_target_pairs={{0,1},{1,0},{2,3},{3,2},{4,5},{5,4},{6,7},{7,6},{8,9},{9,8},{10,11... | collective-permute-start | bytes 9437192 | tf_op jit(solution)/shard_map/cond/branch_1_fun/ppermute | solution.py:30
  83.8 12.1 %collective-permute-start.52 = (bf16[96,2048]{1,0:T(8,128)(2,1)}, bf16[96,2048]{1,0:T(8,128)(2,1)S(1)}, u32[]{:S(2)}, u32[]{:S(2)}) collective-permute-start(bf16[96,2048]{1,0:T(8,128)(2,1)} %get-tuple-element.472), channel_id=1, source_target_pairs={{0,4},{1,5},{2,6},{3,7},{4,0},{5,1},{6,2},{7,3},{8,12},{9,13},{10,... | collective-permute-start | bytes 1179656 | tf_op jit(solution)/shard_map/ppermute | solution.py:30
  84.9 12.3 %collective-permute-start.53 = (bf16[96,2048]{1,0:T(8,128)(2,1)}, bf16[96,2048]{1,0:T(8,128)(2,1)}, u32[]{:S(2)}, u32[]{:S(2)}) collective-permute-start(bf16[96,2048]{1,0:T(8,128)(2,1)} %get-tuple-element.471), channel_id=1, source_target_pairs={{0,2},{1,3},{2,0},{3,1},{4,6},{5,7},{6,4},{7,5},{8,10},{9,11},{10,... | collective-permute-start | bytes 1179656 | tf_op jit(solution)/shard_map/ppermute | solution.py:30
  88.2 289.6 %reduce-scatter.5.cloned.1.call-start = ((), (), s32[]{:S(2)}) async-start(), calls=%async_computation.10 | async-start | bytes 3604480 | tf_op jit(solution)/shard_map/reduce_scatter | solution.py:644
  88.6 31.6 %collective-permute-start.54 = (bf16[96,2048]{1,0:T(8,128)(2,1)}, bf16[96,2048]{1,0:T(8,128)(2,1)}, u32[]{:S(2)}, u32[]{:S(2)}) collective-permute-start(bf16[96,2048]{1,0:T(8,128)(2,1)} %get-tuple-element.471), channel_id=1, source_target_pairs={{0,4},{1,5},{2,6},{3,7},{4,0},{5,1},{6,2},{7,3},{8,12},{9,13},{10,... | collective-permute-start | bytes 1179656 | tf_op jit(solution)/shard_map/ppermute | solution.py:30
  89.7 30.5 %collective-permute-start.55 = (bf16[96,2048]{1,0:T(8,128)(2,1)}, bf16[96,2048]{1,0:T(8,128)(2,1)}, u32[]{:S(2)}, u32[]{:S(2)}) collective-permute-start(bf16[96,2048]{1,0:T(8,128)(2,1)} %get-tuple-element.472), channel_id=1, source_target_pairs={{0,2},{1,3},{2,0},{3,1},{4,6},{5,7},{6,4},{7,5},{8,10},{9,11},{10,... | collective-permute-start | bytes 1179656 | tf_op jit(solution)/shard_map/ppermute | solution.py:30
  96.0 59.0 %collective-permute-start.56 = (bf16[96,2048]{1,0:T(8,128)(2,1)S(1)}, bf16[96,2048]{1,0:T(8,128)(2,1)}, u32[]{:S(2)}, u32[]{:S(2)}) collective-permute-start(bf16[96,2048]{1,0:T(8,128)(2,1)S(1)} %collective-permute-done.52), channel_id=1, source_target_pairs={{0,2},{1,3},{2,0},{3,1},{4,6},{5,7},{6,4},{7,5},{8,10},{9,11},{10,... | collective-permute-start | bytes 1179656 | tf_op jit(solution)/shard_map/ppermute | solution.py:30
  97.2 57.8 %collective-permute-start.57 = (bf16[96,2048]{1,0:T(8,128)(2,1)}, bf16[96,2048]{1,0:T(8,128)(2,1)}, u32[]{:S(2)}, u32[]{:S(2)}) collective-permute-start(bf16[96,2048]{1,0:T(8,128)(2,1)} %collective-permute-done.53), channel_id=1, source_target_pairs={{0,4},{1,5},{2,6},{3,7},{4,0},{5,1},{6,2},{7,3},{8,12},{9,13},{10,... | collective-permute-start | bytes 1179656 | tf_op jit(solution)/shard_map/ppermute | solution.py:30
  166.9 12.0 %collective-permute-start.27 = (bf16[96,2048]{1,0:T(8,128)(2,1)S(1)}, bf16[96,2048]{1,0:T(8,128)(2,1)S(1)}, u32[]{:S(2)}, u32[]{:S(2)}) collective-permute-start(bf16[96,2048]{1,0:T(8,128)(2,1)S(1)} %get-tuple-element.437), channel_id=1, source_target_pairs={{0,2},{1,3},{2,0},{3,1},{4,6},{5,7},{6,4},{7,5},{8,10},{9,11},{10,... | collective-permute-start | bytes 1179656 | tf_op jit(solution)/shard_map/cond/branch_1_fun/ppermute | solution.py:30
  171.0 15.8 %collective-permute-start.26 = (bf16[96,2048]{1,0:T(8,128)(2,1)S(1)}, bf16[96,2048]{1,0:T(8,128)(2,1)S(1)}, u32[]{:S(2)}, u32[]{:S(2)}) collective-permute-start(bf16[96,2048]{1,0:T(8,128)(2,1)S(1)} %get-tuple-element.434), channel_id=1, source_target_pairs={{0,2},{1,3},{2,0},{3,1},{4,6},{5,7},{6,4},{7,5},{8,10},{9,11},{10,... | collective-permute-start | bytes 1179656 | tf_op jit(solution)/shard_map/cond/branch_1_fun/ppermute | solution.py:30
  171.9 15.0 %collective-permute-start.30 = (bf16[96,2048]{1,0:T(8,128)(2,1)S(1)}, bf16[96,2048]{1,0:T(8,128)(2,1)S(1)}, u32[]{:S(2)}, u32[]{:S(2)}) collective-permute-start(bf16[96,2048]{1,0:T(8,128)(2,1)S(1)} %get-tuple-element.435), channel_id=1, source_target_pairs={{0,4},{1,5},{2,6},{3,7},{4,0},{5,1},{6,2},{7,3},{8,12},{9,13},{10,... | collective-permute-start | bytes 1179656 | tf_op jit(solution)/shard_map/cond/branch_1_fun/ppermute | solution.py:30
  179.0 13.3 %collective-permute-start.28 = (bf16[96,2048]{1,0:T(8,128)(2,1)S(1)}, bf16[96,2048]{1,0:T(8,128)(2,1)S(1)}, u32[]{:S(2)}, u32[]{:S(2)}) collective-permute-start(bf16[96,2048]{1,0:T(8,128)(2,1)S(1)} %add_convert_fusion.3), channel_id=1, source_target_pairs={{0,4},{1,5},{2,6},{3,7},{4,0},{5,1},{6,2},{7,3},{8,12},{9,13},{10,... | collective-permute-start | bytes 1179656 | tf_op jit(solution)/shard_map/cond/branch_1_fun/ppermute | solution.py:30
  184.2 25.2 %collective-permute-start.38 = (bf16[768,2048]{1,0:T(8,128)(2,1)S(1)}, bf16[768,2048]{1,0:T(8,128)(2,1)S(1)}, u32[]{:S(2)}, u32[]{:S(2)}) collective-permute-start(bf16[768,2048]{1,0:T(8,128)(2,1)S(1)} %get-tuple-element.450), channel_id=1, source_target_pairs={{0,1},{1,0},{2,3},{3,2},{4,5},{5,4},{6,7},{7,6},{8,9},{9,8},{10,11... | collective-permute-start | bytes 9437192 | tf_op jit(solution)/shard_map/cond/branch_1_fun/ppermute | solution.py:30
  184.2 15.7 %collective-permute-start.29 = (bf16[96,2048]{1,0:T(8,128)(2,1)S(1)}, bf16[96,2048]{1,0:T(8,128)(2,1)S(1)}, u32[]{:S(2)}, u32[]{:S(2)}) collective-permute-start(bf16[96,2048]{1,0:T(8,128)(2,1)S(1)} %get-tuple-element.436), channel_id=1, source_target_pairs={{0,4},{1,5},{2,6},{3,7},{4,0},{5,1},{6,2},{7,3},{8,12},{9,13},{10,... | collective-permute-start | bytes 1179656 | tf_op jit(solution)/shard_map/cond/branch_1_fun/ppermute | solution.py:30
  192.5 9.8 %collective-permute-start.31 = (bf16[96,2048]{1,0:T(8,128)(2,1)S(1)}, bf16[96,2048]{1,0:T(8,128)(2,1)S(1)}, u32[]{:S(2)}, u32[]{:S(2)}) collective-permute-start(bf16[96,2048]{1,0:T(8,128)(2,1)S(1)} %get-tuple-element.433), channel_id=1, source_target_pairs={{0,2},{1,3},{2,0},{3,1},{4,6},{5,7},{6,4},{7,5},{8,10},{9,11},{10,... | collective-permute-start | bytes 1179656 | tf_op jit(solution)/shard_map/cond/branch_1_fun/ppermute | solution.py:30
  205.9 12.1 %collective-permute-start.34 = (bf16[96,2048]{1,0:T(8,128)(2,1)S(1)}, bf16[96,2048]{1,0:T(8,128)(2,1)S(1)}, u32[]{:S(2)}, u32[]{:S(2)}) collective-permute-start(bf16[96,2048]{1,0:T(8,128)(2,1)S(1)} %get-tuple-element.441), channel_id=1, source_target_pairs={{0,4},{1,5},{2,6},{3,7},{4,0},{5,1},{6,2},{7,3},{8,12},{9,13},{10,... | collective-permute-start | bytes 1179656 | tf_op jit(solution)/shard_map/cond/branch_1_fun/ppermute | solution.py:30
  207.4 12.1 %collective-permute-start.33 = (bf16[96,2048]{1,0:T(8,128)(2,1)S(1)}, bf16[96,2048]{1,0:T(8,128)(2,1)S(1)}, u32[]{:S(2)}, u32[]{:S(2)}) collective-permute-start(bf16[96,2048]{1,0:T(8,128)(2,1)S(1)} %get-tuple-element.440), channel_id=1, source_target_pairs={{0,2},{1,3},{2,0},{3,1},{4,6},{5,7},{6,4},{7,5},{8,10},{9,11},{10,... | collective-permute-start | bytes 1179656 | tf_op jit(solution)/shard_map/cond/branch_1_fun/ppermute | solution.py:30
  208.1 19.9 %collective-permute-start.32 = (bf16[96,2048]{1,0:T(8,128)(2,1)S(1)}, bf16[96,2048]{1,0:T(8,128)(2,1)S(1)}, u32[]{:S(2)}, u32[]{:S(2)}) collective-permute-start(bf16[96,2048]{1,0:T(8,128)(2,1)S(1)} %get-tuple-element.441), channel_id=1, source_target_pairs={{0,2},{1,3},{2,0},{3,1},{4,6},{5,7},{6,4},{7,5},{8,10},{9,11},{10,... | collective-permute-start | bytes 1179656 | tf_op jit(solution)/shard_map/cond/branch_1_fun/ppermute | solution.py:30
  211.6 18.6 %collective-permute-start.35 = (bf16[96,2048]{1,0:T(8,128)(2,1)S(1)}, bf16[96,2048]{1,0:T(8,128)(2,1)S(1)}, u32[]{:S(2)}, u32[]{:S(2)}) collective-permute-start(bf16[96,2048]{1,0:T(8,128)(2,1)S(1)} %get-tuple-element.440), channel_id=1, source_target_pairs={{0,4},{1,5},{2,6},{3,7},{4,0},{5,1},{6,2},{7,3},{8,12},{9,13},{10,... | collective-permute-start | bytes 1179656 | tf_op jit(solution)/shard_map/cond/branch_1_fun/ppermute | solution.py:30
  218.0 14.9 %collective-permute-start.36 = (bf16[96,2048]{1,0:T(8,128)(2,1)S(1)}, bf16[96,2048]{1,0:T(8,128)(2,1)S(1)}, u32[]{:S(2)}, u32[]{:S(2)}) collective-permute-start(bf16[96,2048]{1,0:T(8,128)(2,1)S(1)} %collective-permute-done.34), channel_id=1, source_target_pairs={{0,2},{1,3},{2,0},{3,1},{4,6},{5,7},{6,4},{7,5},{8,10},{9,11},{10,... | collective-permute-start | bytes 1179656 | tf_op jit(solution)/shard_map/cond/branch_1_fun/ppermute | solution.py:30
  219.5 14.2 %collective-permute-start.37 = (bf16[96,2048]{1,0:T(8,128)(2,1)S(1)}, bf16[96,2048]{1,0:T(8,128)(2,1)S(1)}, u32[]{:S(2)}, u32[]{:S(2)}) collective-permute-start(bf16[96,2048]{1,0:T(8,128)(2,1)S(1)} %collective-permute-done.33), channel_id=1, source_target_pairs={{0,4},{1,5},{2,6},{3,7},{4,0},{5,1},{6,2},{7,3},{8,12},{9,13},{10,... | collective-permute-start | bytes 1179656 | tf_op jit(solution)/shard_map/cond/branch_1_fun/ppermute | solution.py:30
  245.4 16.9 %collective-permute-start.39 = (bf16[768,2048]{1,0:T(8,128)(2,1)}, bf16[768,2048]{1,0:T(8,128)(2,1)}, u32[]{:S(2)}, u32[]{:S(2)}) collective-permute-start(bf16[768,2048]{1,0:T(8,128)(2,1)} %get-tuple-element.520), channel_id=1, source_target_pairs={{0,1},{1,0},{2,3},{3,2},{4,5},{5,4},{6,7},{7,6},{8,9},{9,8},{10,11... | collective-permute-start | bytes 9437192 | tf_op jit(solution)/shard_map/cond/branch_1_fun/ppermute | solution.py:30
  284.8 197.6 %reduce-scatter.7.cloned.1.call-start = ((), (), s32[]{:S(2)}) async-start(), calls=%async_computation.11 | async-start | bytes 7208960 | tf_op jit(solution)/shard_map/reduce_scatter | solution.py:644
  300.2 25.7 %collective-permute-start.40 = (bf16[768,2048]{1,0:T(8,128)(2,1)}, bf16[768,2048]{1,0:T(8,128)(2,1)S(1)}, u32[]{:S(2)}, u32[]{:S(2)}) collective-permute-start(bf16[768,2048]{1,0:T(8,128)(2,1)} %convolution_convert_fusion.4), channel_id=1, source_target_pairs={{0,1},{1,0},{2,3},{3,2},{4,5},{5,4},{6,7},{7,6},{8,9},{9,8},{10,11... | collective-permute-start | bytes 9437192 | tf_op jit(solution)/shard_map/cond/branch_1_fun/ppermute | solution.py:30
  329.1 153.3 %reduce-scatter.9.cloned.1.call-start = ((), (), s32[]{:S(2)}) async-start(), calls=%async_computation.12 | async-start | bytes 1310720 | tf_op jit(solution)/shard_map/reduce_scatter | solution.py:644
  331.8 12.0 %collective-permute-start.42 = (bf16[96,2048]{1,0:T(8,128)(2,1)S(1)}, bf16[96,2048]{1,0:T(8,128)(2,1)S(1)}, u32[]{:S(2)}, u32[]{:S(2)}) collective-permute-start(bf16[96,2048]{1,0:T(8,128)(2,1)S(1)} %get-tuple-element.466), channel_id=1, source_target_pairs={{0,2},{1,3},{2,0},{3,1},{4,6},{5,7},{6,4},{7,5},{8,10},{9,11},{10,... | collective-permute-start | bytes 1179656 | tf_op jit(solution)/shard_map/cond/branch_1_fun/ppermute | solution.py:30
  336.7 37.9 %collective-permute-start.47 = (bf16[768,2048]{1,0:T(8,128)(2,1)S(1)}, bf16[768,2048]{1,0:T(8,128)(2,1)S(1)}, u32[]{:S(2)}, u32[]{:S(2)}) collective-permute-start(bf16[768,2048]{1,0:T(8,128)(2,1)S(1)} %convolution_convert_fusion.6), channel_id=1, source_target_pairs={{0,1},{1,0},{2,3},{3,2},{4,5},{5,4},{6,7},{7,6},{8,9},{9,8},{10,11... | collective-permute-start | bytes 9437192 | tf_op jit(solution)/shard_map/cond/branch_1_fun/ppermute | solution.py:30
  336.9 14.5 %collective-permute-start.41 = (bf16[96,2048]{1,0:T(8,128)(2,1)S(1)}, bf16[96,2048]{1,0:T(8,128)(2,1)S(1)}, u32[]{:S(2)}, u32[]{:S(2)}) collective-permute-start(bf16[96,2048]{1,0:T(8,128)(2,1)S(1)} %get-tuple-element.463), channel_id=1, source_target_pairs={{0,2},{1,3},{2,0},{3,1},{4,6},{5,7},{6,4},{7,5},{8,10},{9,11},{10,... | collective-permute-start | bytes 1179656 | tf_op jit(solution)/shard_map/cond/branch_1_fun/ppermute | solution.py:30
  338.2 13.2 %collective-permute-start.45 = (bf16[96,2048]{1,0:T(8,128)(2,1)S(1)}, bf16[96,2048]{1,0:T(8,128)(2,1)S(1)}, u32[]{:S(2)}, u32[]{:S(2)}) collective-permute-start(bf16[96,2048]{1,0:T(8,128)(2,1)S(1)} %get-tuple-element.464), channel_id=1, source_target_pairs={{0,4},{1,5},{2,6},{3,7},{4,0},{5,1},{6,2},{7,3},{8,12},{9,13},{10,... | collective-permute-start | bytes 1179656 | tf_op jit(solution)/shard_map/cond/branch_1_fun/ppermute | solution.py:30
  344.9 13.7 %collective-permute-start.43 = (bf16[96,2048]{1,0:T(8,128)(2,1)S(1)}, bf16[96,2048]{1,0:T(8,128)(2,1)S(1)}, u32[]{:S(2)}, u32[]{:S(2)}) collective-permute-start(bf16[96,2048]{1,0:T(8,128)(2,1)S(1)} %add_convert_fusion.7), channel_id=1, source_target_pairs={{0,4},{1,5},{2,6},{3,7},{4,0},{5,1},{6,2},{7,3},{8,12},{9,13},{10,... | collective-permute-start | bytes 1179656 | tf_op jit(solution)/shard_map/cond/branch_1_fun/ppermute | solution.py:30
  345.5 20.7 %collective-permute-start.44 = (bf16[96,2048]{1,0:T(8,128)(2,1)S(1)}, bf16[96,2048]{1,0:T(8,128)(2,1)S(1)}, u32[]{:S(2)}, u32[]{:S(2)}) collective-permute-start(bf16[96,2048]{1,0:T(8,128)(2,1)S(1)} %get-tuple-element.465), channel_id=1, source_target_pairs={{0,4},{1,5},{2,6},{3,7},{4,0},{5,1},{6,2},{7,3},{8,12},{9,13},{10,... | collective-permute-start | bytes 1179656 | tf_op jit(solution)/shard_map/cond/branch_1_fun/ppermute | solution.py:30
  360.0 9.8 %collective-permute-start.46 = (bf16[96,2048]{1,0:T(8,128)(2,1)S(1)}, bf16[96,2048]{1,0:T(8,128)(2,1)S(1)}, u32[]{:S(2)}, u32[]{:S(2)}) collective-permute-start(bf16[96,2048]{1,0:T(8,128)(2,1)S(1)} %get-tuple-element.462), channel_id=1, source_target_pairs={{0,2},{1,3},{2,0},{3,1},{4,6},{5,7},{6,4},{7,5},{8,10},{9,11},{10,... | collective-permute-start | bytes 1179656 | tf_op jit(solution)/shard_map/cond/branch_1_fun/ppermute | solution.py:30
  380.2 12.1 %collective-permute-start.2 = (bf16[96,2048]{1,0:T(8,128)(2,1)S(1)}, bf16[96,2048]{1,0:T(8,128)(2,1)S(1)}, u32[]{:S(2)}, u32[]{:S(2)}) collective-permute-start(bf16[96,2048]{1,0:T(8,128)(2,1)S(1)} %get-tuple-element.404), channel_id=1, source_target_pairs={{0,4},{1,5},{2,6},{3,7},{4,0},{5,1},{6,2},{7,3},{8,12},{9,13},{10,... | collective-permute-start | bytes 1179656 | tf_op jit(solution)/shard_map/cond/branch_1_fun/ppermute | solution.py:30
  380.8 12.1 %collective-permute-start.1 = (bf16[96,2048]{1,0:T(8,128)(2,1)S(1)}, bf16[96,2048]{1,0:T(8,128)(2,1)S(1)}, u32[]{:S(2)}, u32[]{:S(2)}) collective-permute-start(bf16[96,2048]{1,0:T(8,128)(2,1)S(1)} %get-tuple-element.403), channel_id=1, source_target_pairs={{0,2},{1,3},{2,0},{3,1},{4,6},{5,7},{6,4},{7,5},{8,10},{9,11},{10,... | collective-permute-start | bytes 1179656 | tf_op jit(solution)/shard_map/cond/branch_1_fun/ppermute | solution.py:30
  381.5 19.8 %collective-permute-start = (bf16[96,2048]{1,0:T(8,128)(2,1)S(1)}, bf16[96,2048]{1,0:T(8,128)(2,1)S(1)}, u32[]{:S(2)}, u32[]{:S(2)}) collective-permute-start(bf16[96,2048]{1,0:T(8,128)(2,1)S(1)} %get-tuple-element.404), channel_id=1, source_target_pairs={{0,2},{1,3},{2,0},{3,1},{4,6},{5,7},{6,4},{7,5},{8,10},{9,11},{10,... | collective-permute-start | bytes 1179656 | tf_op jit(solution)/shard_map/cond/branch_1_fun/ppermute | solution.py:30
  382.9 20.8 %collective-permute-start.3 = (bf16[96,2048]{1,0:T(8,128)(2,1)S(1)}, bf16[96,2048]{1,0:T(8,128)(2,1)S(1)}, u32[]{:S(2)}, u32[]{:S(2)}) collective-permute-start(bf16[96,2048]{1,0:T(8,128)(2,1)S(1)} %get-tuple-element.403), channel_id=1, source_target_pairs={{0,4},{1,5},{2,6},{3,7},{4,0},{5,1},{6,2},{7,3},{8,12},{9,13},{10,... | collective-permute-start | bytes 1179656 | tf_op jit(solution)/shard_map/cond/branch_1_fun/ppermute | solution.py:30
  392.3 14.0 %collective-permute-start.4 = (bf16[96,2048]{1,0:T(8,128)(2,1)S(1)}, bf16[96,2048]{1,0:T(8,128)(2,1)S(1)}, u32[]{:S(2)}, u32[]{:S(2)}) collective-permute-start(bf16[96,2048]{1,0:T(8,128)(2,1)S(1)} %collective-permute-done.2), channel_id=1, source_target_pairs={{0,2},{1,3},{2,0},{3,1},{4,6},{5,7},{6,4},{7,5},{8,10},{9,11},{10,... | collective-permute-start | bytes 1179656 | tf_op jit(solution)/shard_map/cond/branch_1_fun/ppermute | solution.py:30
  392.9 14.2 %collective-permute-start.5 = (bf16[96,2048]{1,0:T(8,128)(2,1)S(1)}, bf16[96,2048]{1,0:T(8,128)(2,1)S(1)}, u32[]{:S(2)}, u32[]{:S(2)}) collective-permute-start(bf16[96,2048]{1,0:T(8,128)(2,1)S(1)} %collective-permute-done.1), channel_id=1, source_target_pairs={{0,4},{1,5},{2,6},{3,7},{4,0},{5,1},{6,2},{7,3},{8,12},{9,13},{10,... | collective-permute-start | bytes 1179656 | tf_op jit(solution)/shard_map/cond/branch_1_fun/ppermute | solution.py:30
  420.3 137.8 %reduce-scatter.11.cloned.1.call-start = ((), (), s32[]{:S(2)}) async-start(), calls=%async_computation.13 | async-start | bytes 3932160 | tf_op jit(solution)/shard_map/reduce_scatter | solution.py:644
  423.1 59.1 %collective-permute-start.48 = (bf16[96,2048]{1,0:T(8,128)(2,1)}, bf16[96,2048]{1,0:T(8,128)(2,1)}, u32[]{:S(2)}, u32[]{:S(2)}) collective-permute-start(bf16[96,2048]{1,0:T(8,128)(2,1)} %get-tuple-element.408), channel_id=1, source_target_pairs={{0,2},{1,3},{2,0},{3,1},{4,6},{5,7},{6,4},{7,5},{8,10},{9,11},{10,... | collective-permute-start | bytes 1179656 | tf_op jit(solution)/shard_map/cond/branch_1_fun/ppermute | solution.py:30
  423.7 58.6 %collective-permute-start.49 = (bf16[96,2048]{1,0:T(8,128)(2,1)}, bf16[96,2048]{1,0:T(8,128)(2,1)}, u32[]{:S(2)}, u32[]{:S(2)}) collective-permute-start(bf16[96,2048]{1,0:T(8,128)(2,1)} %get-tuple-element.407), channel_id=1, source_target_pairs={{0,4},{1,5},{2,6},{3,7},{4,0},{5,1},{6,2},{7,3},{8,12},{9,13},{10,... | collective-permute-start | bytes 1179656 | tf_op jit(solution)/shard_map/cond/branch_1_fun/ppermute | solution.py:30
  425.0 57.3 %collective-permute-start.50 = (bf16[96,2048]{1,0:T(8,128)(2,1)}, bf16[96,2048]{1,0:T(8,128)(2,1)}, u32[]{:S(2)}, u32[]{:S(2)}) collective-permute-start(bf16[96,2048]{1,0:T(8,128)(2,1)} %get-tuple-element.406), channel_id=1, source_target_pairs={{0,2},{1,3},{2,0},{3,1},{4,6},{5,7},{6,4},{7,5},{8,10},{9,11},{10,... | collective-permute-start | bytes 1179656 | tf_op jit(solution)/shard_map/cond/branch_1_fun/ppermute | solution.py:30
  426.6 55.7 %collective-permute-start.51 = (bf16[96,2048]{1,0:T(8,128)(2,1)}, bf16[96,2048]{1,0:T(8,128)(2,1)}, u32[]{:S(2)}, u32[]{:S(2)}) collective-permute-start(bf16[96,2048]{1,0:T(8,128)(2,1)} %get-tuple-element.405), channel_id=1, source_target_pairs={{0,4},{1,5},{2,6},{3,7},{4,0},{5,1},{6,2},{7,3},{8,12},{9,13},{10,... | collective-permute-start | bytes 1179656 | tf_op jit(solution)/shard_map/cond/branch_1_fun/ppermute | solution.py:30
  492.6 18.0 %collective-permute-start.18 = (bf16[768,2048]{1,0:T(8,128)(2,1)}, bf16[768,2048]{1,0:T(8,128)(2,1)}, u32[]{:S(2)}, u32[]{:S(2)}) collective-permute-start(bf16[768,2048]{1,0:T(8,128)(2,1)} %get-tuple-element.223), channel_id=1, source_target_pairs={{0,1},{1,0},{2,3},{3,2},{4,5},{5,4},{6,7},{7,6},{8,9},{9,8},{10,11... | collective-permute-start | bytes 9437192 | tf_op jit(solution)/shard_map/cond/branch_1_fun/ppermute | solution.py:30
  507.8 22.5 %collective-permute-start.16 = (bf16[96,2048]{1,0:T(8,128)(2,1)}, bf16[96,2048]{1,0:T(8,128)(2,1)S(1)}, u32[]{:S(2)}, u32[]{:S(2)}) collective-permute-start(bf16[96,2048]{1,0:T(8,128)(2,1)} %add_convert_fusion.12), channel_id=1, source_target_pairs={{0,4},{1,5},{2,6},{3,7},{4,0},{5,1},{6,2},{7,3},{8,12},{9,13},{10,... | collective-permute-start | bytes 1179656 | tf_op jit(solution)/shard_map/cond/branch_1_fun/ppermute | solution.py:30
  515.6 12.1 %collective-permute-start.20 = (bf16[96,2048]{1,0:T(8,128)(2,1)S(1)}, bf16[96,2048]{1,0:T(8,128)(2,1)S(1)}, u32[]{:S(2)}, u32[]{:S(2)}) collective-permute-start(bf16[96,2048]{1,0:T(8,128)(2,1)S(1)} %get-tuple-element.427), channel_id=1, source_target_pairs={{0,2},{1,3},{2,0},{3,1},{4,6},{5,7},{6,4},{7,5},{8,10},{9,11},{10,... | collective-permute-start | bytes 1179656 | tf_op jit(solution)/shard_map/cond/branch_1_fun/ppermute | solution.py:30
  519.7 16.4 %collective-permute-start.19 = (bf16[96,2048]{1,0:T(8,128)(2,1)S(1)}, bf16[96,2048]{1,0:T(8,128)(2,1)S(1)}, u32[]{:S(2)}, u32[]{:S(2)}) collective-permute-start(bf16[96,2048]{1,0:T(8,128)(2,1)S(1)} %get-tuple-element.424), channel_id=1, source_target_pairs={{0,2},{1,3},{2,0},{3,1},{4,6},{5,7},{6,4},{7,5},{8,10},{9,11},{10,... | collective-permute-start | bytes 1179656 | tf_op jit(solution)/shard_map/cond/branch_1_fun/ppermute | solution.py:30
  520.4 15.7 %collective-permute-start.23 = (bf16[96,2048]{1,0:T(8,128)(2,1)S(1)}, bf16[96,2048]{1,0:T(8,128)(2,1)S(1)}, u32[]{:S(2)}, u32[]{:S(2)}) collective-permute-start(bf16[96,2048]{1,0:T(8,128)(2,1)S(1)} %get-tuple-element.425), channel_id=1, source_target_pairs={{0,4},{1,5},{2,6},{3,7},{4,0},{5,1},{6,2},{7,3},{8,12},{9,13},{10,... | collective-permute-start | bytes 1179656 | tf_op jit(solution)/shard_map/cond/branch_1_fun/ppermute | solution.py:30
  528.8 12.1 %collective-permute-start.21 = (bf16[96,2048]{1,0:T(8,128)(2,1)S(1)}, bf16[96,2048]{1,0:T(8,128)(2,1)S(1)}, u32[]{:S(2)}, u32[]{:S(2)}) collective-permute-start(bf16[96,2048]{1,0:T(8,128)(2,1)S(1)} %add_convert_fusion.10), channel_id=1, source_target_pairs={{0,4},{1,5},{2,6},{3,7},{4,0},{5,1},{6,2},{7,3},{8,12},{9,13},{10,... | collective-permute-start | bytes 1179656 | tf_op jit(solution)/shard_map/cond/branch_1_fun/ppermute | solution.py:30
  531.9 11.8 %collective-permute-start.17 = (bf16[96,2048]{1,0:T(8,128)(2,1)S(1)}, bf16[96,2048]{1,0:T(8,128)(2,1)S(1)}, u32[]{:S(2)}, u32[]{:S(2)}) collective-permute-start(bf16[96,2048]{1,0:T(8,128)(2,1)S(1)} %get-tuple-element.429), channel_id=1, source_target_pairs={{0,2},{1,3},{2,0},{3,1},{4,6},{5,7},{6,4},{7,5},{8,10},{9,11},{10,... | collective-permute-start | bytes 1179656 | tf_op jit(solution)/shard_map/cond/branch_1_fun/ppermute | solution.py:30
  532.5 15.9 %collective-permute-start.22 = (bf16[96,2048]{1,0:T(8,128)(2,1)S(1)}, bf16[96,2048]{1,0:T(8,128)(2,1)S(1)}, u32[]{:S(2)}, u32[]{:S(2)}) collective-permute-start(bf16[96,2048]{1,0:T(8,128)(2,1)S(1)} %get-tuple-element.426), channel_id=1, source_target_pairs={{0,4},{1,5},{2,6},{3,7},{4,0},{5,1},{6,2},{7,3},{8,12},{9,13},{10,... | collective-permute-start | bytes 1179656 | tf_op jit(solution)/shard_map/cond/branch_1_fun/ppermute | solution.py:30
  542.3 9.6 %collective-permute-start.24 = (bf16[96,2048]{1,0:T(8,128)(2,1)S(1)}, bf16[96,2048]{1,0:T(8,128)(2,1)S(1)}, u32[]{:S(2)}, u32[]{:S(2)}) collective-permute-start(bf16[96,2048]{1,0:T(8,128)(2,1)S(1)} %get-tuple-element.423), channel_id=1, source_target_pairs={{0,2},{1,3},{2,0},{3,1},{4,6},{5,7},{6,4},{7,5},{8,10},{9,11},{10,... | collective-permute-start | bytes 1179656 | tf_op jit(solution)/shard_map/cond/branch_1_fun/ppermute | solution.py:30
  558.9 8.3 %collective-permute-start.59 = (f32[2,448]{1,0:T(2,128)S(1)}, f32[2,448]{1,0:T(2,128)S(1)}, u32[]{:S(2)}, u32[]{:S(2)}) collective-permute-start(f32[2,448]{1,0:T(2,128)S(1)} %dynamic-slice_bitcast_fusion.11), channel_id=1, source_target_pairs={{0,16},{8,24},{16,0},{24,8},{1,17},{9,25},{17,1},{25,9},{2,18},{10... | collective-permute-start | bytes 10760 | tf_op jit(solution)/shard_map/ppermute | solution.py:30
  563.5 16.2 %all-to-all-start.1 = ((bf16[8,64,768]{2,1,0:T(8,128)(2,1)}), bf16[8,64,768]{2,1,0:T(8,128)(2,1)S(1)}, u32[]{:S(2)}, u32[]{:S(2)}) async-start(bf16[8,64,768]{2,1,0:T(8,128)(2,1)} %bitcast.56), calls=%async_computation.5 | async-start | bytes 1572864 | tf_op jit(solution)/shard_map/all_to_all | solution.py:887
  (53 other events, 625.9 us)
Sparse Core Ops, SparseCore 0:
  9.6 30.6 all-gather.8
  41.8 63.0 all-gather.10
  107.0 105.3 all-gather.14
  214.4 61.7 all-gather.12
  284.9 52.9 reduce-scatter.4
  340.1 102.1 reduce-scatter.6
  445.1 27.6 reduce-scatter.8
  482.5 58.0 reduce-scatter.10

commit v3 on v2

--- a/solution.py
+++ b/solution.py
@@ -36,33 +36,23 @@
 
 def gather_first(x):
     bits = upper_bits()
-    if len(bits) != 2:
+    return tuple(swap(x, bit) for bit in bits) if len(bits) == 2 else ()
+
+
+def gather_second(x, got):
+    if not got:
         return ()
-    one, two = bits
+    one, two = upper_bits()
     half = x.shape[0] // 2
-    top, low = x[:half], x[half:]
-    return swap(top, two), swap(low, one), swap(low, two), swap(top, one)
-
-
-def gather_second(x, got):
-    bits = upper_bits()
-    if len(bits) != 2:
-        return ()
-    one, two = bits
-    return swap(got[0], one), swap(got[1], two)
+    return swap(got[1][:half], one), swap(got[0][half:], two)
 
 
 def gather_third(x, got, passed):
-    if not got:
-        own = x
-        for bit in upper_bits():
-            own = jnp.concatenate([own, swap(own, bit)])
-        return own
-    half = x.shape[0] // 2
-    top_two, low_one, low_two, top_one = got
-    return jnp.concatenate(
-        [x[:half], x[half:], top_one, low_one, top_two, low_two, passed[0], passed[1]]
-    )
+    if got:
+        return jnp.concatenate([x, *got, *passed])
+    for bit in upper_bits():
+        x = jnp.concatenate([x, swap(x, bit)])
+    return x
 
 
 def gather_last(x, got, passed):
@@ -101,15 +91,17 @@
     )
 
 
-def scatter_second(total, got):
-    bits = upper_bits()
-    if len(bits) != 2:
+def scatter_between(total, got):
+    if not got:
         return ()
-    one, two = bits
-    return (
-        swap(add_low(block_of(total, 2, 0), got[0]), two),
-        swap(add_low(block_of(total, 1, 1), got[1]), one),
-    )
+    return add_low(block_of(total, 2, 0), got[0]), add_low(block_of(total, 1, 1), got[1])
+
+
+def scatter_second(between):
+    if not between:
+        return ()
+    one, two = upper_bits()
+    return swap(between[0], two), swap(between[1], one)
 
 
 def scatter_last(total, got, passed):
@@ -130,7 +122,7 @@
 
 def scatter_plane(total):
     got = scatter_first(total)
-    return scatter_last(total, got, scatter_second(total, got))
+    return scatter_last(total, got, scatter_second(scatter_between(total, got)))
 
 
 def after(x, *others):
@@ -306,7 +298,7 @@
     count = lax.axis_size("wide")
     total = x.shape[0]
     depth, columns = weight.shape
-    block = math.gcd(depth, 1024)
+    block = math.gcd(depth, 512)
     order = jnp.stack([lax.axis_index("wide") ^ m for m in range(first, count, 2)])
     vec = pl.BlockSpec((1, block), lambda j, order: (0, j))
     return pl.pallas_call(
@@ -361,17 +353,19 @@
     own_first = first[...]
     own_place = at * block + lax.broadcasted_iota(jnp.int32, (1, block), 1)
 
-    def step(number, state):
+    def step(number, state, diagonal=False):
         keys = k_ref[pl.ds(number * block, block), :]
         values = v_turned[:, pl.ds(number * block, block)]
         place = number * block + lax.broadcasted_iota(jnp.int32, (block, block), 0)
-        visible = (place >= own_first) & (place <= own_place)
+        visible = place >= own_first
+        if diagonal:
+            visible = visible & (place <= own_place)
         out = []
         for h in range(2):
             peak, total, mix = state[h]
             scores = jnp.where(visible, dot(keys, queries[h], NT), neg_large)
             new_peak = jnp.maximum(peak, jnp.max(scores, axis=0, keepdims=True))
-            terms = jnp.where(visible, jnp.exp(scores - new_peak), 0.0)
+            terms = jnp.exp(scores - new_peak)
             decay = jnp.exp(peak - new_peak)
             out.append(
                 (
@@ -388,7 +382,7 @@
         jnp.zeros((1, block), F32),
         jnp.zeros((HEAD_DIM, block), F32),
     )
-    state = lax.fori_loop(0, at + 1, step, (start, start))
+    state = step(at, lax.fori_loop(0, at, step, (start, start)), True)
     mixes = []
     for h in range(2):
         peak, total, mix = state[h]
@@ -429,15 +423,14 @@
 
 def attend_back_kernel(
     first, q_ref, k_ref, v_ref, o_ref, g_ref, log_ref, cosine, ahead, behind,
-    gq_ref, gk_ref, gv_ref, k_turned, delta, sum_q,
+    out_ref, k_turned, delta, sum_q, sum_k, sum_v,
 ):
-    total = q_ref.shape[0]
-    block = k_ref.shape[0]
-    at = pl.program_id(1)
-    last = pl.num_programs(1)
+    block, width = k_ref.shape
+    pairs = width // PAIR
+    at = pl.program_id(0)
+    last = pl.num_programs(0)
     scale = HEAD_DIM ** (-0.5)
-    k = k_ref[...]
-    k_turned[...] = k.astype(F32).T.astype(BF)
+    k_turned[...] = k_ref[...].astype(F32).T.astype(BF)
 
     @pl.when(at == 0)
     def _():
@@ -446,7 +439,7 @@
         def fill(number, carry):
             spot = pl.ds(number * block, block)
             both = (g_ref[spot, :].astype(F32) * o_ref[spot, :].astype(F32)).T
-            for h in range(2):
+            for h in range(2 * pairs):
                 delta[h : h + 1, spot] = jnp.sum(
                     both[h * HEAD_DIM : (h + 1) * HEAD_DIM], axis=0, keepdims=True
                 )
@@ -454,47 +447,72 @@
 
         lax.fori_loop(0, last, fill, 0)
 
-    v = v_ref[...]
     place = at * block + lax.broadcasted_iota(jnp.int32, (block, block), 0)
 
-    def step(number, state):
-        sum_k, sum_v = state
+    def step(number, diagonal=False):
         spot = pl.ds(number * block, block)
-        q = q_ref[spot, :] * jnp.asarray(scale, BF)
-        g = g_ref[spot, :]
-        own_place = number * block + lax.broadcasted_iota(jnp.int32, (1, block), 1)
-        visible = (place >= first[:, spot]) & (place <= own_place)
-        for h in range(2):
-            mask = head_mask(h, q.shape)
-            q_head = jnp.where(mask, q, jnp.zeros_like(q))
-            g_head = jnp.where(mask, g, jnp.zeros_like(g))
-            scores = dot(k, q_head, NT)
-            probs = jnp.where(
-                visible,
-                jnp.exp(jnp.where(visible, scores - log_ref[0, h : h + 1, spot], neg_large)),
-                0.0,
-            )
-            slopes = dot(v, g_head, NT)
-            low = (probs * (slopes - delta[h : h + 1, spot])).astype(BF)
-            sum_v = sum_v + dot(probs.astype(BF), g_head)
-            sum_k = sum_k + dot(low, q_head)
-            span = slice(h * HEAD_DIM, (h + 1) * HEAD_DIM)
-            sum_q[span, spot] += dot(k_turned[span, :], low)
-        return (sum_k, sum_v)
-
-    zeros = jnp.zeros((block, PAIR), F32)
-    sum_k, sum_v = lax.fori_loop(at, last, step, (zeros, zeros))
-    gv_ref[...] = sum_v.astype(BF)
+        visible = place >= first[:, spot]
+        if diagonal:
+            own_place = number * block + lax.broadcasted_iota(jnp.int32, (1, block), 1)
+            visible = visible & (place <= own_place)
+        for p in range(pairs):
+            pair = slice(p * PAIR, (p + 1) * PAIR)
+            q = q_ref[spot, pair] * jnp.asarray(scale, BF)
+            g = g_ref[spot, pair]
+            k, v = k_ref[:, pair], v_ref[:, pair]
+            more_k = more_v = 0.0
+            for h in range(2):
+                mask = head_mask(h, q.shape)
+                q_head = jnp.where(mask, q, jnp.zeros_like(q))
+                g_head = jnp.where(mask, g, jnp.zeros_like(g))
+                scores = dot(k, q_head, NT)
+                probs = jnp.exp(
+                    jnp.where(visible, scores - log_ref[p, h : h + 1, spot], neg_large)
+                )
+                slopes = dot(v, g_head, NT)
+                head = 2 * p + h
+                low = (probs * (slopes - delta[head : head + 1, spot])).astype(BF)
+                more_v = more_v + dot(probs.astype(BF), g_head)
+                more_k = more_k + dot(low, q_head)
+                span = slice(head * HEAD_DIM, (head + 1) * HEAD_DIM)
+                sum_q[span, spot] += dot(k_turned[span, :], low)
+            if diagonal:
+                sum_k[:, pair] = more_k
+                sum_v[:, pair] = more_v
+            else:
+                sum_k[:, pair] += more_k
+                sum_v[:, pair] += more_v
+
+    step(at, True)
+
+    def later(number, carry):
+        step(number)
+        return carry
+
+    lax.fori_loop(at + 1, last, later, 0)
     mine = pl.ds(at * block, block)
-    gk_ref[...] = turn_lanes(sum_k, cosine[mine, :], -ahead[mine, :], -behind[mine, :]).astype(BF)
+    out_ref[mine, 2 * width :] = sum_v[...].astype(BF)
+    for p in range(pairs):
+        start = width + p * PAIR
+        out_ref[mine, start : start + PAIR] = turn_lanes(
+            sum_k[:, p * PAIR : (p + 1) * PAIR],
+            cosine[mine, :],
+            -ahead[mine, :],
+            -behind[mine, :],
+        ).astype(BF)
 
     @pl.when(at == last - 1)
     def _():
         def finish(number, carry):
             spot = pl.ds(number * block, block)
-            gq_ref[spot, :] = turn_lanes(
-                sum_q[:, spot].T * scale, cosine[spot, :], -ahead[spot, :], -behind[spot, :]
-            ).astype(BF)
+            for p in range(pairs):
+                pair = slice(p * PAIR, (p + 1) * PAIR)
+                out_ref[spot, pair] = turn_lanes(
+                    sum_q[pair, spot].T * scale,
+                    cosine[spot, :],
+                    -ahead[spot, :],
+                    -behind[spot, :],
+                ).astype(BF)
             return carry
 
         lax.fori_loop(0, last, finish, 0)
@@ -502,37 +520,39 @@
 
 def attend_back(first, q, k, v, o, g, logs, tables):
     total, width = q.shape
-    pairs = width // PAIR
     block = math.gcd(total, 256)
-    whole = pl.BlockSpec((total, PAIR), lambda p, i: (0, p))
-    part = pl.BlockSpec((block, PAIR), lambda p, i: (i, p))
-    table = pl.BlockSpec((total, PAIR), lambda p, i: (0, 0))
-    shape = jax.ShapeDtypeStruct((total, width), BF)
+
+    def whole(*shape):
+        return pl.BlockSpec(shape, lambda i: (0,) * len(shape))
+
+    part = pl.BlockSpec((block, width), lambda i: (i, 0))
     return pl.pallas_call(
         attend_back_kernel,
-        grid=(pairs, total // block),
+        grid=(total // block,),
         in_specs=[
-            pl.BlockSpec((1, total), lambda p, i: (0, 0)),
-            whole,
+            whole(1, total),
+            whole(total, width),
             part,
             part,
-            whole,
-            whole,
-            pl.BlockSpec((1, 2, total), lambda p, i: (p, 0, 0)),
-            table,
-            table,
-            table,
+            whole(total, width),
+            whole(total, width),
+            whole(*logs.shape),
+            whole(total, PAIR),
+            whole(total, PAIR),
+            whole(total, PAIR),
         ],
-        out_specs=[whole, part, part],
-        out_shape=[shape, shape, shape],
+        out_specs=whole(total, 3 * width),
+        out_shape=jax.ShapeDtypeStruct((total, 3 * width), BF),
         scratch_shapes=[
-            pltpu.VMEM((PAIR, block), BF),
-            pltpu.VMEM((2, total), F32),
-            pltpu.VMEM((PAIR, total), F32),
+            pltpu.VMEM((width, block), BF),
+            pltpu.VMEM((width // HEAD_DIM, total), F32),
+            pltpu.VMEM((width, total), F32),
+            pltpu.VMEM((block, width), F32),
+            pltpu.VMEM((block, width), F32),
         ],
         cost_estimate=pl.CostEstimate(flops=44 * 10**9, bytes_accessed=1, transcendentals=0),
         compiler_params=pltpu.CompilerParams(
-            dimension_semantics=("arbitrary", "arbitrary"), vmem_limit_bytes=48 * 2**20
+            dimension_semantics=("arbitrary",), vmem_limit_bytes=48 * 2**20
         ),
         name="attend_back",
     )(first, q, k, v, o, g, logs, *tables)
@@ -745,15 +765,16 @@
     over_second = (((1,), (0,)), ((), ()))
 
     def enter_stage(act_own, enter_slab, row_grad):
-        act_halves = (act_own, swap(act_own, 1))
-        entered = [dot(enter_slab, act, over_first) for act in act_halves]
+        act_other = swap(act_own, 1)
+        entered = [dot(enter_slab, act, over_first) for act in (act_own, act_other)]
         hidden = [(jax.nn.silu(e[:units]) * e[units:]).astype(BF) for e in entered]
         grad_down = dot(
             row_grad, jnp.concatenate(hidden, axis=1), (((0,), (1,)), ((), ()))
         ).astype(BF)
-        return act_halves, entered, hidden, grad_down
-
-    act_halves, entered, hidden, grad_down = stage(enter_stage, act_own, enter_slab, row_grad)
+        return act_other, entered, hidden, grad_down
+
+    act_other, entered, hidden, grad_down = stage(enter_stage, act_own, enter_slab, row_grad)
+    act_halves = (act_own, act_other)
     sum_down = sum_rows(grad_down, 0)
 
     def hidden_stage(act_halves, entered, row_grad, enter_slab, down_slab):
@@ -782,7 +803,8 @@
     sum_enter = sum_rows(grad_enter, 1)
 
     def norm_stage(act_sum, unit, rate, gain, grad_low, hidden, down_slab):
-        grad_act_two = scatter_plane(act_sum)
+        got = scatter_first(act_sum)
+        grad_act_two = scatter_last(act_sum, got, scatter_second(scatter_between(act_sum, got)))
         grad_norm = norm_back(grad_act_two, unit, rate, gain)
         return (
             grad_low.astype(F32) + grad_norm,
@@ -795,33 +817,25 @@
         norm_stage, act_sum, unit_two, rate_two, gain_two, grad_low, hidden, down_slab
     )
 
-    branch_own = stage(gather_own, after(grad_middle, sum_down).astype(BF))
+
+    def branch_stage(branch, sum_down):
+        return gather_own(branch), sum_down.astype(F32)
+
+    branch_own, out_down = stage(branch_stage, grad_middle.astype(BF), sum_down)
     branch_halves = (branch_own, swap(branch_own, 1))
-    grad_w_out = dot(
-        jnp.concatenate(attn_halves), jnp.concatenate(branch_halves), TN
-    ).astype(BF)
-    if fast_out:
-        sum_w_out = sum_rows(grad_w_out, 0)
-    else:
-        spread_out = lax.dynamic_update_index_in_dim(
-            jnp.zeros((per, wide_n, HEAD_DIM, width), BF),
-            grad_w_out.reshape(per, HEAD_DIM, width),
-            me,
-            1,
-        )
-        sum_w_out = lax.psum_scatter(
-            spread_out.reshape(width, width), ALL, scatter_dimension=0, tiled=True
-        )
-
-    def back_stage(branch_halves, w_out_own, first, q, k, v, attn_low, logs, tables, act_one, mixed_sum):
-        grad_attn = to_absolute(*[dot(b, w_out_own, NT).astype(BF) for b in branch_halves])
-        grads = attend_back(first, q, k, v, attn_low, grad_attn, logs, tables)
-        grad_proj = jnp.concatenate(grads, axis=1)
+    attn_own_grad = dot(branch_own, w_out_own, NT).astype(BF)
+
+    def back_stage(
+        branch_other, own_grad, w_out_own, first, q, k, v, attn_low, logs, tables, act_one, mixed_sum
+    ):
+        grad_attn = to_absolute(own_grad, dot(branch_other, w_out_own, NT).astype(BF))
+        grad_proj = attend_back(first, q, k, v, attn_low, grad_attn, logs, tables)
         return grad_proj, dot(act_one, grad_proj, TN).astype(BF), scatter_first(mixed_sum)
 
     grad_proj, grad_w_qkv, mixed_got = stage(
         back_stage,
-        after(branch_halves, grad_w_out),
+        branch_halves[1],
+        attn_own_grad,
         w_out_own,
         first,
         q,
@@ -834,17 +848,38 @@
         mixed_sum,
     )
     grad_proj, grad_w_qkv = after((grad_proj, grad_w_qkv), sum_enter)
-    grad_w_qkv = after(grad_w_qkv, sum_w_out)
     sum_qkv = sum_rows(grad_w_qkv, 0)
+
+    attn_halves, branch_halves, mixed_got = after(
+        (attn_halves, branch_halves, mixed_got), grad_w_qkv
+    )
+    grad_w_out = dot(attn_halves[0], branch_halves[0], TN)
+    grad_w_out = (grad_w_out + dot(attn_halves[1], branch_halves[1], TN)).astype(BF)
+    mixed_between = scatter_between(mixed_sum, mixed_got)
+    if fast_out:
+        sum_w_out = sum_rows(grad_w_out, 0)
+    else:
+        spread_out = lax.dynamic_update_index_in_dim(
+            jnp.zeros((per, wide_n, HEAD_DIM, width), BF),
+            grad_w_out.reshape(per, HEAD_DIM, width),
+            me,
+            1,
+        )
+        sum_w_out = lax.psum_scatter(
+            spread_out.reshape(width, width), ALL, scatter_dimension=0, tiled=True
+        )
 
     def last_stage(
         grad_proj, w_qkv_own, own, other, stats, gain, grad_middle, grad_gain_two, grad_shift_two,
-        mixed_sum, mixed_got,
+        mixed_sum, mixed_got, mixed_between, middle,
     ):
-        mixed = scatter_last(mixed_sum, mixed_got, scatter_second(mixed_sum, mixed_got))
         part_other, *sums_other = unproject(grad_proj, other, stats, w_qkv_own, 1)
         part_own, *sums_own = unproject(grad_proj, own, stats, w_qkv_own, 0)
         total = start_scatter(part_own, part_other)
+        got = scatter_first(total)
+        sums_own, sums_other, got = after((sums_own, sums_other, got))
+        passed = scatter_second(scatter_between(total, got))
+        total, got = after((total, got), *passed)
         grad_gain, grad_shift, grad_bias = (a + b for a, b in zip(sums_own, sums_other))
         full_bias = lax.dynamic_update_index_in_dim(
             jnp.zeros((3, per, wide_n, HEAD_DIM), F32),
@@ -866,11 +901,20 @@
         sums = halve(small.reshape(wide_n, -1), "wide").reshape(rows_n, -1)
         rate = stats[:local, 1:2]
         unit = (own[:local].astype(F32) - stats[:local, 0:1]) * rate
-        return grad_middle + norm_back(scatter_plane(total), unit, rate, gain), sums, mixed
-
-    grad_tokens, sums, mixed = stage(
+        grad_act_one = scatter_last(total, got, passed)
+        mixed_passed = scatter_second(mixed_between)
+        if passed:
+            mixed_passed = after(mixed_passed, *passed)
+        mixed = scatter_last(mixed_sum, mixed_got, mixed_passed)
+        return (
+            (grad_middle + norm_back(grad_act_one, unit, rate, gain))[None],
+            sums,
+            (middle + mixed).astype(BF)[None],
+        )
+
+    grad_tokens, sums, result = stage(
         last_stage,
-        after(grad_proj, grad_w_qkv),
+        after(grad_proj, grad_w_qkv, grad_w_out),
         w_qkv_own,
         own,
         other,
@@ -881,17 +925,16 @@
         grad_shift_two,
         mixed_sum,
         mixed_got,
-    )
-    grad_tokens = grad_tokens[None]
-    mixed, sum_down, sum_enter = after((mixed, sum_down, sum_enter), sums)
+        mixed_between,
+        middle,
+    )
+    sum_enter = after(sum_enter, sums)
+    out_gate, out_up = sum_enter[:units].T.astype(F32), sum_enter[units:].T.astype(F32)
+    out_w_out = sum_w_out.astype(F32)
     part_qkv = lax.all_to_all(
         after(sum_qkv, sums).reshape(wide_n, slab, 3 * span), "wide", 0, 0, tiled=True
     )
     sums = halve(after(sums, sum_qkv), "rows")
-    result = (middle + mixed).astype(BF)[None]
-    out_down = sum_down.astype(F32)
-    out_gate, out_up = sum_enter[:units].T.astype(F32), sum_enter[units:].T.astype(F32)
-    out_w_out = after(sum_w_out, sums).astype(F32)
     out_qkv = regroup_back(part_qkv[None])
     out_bias = sums[:bias_slab]
     small_outs = [

time: 597 us -> 589 us (0.987)
  waiting for transfers between devices: 131 us -> 142 us
  Pallas kernels: 106 us -> 96.5 us
  starting transfers between devices: 56.8 us -> 47.7 us
  local copies, waits for them, and re-layouts: 69.3 us -> 62 us
  other arithmetic: 63 us -> 55.8 us
  matrix products: 96.2 us -> 103 us
    ppermute x61 -> x53, waiting for transfers between devices: 116 us -> 129 us  [swap(): lax.ppermute(x, axis, [(i, i ^ bit) for i in range(lax.axis_size(axis))])]
    ppermute x61 -> x53, starting transfers between devices: 52.6 us -> 43.8 us  [swap(): lax.ppermute(x, axis, [(i, i ^ bit) for i in range(lax.axis_size(axis))])]
    pallas_call x1, Pallas kernels: 38.6 us -> 31.4 us  [attend_back(): pl.pallas_call(attend_back_kernel, grid=(total // block,), in_specs=[whol...]
    dot_general x16 -> x17, matrix products: 96.2 us -> 103 us  [dot(): return lax.dot_general(left, right, dims, preferred_element_type=F32)]
    cond x78 -> x68, local copies, waits for them, and re-layouts: 31.1 us -> 30.9 us
  transfers between devices with their start and end apart: 70 -> 62, of which waited for: 31 -> 33; matrix products, arithmetic and copies ran while one was open for 37% -> 37% of each run, Pallas kernels for 18% -> 16%
where the time goes in v3:
time: 589 us; the launch traced here: 579 us
  waiting for transfers between devices  142 us (24%)
  matrix products  103 us (17%)
  Pallas kernels  96.5 us (16%)
  local copies, waits for them, and re-layouts  62 us (11%)
  other arithmetic  55.8 us (9%)
  starting transfers between devices  47.7 us (8%)
  blocking collectives  40 us (7%)
  loops' own time  16.9 us (3%)
  between operations  15.4 us (3%)
    ppermute x53, waiting for transfers between devices, swap(): lax.ppermute(x, axis, [(i, i ^ bit) for i in range(lax.axis_size(axis))])  129 us
    dot_general x17, matrix products, dot(): return lax.dot_general(left, right, dims, preferred_element_type=F32)  103 us
    ppermute x53, starting transfers between devices, swap(): lax.ppermute(x, axis, [(i, i ^ bit) for i in range(lax.axis_size(axis))])  43.8 us
    pallas_call x1, Pallas kernels, attend(): pl.pallas_call(attend_kernel, grid=(pairs, total // block), in_specs=[pl....  33.1 us
    pallas_call x1, Pallas kernels, attend_back(): pl.pallas_call(attend_back_kernel, grid=(total // block,), in_specs=[whol...  31.4 us
    cond x67, local copies, waits for them, and re-layouts  26.3 us
    all_gather x2, blocking collectives, first_stage(): small = lax.all_gather(lax.all_gather(packed, 'rows'), 'wide')  22.2 us
    all_to_all x1, blocking collectives, shards(): lax.all_to_all(regroup(w_qkv, wide_n), 'wide', 0, 0, tiled=True)  17.8 us
  transfers between devices with their start and end apart: 62, of which 33 were waited for; matrix products, arithmetic and copies ran while one was open for 37% of the time, Pallas kernels for 16%

profile of v3, /device:TPU:0, one launch (start us, length us, event | category | flops | bytes accessed | tf_op | source)
XLA Modules:
  0.0 578.8 jit_solution(11355145407115907730)
XLA Ops:
  9.5 17.8 %all_to_all.10 = bf16[8,64,768]{2,1,0:T(8,128)(2,1)} all-to-all(bf16[8,64,768]{2,1,0:T(8,128)(2,1)S(1)} %regroup.1), channel_id=1, replica_groups=mesh['rows'=4,'wide'=8] {'wide'}, dimensions={0} | all-to-all | bytes 1572864 | tf_op jit(solution)/shard_map/all_to_all | solution.py:678
  30.8 44.4 %conditional.8 = (bf16[768,2048]{1,0:T(8,128)(2,1)}, bf16[768,2048]{1,0:T(8,128)(2,1)}, f32[1,768]{1,0:T(1,128)S(1)}, f32[1,2048]{1,0:T(1,128)S(1)}, f32[1,2048]...) conditional(s32[]{:T(128)} %bitcast.44, () %tuple.90, ...), branch_computations={%region_0.0_spmd, %region_1.3_spmd} | conditional | flops 7882702 | bytes 32684328 | solution.py:661
  32.1 13.2 %all-gather.2 = bf16[4,1,640]{2,1,0:T(2,128)(2,1)S(1)} all-gather(bf16[1,1,640]{2,1,0:T(2,128)(2,1)S(1)} %reshape.245), channel_id=2, replica_groups=mesh['rows'=4,'wide'=8] {'rows'}, dimensions={0}, use_global_device_ids=true | all-gather | bytes 6400 | tf_op jit(solution)/shard_map/cond/branch_1_fun/all_gather | solution.py:692
  45.3 9.1 %all-gather.3 = bf16[8,4,640]{2,1,0:T(4,128)(2,1)S(1)} all-gather(bf16[1,4,640]{2,1,0:T(4,128)(2,1)S(1)} %bitcast.156), channel_id=3, replica_groups=mesh['rows'=4,'wide'=8] {'wide'}, dimensions={0}, use_global_device_ids=true | all-gather | bytes 46080 | tf_op jit(solution)/shard_map/cond/branch_1_fun/all_gather | solution.py:692
  59.4 7.3 %collective-permute-done.6 = bf16[96,2048]{1,0:T(8,128)(2,1)S(1)} collective-permute-done((bf16[96,2048]{1,0:T(8,128)(2,1)S(1)}, bf16[96,2048]{1,0:T(8,128)(2,1)S(1)}, u32[]{:S(2)}, u32[]{:S(2)}) %collective-permute-start.6) | collective-permute-done | bytes 393248 | tf_op jit(solution)/shard_map/cond/branch_1_fun/ppermute | solution.py:30
  70.8 4.3 fusion.31
  79.7 15.8 %collective-permute-done.47 = bf16[192,2048]{1,0:T(8,128)(2,1)} collective-permute-done((bf16[192,2048]{1,0:T(8,128)(2,1)}, bf16[192,2048]{1,0:T(8,128)(2,1)}, u32[]{:S(2)}, u32[]{:S(2)}) %collective-permute-start.47) | collective-permute-done | bytes 786464 | tf_op jit(solution)/shard_map/ppermute | solution.py:30
  99.7 5.2 all-gather.11.cloned.1.call-done.weight
  105.0 15.3 %project.1 = (bf16[1536,2048]{1,0:T(8,128)(2,1)}, bf16[1536,256]{1,0:T(8,128)(2,1)S(1)}, bf16[1536,256]{1,0:T(8,128)(2,1)S(1)}, bf16[1536,256]{1,0:T(8,128)(2,1)S(1)}, f32[1536,128]{1,0:T(8,128)}) custom-call(s32[8]{0:T(128)S(1)} %stack.65.order, bf16[768,2048]{1,0:T(8,128)(2,1)} %get-tuple-element.317.own_ref, ...), custom_call_target="tpu_custom_call" | custom-call | flops 16999999488 | bytes 1 | tf_op jit(solution)/shard_map/project/pallas_call | solution.py:240
  120.3 33.1 %attend.1 = (bf16[1536,256]{1,0:T(8,128)(2,1)}, f32[2,2,1536]{2,1,0:T(2,128)}) custom-call(s32[1,1536]{1,0:T(1,128)S(1)} %get-tuple-element.326.first, bf16[1536,256]{1,0:T(8,128)(2,1)S(1)} %get-tuple-element.329.q_ref, bf16[1536,256]{1,0:T(8,128)(2,1)S(1)} %get-tuple-element.330.k_ref, bf16[1536,256]{1,0:T(8,128)(2,1)S(1)} %get-tuple-element.331.v_ref), custom_call_target="tpu_custom_call" | custom-call | flops 38999998464 | bytes 1 | tf_op jit(solution)/shard_map/attend/pallas_call | solution.py:398
  153.5 94.3 %conditional.9 = (bf16[768,256]{1,0:T(8,128)(2,1)S(1)}, bf16[768,256]{1,0:T(8,128)(2,1)}, f32[192,2048]{1,0:T(8,128)S(1)}, f32[192,2048]{1,0:T(8,128)S(1)}, f32[...) conditional(s32[]{:T(128)} %bitcast.44, () %tuple.97, (bf16[1536,256]{1,0:T(8,128)(2,1)}, ...), branch_computations={%region_3.4_spmd, %region_4.7_spmd} | conditional | flops 1631453312 | bytes 130572120 | solution.py:661
  176.0 2.4 collective-permute-done.21
  188.1 4.0 collective-permute-done.23
  199.7 7.3 %collective-permute-done.24 = bf16[96,2048]{1,0:T(8,128)(2,1)S(1)} collective-permute-done((bf16[96,2048]{1,0:T(8,128)(2,1)S(1)}, bf16[96,2048]{1,0:T(8,128)(2,1)S(1)}, u32[]{:S(2)}, u32[]{:S(2)}) %collective-permute-start.24) | collective-permute-done | bytes 393248 | tf_op jit(solution)/shard_map/cond/branch_1_fun/ppermute | solution.py:30
  208.9 5.1 collective-permute-done.25
  224.4 11.2 %collective-permute-done.29 = bf16[192,2048]{1,0:T(8,128)(2,1)S(1)} collective-permute-done((bf16[192,2048]{1,0:T(8,128)(2,1)S(1)}, bf16[192,2048]{1,0:T(8,128)(2,1)S(1)}, u32[]{:S(2)}, u32[]{:S(2)}) %collective-permute-start.29) | collective-permute-done | bytes 786464 | tf_op jit(solution)/shard_map/cond/branch_1_fun/ppermute | solution.py:30
  241.5 3.7 collective-permute-done.30
  249.1 37.1 %conditional.10 = (bf16[768,2048]{1,0:T(8,128)(2,1)}, f32[1408,768]{1,0:T(8,128)}, f32[1408,768]{1,0:T(8,128)}, bf16[704,768]{1,0:T(8,128)(2,1)}, bf16[704,768]{1,0:T(8,128)(2,1)}, /*index=5*/bf16[2048,704]{0,1:T(8,128)(2,1)}) conditional(s32[]{:T(128)} %bitcast.44, () %tuple.103, (bf16[768,2048]{1,0:T(8,128)(2,1)}, bf16[2048,1408]{1,0:T(8,128)(2,1)}, ...), branch_computations={%region_7.8_spmd, %region_8.9_spmd} | conditional | flops 13299810304 | bytes 84279408 | solution.py:661
  249.1 10.6 %fusion.47 = f32[1408,768]{1,0:T(8,128)} fusion(bf16[2048,1408]{1,0:T(8,128)(2,1)} %get-tuple-element.163, bf16[768,2048]{1,0:T(8,128)(2,1)} %get-tuple-element.162), kind=kOutput, calls=%fused_computation.195 | convolution fusion | flops 4429185024 | bytes 13238272 | tf_op jit(solution)/shard_map/cond/branch_1_fun/dot_general | solution.py:26
  259.7 3.9 fusion.2
  263.5 8.7 %fusion.48 = f32[1408,768]{1,0:T(8,128)} fusion(bf16[2048,1408]{1,0:T(8,128)(2,1)S(1)} %copy-done.35, bf16[768,2048]{1,0:T(8,128)(2,1)} %collective-permute-done.33), kind=kOutput, calls=%fused_computation.196 | convolution fusion | flops 4429185024 | bytes 13238272 | tf_op jit(solution)/shard_map/cond/branch_1_fun/dot_general | solution.py:26
  272.3 3.9 fusion.1
  276.1 9.7 %fusion = bf16[2048,704]{0,1:T(8,128)(2,1)} fusion(bf16[1536,2048]{1,0:T(8,128)(2,1)} %get-tuple-element.164, bf16[704,768]{1,0:T(8,128)(2,1)} %fusion.1, bf16[704,768]{1,0:T(8,128)(2,1)} %fusion.2), kind=kOutput, calls=%fused_computation.40 | convolution fusion | flops 4434952192 | bytes 11337728 | tf_op jit(solution)/shard_map/cond/branch_1_fun/dot_general | solution.py:26
  286.2 4.7 copy.94
  290.9 43.7 %conditional.11 = (bf16[768,2048]{1,0:T(8,128)(2,1)}, bf16[1408,2048]{1,0:T(8,128)(2,1)}) conditional(s32[]{:T(128)} %bitcast.44, () %tuple.102, (bf16[1536,2048]{1,0:T(8,128)(2,1)}, bf16[2048,704]{1,0:T(8,128)(2,1)}, f32[1408,768]{1,0:T(8,128)}, bf16[2048,1408]{1,0:T(8,128)(2,1)}, f32[1408,768]{1,0:T(8,128)}, ...), branch_computations={%region_9.10_spmd, %region_10.11_spmd} | conditional | flops 22210838528 | bytes 137756912 | solution.py:661
  291.0 7.7 %multiply_convert_fusion.1 = (bf16[704,768]{1,0:T(8,128)(2,1)S(1)}, bf16[704,768]{1,0:T(8,128)(2,1)S(1)}) fusion(f32[1408,768]{1,0:T(8,128)} %get-tuple-element.169, bf16[2048,704]{1,0:T(8,128)(2,1)} %get-tuple-element.165, bf16[1536,2048]{1,0:T(8,128)(2,1)} %get-tuple-element.166), kind=kOutput, calls=%fused_computation.74 | convolution fusion | flops 2221621248 | bytes 12779520 | tf_op jit(solution)/shard_map/cond/branch_1_fun/dot_general | solution.py:26
  298.8 5.5 convolution_convert_fusion.4
  305.1 6.6 %multiply_convert_fusion.3 = (bf16[704,768]{1,0:T(8,128)(2,1)S(1)}, bf16[704,768]{1,0:T(8,128)(2,1)S(1)}) fusion(f32[1408,768]{1,0:T(8,128)} %get-tuple-element.167, bf16[2048,704]{1,0:T(8,128)(2,1)S(1)} %copy-done.37, bf16[1536,2048]{1,0:T(8,128)(2,1)} %get-tuple-element.166), kind=kOutput, calls=%fused_computation.77 | convolution fusion | flops 2221621248 | bytes 12517376 | tf_op jit(solution)/shard_map/cond/branch_1_fun/dot_general | solution.py:26
  311.7 5.4 convolution_convert_fusion.5
  317.0 14.2 %convolution_convert_fusion.3 = bf16[1408,2048]{1,0:T(8,128)(2,1)} fusion(bf16[768,2048]{1,0:T(8,128)(2,1)} %get-tuple-element.171, bf16[768,2048]{1,0:T(8,128)(2,1)} %get-tuple-element.170, bf16[704,768]{1,0:T(8,128)(2,1)} %copy-done.41, bf16[704,768]{1,0:T(8,128)(2,1)} %copy-done.40, bf16[704,768]{1,0:T(8,128)(2,1)} %copy-done.43, ...), kind=kOutput, calls=%fused_computation.49 | convolution fusion | flops 8891138048 | bytes 16384000 | tf_op jit(solution)/shard_map/cond/branch_1_fun/dot_general | solution.py:26
  331.2 3.1 add_convert_fusion.4
  334.8 47.2 %conditional.12 = (f32[192,2048]{1,0:T(8,128)S(1)}, f32[2048]{0:T(1024)S(1)}, f32[2048]{0:T(1024)S(1)}, bf16[768,2048]{1,0:T(8,128)(2,1)}, bf16[192,2048]{1,0:T(8,128)(2,1)}) conditional(s32[]{:T(128)} %bitcast.44, () %tuple.96, (bf16[192,2048]{1,0:T(8,128)(2,1)}, f32[192,1]{0,1:T(1,128)}, bf16[768,2048]{1,0:T(8,128)(2,1)}, ...), branch_computations={%region_11.12_spmd, %region_12.18_spmd} | conditional | flops 4448841728 | bytes 76160088 | solution.py:661
  337.8 4.2 convolution_convert_fusion.6
  342.9 5.6 collective-permute-done.36
  351.7 4.3 collective-permute-done.35
  356.0 7.3 %collective-permute-done.37 = bf16[96,2048]{1,0:T(8,128)(2,1)S(1)} collective-permute-done((bf16[96,2048]{1,0:T(8,128)(2,1)S(1)}, bf16[96,2048]{1,0:T(8,128)(2,1)S(1)}, u32[]{:S(2)}, u32[]{:S(2)}) %collective-permute-start.37) | collective-permute-done | bytes 393248 | tf_op jit(solution)/shard_map/cond/branch_1_fun/ppermute | solution.py:30
  366.1 4.2 convolution_convert_fusion.7
  370.9 3.5 collective-permute-done.40
  376.2 2.6 fusion.39
  378.8 3.1 add_convert_fusion.5
  382.6 29.4 %conditional.13 = (bf16[768,2048]{1,0:T(8,128)(2,1)}, f32[512,704]{0,1:T(8,128)}) conditional(s32[]{:T(128)} %bitcast.44, () %tuple.95, (bf16[192,2048]{1,0:T(8,128)(2,1)}, bf16[512,704]{1,0:T(8,128)(2,1)}) %tuple.107), branch_computations={%region_19.20_spmd, %region_20.21_spmd} | conditional | bytes 19464368 | solution.py:661
  384.4 2.5 copy.98
  389.0 11.0 %collective-permute-done.1 = bf16[192,2048]{1,0:T(8,128)(2,1)S(1)} collective-permute-done((bf16[192,2048]{1,0:T(8,128)(2,1)}, bf16[192,2048]{1,0:T(8,128)(2,1)S(1)}, u32[]{:S(2)}, u32[]{:S(2)}) %collective-permute-start.1) | collective-permute-done | bytes 786464 | tf_op jit(solution)/shard_map/cond/branch_1_fun/ppermute | solution.py:30
  406.8 2.6 collective-permute-done.2
  412.0 3.7 convolution_convert_fusion.10
  418.0 50.4 %conditional.14 = (bf16[1536,768]{1,0:T(8,128)(2,1)}, bf16[2048,768]{0,1:T(8,128)(2,1)}, bf16[96,2048]{1,0:T(8,128)(2,1)}, bf16[96,2048]{1,0:T(8,128)(2,1)}, bf1...) conditional(s32[]{:T(128)} %bitcast.44, () %tuple.94, (bf16[768,2048]{1,0:T(8,128)(2,1)}, ...), branch_computations={%region_21.22_spmd, %region_22.23_spmd} | conditional | flops 49640488960 | bytes 30540804 | solution.py:661
  418.2 2.4 fusion.42
  424.6 3.0 convolution_convert_fusion.9
  427.9 31.4 %attend_back.1 = bf16[1536,768]{1,0:T(8,128)(2,1)} custom-call(s32[1,1536]{1,0:T(1,128)S(1)} %get-tuple-element.182.first, bf16[1536,256]{1,0:T(8,128)(2,1)} %get-tuple-element.183.q_ref, bf16[1536,256]{1,0:T(8,128)(2,1)} %get-tuple-element.184.k_ref, bf16[1536,256]{1,0:T(8,128)(2,1)} %get-tuple-element.185.v_ref, ...), custom_call_target="tpu_custom_call" | custom-call | flops 44000002048 | bytes 1 | tf_op jit(solution)/shard_map/cond/branch_1_fun/attend_back/pallas_call | solution.py:529
  459.3 9.1 %fusion.30 = bf16[2048,768]{0,1:T(8,128)(2,1)} fusion(bf16[1536,768]{1,0:T(8,128)(2,1)} %attend_back.1, bf16[1536,2048]{1,0:T(8,128)(2,1)} %get-tuple-element.194), kind=kOutput, calls=%fused_computation.102 | convolution fusion | flops 4833411072 | bytes 11796480 | tf_op jit(solution)/shard_map/cond/branch_1_fun/dot_general | solution.py:26
  468.5 3.1 fusion.49
  471.6 4.2 fusion.37
  475.9 2.6 add_convert_fusion.11
  478.5 72.4 %conditional.15 = (f32[1,192,2048]{2,1,0:T(8,128)}, f32[4,448]{1,0:T(4,128)}, bf16[1,192,2048]{2,1,0:T(8,128)(2,1)}) conditional(s32[]{:T(128)} %bitcast.44, () %tuple.89, (f32[1536,128]{1,0:T(8,128)}, bf16[1536,768]{1,0:T(8,128)(2,1)}, bf16[768,2048]{1,0:T(8,128)(2,1)}, bf16[2048,768]{1,0:T(8,128)(2,1)}, bf16[768,2048]{1,0:T(8,128)(2,1)}, ...), branch_computations={%region_24.25_spmd, %region_25.28_spmd} | conditional | flops 14020071424 | bytes 76783184 | solution.py:661
  478.6 7.5 %unproject.3 = (bf16[768,2048]{1,0:T(8,128)(2,1)S(1)}, f32[1,2048]{1,0:T(1,128)S(1)}, f32[1,2048]{1,0:T(1,128)S(1)}, f32[1,768]{1,0:T(1,128)S(1)}) custom-call(s32[4]{0:T(128)S(1)} %get-tuple-element.520.order, bf16[1536,768]{1,0:T(8,128)(2,1)} %get-tuple-element.198.g_ref, bf16[768,2048]{1,0:T(8,128)(2,1)} %get-tuple-element.202.x_ref, ...), custom_call_target="tpu_custom_call" | custom-call | flops 7000000000 | bytes 1 | tf_op jit(solution)/shard_map/cond/branch_1_fun/unproject/pallas_call | solution.py:304
  486.2 7.4 %unproject.2 = (bf16[768,2048]{1,0:T(8,128)(2,1)S(1)}, f32[1,2048]{1,0:T(1,128)S(1)}, f32[1,2048]{1,0:T(1,128)S(1)}, f32[1,768]{1,0:T(1,128)S(1)}) custom-call(s32[4]{0:T(128)S(1)} %get-tuple-element.519.order, bf16[1536,768]{1,0:T(8,128)(2,1)} %get-tuple-element.198.g_ref, bf16[768,2048]{1,0:T(8,128)(2,1)} %get-tuple-element.199.x_ref, ...), custom_call_target="tpu_custom_call" | custom-call | flops 7000000000 | bytes 1 | tf_op jit(solution)/shard_map/cond/branch_1_fun/unproject/pallas_call | solution.py:304
  502.2 8.0 %collective-permute-done.10 = bf16[96,2048]{1,0:T(8,128)(2,1)} collective-permute-done((bf16[96,2048]{1,0:T(8,128)(2,1)}, bf16[96,2048]{1,0:T(8,128)(2,1)}, u32[]{:S(2)}, u32[]{:S(2)}) %collective-permute-start.10) | collective-permute-done | bytes 393248 | tf_op jit(solution)/shard_map/cond/branch_1_fun/ppermute | solution.py:30
  511.8 6.4 %collective-permute-done.12 = bf16[96,2048]{1,0:T(8,128)(2,1)} collective-permute-done((bf16[96,2048]{1,0:T(8,128)(2,1)}, bf16[96,2048]{1,0:T(8,128)(2,1)}, u32[]{:S(2)}, u32[]{:S(2)}) %collective-permute-start.12) | collective-permute-done | bytes 393248 | tf_op jit(solution)/shard_map/cond/branch_1_fun/ppermute | solution.py:30
  525.6 2.4 add_convert_fusion.10
  529.7 5.2 collective-permute-done.17
  547.9 2.9 add_bitcast_fusion
  552.0 2.3 copy.95
  554.3 3.5 all-to-all-start.1
  563.1 7.2 %all-to-all-done.1 = bf16[8,64,768]{2,1,0:T(8,128)(2,1)S(1)} async-done(((bf16[8,64,768]{2,1,0:T(8,128)(2,1)}), bf16[8,64,768]{2,1,0:T(8,128)(2,1)S(1)}, u32[]{:S(2)}, u32[]{:S(2)}) %all-to-all-start.1) | async-done | bytes 786464 | tf_op jit(solution)/shard_map/all_to_all | solution.py:934
  (339 shorter events, 144.6 us)
Async XLA Ops:
  7.2 92.6 %all-gather.9.cloned.1.call-start = ((), (), s32[]{:S(2)}) async-start(), calls=%async_computation.6 | async-start | bytes 1310720 | tf_op jit(solution)/shard_map/all_gather | solution.py:668
  7.9 97.0 %all-gather.11.cloned.1.call-start = ((), (), s32[]{:S(2)}) async-start(), calls=%async_computation.7 | async-start | bytes 3932160 | tf_op jit(solution)/shard_map/all_gather | solution.py:681
  27.2 220.6 %all-gather.15.cloned.1.call-start = ((), (), s32[]{:S(2)}) async-start(), calls=%async_computation.9 | async-start | bytes 7208960 | tf_op jit(solution)/shard_map/all_gather | solution.py:683
  29.5 261.4 %all-gather.13.cloned.1.call-start = ((), (), s32[]{:S(2)}) async-start(), calls=%async_computation.8 | async-start | bytes 3932160 | tf_op jit(solution)/shard_map/all_gather | solution.py:686
  30.8 24.5 %collective-permute-start.4 = (bf16[192,2048]{1,0:T(8,128)(2,1)S(1)}, bf16[192,2048]{1,0:T(8,128)(2,1)S(1)}, u32[]{:S(2)}, u32[]{:S(2)}) collective-permute-start(bf16[192,2048]{1,0:T(8,128)(2,1)S(1)} %get-tuple-element.141), channel_id=1, source_target_pairs={{0,2},{1,3},{2,0},{3,1},{4,6},{5,7},{6,4},{7,5},{8,10},{9,11},{10,... | collective-permute-start | bytes 2359304 | tf_op jit(solution)/shard_map/cond/branch_1_fun/ppermute | solution.py:30
  31.4 23.9 %collective-permute-start.5 = (bf16[192,2048]{1,0:T(8,128)(2,1)S(1)}, bf16[192,2048]{1,0:T(8,128)(2,1)S(1)}, u32[]{:S(2)}, u32[]{:S(2)}) collective-permute-start(bf16[192,2048]{1,0:T(8,128)(2,1)S(1)} %get-tuple-element.141), channel_id=1, source_target_pairs={{0,4},{1,5},{2,6},{3,7},{4,0},{5,1},{6,2},{7,3},{8,12},{9,13},{10,... | collective-permute-start | bytes 2359304 | tf_op jit(solution)/shard_map/cond/branch_1_fun/ppermute | solution.py:30
  55.4 11.4 %collective-permute-start.6 = (bf16[96,2048]{1,0:T(8,128)(2,1)S(1)}, bf16[96,2048]{1,0:T(8,128)(2,1)S(1)}, u32[]{:S(2)}, u32[]{:S(2)}) collective-permute-start(bf16[96,2048]{1,0:T(8,128)(2,1)S(1)} %slice.147), channel_id=1, source_target_pairs={{0,2},{1,3},{2,0},{3,1},{4,6},{5,7},{6,4},{7,5},{8,10},{9,11},{10,... | collective-permute-start | bytes 1179656 | tf_op jit(solution)/shard_map/cond/branch_1_fun/ppermute | solution.py:30
  56.9 11.1 %collective-permute-start.7 = (bf16[96,2048]{1,0:T(8,128)(2,1)S(1)}, bf16[96,2048]{1,0:T(8,128)(2,1)S(1)}, u32[]{:S(2)}, u32[]{:S(2)}) collective-permute-start(bf16[96,2048]{1,0:T(8,128)(2,1)S(1)} %slice.148), channel_id=1, source_target_pairs={{0,4},{1,5},{2,6},{3,7},{4,0},{5,1},{6,2},{7,3},{8,12},{9,13},{10,... | collective-permute-start | bytes 1179656 | tf_op jit(solution)/shard_map/cond/branch_1_fun/ppermute | solution.py:30
  68.9 6.3 %collective-permute-start.8 = (bf16[768,2048]{1,0:T(8,128)(2,1)}, bf16[768,2048]{1,0:T(8,128)(2,1)}, u32[]{:S(2)}, u32[]{:S(2)}) collective-permute-start(bf16[768,2048]{1,0:T(8,128)(2,1)} %constant_dynamic-update-slice_fusion.21), channel_id=1, source_target_pairs={{0,1},{1,0},{2,3},{3,2},{4,5},{5,4},{6,7},{7,6},{8,9},{9,8},{10,11... | collective-permute-start | bytes 9437192 | tf_op jit(solution)/shard_map/cond/branch_1_fun/ppermute | solution.py:30
  75.2 45.1 %copy-start.20 = (f32[1,2048]{1,0:T(1,128)}, f32[1,2048]{1,0:T(1,128)S(1)}, u32[]{:S(2)}) copy-start(f32[1,2048]{1,0:T(1,128)S(1)} %get-tuple-element.319.gain) | copy-start | bytes 24580
  75.2 45.1 %copy-start.28 = (s32[1,1536]{1,0:T(1,128)}, s32[1,1536]{1,0:T(1,128)S(1)}, u32[]{:S(2)}) copy-start(s32[1,1536]{1,0:T(1,128)S(1)} %get-tuple-element.326.first) | copy-start | bytes 18436
  75.2 20.3 %collective-permute-start.47 = (bf16[192,2048]{1,0:T(8,128)(2,1)}, bf16[192,2048]{1,0:T(8,128)(2,1)}, u32[]{:S(2)}, u32[]{:S(2)}) collective-permute-start(bf16[192,2048]{1,0:T(8,128)(2,1)} %bitcast.55), channel_id=1, source_target_pairs={{0,4},{1,5},{2,6},{3,7},{4,0},{5,1},{6,2},{7,3},{8,12},{9,13},{10,... | collective-permute-start | bytes 2359304 | tf_op jit(solution)/shard_map/ppermute | solution.py:30
  76.3 21.4 %collective-permute-start.46 = (bf16[192,2048]{1,0:T(8,128)(2,1)}, bf16[192,2048]{1,0:T(8,128)(2,1)}, u32[]{:S(2)}, u32[]{:S(2)}) collective-permute-start(bf16[192,2048]{1,0:T(8,128)(2,1)} %bitcast.55), channel_id=1, source_target_pairs={{0,2},{1,3},{2,0},{3,1},{4,6},{5,7},{6,4},{7,5},{8,10},{9,11},{10,... | collective-permute-start | bytes 2359304 | tf_op jit(solution)/shard_map/ppermute | solution.py:30
  79.6 302.4 %reduce-scatter.5.cloned.1.call-start = ((), (), s32[]{:S(2)}) async-start(), calls=%async_computation.10 | async-start | bytes 3932160 | tf_op jit(solution)/shard_map/reduce_scatter | solution.py:664
  96.5 56.9 %collective-permute-start.48 = (bf16[96,2048]{1,0:T(8,128)(2,1)S(1)}, bf16[96,2048]{1,0:T(8,128)(2,1)}, u32[]{:S(2)}, u32[]{:S(2)}) collective-permute-start(bf16[96,2048]{1,0:T(8,128)(2,1)S(1)} %slice.262), channel_id=1, source_target_pairs={{0,2},{1,3},{2,0},{3,1},{4,6},{5,7},{6,4},{7,5},{8,10},{9,11},{10,... | collective-permute-start | bytes 1179656 | tf_op jit(solution)/shard_map/ppermute | solution.py:30
  98.6 54.8 %collective-permute-start.49 = (bf16[96,2048]{1,0:T(8,128)(2,1)S(1)}, bf16[96,2048]{1,0:T(8,128)(2,1)}, u32[]{:S(2)}, u32[]{:S(2)}) collective-permute-start(bf16[96,2048]{1,0:T(8,128)(2,1)S(1)} %slice.263), channel_id=1, source_target_pairs={{0,4},{1,5},{2,6},{3,7},{4,0},{5,1},{6,2},{7,3},{8,12},{9,13},{10,... | collective-permute-start | bytes 1179656 | tf_op jit(solution)/shard_map/ppermute | solution.py:30
  172.7 5.7 collective-permute-start.21
  180.1 12.0 %collective-permute-start.23 = (bf16[96,2048]{1,0:T(8,128)(2,1)S(1)}, bf16[96,2048]{1,0:T(8,128)(2,1)S(1)}, u32[]{:S(2)}, u32[]{:S(2)}) collective-permute-start(bf16[96,2048]{1,0:T(8,128)(2,1)S(1)} %get-tuple-element.526), channel_id=1, source_target_pairs={{0,2},{1,3},{2,0},{3,1},{4,6},{5,7},{6,4},{7,5},{8,10},{9,11},{10,... | collective-permute-start | bytes 1179656 | tf_op jit(solution)/shard_map/cond/branch_1_fun/ppermute | solution.py:30
  186.0 13.7 %collective-permute-start.22 = (bf16[96,2048]{1,0:T(8,128)(2,1)S(1)}, bf16[96,2048]{1,0:T(8,128)(2,1)S(1)}, u32[]{:S(2)}, u32[]{:S(2)}) collective-permute-start(bf16[96,2048]{1,0:T(8,128)(2,1)S(1)} %get-tuple-element.523), channel_id=1, source_target_pairs={{0,2},{1,3},{2,0},{3,1},{4,6},{5,7},{6,4},{7,5},{8,10},{9,11},{10,... | collective-permute-start | bytes 1179656 | tf_op jit(solution)/shard_map/cond/branch_1_fun/ppermute | solution.py:30
  186.6 13.2 %collective-permute-start.26 = (bf16[96,2048]{1,0:T(8,128)(2,1)S(1)}, bf16[96,2048]{1,0:T(8,128)(2,1)S(1)}, u32[]{:S(2)}, u32[]{:S(2)}) collective-permute-start(bf16[96,2048]{1,0:T(8,128)(2,1)S(1)} %get-tuple-element.524), channel_id=1, source_target_pairs={{0,4},{1,5},{2,6},{3,7},{4,0},{5,1},{6,2},{7,3},{8,12},{9,13},{10,... | collective-permute-start | bytes 1179656 | tf_op jit(solution)/shard_map/cond/branch_1_fun/ppermute | solution.py:30
  192.2 14.8 %collective-permute-start.24 = (bf16[96,2048]{1,0:T(8,128)(2,1)S(1)}, bf16[96,2048]{1,0:T(8,128)(2,1)S(1)}, u32[]{:S(2)}, u32[]{:S(2)}) collective-permute-start(bf16[96,2048]{1,0:T(8,128)(2,1)S(1)} %add_convert_fusion.3), channel_id=1, source_target_pairs={{0,4},{1,5},{2,6},{3,7},{4,0},{5,1},{6,2},{7,3},{8,12},{9,13},{10,... | collective-permute-start | bytes 1179656 | tf_op jit(solution)/shard_map/cond/branch_1_fun/ppermute | solution.py:30
  197.5 24.7 %collective-permute-start.32 = (bf16[768,2048]{1,0:T(8,128)(2,1)S(1)}, bf16[768,2048]{1,0:T(8,128)(2,1)S(1)}, u32[]{:S(2)}, u32[]{:S(2)}) collective-permute-start(bf16[768,2048]{1,0:T(8,128)(2,1)S(1)} %get-tuple-element.541), channel_id=1, source_target_pairs={{0,1},{1,0},{2,3},{3,2},{4,5},{5,4},{6,7},{7,6},{8,9},{9,8},{10,11... | collective-permute-start | bytes 9437192 | tf_op jit(solution)/shard_map/cond/branch_1_fun/ppermute | solution.py:30
  197.5 16.5 %collective-permute-start.25 = (bf16[96,2048]{1,0:T(8,128)(2,1)S(1)}, bf16[96,2048]{1,0:T(8,128)(2,1)S(1)}, u32[]{:S(2)}, u32[]{:S(2)}) collective-permute-start(bf16[96,2048]{1,0:T(8,128)(2,1)S(1)} %get-tuple-element.525), channel_id=1, source_target_pairs={{0,4},{1,5},{2,6},{3,7},{4,0},{5,1},{6,2},{7,3},{8,12},{9,13},{10,... | collective-permute-start | bytes 1179656 | tf_op jit(solution)/shard_map/cond/branch_1_fun/ppermute | solution.py:30
  207.3 8.4 %collective-permute-start.27 = (bf16[96,2048]{1,0:T(8,128)(2,1)S(1)}, bf16[96,2048]{1,0:T(8,128)(2,1)S(1)}, u32[]{:S(2)}, u32[]{:S(2)}) collective-permute-start(bf16[96,2048]{1,0:T(8,128)(2,1)S(1)} %get-tuple-element.522), channel_id=1, source_target_pairs={{0,2},{1,3},{2,0},{3,1},{4,6},{5,7},{6,4},{7,5},{8,10},{9,11},{10,... | collective-permute-start | bytes 1179656 | tf_op jit(solution)/shard_map/cond/branch_1_fun/ppermute | solution.py:30
  219.2 16.4 %collective-permute-start.29 = (bf16[192,2048]{1,0:T(8,128)(2,1)S(1)}, bf16[192,2048]{1,0:T(8,128)(2,1)S(1)}, u32[]{:S(2)}, u32[]{:S(2)}) collective-permute-start(bf16[192,2048]{1,0:T(8,128)(2,1)S(1)} %get-tuple-element.480), channel_id=1, source_target_pairs={{0,4},{1,5},{2,6},{3,7},{4,0},{5,1},{6,2},{7,3},{8,12},{9,13},{10,... | collective-permute-start | bytes 2359304 | tf_op jit(solution)/shard_map/cond/branch_1_fun/ppermute | solution.py:30
  220.7 18.5 %collective-permute-start.28 = (bf16[192,2048]{1,0:T(8,128)(2,1)S(1)}, bf16[192,2048]{1,0:T(8,128)(2,1)S(1)}, u32[]{:S(2)}, u32[]{:S(2)}) collective-permute-start(bf16[192,2048]{1,0:T(8,128)(2,1)S(1)} %get-tuple-element.480), channel_id=1, source_target_pairs={{0,2},{1,3},{2,0},{3,1},{4,6},{5,7},{6,4},{7,5},{8,10},{9,11},{10,... | collective-permute-start | bytes 2359304 | tf_op jit(solution)/shard_map/cond/branch_1_fun/ppermute | solution.py:30
  235.6 9.6 %collective-permute-start.30 = (bf16[96,2048]{1,0:T(8,128)(2,1)S(1)}, bf16[96,2048]{1,0:T(8,128)(2,1)S(1)}, u32[]{:S(2)}, u32[]{:S(2)}) collective-permute-start(bf16[96,2048]{1,0:T(8,128)(2,1)S(1)} %slice.242), channel_id=1, source_target_pairs={{0,2},{1,3},{2,0},{3,1},{4,6},{5,7},{6,4},{7,5},{8,10},{9,11},{10,... | collective-permute-start | bytes 1179656 | tf_op jit(solution)/shard_map/cond/branch_1_fun/ppermute | solution.py:30
  239.2 7.8 %collective-permute-start.31 = (bf16[96,2048]{1,0:T(8,128)(2,1)S(1)}, bf16[96,2048]{1,0:T(8,128)(2,1)S(1)}, u32[]{:S(2)}, u32[]{:S(2)}) collective-permute-start(bf16[96,2048]{1,0:T(8,128)(2,1)S(1)} %slice.243), channel_id=1, source_target_pairs={{0,4},{1,5},{2,6},{3,7},{4,0},{5,1},{6,2},{7,3},{8,12},{9,13},{10,... | collective-permute-start | bytes 1179656 | tf_op jit(solution)/shard_map/cond/branch_1_fun/ppermute | solution.py:30
  249.1 14.5 %collective-permute-start.33 = (bf16[768,2048]{1,0:T(8,128)(2,1)}, bf16[768,2048]{1,0:T(8,128)(2,1)}, u32[]{:S(2)}, u32[]{:S(2)}) collective-permute-start(bf16[768,2048]{1,0:T(8,128)(2,1)} %get-tuple-element.162), channel_id=1, source_target_pairs={{0,1},{1,0},{2,3},{3,2},{4,5},{5,4},{6,7},{7,6},{8,9},{9,8},{10,11... | collective-permute-start | bytes 9437192 | tf_op jit(solution)/shard_map/cond/branch_1_fun/ppermute | solution.py:30
  290.9 177.6 %reduce-scatter.7.cloned.1.call-start = ((), (), s32[]{:S(2)}) async-start(), calls=%async_computation.11 | async-start | bytes 7208960 | tf_op jit(solution)/shard_map/reduce_scatter | solution.py:664
  304.3 26.9 %collective-permute-start.34 = (bf16[768,2048]{1,0:T(8,128)(2,1)S(1)}, bf16[768,2048]{1,0:T(8,128)(2,1)S(1)}, u32[]{:S(2)}, u32[]{:S(2)}) collective-permute-start(bf16[768,2048]{1,0:T(8,128)(2,1)S(1)} %convolution_convert_fusion.4), channel_id=1, source_target_pairs={{0,1},{1,0},{2,3},{3,2},{4,5},{5,4},{6,7},{7,6},{8,9},{9,8},{10,11... | collective-permute-start | bytes 9437192 | tf_op jit(solution)/shard_map/cond/branch_1_fun/ppermute | solution.py:30
  334.7 216.1 %reduce-scatter.9.cloned.1.call-start = ((), (), s32[]{:S(2)}) async-start(), calls=%async_computation.12 | async-start | bytes 3932160 | tf_op jit(solution)/shard_map/reduce_scatter | solution.py:664
  336.4 12.0 %collective-permute-start.36 = (bf16[96,2048]{1,0:T(8,128)(2,1)S(1)}, bf16[96,2048]{1,0:T(8,128)(2,1)S(1)}, u32[]{:S(2)}, u32[]{:S(2)}) collective-permute-start(bf16[96,2048]{1,0:T(8,128)(2,1)S(1)} %get-tuple-element.549), channel_id=1, source_target_pairs={{0,2},{1,3},{2,0},{3,1},{4,6},{5,7},{6,4},{7,5},{8,10},{9,11},{10,... | collective-permute-start | bytes 1179656 | tf_op jit(solution)/shard_map/cond/branch_1_fun/ppermute | solution.py:30
  342.0 36.8 %collective-permute-start.41 = (bf16[768,2048]{1,0:T(8,128)(2,1)S(1)}, bf16[768,2048]{1,0:T(8,128)(2,1)S(1)}, u32[]{:S(2)}, u32[]{:S(2)}) collective-permute-start(bf16[768,2048]{1,0:T(8,128)(2,1)S(1)} %convolution_convert_fusion.6), channel_id=1, source_target_pairs={{0,1},{1,0},{2,3},{3,2},{4,5},{5,4},{6,7},{7,6},{8,9},{9,8},{10,11... | collective-permute-start | bytes 9437192 | tf_op jit(solution)/shard_map/cond/branch_1_fun/ppermute | solution.py:30
  342.1 13.9 %collective-permute-start.35 = (bf16[96,2048]{1,0:T(8,128)(2,1)S(1)}, bf16[96,2048]{1,0:T(8,128)(2,1)S(1)}, u32[]{:S(2)}, u32[]{:S(2)}) collective-permute-start(bf16[96,2048]{1,0:T(8,128)(2,1)S(1)} %get-tuple-element.546), channel_id=1, source_target_pairs={{0,2},{1,3},{2,0},{3,1},{4,6},{5,7},{6,4},{7,5},{8,10},{9,11},{10,... | collective-permute-start | bytes 1179656 | tf_op jit(solution)/shard_map/cond/branch_1_fun/ppermute | solution.py:30
  342.9 13.1 %collective-permute-start.39 = (bf16[96,2048]{1,0:T(8,128)(2,1)S(1)}, bf16[96,2048]{1,0:T(8,128)(2,1)S(1)}, u32[]{:S(2)}, u32[]{:S(2)}) collective-permute-start(bf16[96,2048]{1,0:T(8,128)(2,1)S(1)} %get-tuple-element.547), channel_id=1, source_target_pairs={{0,4},{1,5},{2,6},{3,7},{4,0},{5,1},{6,2},{7,3},{8,12},{9,13},{10,... | collective-permute-start | bytes 1179656 | tf_op jit(solution)/shard_map/cond/branch_1_fun/ppermute | solution.py:30
  349.6 13.7 %collective-permute-start.37 = (bf16[96,2048]{1,0:T(8,128)(2,1)S(1)}, bf16[96,2048]{1,0:T(8,128)(2,1)S(1)}, u32[]{:S(2)}, u32[]{:S(2)}) collective-permute-start(bf16[96,2048]{1,0:T(8,128)(2,1)S(1)} %add_convert_fusion.7), channel_id=1, source_target_pairs={{0,4},{1,5},{2,6},{3,7},{4,0},{5,1},{6,2},{7,3},{8,12},{9,13},{10,... | collective-permute-start | bytes 1179656 | tf_op jit(solution)/shard_map/cond/branch_1_fun/ppermute | solution.py:30
  349.6 21.3 %collective-permute-start.38 = (bf16[96,2048]{1,0:T(8,128)(2,1)S(1)}, bf16[96,2048]{1,0:T(8,128)(2,1)S(1)}, u32[]{:S(2)}, u32[]{:S(2)}) collective-permute-start(bf16[96,2048]{1,0:T(8,128)(2,1)S(1)} %get-tuple-element.548), channel_id=1, source_target_pairs={{0,4},{1,5},{2,6},{3,7},{4,0},{5,1},{6,2},{7,3},{8,12},{9,13},{10,... | collective-permute-start | bytes 1179656 | tf_op jit(solution)/shard_map/cond/branch_1_fun/ppermute | solution.py:30
  364.7 9.8 %collective-permute-start.40 = (bf16[96,2048]{1,0:T(8,128)(2,1)S(1)}, bf16[96,2048]{1,0:T(8,128)(2,1)S(1)}, u32[]{:S(2)}, u32[]{:S(2)}) collective-permute-start(bf16[96,2048]{1,0:T(8,128)(2,1)S(1)} %get-tuple-element.545), channel_id=1, source_target_pairs={{0,2},{1,3},{2,0},{3,1},{4,6},{5,7},{6,4},{7,5},{8,10},{9,11},{10,... | collective-permute-start | bytes 1179656 | tf_op jit(solution)/shard_map/cond/branch_1_fun/ppermute | solution.py:30
  382.6 17.5 %collective-permute-start.1 = (bf16[192,2048]{1,0:T(8,128)(2,1)}, bf16[192,2048]{1,0:T(8,128)(2,1)S(1)}, u32[]{:S(2)}, u32[]{:S(2)}) collective-permute-start(bf16[192,2048]{1,0:T(8,128)(2,1)} %get-tuple-element.180), channel_id=1, source_target_pairs={{0,4},{1,5},{2,6},{3,7},{4,0},{5,1},{6,2},{7,3},{8,12},{9,13},{10,... | collective-permute-start | bytes 2359304 | tf_op jit(solution)/shard_map/cond/branch_1_fun/ppermute | solution.py:30
  383.1 19.2 %collective-permute-start = (bf16[192,2048]{1,0:T(8,128)(2,1)}, bf16[192,2048]{1,0:T(8,128)(2,1)}, u32[]{:S(2)}, u32[]{:S(2)}) collective-permute-start(bf16[192,2048]{1,0:T(8,128)(2,1)} %get-tuple-element.180), channel_id=1, source_target_pairs={{0,2},{1,3},{2,0},{3,1},{4,6},{5,7},{6,4},{7,5},{8,10},{9,11},{10,... | collective-permute-start | bytes 2359304 | tf_op jit(solution)/shard_map/cond/branch_1_fun/ppermute | solution.py:30
  400.1 9.4 %collective-permute-start.2 = (bf16[96,2048]{1,0:T(8,128)(2,1)S(1)}, bf16[96,2048]{1,0:T(8,128)(2,1)S(1)}, u32[]{:S(2)}, u32[]{:S(2)}) collective-permute-start(bf16[96,2048]{1,0:T(8,128)(2,1)S(1)} %slice.248), channel_id=1, source_target_pairs={{0,2},{1,3},{2,0},{3,1},{4,6},{5,7},{6,4},{7,5},{8,10},{9,11},{10,... | collective-permute-start | bytes 1179656 | tf_op jit(solution)/shard_map/cond/branch_1_fun/ppermute | solution.py:30
  403.4 7.8 %collective-permute-start.3 = (bf16[96,2048]{1,0:T(8,128)(2,1)S(1)}, bf16[96,2048]{1,0:T(8,128)(2,1)S(1)}, u32[]{:S(2)}, u32[]{:S(2)}) collective-permute-start(bf16[96,2048]{1,0:T(8,128)(2,1)S(1)} %slice.249), channel_id=1, source_target_pairs={{0,4},{1,5},{2,6},{3,7},{4,0},{5,1},{6,2},{7,3},{8,12},{9,13},{10,... | collective-permute-start | bytes 1179656 | tf_op jit(solution)/shard_map/cond/branch_1_fun/ppermute | solution.py:30
  412.0 6.0 %collective-permute-start.50 = (bf16[768,2048]{1,0:T(8,128)(2,1)}, bf16[768,2048]{1,0:T(8,128)(2,1)}, u32[]{:S(2)}, u32[]{:S(2)}) collective-permute-start(bf16[768,2048]{1,0:T(8,128)(2,1)} %get-tuple-element.364), channel_id=1, source_target_pairs={{0,1},{1,0},{2,3},{3,2},{4,5},{5,4},{6,7},{7,6},{8,9},{9,8},{10,11... | collective-permute-start | bytes 9437192 | tf_op jit(solution)/shard_map/ppermute | solution.py:30
  420.5 47.9 %collective-permute-start.42 = (bf16[96,2048]{1,0:T(8,128)(2,1)}, bf16[96,2048]{1,0:T(8,128)(2,1)}, u32[]{:S(2)}, u32[]{:S(2)}) collective-permute-start(bf16[96,2048]{1,0:T(8,128)(2,1)} %get-tuple-element.497), channel_id=1, source_target_pairs={{0,2},{1,3},{2,0},{3,1},{4,6},{5,7},{6,4},{7,5},{8,10},{9,11},{10,... | collective-permute-start | bytes 1179656 | tf_op jit(solution)/shard_map/cond/branch_1_fun/ppermute | solution.py:30
  421.8 46.6 %collective-permute-start.43 = (bf16[96,2048]{1,0:T(8,128)(2,1)}, bf16[96,2048]{1,0:T(8,128)(2,1)}, u32[]{:S(2)}, u32[]{:S(2)}) collective-permute-start(bf16[96,2048]{1,0:T(8,128)(2,1)} %get-tuple-element.496), channel_id=1, source_target_pairs={{0,4},{1,5},{2,6},{3,7},{4,0},{5,1},{6,2},{7,3},{8,12},{9,13},{10,... | collective-permute-start | bytes 1179656 | tf_op jit(solution)/shard_map/cond/branch_1_fun/ppermute | solution.py:30
  422.3 46.1 %collective-permute-start.44 = (bf16[96,2048]{1,0:T(8,128)(2,1)}, bf16[96,2048]{1,0:T(8,128)(2,1)}, u32[]{:S(2)}, u32[]{:S(2)}) collective-permute-start(bf16[96,2048]{1,0:T(8,128)(2,1)} %get-tuple-element.495), channel_id=1, source_target_pairs={{0,2},{1,3},{2,0},{3,1},{4,6},{5,7},{6,4},{7,5},{8,10},{9,11},{10,... | collective-permute-start | bytes 1179656 | tf_op jit(solution)/shard_map/cond/branch_1_fun/ppermute | solution.py:30
  423.6 44.9 %collective-permute-start.45 = (bf16[96,2048]{1,0:T(8,128)(2,1)S(1)}, bf16[96,2048]{1,0:T(8,128)(2,1)}, u32[]{:S(2)}, u32[]{:S(2)}) collective-permute-start(bf16[96,2048]{1,0:T(8,128)(2,1)S(1)} %get-tuple-element.494), channel_id=1, source_target_pairs={{0,4},{1,5},{2,6},{3,7},{4,0},{5,1},{6,2},{7,3},{8,12},{9,13},{10,... | collective-permute-start | bytes 1179656 | tf_op jit(solution)/shard_map/cond/branch_1_fun/ppermute | solution.py:30
  468.5 91.7 %reduce-scatter.11.cloned.1.call-start = ((), (), s32[]{:S(2)}) async-start(), calls=%async_computation.13 | async-start | bytes 1310720 | tf_op jit(solution)/shard_map/reduce_scatter | solution.py:664
  486.1 7.5 %collective-permute-start.9 = (bf16[768,2048]{1,0:T(8,128)(2,1)S(1)}, bf16[768,2048]{1,0:T(8,128)(2,1)S(1)}, u32[]{:S(2)}, u32[]{:S(2)}) collective-permute-start(bf16[768,2048]{1,0:T(8,128)(2,1)S(1)} %get-tuple-element.203), channel_id=1, source_target_pairs={{0,1},{1,0},{2,3},{3,2},{4,5},{5,4},{6,7},{7,6},{8,9},{9,8},{10,11... | collective-permute-start | bytes 9437192 | tf_op jit(solution)/shard_map/cond/branch_1_fun/ppermute | solution.py:30
  498.0 12.2 %collective-permute-start.10 = (bf16[96,2048]{1,0:T(8,128)(2,1)}, bf16[96,2048]{1,0:T(8,128)(2,1)}, u32[]{:S(2)}, u32[]{:S(2)}) collective-permute-start(bf16[96,2048]{1,0:T(8,128)(2,1)} %get-tuple-element.518), channel_id=1, source_target_pairs={{0,2},{1,3},{2,0},{3,1},{4,6},{5,7},{6,4},{7,5},{8,10},{9,11},{10,... | collective-permute-start | bytes 1179656 | tf_op jit(solution)/shard_map/cond/branch_1_fun/ppermute | solution.py:30
  499.5 12.3 %collective-permute-start.11 = (bf16[96,2048]{1,0:T(8,128)(2,1)}, bf16[96,2048]{1,0:T(8,128)(2,1)}, u32[]{:S(2)}, u32[]{:S(2)}) collective-permute-start(bf16[96,2048]{1,0:T(8,128)(2,1)} %get-tuple-element.517), channel_id=1, source_target_pairs={{0,4},{1,5},{2,6},{3,7},{4,0},{5,1},{6,2},{7,3},{8,12},{9,13},{10,... | collective-permute-start | bytes 1179656 | tf_op jit(solution)/shard_map/cond/branch_1_fun/ppermute | solution.py:30
  499.5 18.7 %collective-permute-start.12 = (bf16[96,2048]{1,0:T(8,128)(2,1)}, bf16[96,2048]{1,0:T(8,128)(2,1)}, u32[]{:S(2)}, u32[]{:S(2)}) collective-permute-start(bf16[96,2048]{1,0:T(8,128)(2,1)} %get-tuple-element.516), channel_id=1, source_target_pairs={{0,2},{1,3},{2,0},{3,1},{4,6},{5,7},{6,4},{7,5},{8,10},{9,11},{10,... | collective-permute-start | bytes 1179656 | tf_op jit(solution)/shard_map/cond/branch_1_fun/ppermute | solution.py:30
  501.3 18.2 %collective-permute-start.13 = (bf16[96,2048]{1,0:T(8,128)(2,1)}, bf16[96,2048]{1,0:T(8,128)(2,1)}, u32[]{:S(2)}, u32[]{:S(2)}) collective-permute-start(bf16[96,2048]{1,0:T(8,128)(2,1)} %get-tuple-element.515), channel_id=1, source_target_pairs={{0,4},{1,5},{2,6},{3,7},{4,0},{5,1},{6,2},{7,3},{8,12},{9,13},{10,... | collective-permute-start | bytes 1179656 | tf_op jit(solution)/shard_map/cond/branch_1_fun/ppermute | solution.py:30
  520.2 4.2 collective-permute-start.16
  520.5 18.9 %collective-permute-start.19 = (bf16[96,2048]{1,0:T(8,128)(2,1)}, bf16[96,2048]{1,0:T(8,128)(2,1)}, u32[]{:S(2)}, u32[]{:S(2)}) collective-permute-start(bf16[96,2048]{1,0:T(8,128)(2,1)} %get-tuple-element.230), channel_id=1, source_target_pairs={{0,4},{1,5},{2,6},{3,7},{4,0},{5,1},{6,2},{7,3},{8,12},{9,13},{10,... | collective-permute-start | bytes 1179656 | tf_op jit(solution)/shard_map/cond/branch_1_fun/ppermute | solution.py:30
  522.3 17.2 %collective-permute-start.20 = (bf16[96,2048]{1,0:T(8,128)(2,1)}, bf16[96,2048]{1,0:T(8,128)(2,1)}, u32[]{:S(2)}, u32[]{:S(2)}) collective-permute-start(bf16[96,2048]{1,0:T(8,128)(2,1)} %get-tuple-element.231), channel_id=1, source_target_pairs={{0,2},{1,3},{2,0},{3,1},{4,6},{5,7},{6,4},{7,5},{8,10},{9,11},{10,... | collective-permute-start | bytes 1179656 | tf_op jit(solution)/shard_map/cond/branch_1_fun/ppermute | solution.py:30
  525.1 9.8 %collective-permute-start.17 = (f32[2,1792]{1,0:T(2,128)S(1)}, f32[2,1792]{1,0:T(2,128)S(1)}, u32[]{:S(2)}, u32[]{:S(2)}) collective-permute-start(f32[2,1792]{1,0:T(2,128)S(1)} %dynamic-slice_bitcast_fusion.10), channel_id=1, source_target_pairs={{0,2},{1,3},{2,0},{3,1},{4,6},{5,7},{6,4},{7,5},{8,10},{9,11},{10,... | collective-permute-start | bytes 43016 | tf_op jit(solution)/shard_map/cond/branch_1_fun/ppermute | solution.py:30
  528.0 12.0 %collective-permute-start.14 = (bf16[96,2048]{1,0:T(8,128)(2,1)}, bf16[96,2048]{1,0:T(8,128)(2,1)}, u32[]{:S(2)}, u32[]{:S(2)}) collective-permute-start(bf16[96,2048]{1,0:T(8,128)(2,1)} %get-tuple-element.513), channel_id=1, source_target_pairs={{0,4},{1,5},{2,6},{3,7},{4,0},{5,1},{6,2},{7,3},{8,12},{9,13},{10,... | collective-permute-start | bytes 1179656 | tf_op jit(solution)/shard_map/cond/branch_1_fun/ppermute | solution.py:30
  529.3 11.9 %collective-permute-start.15 = (bf16[96,2048]{1,0:T(8,128)(2,1)S(1)}, bf16[96,2048]{1,0:T(8,128)(2,1)}, u32[]{:S(2)}, u32[]{:S(2)}) collective-permute-start(bf16[96,2048]{1,0:T(8,128)(2,1)S(1)} %get-tuple-element.514), channel_id=1, source_target_pairs={{0,2},{1,3},{2,0},{3,1},{4,6},{5,7},{6,4},{7,5},{8,10},{9,11},{10,... | collective-permute-start | bytes 1179656 | tf_op jit(solution)/shard_map/cond/branch_1_fun/ppermute | solution.py:30
  536.2 1.8 collective-permute-start.18
  551.7 6.1 %collective-permute-start.51 = (f32[2,448]{1,0:T(2,128)S(1)}, f32[2,448]{1,0:T(2,128)S(1)}, u32[]{:S(2)}, u32[]{:S(2)}) collective-permute-start(f32[2,448]{1,0:T(2,128)S(1)} %dynamic-slice_bitcast_fusion.11), channel_id=1, source_target_pairs={{0,16},{8,24},{16,0},{24,8},{1,17},{9,25},{17,1},{25,9},{2,18},{10... | collective-permute-start | bytes 10760 | tf_op jit(solution)/shard_map/ppermute | solution.py:30
  554.3 16.1 %all-to-all-start.1 = ((bf16[8,64,768]{2,1,0:T(8,128)(2,1)}), bf16[8,64,768]{2,1,0:T(8,128)(2,1)S(1)}, u32[]{:S(2)}, u32[]{:S(2)}) async-start(bf16[8,64,768]{2,1,0:T(8,128)(2,1)} %bitcast.56), calls=%async_computation.4 | async-start | bytes 1572864 | tf_op jit(solution)/shard_map/all_to_all | solution.py:934
  557.9 4.1 collective-permute-start.52
  (45 other events, 408.3 us)
Sparse Core Ops, SparseCore 0:
  9.6 30.6 all-gather.8
  41.9 63.0 all-gather.10
  107.1 105.3 all-gather.14
  214.5 61.7 all-gather.12
  291.0 58.1 reduce-scatter.4
  351.4 102.2 reduce-scatter.6
  468.6 57.6 reduce-scatter.8
  528.6 27.2 reduce-scatter.10

commit v4 on v3

--- a/solution.py
+++ b/solution.py
@@ -187,35 +187,24 @@
     order, own_ref, other_ref, gain, shift, weight, bias, cosine, ahead, behind,
     act, q, k, v, stats,
 ):
-    count = pl.num_programs(0)
-    step = pl.program_id(0)
+    half = pl.num_programs(0) // 2
     width = q.shape[1]
-
-    def work(x_ref):
-        x = x_ref[...].astype(F32)
-        centre = jnp.mean(x, axis=1, keepdims=True)
-        centred = x - centre
-        rate = lax.rsqrt(jnp.mean(centred * centred, axis=1, keepdims=True) + epsilon)
-        lane = lax.broadcasted_iota(jnp.int32, stats.shape, 1)
-        stats[...] = jnp.where(lane == 0, centre, rate)
-        normed = (centred * rate * gain[...] + shift[...]).astype(BF)
-        act[...] = normed
-        projected = dot(normed, weight[...]) + bias[...]
-        for at in range(0, width, PAIR):
-            angles = (cosine[...], ahead[...], behind[...])
-            q[:, at : at + PAIR] = turn_lanes(projected[:, at : at + PAIR], *angles).astype(BF)
-            k[:, at : at + PAIR] = turn_lanes(
-                projected[:, width + at : width + at + PAIR], *angles
-            ).astype(BF)
-        v[...] = projected[:, 2 * width :].astype(BF)
-
-    @pl.when(step < count // 2)
-    def _():
-        work(own_ref)
-
-    @pl.when(step >= count // 2)
-    def _():
-        work(other_ref)
+    x = jnp.where(pl.program_id(0) < half, own_ref[...], other_ref[...]).astype(F32)
+    centre = jnp.mean(x, axis=1, keepdims=True)
+    centred = x - centre
+    rate = lax.rsqrt(jnp.mean(centred * centred, axis=1, keepdims=True) + epsilon)
+    lane = lax.broadcasted_iota(jnp.int32, stats.shape, 1)
+    stats[...] = jnp.where(lane == 0, centre, rate)
+    normed = (centred * rate * gain[...] + shift[...]).astype(BF)
+    act[...] = normed
+    projected = dot(normed, weight[...]) + bias[...]
+    for at in range(0, width, PAIR):
+        angles = (cosine[...], ahead[...], behind[...])
+        q[:, at : at + PAIR] = turn_lanes(projected[:, at : at + PAIR], *angles).astype(BF)
+        k[:, at : at + PAIR] = turn_lanes(
+            projected[:, width + at : width + at + PAIR], *angles
+        ).astype(BF)
+    v[...] = projected[:, 2 * width :].astype(BF)
 
 
 def project(own, other, gain, shift, weight, bias, tables):
@@ -353,13 +342,11 @@
     own_first = first[...]
     own_place = at * block + lax.broadcasted_iota(jnp.int32, (1, block), 1)
 
-    def step(number, state, diagonal=False):
+    def step(number, state):
         keys = k_ref[pl.ds(number * block, block), :]
         values = v_turned[:, pl.ds(number * block, block)]
         place = number * block + lax.broadcasted_iota(jnp.int32, (block, block), 0)
-        visible = place >= own_first
-        if diagonal:
-            visible = visible & (place <= own_place)
+        visible = (place >= own_first) & (place <= own_place)
         out = []
         for h in range(2):
             peak, total, mix = state[h]
@@ -382,7 +369,7 @@
         jnp.zeros((1, block), F32),
         jnp.zeros((HEAD_DIM, block), F32),
     )
-    state = step(at, lax.fori_loop(0, at, step, (start, start)), True)
+    state = lax.fori_loop(0, at + 1, step, (start, start))
     mixes = []
     for h in range(2):
         peak, total, mix = state[h]
@@ -449,12 +436,10 @@
 
     place = at * block + lax.broadcasted_iota(jnp.int32, (block, block), 0)
 
-    def step(number, diagonal=False):
+    def step(number, carry):
         spot = pl.ds(number * block, block)
-        visible = place >= first[:, spot]
-        if diagonal:
-            own_place = number * block + lax.broadcasted_iota(jnp.int32, (1, block), 1)
-            visible = visible & (place <= own_place)
+        own_place = number * block + lax.broadcasted_iota(jnp.int32, (1, block), 1)
+        visible = (place >= first[:, spot]) & (place <= own_place)
         for p in range(pairs):
             pair = slice(p * PAIR, (p + 1) * PAIR)
             q = q_ref[spot, pair] * jnp.asarray(scale, BF)
@@ -476,20 +461,13 @@
                 more_k = more_k + dot(low, q_head)
                 span = slice(head * HEAD_DIM, (head + 1) * HEAD_DIM)
                 sum_q[span, spot] += dot(k_turned[span, :], low)
-            if diagonal:
-                sum_k[:, pair] = more_k
-                sum_v[:, pair] = more_v
-            else:
-                sum_k[:, pair] += more_k
-                sum_v[:, pair] += more_v
-
-    step(at, True)
-
-    def later(number, carry):
-        step(number)
+            sum_k[:, pair] += more_k
+            sum_v[:, pair] += more_v
         return carry
 
-    lax.fori_loop(at + 1, last, later, 0)
+    sum_k[...] = jnp.zeros_like(sum_k)
+    sum_v[...] = jnp.zeros_like(sum_v)
+    lax.fori_loop(at, last, step, 0)
     mine = pl.ds(at * block, block)
     out_ref[mine, 2 * width :] = sum_v[...].astype(BF)
     for p in range(pairs):
@@ -751,8 +729,7 @@
         act_two = (unit * gain_two + shift_two).astype(BF)
         return attn_halves, middle, unit, rate, gather_own(act_two), row_grad
 
-    attn_halves, middle, unit_two, rate_two, act_own, row_grad = stage(
-        middle_stage,
+    attn_halves, middle, unit_two, rate_two, act_own, row_grad = middle_stage(
         attn_low,
         w_out_own,
         gain_two,

time: 589 us -> 569 us (0.966)
  starting transfers between devices: 47.7 us -> 66.3 us
  loops' own time: 16.9 us -> 1.7 us
  waiting for transfers between devices: 142 us -> 127 us
    ppermute x53, waiting for transfers between devices: 129 us -> 109 us  [swap(): lax.ppermute(x, axis, [(i, i ^ bit) for i in range(lax.axis_size(axis))])]
    all_gather x1, starting transfers between devices: 0.04 us -> 16 us  [shards(): down_slab = lax.all_gather(w_down, 'rows', axis=0, tiled=True)]
    another operation x8 -> x7, loops' own time: 16.9 us -> 1.7 us  [stage(): return lax.cond(segments[0, 0] >= 0, run, blank, *args)]
    unnamed x55 -> x119, local copies, waits for them, and re-layouts: 5.86 us -> 15.7 us
    cond x67 -> x60, local copies, waits for them, and re-layouts: 26.3 us -> 17.4 us
    all_gather x1, waiting for transfers between devices: 0.02 us -> 6.15 us  [shards(): down_slab = lax.all_gather(w_down, 'rows', axis=0, tiled=True)]
  transfers between devices with their start and end apart: 62 -> 62, of which waited for: 33 -> 33; matrix products, arithmetic and copies ran while one was open for 37% -> 36% of each run, Pallas kernels for 16% -> 17%
where the time goes in v4:
time: 569 us; the launch traced here: 561 us
  waiting for transfers between devices  127 us (22%)
  matrix products  100 us (18%)
  Pallas kernels  98 us (17%)
  starting transfers between devices  66.3 us (12%)
  local copies, waits for them, and re-layouts  58.9 us (10%)
  other arithmetic  52.9 us (9%)
  blocking collectives  40 us (7%)
  between operations  15.9 us (3%)
    ppermute x53, waiting for transfers between devices, swap(): lax.ppermute(x, axis, [(i, i ^ bit) for i in range(lax.axis_size(axis))])  109 us
    dot_general x17, matrix products, dot(): return lax.dot_general(left, right, dims, preferred_element_type=F32)  100 us
    ppermute x53, starting transfers between devices, swap(): lax.ppermute(x, axis, [(i, i ^ bit) for i in range(lax.axis_size(axis))])  46.5 us
    pallas_call x1, Pallas kernels, attend(): pl.pallas_call(attend_kernel, grid=(pairs, total // block), in_specs=[pl....  33.8 us
    pallas_call x1, Pallas kernels, attend_back(): pl.pallas_call(attend_back_kernel, grid=(total // block,), in_specs=[whol...  32.1 us
    all_gather x2, blocking collectives, first_stage(): small = lax.all_gather(lax.all_gather(packed, 'rows'), 'wide')  22.2 us
    all_to_all x1, blocking collectives, shards(): lax.all_to_all(regroup(w_qkv, wide_n), 'wide', 0, 0, tiled=True)  17.8 us
    cond x60, local copies, waits for them, and re-layouts  17.4 us
  transfers between devices with their start and end apart: 62, of which 33 were waited for; matrix products, arithmetic and copies ran while one was open for 36% of the time, Pallas kernels for 17%

profile of v4, /device:TPU:0, one launch (start us, length us, event | category | flops | bytes accessed | tf_op | source)
XLA Modules:
  0.0 561.1 jit_solution(18346582714010901724)
XLA Ops:
  9.5 17.8 %all_to_all.10 = bf16[8,64,768]{2,1,0:T(8,128)(2,1)} all-to-all(bf16[8,64,768]{2,1,0:T(8,128)(2,1)S(1)} %regroup.1), channel_id=1, replica_groups=mesh['rows'=4,'wide'=8] {'wide'}, dimensions={0} | all-to-all | bytes 1572864 | tf_op jit(solution)/shard_map/all_to_all | solution.py:656
  30.3 46.1 %conditional.7 = (bf16[768,2048]{1,0:T(8,128)(2,1)}, bf16[768,2048]{1,0:T(8,128)(2,1)}, f32[1,768]{1,0:T(1,128)S(1)}, f32[1,2048]{1,0:T(1,128)S(1)}, f32[1,2048]...) conditional(s32[]{:T(128)} %bitcast.31, () %tuple.82, ...), branch_computations={%region_0.0_spmd, %region_1.3_spmd} | conditional | flops 7882702 | bytes 32684328 | solution.py:639
  31.6 13.2 %all-gather.2 = bf16[4,1,640]{2,1,0:T(2,128)(2,1)S(1)} all-gather(bf16[1,1,640]{2,1,0:T(2,128)(2,1)S(1)} %reshape.238), channel_id=2, replica_groups=mesh['rows'=4,'wide'=8] {'rows'}, dimensions={0}, use_global_device_ids=true | all-gather | bytes 6400 | tf_op jit(solution)/shard_map/cond/branch_1_fun/all_gather | solution.py:670
  44.8 9.1 %all-gather.3 = bf16[8,4,640]{2,1,0:T(4,128)(2,1)S(1)} all-gather(bf16[1,4,640]{2,1,0:T(4,128)(2,1)S(1)} %bitcast.162), channel_id=3, replica_groups=mesh['rows'=4,'wide'=8] {'wide'}, dimensions={0}, use_global_device_ids=true | all-gather | bytes 46080 | tf_op jit(solution)/shard_map/cond/branch_1_fun/all_gather | solution.py:670
  63.2 4.1 collective-permute-done.6
  72.4 2.9 fusion.27
  80.9 16.0 %all-gather.13.cloned.1.call-start = ((), (), s32[]{:S(2)}) async-start(), calls=%async_computation.8 | async-start | bytes 3932160 | tf_op jit(solution)/shard_map/all_gather | solution.py:664
  100.6 4.4 all-gather.11.cloned.1.call-done.weight
  105.0 15.5 %project.1 = (bf16[1536,2048]{1,0:T(8,128)(2,1)}, bf16[1536,256]{1,0:T(8,128)(2,1)S(1)}, bf16[1536,256]{1,0:T(8,128)(2,1)S(1)}, bf16[1536,256]{1,0:T(8,128)(2,1)S(1)}, f32[1536,128]{1,0:T(8,128)}) custom-call(s32[8]{0:T(128)S(1)} %stack.65.order, bf16[768,2048]{1,0:T(8,128)(2,1)} %get-tuple-element.291.own_ref, ...), custom_call_target="tpu_custom_call" | custom-call | flops 16999999488 | bytes 1 | tf_op jit(solution)/shard_map/project/pallas_call | solution.py:229
  120.5 33.8 %attend.1 = (bf16[1536,256]{1,0:T(8,128)(2,1)S(1)}, f32[2,2,1536]{2,1,0:T(2,128)}) custom-call(s32[1,1536]{1,0:T(1,128)S(1)} %get-tuple-element.300.first, bf16[1536,256]{1,0:T(8,128)(2,1)S(1)} %get-tuple-element.303.q_ref, bf16[1536,256]{1,0:T(8,128)(2,1)S(1)} %get-tuple-element.304.k_ref, bf16[1536,256]{1,0:T(8,128)(2,1)S(1)} %get-tuple-element.305.v_ref), custom_call_target="tpu_custom_call" | custom-call | flops 38999998464 | bytes 1 | tf_op jit(solution)/shard_map/attend/pallas_call | solution.py:385
  162.4 3.2 add_convert_fusion.7
  171.0 6.8 %collective-permute-done.40 = bf16[96,2048]{1,0:T(8,128)(2,1)S(1)} collective-permute-done((bf16[96,2048]{1,0:T(8,128)(2,1)S(1)}, bf16[96,2048]{1,0:T(8,128)(2,1)S(1)}, u32[]{:S(2)}, u32[]{:S(2)}) %collective-permute-start.40) | collective-permute-done | bytes 393248 | tf_op jit(solution)/shard_map/ppermute | solution.py:30
  180.3 5.5 collective-permute-done.39
  185.8 4.2 collective-permute-done.41
  191.8 5.5 collective-permute-done.42
  206.2 12.0 %collective-permute-done.46 = bf16[192,2048]{1,0:T(8,128)(2,1)S(1)} collective-permute-done((bf16[192,2048]{1,0:T(8,128)(2,1)S(1)}, bf16[192,2048]{1,0:T(8,128)(2,1)S(1)}, u32[]{:S(2)}, u32[]{:S(2)}) %collective-permute-start.46) | collective-permute-done | bytes 786464 | tf_op jit(solution)/shard_map/ppermute | solution.py:30
  223.9 3.9 collective-permute-done.47
  230.2 35.3 %conditional.8 = (bf16[768,2048]{1,0:T(8,128)(2,1)}, f32[1408,768]{1,0:T(8,128)}, f32[1408,768]{1,0:T(8,128)}, bf16[704,768]{1,0:T(8,128)(2,1)}, bf16[704,768]{1,0:T(8,128)(2,1)}, /*index=5*/bf16[2048,704]{0,1:T(8,128)(2,1)}) conditional(s32[]{:T(128)} %bitcast.31, () %tuple.93, (bf16[768,2048]{1,0:T(8,128)(2,1)}, bf16[2048,1408]{1,0:T(8,128)(2,1)}, ...), branch_computations={%region_5.6_spmd, %region_6.7_spmd} | conditional | flops 13299810304 | bytes 103153824 | solution.py:639
  230.2 10.5 %fusion.44 = f32[1408,768]{1,0:T(8,128)} fusion(bf16[2048,1408]{1,0:T(8,128)(2,1)} %get-tuple-element.143, bf16[768,2048]{1,0:T(8,128)(2,1)} %get-tuple-element.142), kind=kOutput, calls=%fused_computation.193 | convolution fusion | flops 4429185024 | bytes 13238272 | tf_op jit(solution)/shard_map/cond/branch_1_fun/dot_general | solution.py:26
  240.7 4.0 fusion.2
  244.7 8.9 %fusion.45 = f32[1408,768]{1,0:T(8,128)} fusion(bf16[2048,1408]{1,0:T(8,128)(2,1)S(1)} %copy-done.59, bf16[768,2048]{1,0:T(8,128)(2,1)} %collective-permute-done.21), kind=kOutput, calls=%fused_computation.194 | convolution fusion | flops 4429185024 | bytes 13238272 | tf_op jit(solution)/shard_map/cond/branch_1_fun/dot_general | solution.py:26
  253.6 3.9 fusion.1
  257.4 7.6 %fusion = bf16[2048,704]{0,1:T(8,128)(2,1)} fusion(bf16[1536,2048]{1,0:T(8,128)(2,1)S(1)} %bitcast.157, bf16[704,768]{1,0:T(8,128)(2,1)} %fusion.1, bf16[704,768]{1,0:T(8,128)(2,1)} %fusion.2), kind=kOutput, calls=%fused_computation.1 | convolution fusion | flops 4434952192 | bytes 11337728 | tf_op jit(solution)/shard_map/cond/branch_1_fun/dot_general | solution.py:26
  265.5 4.6 copy.93
  270.2 6.1 %all-gather.13.cloned.1.call-done = bf16[2048,704]{1,0:T(8,128)(2,1)} async-done(((bf16[512,704]{1,0:T(8,128)(2,1)}), bf16[2048,704]{1,0:T(8,128)(2,1)}) %all-gather.13.cloned.1.call-update) | async-done | bytes 2883600 | tf_op jit(solution)/shard_map/all_gather | solution.py:664
  276.3 42.4 %conditional.9 = (bf16[768,2048]{1,0:T(8,128)(2,1)}, bf16[1408,2048]{1,0:T(8,128)(2,1)}) conditional(s32[]{:T(128)} %bitcast.31, () %tuple.92, (bf16[2048,704]{1,0:T(8,128)(2,1)}, bf16[768,2048]{1,0:T(8,128)(2,1)}, f32[1408,768]{1,0:T(8,128)}, bf16[2048,1408]{1,0:T(8,128)(2,1)}, bf16[768,2048]{1,0:T(8,128)(2,1)}, /*index=5*/f32[1408,768]{1,0:T(8,128)}, ...), branch_computations={%region_7.8_spmd, %region_8.9_spmd} | conditional | flops 22210838528 | bytes 158728528 | solution.py:639
  276.3 7.5 %multiply_convert_fusion.1 = (bf16[704,768]{1,0:T(8,128)(2,1)S(1)}, bf16[704,768]{1,0:T(8,128)(2,1)S(1)}) fusion(f32[1408,768]{1,0:T(8,128)} %get-tuple-element.150, bf16[2048,704]{1,0:T(8,128)(2,1)} %get-tuple-element.145, bf16[768,2048]{1,0:T(8,128)(2,1)} %get-tuple-element.149), kind=kOutput, calls=%fused_computation.31 | convolution fusion | flops 2221621248 | bytes 12517376 | tf_op jit(solution)/shard_map/cond/branch_1_fun/dot_general | solution.py:26
  283.9 6.7 %convolution_convert_fusion.2 = bf16[768,2048]{1,0:T(8,128)(2,1)} fusion(bf16[2048,1408]{1,0:T(8,128)(2,1)S(1)} %copy-done.60, bf16[704,768]{1,0:T(8,128)(2,1)S(1)} %get-tuple-element.452, bf16[704,768]{1,0:T(8,128)(2,1)S(1)} %get-tuple-element.451), kind=kOutput, calls=%fused_computation.22 | convolution fusion | flops 4435083264 | bytes 11075584 | tf_op jit(solution)/shard_map/cond/branch_1_fun/dot_general | solution.py:26
  290.6 5.6 multiply_convert_fusion.3
  296.3 5.4 convolution_convert_fusion.3
  301.7 13.6 %convolution_convert_fusion.1 = bf16[1408,2048]{1,0:T(8,128)(2,1)} fusion(bf16[768,2048]{1,0:T(8,128)(2,1)} %get-tuple-element.152, bf16[768,2048]{1,0:T(8,128)(2,1)} %get-tuple-element.151, bf16[704,768]{1,0:T(8,128)(2,1)S(1)} %copy-done.67, bf16[704,768]{1,0:T(8,128)(2,1)S(1)} %copy-done.65, bf16[704,768]{1,0:T(8,128)(2,1)} %copy-done.69, ...), kind=kOutput, calls=%fused_computation.10 | convolution fusion | flops 8891138048 | bytes 16384000 | tf_op jit(solution)/shard_map/cond/branch_1_fun/dot_general | solution.py:26
  315.3 3.1 add_convert_fusion
  318.9 42.7 %conditional.10 = (f32[192,2048]{1,0:T(8,128)S(1)}, f32[2048]{0:T(1024)S(1)}, f32[2048]{0:T(1024)S(1)}, bf16[768,2048]{1,0:T(8,128)(2,1)}, bf16[192,2048]{1,0:T(8,128)(2,1)}) conditional(s32[]{:T(128)} %bitcast.31, () %tuple.88, (bf16[192,2048]{1,0:T(8,128)(2,1)}, f32[192]{0:T(256)S(1)}, bf16[768,2048]{1,0:T(8,128)(2,1)}, f32[1,2048]{1,0:T(1,128)S(1)}, ...), branch_computations={%region_9.10_spmd, %region_10.16_spmd} | conditional | flops 4448842240 | bytes 79307384 | solution.py:639
  324.1 4.2 convolution_convert_fusion.4
  328.4 4.1 collective-permute-done.24
  335.7 4.8 collective-permute-done.23
  340.5 5.2 collective-permute-done.25
  348.9 4.2 convolution_convert_fusion.5
  358.4 3.1 add_convert_fusion.1
  362.1 30.0 %conditional.11 = (bf16[768,2048]{1,0:T(8,128)(2,1)}, f32[512,704]{0,1:T(8,128)}) conditional(s32[]{:T(128)} %bitcast.31, () %tuple.87, (bf16[192,2048]{1,0:T(8,128)(2,1)}, bf16[512,704]{1,0:T(8,128)(2,1)}) %tuple.97), branch_computations={%region_17.18_spmd, %region_18.19_spmd} | conditional | bytes 19464368 | solution.py:639
  365.1 2.5 copy.97
  369.7 7.9 %collective-permute-done.1 = bf16[192,2048]{1,0:T(8,128)(2,1)S(1)} collective-permute-done((bf16[192,2048]{1,0:T(8,128)(2,1)}, bf16[192,2048]{1,0:T(8,128)(2,1)S(1)}, u32[]{:S(2)}, u32[]{:S(2)}) %collective-permute-start.1) | collective-permute-done | bytes 786464 | tf_op jit(solution)/shard_map/cond/branch_1_fun/ppermute | solution.py:30
  379.4 3.0 collective-permute-done
  388.0 3.3 collective-permute-done.3
  392.1 3.8 convolution_convert_fusion.10
  398.1 51.2 %conditional.12 = (bf16[1536,768]{1,0:T(8,128)(2,1)}, bf16[2048,768]{0,1:T(8,128)(2,1)}, bf16[96,2048]{1,0:T(8,128)(2,1)}, bf16[96,2048]{1,0:T(8,128)(2,1)}, bf1...) conditional(s32[]{:T(128)} %bitcast.31, () %tuple.86, (bf16[768,2048]{1,0:T(8,128)(2,1)}, ...), branch_computations={%region_19.20_spmd, %region_20.21_spmd} | conditional | flops 49640488960 | bytes 30540804 | solution.py:639
  398.3 2.4 fusion.39
  404.7 3.0 convolution_convert_fusion.7
  407.9 32.1 %attend_back.1 = bf16[1536,768]{1,0:T(8,128)(2,1)} custom-call(s32[1,1536]{1,0:T(1,128)S(1)} %get-tuple-element.163.first, bf16[1536,256]{1,0:T(8,128)(2,1)} %get-tuple-element.164.q_ref, bf16[1536,256]{1,0:T(8,128)(2,1)} %get-tuple-element.165.k_ref, bf16[1536,256]{1,0:T(8,128)(2,1)} %get-tuple-element.166.v_ref, ...), custom_call_target="tpu_custom_call" | custom-call | flops 44000002048 | bytes 1 | tf_op jit(solution)/shard_map/cond/branch_1_fun/attend_back/pallas_call | solution.py:507
  440.0 9.2 %fusion.26 = bf16[2048,768]{0,1:T(8,128)(2,1)} fusion(bf16[1536,768]{1,0:T(8,128)(2,1)} %attend_back.1, bf16[1536,2048]{1,0:T(8,128)(2,1)} %get-tuple-element.175), kind=kOutput, calls=%fused_computation.60 | convolution fusion | flops 4833411072 | bytes 11796480 | tf_op jit(solution)/shard_map/cond/branch_1_fun/dot_general | solution.py:26
  450.5 2.9 fusion.46
  453.4 3.9 fusion.33
  457.4 2.6 add_convert_fusion.9
  460.0 72.3 %conditional.13 = (f32[1,192,2048]{2,1,0:T(8,128)}, f32[4,448]{1,0:T(4,128)}, bf16[1,192,2048]{2,1,0:T(8,128)(2,1)}) conditional(s32[]{:T(128)} %bitcast.31, () %tuple.81, (f32[1536,128]{1,0:T(8,128)}, bf16[1536,768]{1,0:T(8,128)(2,1)}, bf16[768,2048]{1,0:T(8,128)(2,1)}, bf16[2048,768]{1,0:T(8,128)(2,1)}, bf16[768,2048]{1,0:T(8,128)(2,1)}, ...), branch_computations={%region_22.23_spmd, %region_23.26_spmd} | conditional | flops 14020071424 | bytes 76783184 | solution.py:639
  460.1 7.4 %unproject.3 = (bf16[768,2048]{1,0:T(8,128)(2,1)S(1)}, f32[1,2048]{1,0:T(1,128)S(1)}, f32[1,2048]{1,0:T(1,128)S(1)}, f32[1,768]{1,0:T(1,128)S(1)}) custom-call(s32[4]{0:T(128)S(1)} %get-tuple-element.479.order, bf16[1536,768]{1,0:T(8,128)(2,1)} %get-tuple-element.179.g_ref, bf16[768,2048]{1,0:T(8,128)(2,1)} %get-tuple-element.183.x_ref, ...), custom_call_target="tpu_custom_call" | custom-call | flops 7000000000 | bytes 1 | tf_op jit(solution)/shard_map/cond/branch_1_fun/unproject/pallas_call | solution.py:293
  467.6 7.4 %unproject.2 = (bf16[768,2048]{1,0:T(8,128)(2,1)S(1)}, f32[1,2048]{1,0:T(1,128)S(1)}, f32[1,2048]{1,0:T(1,128)S(1)}, f32[1,768]{1,0:T(1,128)S(1)}) custom-call(s32[4]{0:T(128)S(1)} %get-tuple-element.478.order, bf16[1536,768]{1,0:T(8,128)(2,1)} %get-tuple-element.179.g_ref, bf16[768,2048]{1,0:T(8,128)(2,1)} %get-tuple-element.180.x_ref, ...), custom_call_target="tpu_custom_call" | custom-call | flops 7000000000 | bytes 1 | tf_op jit(solution)/shard_map/cond/branch_1_fun/unproject/pallas_call | solution.py:293
  483.7 8.0 %collective-permute-done.10 = bf16[96,2048]{1,0:T(8,128)(2,1)} collective-permute-done((bf16[96,2048]{1,0:T(8,128)(2,1)}, bf16[96,2048]{1,0:T(8,128)(2,1)}, u32[]{:S(2)}, u32[]{:S(2)}) %collective-permute-start.10) | collective-permute-done | bytes 393248 | tf_op jit(solution)/shard_map/cond/branch_1_fun/ppermute | solution.py:30
  493.4 6.3 %collective-permute-done.12 = bf16[96,2048]{1,0:T(8,128)(2,1)} collective-permute-done((bf16[96,2048]{1,0:T(8,128)(2,1)}, bf16[96,2048]{1,0:T(8,128)(2,1)}, u32[]{:S(2)}, u32[]{:S(2)}) %collective-permute-start.12) | collective-permute-done | bytes 393248 | tf_op jit(solution)/shard_map/cond/branch_1_fun/ppermute | solution.py:30
  507.1 2.4 add_convert_fusion.6
  511.3 5.1 collective-permute-done.17
  529.4 2.9 add_bitcast_fusion
  534.2 2.3 copy.94
  536.5 3.5 all-to-all-start.1
  545.4 7.2 %all-to-all-done.1 = bf16[8,64,768]{2,1,0:T(8,128)(2,1)S(1)} async-done(((bf16[8,64,768]{2,1,0:T(8,128)(2,1)}), bf16[8,64,768]{2,1,0:T(8,128)(2,1)S(1)}, u32[]{:S(2)}, u32[]{:S(2)}) %all-to-all-start.1) | async-done | bytes 786464 | tf_op jit(solution)/shard_map/all_to_all | solution.py:911
  (395 shorter events, 143.5 us)
Async XLA Ops:
  7.2 93.4 %all-gather.9.cloned.1.call-start = ((), (), s32[]{:S(2)}) async-start(), calls=%async_computation.6 | async-start | bytes 1310720 | tf_op jit(solution)/shard_map/all_gather | solution.py:646
  7.9 97.0 %all-gather.11.cloned.1.call-start = ((), (), s32[]{:S(2)}) async-start(), calls=%async_computation.7 | async-start | bytes 3932160 | tf_op jit(solution)/shard_map/all_gather | solution.py:659
  27.3 202.9 %all-gather.15.cloned.1.call-start = ((), (), s32[]{:S(2)}) async-start(), calls=%async_computation.9 | async-start | bytes 7208960 | tf_op jit(solution)/shard_map/all_gather | solution.py:661
  30.3 47.0 %copy-start.7 = (bf16[1,192,2048]{2,1,0:T(8,128)(2,1)S(1)}, bf16[1,192,2048]{2,1,0:T(8,128)(2,1)}, u32[]{:S(2)}) copy-start(bf16[1,192,2048]{2,1,0:T(8,128)(2,1)} %param.39) | copy-start | bytes 2359300
  30.3 24.5 %collective-permute-start.4 = (bf16[192,2048]{1,0:T(8,128)(2,1)S(1)}, bf16[192,2048]{1,0:T(8,128)(2,1)}, u32[]{:S(2)}, u32[]{:S(2)}) collective-permute-start(bf16[192,2048]{1,0:T(8,128)(2,1)S(1)} %get-tuple-element.131), channel_id=1, source_target_pairs={{0,2},{1,3},{2,0},{3,1},{4,6},{5,7},{6,4},{7,5},{8,10},{9,11},{10,... | collective-permute-start | bytes 2359304 | tf_op jit(solution)/shard_map/cond/branch_1_fun/ppermute | solution.py:30
  30.9 23.9 %collective-permute-start.5 = (bf16[192,2048]{1,0:T(8,128)(2,1)S(1)}, bf16[192,2048]{1,0:T(8,128)(2,1)}, u32[]{:S(2)}, u32[]{:S(2)}) collective-permute-start(bf16[192,2048]{1,0:T(8,128)(2,1)S(1)} %get-tuple-element.131), channel_id=1, source_target_pairs={{0,4},{1,5},{2,6},{3,7},{4,0},{5,1},{6,2},{7,3},{8,12},{9,13},{10,... | collective-permute-start | bytes 2359304 | tf_op jit(solution)/shard_map/cond/branch_1_fun/ppermute | solution.py:30
  55.9 11.4 %collective-permute-start.6 = (bf16[96,2048]{1,0:T(8,128)(2,1)S(1)}, bf16[96,2048]{1,0:T(8,128)(2,1)S(1)}, u32[]{:S(2)}, u32[]{:S(2)}) collective-permute-start(bf16[96,2048]{1,0:T(8,128)(2,1)S(1)} %slice.146), channel_id=1, source_target_pairs={{0,2},{1,3},{2,0},{3,1},{4,6},{5,7},{6,4},{7,5},{8,10},{9,11},{10,... | collective-permute-start | bytes 1179656 | tf_op jit(solution)/shard_map/cond/branch_1_fun/ppermute | solution.py:30
  58.4 11.1 %collective-permute-start.7 = (bf16[96,2048]{1,0:T(8,128)(2,1)S(1)}, bf16[96,2048]{1,0:T(8,128)(2,1)S(1)}, u32[]{:S(2)}, u32[]{:S(2)}) collective-permute-start(bf16[96,2048]{1,0:T(8,128)(2,1)S(1)} %slice.147), channel_id=1, source_target_pairs={{0,4},{1,5},{2,6},{3,7},{4,0},{5,1},{6,2},{7,3},{8,12},{9,13},{10,... | collective-permute-start | bytes 1179656 | tf_op jit(solution)/shard_map/cond/branch_1_fun/ppermute | solution.py:30
  70.4 6.0 %collective-permute-start.8 = (bf16[768,2048]{1,0:T(8,128)(2,1)}, bf16[768,2048]{1,0:T(8,128)(2,1)}, u32[]{:S(2)}, u32[]{:S(2)}) collective-permute-start(bf16[768,2048]{1,0:T(8,128)(2,1)} %constant_dynamic-update-slice_fusion.5), channel_id=1, source_target_pairs={{0,1},{1,0},{2,3},{3,2},{4,5},{5,4},{6,7},{7,6},{8,9},{9,8},{10,11... | collective-permute-start | bytes 9437192 | tf_op jit(solution)/shard_map/cond/branch_1_fun/ppermute | solution.py:30
  76.4 44.1 %copy-start.52 = (s32[1,1536]{1,0:T(1,128)}, s32[1,1536]{1,0:T(1,128)S(1)}, u32[]{:S(2)}) copy-start(s32[1,1536]{1,0:T(1,128)S(1)} %get-tuple-element.300.first) | copy-start | bytes 18436
  77.3 21.4 %collective-permute-start.34 = (bf16[192,2048]{1,0:T(8,128)(2,1)S(1)}, bf16[192,2048]{1,0:T(8,128)(2,1)}, u32[]{:S(2)}, u32[]{:S(2)}) collective-permute-start(bf16[192,2048]{1,0:T(8,128)(2,1)S(1)} %bitcast.145), channel_id=1, source_target_pairs={{0,2},{1,3},{2,0},{3,1},{4,6},{5,7},{6,4},{7,5},{8,10},{9,11},{10,... | collective-permute-start | bytes 2359304 | tf_op jit(solution)/shard_map/ppermute | solution.py:30
  77.8 19.6 %collective-permute-start.35 = (bf16[192,2048]{1,0:T(8,128)(2,1)S(1)}, bf16[192,2048]{1,0:T(8,128)(2,1)S(1)}, u32[]{:S(2)}, u32[]{:S(2)}) collective-permute-start(bf16[192,2048]{1,0:T(8,128)(2,1)S(1)} %bitcast.146), channel_id=1, source_target_pairs={{0,4},{1,5},{2,6},{3,7},{4,0},{5,1},{6,2},{7,3},{8,12},{9,13},{10,... | collective-permute-start | bytes 2359304 | tf_op jit(solution)/shard_map/ppermute | solution.py:30
  80.9 195.5 %all-gather.13.cloned.1.call-start = ((), (), s32[]{:S(2)}) async-start(), calls=%async_computation.8 | async-start | bytes 3932160 | tf_op jit(solution)/shard_map/all_gather | solution.py:664
  97.4 57.0 %collective-permute-start.36 = (bf16[96,2048]{1,0:T(8,128)(2,1)S(1)}, bf16[96,2048]{1,0:T(8,128)(2,1)S(1)}, u32[]{:S(2)}, u32[]{:S(2)}) collective-permute-start(bf16[96,2048]{1,0:T(8,128)(2,1)S(1)} %slice.261), channel_id=1, source_target_pairs={{0,2},{1,3},{2,0},{3,1},{4,6},{5,7},{6,4},{7,5},{8,10},{9,11},{10,... | collective-permute-start | bytes 1179656 | tf_op jit(solution)/shard_map/ppermute | solution.py:30
  99.7 54.7 %collective-permute-start.37 = (bf16[96,2048]{1,0:T(8,128)(2,1)S(1)}, bf16[96,2048]{1,0:T(8,128)(2,1)S(1)}, u32[]{:S(2)}, u32[]{:S(2)}) collective-permute-start(bf16[96,2048]{1,0:T(8,128)(2,1)S(1)} %slice.262), channel_id=1, source_target_pairs={{0,4},{1,5},{2,6},{3,7},{4,0},{5,1},{6,2},{7,3},{8,12},{9,13},{10,... | collective-permute-start | bytes 1179656 | tf_op jit(solution)/shard_map/ppermute | solution.py:30
  156.4 6.0 %collective-permute-start.38 = (bf16[768,2048]{1,0:T(8,128)(2,1)S(1)}, bf16[768,2048]{1,0:T(8,128)(2,1)}, u32[]{:S(2)}, u32[]{:S(2)}) collective-permute-start(bf16[768,2048]{1,0:T(8,128)(2,1)S(1)} %convolution_convert_fusion.8), channel_id=1, source_target_pairs={{0,1},{1,0},{2,3},{3,2},{4,5},{5,4},{6,7},{7,6},{8,9},{9,8},{10,11... | collective-permute-start | bytes 9437192 | tf_op jit(solution)/shard_map/ppermute | solution.py:30
  158.8 202.8 %reduce-scatter.5.cloned.1.call-start = ((), (), s32[]{:S(2)}) async-start(), calls=%async_computation.10 | async-start | bytes 3932160 | tf_op jit(solution)/shard_map/reduce_scatter | solution.py:642
  165.8 12.0 %collective-permute-start.40 = (bf16[96,2048]{1,0:T(8,128)(2,1)S(1)}, bf16[96,2048]{1,0:T(8,128)(2,1)S(1)}, u32[]{:S(2)}, u32[]{:S(2)}) collective-permute-start(bf16[96,2048]{1,0:T(8,128)(2,1)S(1)} %get-tuple-element.494), channel_id=1, source_target_pairs={{0,2},{1,3},{2,0},{3,1},{4,6},{5,7},{6,4},{7,5},{8,10},{9,11},{10,... | collective-permute-start | bytes 1179656 | tf_op jit(solution)/shard_map/ppermute | solution.py:30
  168.9 16.9 %collective-permute-start.39 = (bf16[96,2048]{1,0:T(8,128)(2,1)S(1)}, bf16[96,2048]{1,0:T(8,128)(2,1)S(1)}, u32[]{:S(2)}, u32[]{:S(2)}) collective-permute-start(bf16[96,2048]{1,0:T(8,128)(2,1)S(1)} %get-tuple-element.491), channel_id=1, source_target_pairs={{0,2},{1,3},{2,0},{3,1},{4,6},{5,7},{6,4},{7,5},{8,10},{9,11},{10,... | collective-permute-start | bytes 1179656 | tf_op jit(solution)/shard_map/ppermute | solution.py:30
  169.5 16.3 %collective-permute-start.43 = (bf16[96,2048]{1,0:T(8,128)(2,1)S(1)}, bf16[96,2048]{1,0:T(8,128)(2,1)S(1)}, u32[]{:S(2)}, u32[]{:S(2)}) collective-permute-start(bf16[96,2048]{1,0:T(8,128)(2,1)S(1)} %get-tuple-element.492), channel_id=1, source_target_pairs={{0,4},{1,5},{2,6},{3,7},{4,0},{5,1},{6,2},{7,3},{8,12},{9,13},{10,... | collective-permute-start | bytes 1179656 | tf_op jit(solution)/shard_map/ppermute | solution.py:30
  177.9 12.1 %collective-permute-start.41 = (bf16[96,2048]{1,0:T(8,128)(2,1)S(1)}, bf16[96,2048]{1,0:T(8,128)(2,1)S(1)}, u32[]{:S(2)}, u32[]{:S(2)}) collective-permute-start(bf16[96,2048]{1,0:T(8,128)(2,1)S(1)} %add_convert_fusion.12), channel_id=1, source_target_pairs={{0,4},{1,5},{2,6},{3,7},{4,0},{5,1},{6,2},{7,3},{8,12},{9,13},{10,... | collective-permute-start | bytes 1179656 | tf_op jit(solution)/shard_map/ppermute | solution.py:30
  179.6 24.9 %collective-permute-start.49 = (bf16[768,2048]{1,0:T(8,128)(2,1)S(1)}, bf16[768,2048]{1,0:T(8,128)(2,1)S(1)}, u32[]{:S(2)}, u32[]{:S(2)}) collective-permute-start(bf16[768,2048]{1,0:T(8,128)(2,1)S(1)} %get-tuple-element.512), channel_id=1, source_target_pairs={{0,1},{1,0},{2,3},{3,2},{4,5},{5,4},{6,7},{7,6},{8,9},{9,8},{10,11... | collective-permute-start | bytes 9437192 | tf_op jit(solution)/shard_map/ppermute | solution.py:30
  179.7 17.6 %collective-permute-start.42 = (bf16[96,2048]{1,0:T(8,128)(2,1)S(1)}, bf16[96,2048]{1,0:T(8,128)(2,1)S(1)}, u32[]{:S(2)}, u32[]{:S(2)}) collective-permute-start(bf16[96,2048]{1,0:T(8,128)(2,1)S(1)} %get-tuple-element.493), channel_id=1, source_target_pairs={{0,4},{1,5},{2,6},{3,7},{4,0},{5,1},{6,2},{7,3},{8,12},{9,13},{10,... | collective-permute-start | bytes 1179656 | tf_op jit(solution)/shard_map/ppermute | solution.py:30
  190.3 9.1 %collective-permute-start.44 = (bf16[96,2048]{1,0:T(8,128)(2,1)S(1)}, bf16[96,2048]{1,0:T(8,128)(2,1)S(1)}, u32[]{:S(2)}, u32[]{:S(2)}) collective-permute-start(bf16[96,2048]{1,0:T(8,128)(2,1)S(1)} %get-tuple-element.490), channel_id=1, source_target_pairs={{0,2},{1,3},{2,0},{3,1},{4,6},{5,7},{6,4},{7,5},{8,10},{9,11},{10,... | collective-permute-start | bytes 1179656 | tf_op jit(solution)/shard_map/ppermute | solution.py:30
  201.5 16.7 %collective-permute-start.46 = (bf16[192,2048]{1,0:T(8,128)(2,1)S(1)}, bf16[192,2048]{1,0:T(8,128)(2,1)S(1)}, u32[]{:S(2)}, u32[]{:S(2)}) collective-permute-start(bf16[192,2048]{1,0:T(8,128)(2,1)S(1)} %get-tuple-element.445), channel_id=1, source_target_pairs={{0,4},{1,5},{2,6},{3,7},{4,0},{5,1},{6,2},{7,3},{8,12},{9,13},{10,... | collective-permute-start | bytes 2359304 | tf_op jit(solution)/shard_map/ppermute | solution.py:30
  203.0 18.5 %collective-permute-start.45 = (bf16[192,2048]{1,0:T(8,128)(2,1)S(1)}, bf16[192,2048]{1,0:T(8,128)(2,1)S(1)}, u32[]{:S(2)}, u32[]{:S(2)}) collective-permute-start(bf16[192,2048]{1,0:T(8,128)(2,1)S(1)} %get-tuple-element.445), channel_id=1, source_target_pairs={{0,2},{1,3},{2,0},{3,1},{4,6},{5,7},{6,4},{7,5},{8,10},{9,11},{10,... | collective-permute-start | bytes 2359304 | tf_op jit(solution)/shard_map/ppermute | solution.py:30
  218.2 9.6 %collective-permute-start.47 = (bf16[96,2048]{1,0:T(8,128)(2,1)S(1)}, bf16[96,2048]{1,0:T(8,128)(2,1)S(1)}, u32[]{:S(2)}, u32[]{:S(2)}) collective-permute-start(bf16[96,2048]{1,0:T(8,128)(2,1)S(1)} %slice.271), channel_id=1, source_target_pairs={{0,2},{1,3},{2,0},{3,1},{4,6},{5,7},{6,4},{7,5},{8,10},{9,11},{10,... | collective-permute-start | bytes 1179656 | tf_op jit(solution)/shard_map/ppermute | solution.py:30
  221.5 7.8 %collective-permute-start.48 = (bf16[96,2048]{1,0:T(8,128)(2,1)S(1)}, bf16[96,2048]{1,0:T(8,128)(2,1)S(1)}, u32[]{:S(2)}, u32[]{:S(2)}) collective-permute-start(bf16[96,2048]{1,0:T(8,128)(2,1)S(1)} %slice.272), channel_id=1, source_target_pairs={{0,4},{1,5},{2,6},{3,7},{4,0},{5,1},{6,2},{7,3},{8,12},{9,13},{10,... | collective-permute-start | bytes 1179656 | tf_op jit(solution)/shard_map/ppermute | solution.py:30
  230.2 14.5 %collective-permute-start.21 = (bf16[768,2048]{1,0:T(8,128)(2,1)}, bf16[768,2048]{1,0:T(8,128)(2,1)}, u32[]{:S(2)}, u32[]{:S(2)}) collective-permute-start(bf16[768,2048]{1,0:T(8,128)(2,1)} %get-tuple-element.142), channel_id=1, source_target_pairs={{0,1},{1,0},{2,3},{3,2},{4,5},{5,4},{6,7},{7,6},{8,9},{9,8},{10,11... | collective-permute-start | bytes 9437192 | tf_op jit(solution)/shard_map/cond/branch_1_fun/ppermute | solution.py:30
  270.1 179.2 %reduce-scatter.7.cloned.1.call-start = ((), (), s32[]{:S(2)}) async-start(), calls=%async_computation.11 | async-start | bytes 7208960 | tf_op jit(solution)/shard_map/reduce_scatter | solution.py:642
  290.6 24.7 %collective-permute-start.22 = (bf16[768,2048]{1,0:T(8,128)(2,1)}, bf16[768,2048]{1,0:T(8,128)(2,1)S(1)}, u32[]{:S(2)}, u32[]{:S(2)}) collective-permute-start(bf16[768,2048]{1,0:T(8,128)(2,1)} %convolution_convert_fusion.2), channel_id=1, source_target_pairs={{0,1},{1,0},{2,3},{3,2},{4,5},{5,4},{6,7},{7,6},{8,9},{9,8},{10,11... | collective-permute-start | bytes 9437192 | tf_op jit(solution)/shard_map/cond/branch_1_fun/ppermute | solution.py:30
  318.8 213.5 %reduce-scatter.9.cloned.1.call-start = ((), (), s32[]{:S(2)}) async-start(), calls=%async_computation.12 | async-start | bytes 3932160 | tf_op jit(solution)/shard_map/reduce_scatter | solution.py:642
  320.5 12.0 %collective-permute-start.24 = (bf16[96,2048]{1,0:T(8,128)(2,1)S(1)}, bf16[96,2048]{1,0:T(8,128)(2,1)S(1)}, u32[]{:S(2)}, u32[]{:S(2)}) collective-permute-start(bf16[96,2048]{1,0:T(8,128)(2,1)S(1)} %get-tuple-element.484), channel_id=1, source_target_pairs={{0,2},{1,3},{2,0},{3,1},{4,6},{5,7},{6,4},{7,5},{8,10},{9,11},{10,... | collective-permute-start | bytes 1179656 | tf_op jit(solution)/shard_map/cond/branch_1_fun/ppermute | solution.py:30
  322.0 18.4 %collective-permute-start.23 = (bf16[96,2048]{1,0:T(8,128)(2,1)S(1)}, bf16[96,2048]{1,0:T(8,128)(2,1)S(1)}, u32[]{:S(2)}, u32[]{:S(2)}) collective-permute-start(bf16[96,2048]{1,0:T(8,128)(2,1)S(1)} %get-tuple-element.481), channel_id=1, source_target_pairs={{0,2},{1,3},{2,0},{3,1},{4,6},{5,7},{6,4},{7,5},{8,10},{9,11},{10,... | collective-permute-start | bytes 1179656 | tf_op jit(solution)/shard_map/cond/branch_1_fun/ppermute | solution.py:30
  322.6 17.9 %collective-permute-start.27 = (bf16[96,2048]{1,0:T(8,128)(2,1)S(1)}, bf16[96,2048]{1,0:T(8,128)(2,1)S(1)}, u32[]{:S(2)}, u32[]{:S(2)}) collective-permute-start(bf16[96,2048]{1,0:T(8,128)(2,1)S(1)} %get-tuple-element.482), channel_id=1, source_target_pairs={{0,4},{1,5},{2,6},{3,7},{4,0},{5,1},{6,2},{7,3},{8,12},{9,13},{10,... | collective-permute-start | bytes 1179656 | tf_op jit(solution)/shard_map/cond/branch_1_fun/ppermute | solution.py:30
  328.3 30.1 %collective-permute-start.29 = (bf16[768,2048]{1,0:T(8,128)(2,1)S(1)}, bf16[768,2048]{1,0:T(8,128)(2,1)S(1)}, u32[]{:S(2)}, u32[]{:S(2)}) collective-permute-start(bf16[768,2048]{1,0:T(8,128)(2,1)S(1)} %convolution_convert_fusion.4), channel_id=1, source_target_pairs={{0,1},{1,0},{2,3},{3,2},{4,5},{5,4},{6,7},{7,6},{8,9},{9,8},{10,11... | collective-permute-start | bytes 9437192 | tf_op jit(solution)/shard_map/cond/branch_1_fun/ppermute | solution.py:30
  333.6 12.1 %collective-permute-start.25 = (bf16[96,2048]{1,0:T(8,128)(2,1)S(1)}, bf16[96,2048]{1,0:T(8,128)(2,1)S(1)}, u32[]{:S(2)}, u32[]{:S(2)}) collective-permute-start(bf16[96,2048]{1,0:T(8,128)(2,1)S(1)} %add_convert_fusion.3), channel_id=1, source_target_pairs={{0,4},{1,5},{2,6},{3,7},{4,0},{5,1},{6,2},{7,3},{8,12},{9,13},{10,... | collective-permute-start | bytes 1179656 | tf_op jit(solution)/shard_map/cond/branch_1_fun/ppermute | solution.py:30
  335.1 18.0 %collective-permute-start.26 = (bf16[96,2048]{1,0:T(8,128)(2,1)S(1)}, bf16[96,2048]{1,0:T(8,128)(2,1)S(1)}, u32[]{:S(2)}, u32[]{:S(2)}) collective-permute-start(bf16[96,2048]{1,0:T(8,128)(2,1)S(1)} %get-tuple-element.483), channel_id=1, source_target_pairs={{0,4},{1,5},{2,6},{3,7},{4,0},{5,1},{6,2},{7,3},{8,12},{9,13},{10,... | collective-permute-start | bytes 1179656 | tf_op jit(solution)/shard_map/cond/branch_1_fun/ppermute | solution.py:30
  347.4 7.8 %collective-permute-start.28 = (bf16[96,2048]{1,0:T(8,128)(2,1)S(1)}, bf16[96,2048]{1,0:T(8,128)(2,1)S(1)}, u32[]{:S(2)}, u32[]{:S(2)}) collective-permute-start(bf16[96,2048]{1,0:T(8,128)(2,1)S(1)} %get-tuple-element.480), channel_id=1, source_target_pairs={{0,2},{1,3},{2,0},{3,1},{4,6},{5,7},{6,4},{7,5},{8,10},{9,11},{10,... | collective-permute-start | bytes 1179656 | tf_op jit(solution)/shard_map/cond/branch_1_fun/ppermute | solution.py:30
  362.1 15.5 %collective-permute-start.1 = (bf16[192,2048]{1,0:T(8,128)(2,1)}, bf16[192,2048]{1,0:T(8,128)(2,1)S(1)}, u32[]{:S(2)}, u32[]{:S(2)}) collective-permute-start(bf16[192,2048]{1,0:T(8,128)(2,1)} %get-tuple-element.161), channel_id=1, source_target_pairs={{0,4},{1,5},{2,6},{3,7},{4,0},{5,1},{6,2},{7,3},{8,12},{9,13},{10,... | collective-permute-start | bytes 2359304 | tf_op jit(solution)/shard_map/cond/branch_1_fun/ppermute | solution.py:30
  363.6 18.8 %collective-permute-start = (bf16[192,2048]{1,0:T(8,128)(2,1)}, bf16[192,2048]{1,0:T(8,128)(2,1)}, u32[]{:S(2)}, u32[]{:S(2)}) collective-permute-start(bf16[192,2048]{1,0:T(8,128)(2,1)} %get-tuple-element.161), channel_id=1, source_target_pairs={{0,2},{1,3},{2,0},{3,1},{4,6},{5,7},{6,4},{7,5},{8,10},{9,11},{10,... | collective-permute-start | bytes 2359304 | tf_op jit(solution)/shard_map/cond/branch_1_fun/ppermute | solution.py:30
  377.6 9.6 %collective-permute-start.2 = (bf16[96,2048]{1,0:T(8,128)(2,1)S(1)}, bf16[96,2048]{1,0:T(8,128)(2,1)S(1)}, u32[]{:S(2)}, u32[]{:S(2)}) collective-permute-start(bf16[96,2048]{1,0:T(8,128)(2,1)S(1)} %slice.247), channel_id=1, source_target_pairs={{0,2},{1,3},{2,0},{3,1},{4,6},{5,7},{6,4},{7,5},{8,10},{9,11},{10,... | collective-permute-start | bytes 1179656 | tf_op jit(solution)/shard_map/cond/branch_1_fun/ppermute | solution.py:30
  383.5 7.8 %collective-permute-start.3 = (bf16[96,2048]{1,0:T(8,128)(2,1)S(1)}, bf16[96,2048]{1,0:T(8,128)(2,1)S(1)}, u32[]{:S(2)}, u32[]{:S(2)}) collective-permute-start(bf16[96,2048]{1,0:T(8,128)(2,1)S(1)} %slice.248), channel_id=1, source_target_pairs={{0,4},{1,5},{2,6},{3,7},{4,0},{5,1},{6,2},{7,3},{8,12},{9,13},{10,... | collective-permute-start | bytes 1179656 | tf_op jit(solution)/shard_map/cond/branch_1_fun/ppermute | solution.py:30
  392.1 6.0 %collective-permute-start.50 = (bf16[768,2048]{1,0:T(8,128)(2,1)}, bf16[768,2048]{1,0:T(8,128)(2,1)}, u32[]{:S(2)}, u32[]{:S(2)}) collective-permute-start(bf16[768,2048]{1,0:T(8,128)(2,1)} %get-tuple-element.332), channel_id=1, source_target_pairs={{0,1},{1,0},{2,3},{3,2},{4,5},{5,4},{6,7},{7,6},{8,9},{9,8},{10,11... | collective-permute-start | bytes 9437192 | tf_op jit(solution)/shard_map/ppermute | solution.py:30
  400.6 48.6 %collective-permute-start.30 = (bf16[96,2048]{1,0:T(8,128)(2,1)}, bf16[96,2048]{1,0:T(8,128)(2,1)}, u32[]{:S(2)}, u32[]{:S(2)}) collective-permute-start(bf16[96,2048]{1,0:T(8,128)(2,1)} %get-tuple-element.456), channel_id=1, source_target_pairs={{0,2},{1,3},{2,0},{3,1},{4,6},{5,7},{6,4},{7,5},{8,10},{9,11},{10,... | collective-permute-start | bytes 1179656 | tf_op jit(solution)/shard_map/cond/branch_1_fun/ppermute | solution.py:30
  402.2 47.1 %collective-permute-start.31 = (bf16[96,2048]{1,0:T(8,128)(2,1)}, bf16[96,2048]{1,0:T(8,128)(2,1)}, u32[]{:S(2)}, u32[]{:S(2)}) collective-permute-start(bf16[96,2048]{1,0:T(8,128)(2,1)} %get-tuple-element.455), channel_id=1, source_target_pairs={{0,4},{1,5},{2,6},{3,7},{4,0},{5,1},{6,2},{7,3},{8,12},{9,13},{10,... | collective-permute-start | bytes 1179656 | tf_op jit(solution)/shard_map/cond/branch_1_fun/ppermute | solution.py:30
  402.2 47.1 %collective-permute-start.32 = (bf16[96,2048]{1,0:T(8,128)(2,1)}, bf16[96,2048]{1,0:T(8,128)(2,1)}, u32[]{:S(2)}, u32[]{:S(2)}) collective-permute-start(bf16[96,2048]{1,0:T(8,128)(2,1)} %get-tuple-element.454), channel_id=1, source_target_pairs={{0,2},{1,3},{2,0},{3,1},{4,6},{5,7},{6,4},{7,5},{8,10},{9,11},{10,... | collective-permute-start | bytes 1179656 | tf_op jit(solution)/shard_map/cond/branch_1_fun/ppermute | solution.py:30
  402.7 46.6 %collective-permute-start.33 = (bf16[96,2048]{1,0:T(8,128)(2,1)S(1)}, bf16[96,2048]{1,0:T(8,128)(2,1)}, u32[]{:S(2)}, u32[]{:S(2)}) collective-permute-start(bf16[96,2048]{1,0:T(8,128)(2,1)S(1)} %get-tuple-element.453), channel_id=1, source_target_pairs={{0,4},{1,5},{2,6},{3,7},{4,0},{5,1},{6,2},{7,3},{8,12},{9,13},{10,... | collective-permute-start | bytes 1179656 | tf_op jit(solution)/shard_map/cond/branch_1_fun/ppermute | solution.py:30
  449.4 93.1 %reduce-scatter.11.cloned.1.call-start = ((), (), s32[]{:S(2)}) async-start(), calls=%async_computation.13 | async-start | bytes 1310720 | tf_op jit(solution)/shard_map/reduce_scatter | solution.py:642
  467.5 7.5 %collective-permute-start.9 = (bf16[768,2048]{1,0:T(8,128)(2,1)S(1)}, bf16[768,2048]{1,0:T(8,128)(2,1)S(1)}, u32[]{:S(2)}, u32[]{:S(2)}) collective-permute-start(bf16[768,2048]{1,0:T(8,128)(2,1)S(1)} %get-tuple-element.184), channel_id=1, source_target_pairs={{0,1},{1,0},{2,3},{3,2},{4,5},{5,4},{6,7},{7,6},{8,9},{9,8},{10,11... | collective-permute-start | bytes 9437192 | tf_op jit(solution)/shard_map/cond/branch_1_fun/ppermute | solution.py:30
  479.5 12.2 %collective-permute-start.10 = (bf16[96,2048]{1,0:T(8,128)(2,1)}, bf16[96,2048]{1,0:T(8,128)(2,1)}, u32[]{:S(2)}, u32[]{:S(2)}) collective-permute-start(bf16[96,2048]{1,0:T(8,128)(2,1)} %get-tuple-element.477), channel_id=1, source_target_pairs={{0,2},{1,3},{2,0},{3,1},{4,6},{5,7},{6,4},{7,5},{8,10},{9,11},{10,... | collective-permute-start | bytes 1179656 | tf_op jit(solution)/shard_map/cond/branch_1_fun/ppermute | solution.py:30
  481.1 12.3 %collective-permute-start.11 = (bf16[96,2048]{1,0:T(8,128)(2,1)}, bf16[96,2048]{1,0:T(8,128)(2,1)}, u32[]{:S(2)}, u32[]{:S(2)}) collective-permute-start(bf16[96,2048]{1,0:T(8,128)(2,1)} %get-tuple-element.476), channel_id=1, source_target_pairs={{0,4},{1,5},{2,6},{3,7},{4,0},{5,1},{6,2},{7,3},{8,12},{9,13},{10,... | collective-permute-start | bytes 1179656 | tf_op jit(solution)/shard_map/cond/branch_1_fun/ppermute | solution.py:30
  481.2 18.5 %collective-permute-start.12 = (bf16[96,2048]{1,0:T(8,128)(2,1)}, bf16[96,2048]{1,0:T(8,128)(2,1)}, u32[]{:S(2)}, u32[]{:S(2)}) collective-permute-start(bf16[96,2048]{1,0:T(8,128)(2,1)} %get-tuple-element.475), channel_id=1, source_target_pairs={{0,2},{1,3},{2,0},{3,1},{4,6},{5,7},{6,4},{7,5},{8,10},{9,11},{10,... | collective-permute-start | bytes 1179656 | tf_op jit(solution)/shard_map/cond/branch_1_fun/ppermute | solution.py:30
  481.7 19.4 %collective-permute-start.13 = (bf16[96,2048]{1,0:T(8,128)(2,1)}, bf16[96,2048]{1,0:T(8,128)(2,1)}, u32[]{:S(2)}, u32[]{:S(2)}) collective-permute-start(bf16[96,2048]{1,0:T(8,128)(2,1)} %get-tuple-element.474), channel_id=1, source_target_pairs={{0,4},{1,5},{2,6},{3,7},{4,0},{5,1},{6,2},{7,3},{8,12},{9,13},{10,... | collective-permute-start | bytes 1179656 | tf_op jit(solution)/shard_map/cond/branch_1_fun/ppermute | solution.py:30
  501.7 4.3 collective-permute-start.16
  502.1 18.9 %collective-permute-start.19 = (bf16[96,2048]{1,0:T(8,128)(2,1)}, bf16[96,2048]{1,0:T(8,128)(2,1)}, u32[]{:S(2)}, u32[]{:S(2)}) collective-permute-start(bf16[96,2048]{1,0:T(8,128)(2,1)} %get-tuple-element.211), channel_id=1, source_target_pairs={{0,4},{1,5},{2,6},{3,7},{4,0},{5,1},{6,2},{7,3},{8,12},{9,13},{10,... | collective-permute-start | bytes 1179656 | tf_op jit(solution)/shard_map/cond/branch_1_fun/ppermute | solution.py:30
  503.8 17.2 %collective-permute-start.20 = (bf16[96,2048]{1,0:T(8,128)(2,1)}, bf16[96,2048]{1,0:T(8,128)(2,1)}, u32[]{:S(2)}, u32[]{:S(2)}) collective-permute-start(bf16[96,2048]{1,0:T(8,128)(2,1)} %get-tuple-element.212), channel_id=1, source_target_pairs={{0,2},{1,3},{2,0},{3,1},{4,6},{5,7},{6,4},{7,5},{8,10},{9,11},{10,... | collective-permute-start | bytes 1179656 | tf_op jit(solution)/shard_map/cond/branch_1_fun/ppermute | solution.py:30
  506.6 9.7 %collective-permute-start.17 = (f32[2,1792]{1,0:T(2,128)S(1)}, f32[2,1792]{1,0:T(2,128)S(1)}, u32[]{:S(2)}, u32[]{:S(2)}) collective-permute-start(f32[2,1792]{1,0:T(2,128)S(1)} %dynamic-slice_bitcast_fusion.2), channel_id=1, source_target_pairs={{0,2},{1,3},{2,0},{3,1},{4,6},{5,7},{6,4},{7,5},{8,10},{9,11},{10,... | collective-permute-start | bytes 43016 | tf_op jit(solution)/shard_map/cond/branch_1_fun/ppermute | solution.py:30
  509.5 11.9 %collective-permute-start.14 = (bf16[96,2048]{1,0:T(8,128)(2,1)}, bf16[96,2048]{1,0:T(8,128)(2,1)}, u32[]{:S(2)}, u32[]{:S(2)}) collective-permute-start(bf16[96,2048]{1,0:T(8,128)(2,1)} %get-tuple-element.472), channel_id=1, source_target_pairs={{0,4},{1,5},{2,6},{3,7},{4,0},{5,1},{6,2},{7,3},{8,12},{9,13},{10,... | collective-permute-start | bytes 1179656 | tf_op jit(solution)/shard_map/cond/branch_1_fun/ppermute | solution.py:30
  509.5 13.1 %collective-permute-start.15 = (bf16[96,2048]{1,0:T(8,128)(2,1)S(1)}, bf16[96,2048]{1,0:T(8,128)(2,1)}, u32[]{:S(2)}, u32[]{:S(2)}) collective-permute-start(bf16[96,2048]{1,0:T(8,128)(2,1)S(1)} %get-tuple-element.473), channel_id=1, source_target_pairs={{0,2},{1,3},{2,0},{3,1},{4,6},{5,7},{6,4},{7,5},{8,10},{9,11},{10,... | collective-permute-start | bytes 1179656 | tf_op jit(solution)/shard_map/cond/branch_1_fun/ppermute | solution.py:30
  517.7 1.8 collective-permute-start.18
  533.2 6.9 %collective-permute-start.51 = (f32[2,448]{1,0:T(2,128)S(1)}, f32[2,448]{1,0:T(2,128)S(1)}, u32[]{:S(2)}, u32[]{:S(2)}) collective-permute-start(f32[2,448]{1,0:T(2,128)S(1)} %dynamic-slice_bitcast_fusion.11), channel_id=1, source_target_pairs={{0,16},{8,24},{16,0},{24,8},{1,17},{9,25},{17,1},{25,9},{2,18},{10... | collective-permute-start | bytes 10760 | tf_op jit(solution)/shard_map/ppermute | solution.py:30
  536.5 16.1 %all-to-all-start.1 = ((bf16[8,64,768]{2,1,0:T(8,128)(2,1)}), bf16[8,64,768]{2,1,0:T(8,128)(2,1)S(1)}, u32[]{:S(2)}, u32[]{:S(2)}) async-start(bf16[8,64,768]{2,1,0:T(8,128)(2,1)} %bitcast.54), calls=%async_computation.4 | async-start | bytes 1572864 | tf_op jit(solution)/shard_map/all_to_all | solution.py:911
  540.1 4.1 collective-permute-start.52
  (73 other events, 695.5 us)
Sparse Core Ops, SparseCore 0:
  9.6 30.6 all-gather.8
  41.9 63.0 all-gather.10
  107.1 105.3 all-gather.14
  214.5 61.7 all-gather.12
  278.5 58.8 reduce-scatter.4
  339.6 102.2 reduce-scatter.6
  449.5 57.6 reduce-scatter.8
  509.5 27.2 reduce-scatter.10

commit v5 on v4

--- a/solution.py
+++ b/solution.py
@@ -801,6 +801,7 @@
     branch_own, out_down = stage(branch_stage, grad_middle.astype(BF), sum_down)
     branch_halves = (branch_own, swap(branch_own, 1))
     attn_own_grad = dot(branch_own, w_out_own, NT).astype(BF)
+    grad_w_out_own = dot(attn_halves[0], branch_own, TN)
 
     def back_stage(
         branch_other, own_grad, w_out_own, first, q, k, v, attn_low, logs, tables, act_one, mixed_sum
@@ -811,7 +812,7 @@
 
     grad_proj, grad_w_qkv, mixed_got = stage(
         back_stage,
-        branch_halves[1],
+        after(branch_halves[1], grad_w_out_own),
         attn_own_grad,
         w_out_own,
         first,
@@ -827,12 +828,8 @@
     grad_proj, grad_w_qkv = after((grad_proj, grad_w_qkv), sum_enter)
     sum_qkv = sum_rows(grad_w_qkv, 0)
 
-    attn_halves, branch_halves, mixed_got = after(
-        (attn_halves, branch_halves, mixed_got), grad_w_qkv
-    )
-    grad_w_out = dot(attn_halves[0], branch_halves[0], TN)
-    grad_w_out = (grad_w_out + dot(attn_halves[1], branch_halves[1], TN)).astype(BF)
-    mixed_between = scatter_between(mixed_sum, mixed_got)
+    branch_other = after(branch_halves[1], grad_w_qkv)
+    grad_w_out = (grad_w_out_own + dot(attn_halves[1], branch_other, TN)).astype(BF)
     if fast_out:
         sum_w_out = sum_rows(grad_w_out, 0)
     else:
@@ -848,13 +845,13 @@
 
     def last_stage(
         grad_proj, w_qkv_own, own, other, stats, gain, grad_middle, grad_gain_two, grad_shift_two,
-        mixed_sum, mixed_got, mixed_between, middle,
+        mixed_sum, mixed_got, middle,
     ):
         part_other, *sums_other = unproject(grad_proj, other, stats, w_qkv_own, 1)
         part_own, *sums_own = unproject(grad_proj, own, stats, w_qkv_own, 0)
         total = start_scatter(part_own, part_other)
         got = scatter_first(total)
-        sums_own, sums_other, got = after((sums_own, sums_other, got))
+        sums_own, sums_other, got, mixed_got = after((sums_own, sums_other, got, mixed_got))
         passed = scatter_second(scatter_between(total, got))
         total, got = after((total, got), *passed)
         grad_gain, grad_shift, grad_bias = (a + b for a, b in zip(sums_own, sums_other))
@@ -879,7 +876,7 @@
         rate = stats[:local, 1:2]
         unit = (own[:local].astype(F32) - stats[:local, 0:1]) * rate
         grad_act_one = scatter_last(total, got, passed)
-        mixed_passed = scatter_second(mixed_between)
+        mixed_passed = scatter_second(scatter_between(mixed_sum, mixed_got))
         if passed:
             mixed_passed = after(mixed_passed, *passed)
         mixed = scatter_last(mixed_sum, mixed_got, mixed_passed)
@@ -902,7 +899,6 @@
         grad_shift_two,
         mixed_sum,
         mixed_got,
-        mixed_between,
         middle,
     )
     sum_enter = after(sum_enter, sums)

time: 569 us -> 567 us (level)
  waiting for transfers between devices: 127 us -> 121 us
    cond x60 -> x62, local copies, waits for them, and re-layouts: 17.4 us -> 15.9 us
    unnamed x119 -> x101, local copies, waits for them, and re-layouts: 15.7 us -> 15.6 us
  transfers between devices with their start and end apart: 62 -> 62, of which waited for: 33 -> 31; matrix products, arithmetic and copies ran while one was open for 36% -> 37% of each run, Pallas kernels for 17% -> 17%
where the time goes in v5:
time: 567 us; the launch traced here: 559 us
  waiting for transfers between devices  121 us (21%)
  matrix products  102 us (18%)
  Pallas kernels  97.8 us (17%)
  starting transfers between devices  67 us (12%)
  local copies, waits for them, and re-layouts  59.1 us (10%)
  other arithmetic  54.6 us (10%)
  blocking collectives  40 us (7%)
  between operations  15.8 us (3%)
    ppermute x53, waiting for transfers between devices, swap(): lax.ppermute(x, axis, [(i, i ^ bit) for i in range(lax.axis_size(axis))])  103 us
    dot_general x17, matrix products, dot(): return lax.dot_general(left, right, dims, preferred_element_type=F32)  102 us
    ppermute x53, starting transfers between devices, swap(): lax.ppermute(x, axis, [(i, i ^ bit) for i in range(lax.axis_size(axis))])  47.2 us
    pallas_call x1, Pallas kernels, attend(): pl.pallas_call(attend_kernel, grid=(pairs, total // block), in_specs=[pl....  33.8 us
    pallas_call x1, Pallas kernels, attend_back(): pl.pallas_call(attend_back_kernel, grid=(total // block,), in_specs=[whol...  32 us
    all_gather x2, blocking collectives, first_stage(): small = lax.all_gather(lax.all_gather(packed, 'rows'), 'wide')  22.2 us
    all_to_all x1, blocking collectives, shards(): lax.all_to_all(regroup(w_qkv, wide_n), 'wide', 0, 0, tiled=True)  17.8 us
    convert_element_type x8, other arithmetic, add_low(): return (left.astype(F32) + right.astype(F32)).astype(BF)  17.1 us
  transfers between devices with their start and end apart: 62, of which 31 were waited for; matrix products, arithmetic and copies ran while one was open for 37% of the time, Pallas kernels for 17%

profile of v5, /device:TPU:0, one launch (start us, length us, event | category | flops | bytes accessed | tf_op | source)
XLA Modules:
  0.0 558.9 jit_solution(13830931647939932338)
XLA Ops:
  9.5 17.8 %all_to_all.10 = bf16[8,64,768]{2,1,0:T(8,128)(2,1)} all-to-all(bf16[8,64,768]{2,1,0:T(8,128)(2,1)S(1)} %regroup.1), channel_id=1, replica_groups=mesh['rows'=4,'wide'=8] {'wide'}, dimensions={0} | all-to-all | bytes 1572864 | tf_op jit(solution)/shard_map/all_to_all | solution.py:656
  30.3 46.1 %conditional.7 = (bf16[768,2048]{1,0:T(8,128)(2,1)}, bf16[768,2048]{1,0:T(8,128)(2,1)}, f32[1,768]{1,0:T(1,128)S(1)}, f32[1,2048]{1,0:T(1,128)S(1)}, f32[1,2048]...) conditional(s32[]{:T(128)} %bitcast.31, () %tuple.83, ...), branch_computations={%region_0.0_spmd, %region_1.3_spmd} | conditional | flops 7882702 | bytes 32684328 | solution.py:639
  31.6 13.2 %all-gather.2 = bf16[4,1,640]{2,1,0:T(2,128)(2,1)S(1)} all-gather(bf16[1,1,640]{2,1,0:T(2,128)(2,1)S(1)} %reshape.238), channel_id=2, replica_groups=mesh['rows'=4,'wide'=8] {'rows'}, dimensions={0}, use_global_device_ids=true | all-gather | bytes 6400 | tf_op jit(solution)/shard_map/cond/branch_1_fun/all_gather | solution.py:670
  44.8 9.1 %all-gather.3 = bf16[8,4,640]{2,1,0:T(4,128)(2,1)S(1)} all-gather(bf16[1,4,640]{2,1,0:T(4,128)(2,1)S(1)} %bitcast.160), channel_id=3, replica_groups=mesh['rows'=4,'wide'=8] {'wide'}, dimensions={0}, use_global_device_ids=true | all-gather | bytes 46080 | tf_op jit(solution)/shard_map/cond/branch_1_fun/all_gather | solution.py:670
  63.3 4.0 collective-permute-done.6
  72.4 2.9 fusion.27
  80.9 16.0 %all-gather.13.cloned.1.call-start = ((), (), s32[]{:S(2)}) async-start(), calls=%async_computation.8 | async-start | bytes 3932160 | tf_op jit(solution)/shard_map/all_gather | solution.py:664
  100.6 4.4 all-gather.11.cloned.1.call-done.weight
  105.0 15.5 %project.1 = (bf16[1536,2048]{1,0:T(8,128)(2,1)}, bf16[1536,256]{1,0:T(8,128)(2,1)S(1)}, bf16[1536,256]{1,0:T(8,128)(2,1)S(1)}, bf16[1536,256]{1,0:T(8,128)(2,1)S(1)}, f32[1536,128]{1,0:T(8,128)}) custom-call(s32[8]{0:T(128)S(1)} %stack.65.order, bf16[768,2048]{1,0:T(8,128)(2,1)} %get-tuple-element.289.own_ref, ...), custom_call_target="tpu_custom_call" | custom-call | flops 16999999488 | bytes 1 | tf_op jit(solution)/shard_map/project/pallas_call | solution.py:229
  120.5 33.8 %attend.1 = (bf16[1536,256]{1,0:T(8,128)(2,1)S(1)}, f32[2,2,1536]{2,1,0:T(2,128)}) custom-call(s32[1,1536]{1,0:T(1,128)S(1)} %get-tuple-element.298.first, bf16[1536,256]{1,0:T(8,128)(2,1)S(1)} %get-tuple-element.301.q_ref, bf16[1536,256]{1,0:T(8,128)(2,1)S(1)} %get-tuple-element.302.k_ref, bf16[1536,256]{1,0:T(8,128)(2,1)S(1)} %get-tuple-element.303.v_ref), custom_call_target="tpu_custom_call" | custom-call | flops 38999998464 | bytes 1 | tf_op jit(solution)/shard_map/attend/pallas_call | solution.py:385
  156.4 2.3 copy.90
  162.3 3.2 add_convert_fusion.9
  171.0 6.7 %collective-permute-done.40 = bf16[96,2048]{1,0:T(8,128)(2,1)S(1)} collective-permute-done((bf16[96,2048]{1,0:T(8,128)(2,1)S(1)}, bf16[96,2048]{1,0:T(8,128)(2,1)S(1)}, u32[]{:S(2)}, u32[]{:S(2)}) %collective-permute-start.40) | collective-permute-done | bytes 393248 | tf_op jit(solution)/shard_map/ppermute | solution.py:30
  180.2 5.5 collective-permute-done.39
  185.7 4.2 collective-permute-done.41
  191.8 5.5 collective-permute-done.42
  206.6 12.1 %collective-permute-done.46 = bf16[192,2048]{1,0:T(8,128)(2,1)S(1)} collective-permute-done((bf16[192,2048]{1,0:T(8,128)(2,1)S(1)}, bf16[192,2048]{1,0:T(8,128)(2,1)S(1)}, u32[]{:S(2)}, u32[]{:S(2)}) %collective-permute-start.46) | collective-permute-done | bytes 786464 | tf_op jit(solution)/shard_map/ppermute | solution.py:30
  224.4 4.1 collective-permute-done.47
  230.9 35.4 %conditional.8 = (bf16[768,2048]{1,0:T(8,128)(2,1)}, f32[1408,768]{1,0:T(8,128)}, f32[1408,768]{1,0:T(8,128)}, bf16[704,768]{1,0:T(8,128)(2,1)}, bf16[704,768]{1,0:T(8,128)(2,1)}, /*index=5*/bf16[2048,704]{0,1:T(8,128)(2,1)}) conditional(s32[]{:T(128)} %bitcast.31, () %tuple.94, (bf16[768,2048]{1,0:T(8,128)(2,1)}, bf16[2048,1408]{1,0:T(8,128)(2,1)}, ...), branch_computations={%region_5.6_spmd, %region_6.7_spmd} | conditional | flops 13299810304 | bytes 103153824 | solution.py:639
  230.9 10.6 %fusion.49 = f32[1408,768]{1,0:T(8,128)} fusion(bf16[2048,1408]{1,0:T(8,128)(2,1)} %get-tuple-element.143, bf16[768,2048]{1,0:T(8,128)(2,1)} %get-tuple-element.142), kind=kOutput, calls=%fused_computation.198 | convolution fusion | flops 4429185024 | bytes 13238272 | tf_op jit(solution)/shard_map/cond/branch_1_fun/dot_general | solution.py:26
  241.5 4.0 fusion.2
  245.5 8.9 %fusion.50 = f32[1408,768]{1,0:T(8,128)} fusion(bf16[2048,1408]{1,0:T(8,128)(2,1)S(1)} %copy-done.51, bf16[768,2048]{1,0:T(8,128)(2,1)} %collective-permute-done.21), kind=kOutput, calls=%fused_computation.199 | convolution fusion | flops 4429185024 | bytes 13238272 | tf_op jit(solution)/shard_map/cond/branch_1_fun/dot_general | solution.py:26
  254.4 3.9 fusion.1
  258.3 7.6 %fusion = bf16[2048,704]{0,1:T(8,128)(2,1)} fusion(bf16[1536,2048]{1,0:T(8,128)(2,1)S(1)} %bitcast.155, bf16[704,768]{1,0:T(8,128)(2,1)} %fusion.1, bf16[704,768]{1,0:T(8,128)(2,1)} %fusion.2), kind=kOutput, calls=%fused_computation.1 | convolution fusion | flops 4434952192 | bytes 11337728 | tf_op jit(solution)/shard_map/cond/branch_1_fun/dot_general | solution.py:26
  266.3 4.6 copy.93
  271.0 5.4 all-gather.13.cloned.1.call-done
  276.3 42.4 %conditional.9 = (bf16[768,2048]{1,0:T(8,128)(2,1)}, bf16[1408,2048]{1,0:T(8,128)(2,1)}) conditional(s32[]{:T(128)} %bitcast.31, () %tuple.93, (bf16[2048,704]{1,0:T(8,128)(2,1)}, bf16[768,2048]{1,0:T(8,128)(2,1)}, f32[1408,768]{1,0:T(8,128)}, bf16[2048,1408]{1,0:T(8,128)(2,1)}, bf16[768,2048]{1,0:T(8,128)(2,1)}, /*index=5*/f32[1408,768]{1,0:T(8,128)}, ...), branch_computations={%region_7.8_spmd, %region_8.9_spmd} | conditional | flops 22210838528 | bytes 158728528 | solution.py:639
  276.3 7.5 %multiply_convert_fusion.1 = (bf16[704,768]{1,0:T(8,128)(2,1)S(1)}, bf16[704,768]{1,0:T(8,128)(2,1)S(1)}) fusion(f32[1408,768]{1,0:T(8,128)} %get-tuple-element.150, bf16[2048,704]{1,0:T(8,128)(2,1)} %get-tuple-element.145, bf16[768,2048]{1,0:T(8,128)(2,1)} %get-tuple-element.149), kind=kOutput, calls=%fused_computation.31 | convolution fusion | flops 2221621248 | bytes 12517376 | tf_op jit(solution)/shard_map/cond/branch_1_fun/dot_general | solution.py:26
  283.9 6.7 %convolution_convert_fusion.2 = bf16[768,2048]{1,0:T(8,128)(2,1)} fusion(bf16[2048,1408]{1,0:T(8,128)(2,1)S(1)} %copy-done.52, bf16[704,768]{1,0:T(8,128)(2,1)S(1)} %get-tuple-element.444, bf16[704,768]{1,0:T(8,128)(2,1)S(1)} %get-tuple-element.443), kind=kOutput, calls=%fused_computation.22 | convolution fusion | flops 4435083264 | bytes 11075584 | tf_op jit(solution)/shard_map/cond/branch_1_fun/dot_general | solution.py:26
  290.6 5.6 multiply_convert_fusion.3
  296.3 5.4 convolution_convert_fusion.3
  301.7 13.6 %convolution_convert_fusion.1 = bf16[1408,2048]{1,0:T(8,128)(2,1)} fusion(bf16[768,2048]{1,0:T(8,128)(2,1)} %get-tuple-element.152, bf16[768,2048]{1,0:T(8,128)(2,1)} %get-tuple-element.151, bf16[704,768]{1,0:T(8,128)(2,1)S(1)} %copy-done.59, bf16[704,768]{1,0:T(8,128)(2,1)S(1)} %copy-done.57, bf16[704,768]{1,0:T(8,128)(2,1)} %copy-done.61, ...), kind=kOutput, calls=%fused_computation.10 | convolution fusion | flops 8891138048 | bytes 16384000 | tf_op jit(solution)/shard_map/cond/branch_1_fun/dot_general | solution.py:26
  315.3 3.0 add_convert_fusion
  318.8 43.2 %conditional.10 = (f32[192,2048]{1,0:T(8,128)S(1)}, f32[2048]{0:T(1024)S(1)}, f32[2048]{0:T(1024)}, bf16[768,2048]{1,0:T(8,128)(2,1)}, bf16[192,2048]{1,0:T(8,128)(2,1)}) conditional(s32[]{:T(128)} %bitcast.31, () %tuple.89, (bf16[192,2048]{1,0:T(8,128)(2,1)}, f32[192]{0:T(256)}, bf16[768,2048]{1,0:T(8,128)(2,1)}, f32[1,2048]{1,0:T(1,128)S(1)}, ...), branch_computations={%region_9.10_spmd, %region_10.16_spmd} | conditional | flops 4448842240 | bytes 79310488 | solution.py:639
  324.1 4.2 convolution_convert_fusion.4
  328.3 4.1 collective-permute-done.24
  335.7 4.8 collective-permute-done.23
  340.4 5.2 collective-permute-done.25
  348.9 4.2 convolution_convert_fusion.5
  359.0 3.1 add_convert_fusion.1
  362.1 28.8 %conditional.11 = (bf16[768,2048]{1,0:T(8,128)(2,1)}, f32[512,704]{0,1:T(8,128)}) conditional(s32[]{:T(128)} %bitcast.31, () %tuple.88, (bf16[192,2048]{1,0:T(8,128)(2,1)}, bf16[512,704]{1,0:T(8,128)(2,1)}) %tuple.98), branch_computations={%region_17.18_spmd, %region_18.19_spmd} | conditional | bytes 19464368 | solution.py:639
  365.1 2.5 copy.97
  369.7 8.9 %collective-permute-done.1 = bf16[192,2048]{1,0:T(8,128)(2,1)S(1)} collective-permute-done((bf16[192,2048]{1,0:T(8,128)(2,1)}, bf16[192,2048]{1,0:T(8,128)(2,1)S(1)}, u32[]{:S(2)}, u32[]{:S(2)}) %collective-permute-start.1) | collective-permute-done | bytes 786464 | tf_op jit(solution)/shard_map/cond/branch_1_fun/ppermute | solution.py:30
  384.5 2.6 collective-permute-done.2
  390.9 4.3 fusion.34
  395.3 3.7 convolution_convert_fusion.10
  398.9 51.1 %conditional.12 = (bf16[1536,768]{1,0:T(8,128)(2,1)}, bf16[2048,768]{0,1:T(8,128)(2,1)}, bf16[96,2048]{1,0:T(8,128)(2,1)}, bf16[96,2048]{1,0:T(8,128)(2,1)}, bf1...) conditional(s32[]{:T(128)} %bitcast.31, () %tuple.87, (bf16[768,2048]{1,0:T(8,128)(2,1)}, ...), branch_computations={%region_19.20_spmd, %region_20.21_spmd} | conditional | flops 49640488960 | bytes 30540804 | solution.py:639
  399.1 2.4 fusion.44
  405.5 3.0 convolution_convert_fusion.7
  408.8 32.0 %attend_back.1 = bf16[1536,768]{1,0:T(8,128)(2,1)} custom-call(s32[1,1536]{1,0:T(1,128)S(1)} %get-tuple-element.163.first, bf16[1536,256]{1,0:T(8,128)(2,1)} %get-tuple-element.164.q_ref, bf16[1536,256]{1,0:T(8,128)(2,1)} %get-tuple-element.165.k_ref, bf16[1536,256]{1,0:T(8,128)(2,1)} %get-tuple-element.166.v_ref, ...), custom_call_target="tpu_custom_call" | custom-call | flops 44000002048 | bytes 1 | tf_op jit(solution)/shard_map/cond/branch_1_fun/attend_back/pallas_call | solution.py:507
  440.8 9.2 %fusion.26 = bf16[2048,768]{0,1:T(8,128)(2,1)} fusion(bf16[1536,768]{1,0:T(8,128)(2,1)} %attend_back.1, bf16[1536,2048]{1,0:T(8,128)(2,1)} %get-tuple-element.175), kind=kOutput, calls=%fused_computation.60 | convolution fusion | flops 4833411072 | bytes 11796480 | tf_op jit(solution)/shard_map/cond/branch_1_fun/dot_general | solution.py:26
  451.1 4.6 fusion.33
  455.8 74.6 %conditional.13 = (f32[1,192,2048]{2,1,0:T(8,128)}, f32[4,448]{1,0:T(4,128)}, bf16[1,192,2048]{2,1,0:T(8,128)(2,1)}) conditional(s32[]{:T(128)} %bitcast.31, () %tuple.82, (f32[1536,128]{1,0:T(8,128)}, bf16[1536,768]{1,0:T(8,128)(2,1)}, bf16[768,2048]{1,0:T(8,128)(2,1)}, bf16[2048,768]{1,0:T(8,128)(2,1)}, bf16[768,2048]{1,0:T(8,128)(2,1)}, ...), branch_computations={%region_22.23_spmd, %region_23.26_spmd} | conditional | flops 14021644288 | bytes 79257176 | solution.py:639
  455.9 7.4 %unproject.3 = (bf16[768,2048]{1,0:T(8,128)(2,1)S(1)}, f32[1,2048]{1,0:T(1,128)S(1)}, f32[1,2048]{1,0:T(1,128)S(1)}, f32[1,768]{1,0:T(1,128)S(1)}) custom-call(s32[4]{0:T(128)S(1)} %get-tuple-element.473.order, bf16[1536,768]{1,0:T(8,128)(2,1)} %get-tuple-element.179.g_ref, bf16[768,2048]{1,0:T(8,128)(2,1)} %get-tuple-element.183.x_ref, ...), custom_call_target="tpu_custom_call" | custom-call | flops 7000000000 | bytes 1 | tf_op jit(solution)/shard_map/cond/branch_1_fun/unproject/pallas_call | solution.py:293
  463.4 7.4 %unproject.2 = (bf16[768,2048]{1,0:T(8,128)(2,1)S(1)}, f32[1,2048]{1,0:T(1,128)S(1)}, f32[1,2048]{1,0:T(1,128)S(1)}, f32[1,768]{1,0:T(1,128)S(1)}) custom-call(s32[4]{0:T(128)S(1)} %get-tuple-element.472.order, bf16[1536,768]{1,0:T(8,128)(2,1)} %get-tuple-element.179.g_ref, bf16[768,2048]{1,0:T(8,128)(2,1)} %get-tuple-element.180.x_ref, ...), custom_call_target="tpu_custom_call" | custom-call | flops 7000000000 | bytes 1 | tf_op jit(solution)/shard_map/cond/branch_1_fun/unproject/pallas_call | solution.py:293
  480.0 7.3 %collective-permute-done.10 = bf16[96,2048]{1,0:T(8,128)(2,1)} collective-permute-done((bf16[96,2048]{1,0:T(8,128)(2,1)}, bf16[96,2048]{1,0:T(8,128)(2,1)}, u32[]{:S(2)}, u32[]{:S(2)}) %collective-permute-start.10) | collective-permute-done | bytes 393248 | tf_op jit(solution)/shard_map/cond/branch_1_fun/ppermute | solution.py:30
  488.9 6.6 %collective-permute-done.12 = bf16[96,2048]{1,0:T(8,128)(2,1)} collective-permute-done((bf16[96,2048]{1,0:T(8,128)(2,1)}, bf16[96,2048]{1,0:T(8,128)(2,1)}, u32[]{:S(2)}, u32[]{:S(2)}) %collective-permute-start.12) | collective-permute-done | bytes 393248 | tf_op jit(solution)/shard_map/cond/branch_1_fun/ppermute | solution.py:30
  498.0 2.4 add_convert_fusion.5
  507.4 2.5 add_convert_fusion.8
  517.3 2.4 collective-permute-done.14
  527.5 2.9 add_bitcast_fusion
  532.1 2.3 copy.94
  534.4 3.5 all-to-all-start.1
  543.7 6.7 %all-to-all-done.1 = bf16[8,64,768]{2,1,0:T(8,128)(2,1)S(1)} async-done(((bf16[8,64,768]{2,1,0:T(8,128)(2,1)}), bf16[8,64,768]{2,1,0:T(8,128)(2,1)S(1)}, u32[]{:S(2)}, u32[]{:S(2)}) %all-to-all-start.1) | async-done | bytes 786464 | tf_op jit(solution)/shard_map/all_to_all | solution.py:907
  (378 shorter events, 144.6 us)
Async XLA Ops:
  7.2 93.4 %all-gather.9.cloned.1.call-start = ((), (), s32[]{:S(2)}) async-start(), calls=%async_computation.6 | async-start | bytes 1310720 | tf_op jit(solution)/shard_map/all_gather | solution.py:646
  7.9 97.0 %all-gather.11.cloned.1.call-start = ((), (), s32[]{:S(2)}) async-start(), calls=%async_computation.7 | async-start | bytes 3932160 | tf_op jit(solution)/shard_map/all_gather | solution.py:659
  27.3 203.6 %all-gather.15.cloned.1.call-start = ((), (), s32[]{:S(2)}) async-start(), calls=%async_computation.9 | async-start | bytes 7208960 | tf_op jit(solution)/shard_map/all_gather | solution.py:661
  30.3 47.0 %copy-start.7 = (bf16[1,192,2048]{2,1,0:T(8,128)(2,1)S(1)}, bf16[1,192,2048]{2,1,0:T(8,128)(2,1)}, u32[]{:S(2)}) copy-start(bf16[1,192,2048]{2,1,0:T(8,128)(2,1)} %param.39) | copy-start | bytes 2359300
  30.3 24.5 %collective-permute-start.4 = (bf16[192,2048]{1,0:T(8,128)(2,1)S(1)}, bf16[192,2048]{1,0:T(8,128)(2,1)}, u32[]{:S(2)}, u32[]{:S(2)}) collective-permute-start(bf16[192,2048]{1,0:T(8,128)(2,1)S(1)} %get-tuple-element.131), channel_id=1, source_target_pairs={{0,2},{1,3},{2,0},{3,1},{4,6},{5,7},{6,4},{7,5},{8,10},{9,11},{10,... | collective-permute-start | bytes 2359304 | tf_op jit(solution)/shard_map/cond/branch_1_fun/ppermute | solution.py:30
  30.9 23.9 %collective-permute-start.5 = (bf16[192,2048]{1,0:T(8,128)(2,1)S(1)}, bf16[192,2048]{1,0:T(8,128)(2,1)}, u32[]{:S(2)}, u32[]{:S(2)}) collective-permute-start(bf16[192,2048]{1,0:T(8,128)(2,1)S(1)} %get-tuple-element.131), channel_id=1, source_target_pairs={{0,4},{1,5},{2,6},{3,7},{4,0},{5,1},{6,2},{7,3},{8,12},{9,13},{10,... | collective-permute-start | bytes 2359304 | tf_op jit(solution)/shard_map/cond/branch_1_fun/ppermute | solution.py:30
  55.9 11.4 %collective-permute-start.6 = (bf16[96,2048]{1,0:T(8,128)(2,1)S(1)}, bf16[96,2048]{1,0:T(8,128)(2,1)S(1)}, u32[]{:S(2)}, u32[]{:S(2)}) collective-permute-start(bf16[96,2048]{1,0:T(8,128)(2,1)S(1)} %slice.146), channel_id=1, source_target_pairs={{0,2},{1,3},{2,0},{3,1},{4,6},{5,7},{6,4},{7,5},{8,10},{9,11},{10,... | collective-permute-start | bytes 1179656 | tf_op jit(solution)/shard_map/cond/branch_1_fun/ppermute | solution.py:30
  58.4 11.1 %collective-permute-start.7 = (bf16[96,2048]{1,0:T(8,128)(2,1)S(1)}, bf16[96,2048]{1,0:T(8,128)(2,1)S(1)}, u32[]{:S(2)}, u32[]{:S(2)}) collective-permute-start(bf16[96,2048]{1,0:T(8,128)(2,1)S(1)} %slice.147), channel_id=1, source_target_pairs={{0,4},{1,5},{2,6},{3,7},{4,0},{5,1},{6,2},{7,3},{8,12},{9,13},{10,... | collective-permute-start | bytes 1179656 | tf_op jit(solution)/shard_map/cond/branch_1_fun/ppermute | solution.py:30
  70.4 6.0 %collective-permute-start.8 = (bf16[768,2048]{1,0:T(8,128)(2,1)}, bf16[768,2048]{1,0:T(8,128)(2,1)}, u32[]{:S(2)}, u32[]{:S(2)}) collective-permute-start(bf16[768,2048]{1,0:T(8,128)(2,1)} %constant_dynamic-update-slice_fusion.5), channel_id=1, source_target_pairs={{0,1},{1,0},{2,3},{3,2},{4,5},{5,4},{6,7},{7,6},{8,9},{9,8},{10,11... | collective-permute-start | bytes 9437192 | tf_op jit(solution)/shard_map/cond/branch_1_fun/ppermute | solution.py:30
  76.4 44.1 %copy-start.44 = (s32[1,1536]{1,0:T(1,128)}, s32[1,1536]{1,0:T(1,128)S(1)}, u32[]{:S(2)}) copy-start(s32[1,1536]{1,0:T(1,128)S(1)} %get-tuple-element.298.first) | copy-start | bytes 18436
  77.3 21.4 %collective-permute-start.34 = (bf16[192,2048]{1,0:T(8,128)(2,1)S(1)}, bf16[192,2048]{1,0:T(8,128)(2,1)}, u32[]{:S(2)}, u32[]{:S(2)}) collective-permute-start(bf16[192,2048]{1,0:T(8,128)(2,1)S(1)} %bitcast.143), channel_id=1, source_target_pairs={{0,2},{1,3},{2,0},{3,1},{4,6},{5,7},{6,4},{7,5},{8,10},{9,11},{10,... | collective-permute-start | bytes 2359304 | tf_op jit(solution)/shard_map/ppermute | solution.py:30
  77.8 19.5 %collective-permute-start.35 = (bf16[192,2048]{1,0:T(8,128)(2,1)S(1)}, bf16[192,2048]{1,0:T(8,128)(2,1)S(1)}, u32[]{:S(2)}, u32[]{:S(2)}) collective-permute-start(bf16[192,2048]{1,0:T(8,128)(2,1)S(1)} %bitcast.144), channel_id=1, source_target_pairs={{0,4},{1,5},{2,6},{3,7},{4,0},{5,1},{6,2},{7,3},{8,12},{9,13},{10,... | collective-permute-start | bytes 2359304 | tf_op jit(solution)/shard_map/ppermute | solution.py:30
  80.9 195.5 %all-gather.13.cloned.1.call-start = ((), (), s32[]{:S(2)}) async-start(), calls=%async_computation.8 | async-start | bytes 3932160 | tf_op jit(solution)/shard_map/all_gather | solution.py:664
  97.4 56.9 %collective-permute-start.36 = (bf16[96,2048]{1,0:T(8,128)(2,1)S(1)}, bf16[96,2048]{1,0:T(8,128)(2,1)S(1)}, u32[]{:S(2)}, u32[]{:S(2)}) collective-permute-start(bf16[96,2048]{1,0:T(8,128)(2,1)S(1)} %slice.259), channel_id=1, source_target_pairs={{0,2},{1,3},{2,0},{3,1},{4,6},{5,7},{6,4},{7,5},{8,10},{9,11},{10,... | collective-permute-start | bytes 1179656 | tf_op jit(solution)/shard_map/ppermute | solution.py:30
  99.7 54.6 %collective-permute-start.37 = (bf16[96,2048]{1,0:T(8,128)(2,1)S(1)}, bf16[96,2048]{1,0:T(8,128)(2,1)S(1)}, u32[]{:S(2)}, u32[]{:S(2)}) collective-permute-start(bf16[96,2048]{1,0:T(8,128)(2,1)S(1)} %slice.260), channel_id=1, source_target_pairs={{0,4},{1,5},{2,6},{3,7},{4,0},{5,1},{6,2},{7,3},{8,12},{9,13},{10,... | collective-permute-start | bytes 1179656 | tf_op jit(solution)/shard_map/ppermute | solution.py:30
  156.3 6.0 %collective-permute-start.38 = (bf16[768,2048]{1,0:T(8,128)(2,1)S(1)}, bf16[768,2048]{1,0:T(8,128)(2,1)}, u32[]{:S(2)}, u32[]{:S(2)}) collective-permute-start(bf16[768,2048]{1,0:T(8,128)(2,1)S(1)} %convolution_convert_fusion.8), channel_id=1, source_target_pairs={{0,1},{1,0},{2,3},{3,2},{4,5},{5,4},{6,7},{7,6},{8,9},{9,8},{10,11... | collective-permute-start | bytes 9437192 | tf_op jit(solution)/shard_map/ppermute | solution.py:30
  158.7 203.4 %reduce-scatter.5.cloned.1.call-start = ((), (), s32[]{:S(2)}) async-start(), calls=%async_computation.10 | async-start | bytes 3932160 | tf_op jit(solution)/shard_map/reduce_scatter | solution.py:642
  165.7 12.0 %collective-permute-start.40 = (bf16[96,2048]{1,0:T(8,128)(2,1)S(1)}, bf16[96,2048]{1,0:T(8,128)(2,1)S(1)}, u32[]{:S(2)}, u32[]{:S(2)}) collective-permute-start(bf16[96,2048]{1,0:T(8,128)(2,1)S(1)} %get-tuple-element.486), channel_id=1, source_target_pairs={{0,2},{1,3},{2,0},{3,1},{4,6},{5,7},{6,4},{7,5},{8,10},{9,11},{10,... | collective-permute-start | bytes 1179656 | tf_op jit(solution)/shard_map/ppermute | solution.py:30
  168.8 16.9 %collective-permute-start.39 = (bf16[96,2048]{1,0:T(8,128)(2,1)S(1)}, bf16[96,2048]{1,0:T(8,128)(2,1)S(1)}, u32[]{:S(2)}, u32[]{:S(2)}) collective-permute-start(bf16[96,2048]{1,0:T(8,128)(2,1)S(1)} %get-tuple-element.483), channel_id=1, source_target_pairs={{0,2},{1,3},{2,0},{3,1},{4,6},{5,7},{6,4},{7,5},{8,10},{9,11},{10,... | collective-permute-start | bytes 1179656 | tf_op jit(solution)/shard_map/ppermute | solution.py:30
  169.4 16.3 %collective-permute-start.43 = (bf16[96,2048]{1,0:T(8,128)(2,1)S(1)}, bf16[96,2048]{1,0:T(8,128)(2,1)S(1)}, u32[]{:S(2)}, u32[]{:S(2)}) collective-permute-start(bf16[96,2048]{1,0:T(8,128)(2,1)S(1)} %get-tuple-element.484), channel_id=1, source_target_pairs={{0,4},{1,5},{2,6},{3,7},{4,0},{5,1},{6,2},{7,3},{8,12},{9,13},{10,... | collective-permute-start | bytes 1179656 | tf_op jit(solution)/shard_map/ppermute | solution.py:30
  177.8 12.1 %collective-permute-start.41 = (bf16[96,2048]{1,0:T(8,128)(2,1)S(1)}, bf16[96,2048]{1,0:T(8,128)(2,1)S(1)}, u32[]{:S(2)}, u32[]{:S(2)}) collective-permute-start(bf16[96,2048]{1,0:T(8,128)(2,1)S(1)} %add_convert_fusion.12), channel_id=1, source_target_pairs={{0,4},{1,5},{2,6},{3,7},{4,0},{5,1},{6,2},{7,3},{8,12},{9,13},{10,... | collective-permute-start | bytes 1179656 | tf_op jit(solution)/shard_map/ppermute | solution.py:30
  179.6 25.4 %collective-permute-start.49 = (bf16[768,2048]{1,0:T(8,128)(2,1)S(1)}, bf16[768,2048]{1,0:T(8,128)(2,1)S(1)}, u32[]{:S(2)}, u32[]{:S(2)}) collective-permute-start(bf16[768,2048]{1,0:T(8,128)(2,1)S(1)} %get-tuple-element.504), channel_id=1, source_target_pairs={{0,1},{1,0},{2,3},{3,2},{4,5},{5,4},{6,7},{7,6},{8,9},{9,8},{10,11... | collective-permute-start | bytes 9437192 | tf_op jit(solution)/shard_map/ppermute | solution.py:30
  179.7 17.5 %collective-permute-start.42 = (bf16[96,2048]{1,0:T(8,128)(2,1)S(1)}, bf16[96,2048]{1,0:T(8,128)(2,1)S(1)}, u32[]{:S(2)}, u32[]{:S(2)}) collective-permute-start(bf16[96,2048]{1,0:T(8,128)(2,1)S(1)} %get-tuple-element.485), channel_id=1, source_target_pairs={{0,4},{1,5},{2,6},{3,7},{4,0},{5,1},{6,2},{7,3},{8,12},{9,13},{10,... | collective-permute-start | bytes 1179656 | tf_op jit(solution)/shard_map/ppermute | solution.py:30
  190.2 9.1 %collective-permute-start.44 = (bf16[96,2048]{1,0:T(8,128)(2,1)S(1)}, bf16[96,2048]{1,0:T(8,128)(2,1)S(1)}, u32[]{:S(2)}, u32[]{:S(2)}) collective-permute-start(bf16[96,2048]{1,0:T(8,128)(2,1)S(1)} %get-tuple-element.482), channel_id=1, source_target_pairs={{0,2},{1,3},{2,0},{3,1},{4,6},{5,7},{6,4},{7,5},{8,10},{9,11},{10,... | collective-permute-start | bytes 1179656 | tf_op jit(solution)/shard_map/ppermute | solution.py:30
  202.1 16.7 %collective-permute-start.46 = (bf16[192,2048]{1,0:T(8,128)(2,1)S(1)}, bf16[192,2048]{1,0:T(8,128)(2,1)S(1)}, u32[]{:S(2)}, u32[]{:S(2)}) collective-permute-start(bf16[192,2048]{1,0:T(8,128)(2,1)S(1)} %get-tuple-element.437), channel_id=1, source_target_pairs={{0,4},{1,5},{2,6},{3,7},{4,0},{5,1},{6,2},{7,3},{8,12},{9,13},{10,... | collective-permute-start | bytes 2359304 | tf_op jit(solution)/shard_map/ppermute | solution.py:30
  203.6 18.6 %collective-permute-start.45 = (bf16[192,2048]{1,0:T(8,128)(2,1)S(1)}, bf16[192,2048]{1,0:T(8,128)(2,1)S(1)}, u32[]{:S(2)}, u32[]{:S(2)}) collective-permute-start(bf16[192,2048]{1,0:T(8,128)(2,1)S(1)} %get-tuple-element.437), channel_id=1, source_target_pairs={{0,2},{1,3},{2,0},{3,1},{4,6},{5,7},{6,4},{7,5},{8,10},{9,11},{10,... | collective-permute-start | bytes 2359304 | tf_op jit(solution)/shard_map/ppermute | solution.py:30
  218.7 9.7 %collective-permute-start.47 = (bf16[96,2048]{1,0:T(8,128)(2,1)S(1)}, bf16[96,2048]{1,0:T(8,128)(2,1)S(1)}, u32[]{:S(2)}, u32[]{:S(2)}) collective-permute-start(bf16[96,2048]{1,0:T(8,128)(2,1)S(1)} %slice.269), channel_id=1, source_target_pairs={{0,2},{1,3},{2,0},{3,1},{4,6},{5,7},{6,4},{7,5},{8,10},{9,11},{10,... | collective-permute-start | bytes 1179656 | tf_op jit(solution)/shard_map/ppermute | solution.py:30
  222.3 7.8 %collective-permute-start.48 = (bf16[96,2048]{1,0:T(8,128)(2,1)S(1)}, bf16[96,2048]{1,0:T(8,128)(2,1)S(1)}, u32[]{:S(2)}, u32[]{:S(2)}) collective-permute-start(bf16[96,2048]{1,0:T(8,128)(2,1)S(1)} %slice.270), channel_id=1, source_target_pairs={{0,4},{1,5},{2,6},{3,7},{4,0},{5,1},{6,2},{7,3},{8,12},{9,13},{10,... | collective-permute-start | bytes 1179656 | tf_op jit(solution)/shard_map/ppermute | solution.py:30
  230.9 14.6 %collective-permute-start.21 = (bf16[768,2048]{1,0:T(8,128)(2,1)}, bf16[768,2048]{1,0:T(8,128)(2,1)}, u32[]{:S(2)}, u32[]{:S(2)}) collective-permute-start(bf16[768,2048]{1,0:T(8,128)(2,1)} %get-tuple-element.142), channel_id=1, source_target_pairs={{0,1},{1,0},{2,3},{3,2},{4,5},{5,4},{6,7},{7,6},{8,9},{9,8},{10,11... | collective-permute-start | bytes 9437192 | tf_op jit(solution)/shard_map/cond/branch_1_fun/ppermute | solution.py:30
  270.9 179.2 %reduce-scatter.7.cloned.1.call-start = ((), (), s32[]{:S(2)}) async-start(), calls=%async_computation.11 | async-start | bytes 7208960 | tf_op jit(solution)/shard_map/reduce_scatter | solution.py:642
  290.6 24.7 %collective-permute-start.22 = (bf16[768,2048]{1,0:T(8,128)(2,1)}, bf16[768,2048]{1,0:T(8,128)(2,1)S(1)}, u32[]{:S(2)}, u32[]{:S(2)}) collective-permute-start(bf16[768,2048]{1,0:T(8,128)(2,1)} %convolution_convert_fusion.2), channel_id=1, source_target_pairs={{0,1},{1,0},{2,3},{3,2},{4,5},{5,4},{6,7},{7,6},{8,9},{9,8},{10,11... | collective-permute-start | bytes 9437192 | tf_op jit(solution)/shard_map/cond/branch_1_fun/ppermute | solution.py:30
  318.8 211.6 %reduce-scatter.9.cloned.1.call-start = ((), (), s32[]{:S(2)}) async-start(), calls=%async_computation.12 | async-start | bytes 3932160 | tf_op jit(solution)/shard_map/reduce_scatter | solution.py:642
  320.5 12.0 %collective-permute-start.24 = (bf16[96,2048]{1,0:T(8,128)(2,1)S(1)}, bf16[96,2048]{1,0:T(8,128)(2,1)S(1)}, u32[]{:S(2)}, u32[]{:S(2)}) collective-permute-start(bf16[96,2048]{1,0:T(8,128)(2,1)S(1)} %get-tuple-element.478), channel_id=1, source_target_pairs={{0,2},{1,3},{2,0},{3,1},{4,6},{5,7},{6,4},{7,5},{8,10},{9,11},{10,... | collective-permute-start | bytes 1179656 | tf_op jit(solution)/shard_map/cond/branch_1_fun/ppermute | solution.py:30
  322.0 18.4 %collective-permute-start.23 = (bf16[96,2048]{1,0:T(8,128)(2,1)S(1)}, bf16[96,2048]{1,0:T(8,128)(2,1)S(1)}, u32[]{:S(2)}, u32[]{:S(2)}) collective-permute-start(bf16[96,2048]{1,0:T(8,128)(2,1)S(1)} %get-tuple-element.475), channel_id=1, source_target_pairs={{0,2},{1,3},{2,0},{3,1},{4,6},{5,7},{6,4},{7,5},{8,10},{9,11},{10,... | collective-permute-start | bytes 1179656 | tf_op jit(solution)/shard_map/cond/branch_1_fun/ppermute | solution.py:30
  322.6 17.9 %collective-permute-start.27 = (bf16[96,2048]{1,0:T(8,128)(2,1)S(1)}, bf16[96,2048]{1,0:T(8,128)(2,1)S(1)}, u32[]{:S(2)}, u32[]{:S(2)}) collective-permute-start(bf16[96,2048]{1,0:T(8,128)(2,1)S(1)} %get-tuple-element.476), channel_id=1, source_target_pairs={{0,4},{1,5},{2,6},{3,7},{4,0},{5,1},{6,2},{7,3},{8,12},{9,13},{10,... | collective-permute-start | bytes 1179656 | tf_op jit(solution)/shard_map/cond/branch_1_fun/ppermute | solution.py:30
  328.3 30.7 %collective-permute-start.29 = (bf16[768,2048]{1,0:T(8,128)(2,1)S(1)}, bf16[768,2048]{1,0:T(8,128)(2,1)S(1)}, u32[]{:S(2)}, u32[]{:S(2)}) collective-permute-start(bf16[768,2048]{1,0:T(8,128)(2,1)S(1)} %convolution_convert_fusion.4), channel_id=1, source_target_pairs={{0,1},{1,0},{2,3},{3,2},{4,5},{5,4},{6,7},{7,6},{8,9},{9,8},{10,11... | collective-permute-start | bytes 9437192 | tf_op jit(solution)/shard_map/cond/branch_1_fun/ppermute | solution.py:30
  333.6 12.1 %collective-permute-start.25 = (bf16[96,2048]{1,0:T(8,128)(2,1)S(1)}, bf16[96,2048]{1,0:T(8,128)(2,1)S(1)}, u32[]{:S(2)}, u32[]{:S(2)}) collective-permute-start(bf16[96,2048]{1,0:T(8,128)(2,1)S(1)} %add_convert_fusion.3), channel_id=1, source_target_pairs={{0,4},{1,5},{2,6},{3,7},{4,0},{5,1},{6,2},{7,3},{8,12},{9,13},{10,... | collective-permute-start | bytes 1179656 | tf_op jit(solution)/shard_map/cond/branch_1_fun/ppermute | solution.py:30
  335.1 18.0 %collective-permute-start.26 = (bf16[96,2048]{1,0:T(8,128)(2,1)S(1)}, bf16[96,2048]{1,0:T(8,128)(2,1)S(1)}, u32[]{:S(2)}, u32[]{:S(2)}) collective-permute-start(bf16[96,2048]{1,0:T(8,128)(2,1)S(1)} %get-tuple-element.477), channel_id=1, source_target_pairs={{0,4},{1,5},{2,6},{3,7},{4,0},{5,1},{6,2},{7,3},{8,12},{9,13},{10,... | collective-permute-start | bytes 1179656 | tf_op jit(solution)/shard_map/cond/branch_1_fun/ppermute | solution.py:30
  347.3 7.8 %collective-permute-start.28 = (bf16[96,2048]{1,0:T(8,128)(2,1)S(1)}, bf16[96,2048]{1,0:T(8,128)(2,1)S(1)}, u32[]{:S(2)}, u32[]{:S(2)}) collective-permute-start(bf16[96,2048]{1,0:T(8,128)(2,1)S(1)} %get-tuple-element.474), channel_id=1, source_target_pairs={{0,2},{1,3},{2,0},{3,1},{4,6},{5,7},{6,4},{7,5},{8,10},{9,11},{10,... | collective-permute-start | bytes 1179656 | tf_op jit(solution)/shard_map/cond/branch_1_fun/ppermute | solution.py:30
  362.1 16.4 %collective-permute-start.1 = (bf16[192,2048]{1,0:T(8,128)(2,1)}, bf16[192,2048]{1,0:T(8,128)(2,1)S(1)}, u32[]{:S(2)}, u32[]{:S(2)}) collective-permute-start(bf16[192,2048]{1,0:T(8,128)(2,1)} %get-tuple-element.161), channel_id=1, source_target_pairs={{0,4},{1,5},{2,6},{3,7},{4,0},{5,1},{6,2},{7,3},{8,12},{9,13},{10,... | collective-permute-start | bytes 2359304 | tf_op jit(solution)/shard_map/cond/branch_1_fun/ppermute | solution.py:30
  363.6 18.6 %collective-permute-start = (bf16[192,2048]{1,0:T(8,128)(2,1)}, bf16[192,2048]{1,0:T(8,128)(2,1)S(1)}, u32[]{:S(2)}, u32[]{:S(2)}) collective-permute-start(bf16[192,2048]{1,0:T(8,128)(2,1)} %get-tuple-element.161), channel_id=1, source_target_pairs={{0,2},{1,3},{2,0},{3,1},{4,6},{5,7},{6,4},{7,5},{8,10},{9,11},{10,... | collective-permute-start | bytes 2359304 | tf_op jit(solution)/shard_map/cond/branch_1_fun/ppermute | solution.py:30
  378.6 8.6 %collective-permute-start.2 = (bf16[96,2048]{1,0:T(8,128)(2,1)S(1)}, bf16[96,2048]{1,0:T(8,128)(2,1)S(1)}, u32[]{:S(2)}, u32[]{:S(2)}) collective-permute-start(bf16[96,2048]{1,0:T(8,128)(2,1)S(1)} %slice.245), channel_id=1, source_target_pairs={{0,2},{1,3},{2,0},{3,1},{4,6},{5,7},{6,4},{7,5},{8,10},{9,11},{10,... | collective-permute-start | bytes 1179656 | tf_op jit(solution)/shard_map/cond/branch_1_fun/ppermute | solution.py:30
  382.2 7.8 %collective-permute-start.3 = (bf16[96,2048]{1,0:T(8,128)(2,1)S(1)}, bf16[96,2048]{1,0:T(8,128)(2,1)S(1)}, u32[]{:S(2)}, u32[]{:S(2)}) collective-permute-start(bf16[96,2048]{1,0:T(8,128)(2,1)S(1)} %slice.246), channel_id=1, source_target_pairs={{0,4},{1,5},{2,6},{3,7},{4,0},{5,1},{6,2},{7,3},{8,12},{9,13},{10,... | collective-permute-start | bytes 1179656 | tf_op jit(solution)/shard_map/cond/branch_1_fun/ppermute | solution.py:30
  390.9 8.0 %collective-permute-start.50 = (bf16[768,2048]{1,0:T(8,128)(2,1)}, bf16[768,2048]{1,0:T(8,128)(2,1)}, u32[]{:S(2)}, u32[]{:S(2)}) collective-permute-start(bf16[768,2048]{1,0:T(8,128)(2,1)} %get-tuple-element.316), channel_id=1, source_target_pairs={{0,1},{1,0},{2,3},{3,2},{4,5},{5,4},{6,7},{7,6},{8,9},{9,8},{10,11... | collective-permute-start | bytes 9437192 | tf_op jit(solution)/shard_map/ppermute | solution.py:30
  401.5 48.5 %collective-permute-start.30 = (bf16[96,2048]{1,0:T(8,128)(2,1)}, bf16[96,2048]{1,0:T(8,128)(2,1)}, u32[]{:S(2)}, u32[]{:S(2)}) collective-permute-start(bf16[96,2048]{1,0:T(8,128)(2,1)} %get-tuple-element.448), channel_id=1, source_target_pairs={{0,2},{1,3},{2,0},{3,1},{4,6},{5,7},{6,4},{7,5},{8,10},{9,11},{10,... | collective-permute-start | bytes 1179656 | tf_op jit(solution)/shard_map/cond/branch_1_fun/ppermute | solution.py:30
  403.0 47.1 %collective-permute-start.31 = (bf16[96,2048]{1,0:T(8,128)(2,1)}, bf16[96,2048]{1,0:T(8,128)(2,1)}, u32[]{:S(2)}, u32[]{:S(2)}) collective-permute-start(bf16[96,2048]{1,0:T(8,128)(2,1)} %get-tuple-element.447), channel_id=1, source_target_pairs={{0,4},{1,5},{2,6},{3,7},{4,0},{5,1},{6,2},{7,3},{8,12},{9,13},{10,... | collective-permute-start | bytes 1179656 | tf_op jit(solution)/shard_map/cond/branch_1_fun/ppermute | solution.py:30
  403.0 47.1 %collective-permute-start.32 = (bf16[96,2048]{1,0:T(8,128)(2,1)}, bf16[96,2048]{1,0:T(8,128)(2,1)}, u32[]{:S(2)}, u32[]{:S(2)}) collective-permute-start(bf16[96,2048]{1,0:T(8,128)(2,1)} %get-tuple-element.446), channel_id=1, source_target_pairs={{0,2},{1,3},{2,0},{3,1},{4,6},{5,7},{6,4},{7,5},{8,10},{9,11},{10,... | collective-permute-start | bytes 1179656 | tf_op jit(solution)/shard_map/cond/branch_1_fun/ppermute | solution.py:30
  403.8 46.2 %collective-permute-start.33 = (bf16[96,2048]{1,0:T(8,128)(2,1)S(1)}, bf16[96,2048]{1,0:T(8,128)(2,1)}, u32[]{:S(2)}, u32[]{:S(2)}) collective-permute-start(bf16[96,2048]{1,0:T(8,128)(2,1)S(1)} %get-tuple-element.445), channel_id=1, source_target_pairs={{0,4},{1,5},{2,6},{3,7},{4,0},{5,1},{6,2},{7,3},{8,12},{9,13},{10,... | collective-permute-start | bytes 1179656 | tf_op jit(solution)/shard_map/cond/branch_1_fun/ppermute | solution.py:30
  450.2 90.6 %reduce-scatter.11.cloned.1.call-start = ((), (), s32[]{:S(2)}) async-start(), calls=%async_computation.13 | async-start | bytes 1310720 | tf_op jit(solution)/shard_map/reduce_scatter | solution.py:642
  463.3 7.5 %collective-permute-start.9 = (bf16[768,2048]{1,0:T(8,128)(2,1)S(1)}, bf16[768,2048]{1,0:T(8,128)(2,1)S(1)}, u32[]{:S(2)}, u32[]{:S(2)}) collective-permute-start(bf16[768,2048]{1,0:T(8,128)(2,1)S(1)} %get-tuple-element.184), channel_id=1, source_target_pairs={{0,1},{1,0},{2,3},{3,2},{4,5},{5,4},{6,7},{7,6},{8,9},{9,8},{10,11... | collective-permute-start | bytes 9437192 | tf_op jit(solution)/shard_map/cond/branch_1_fun/ppermute | solution.py:30
  475.1 12.2 %collective-permute-start.10 = (bf16[96,2048]{1,0:T(8,128)(2,1)}, bf16[96,2048]{1,0:T(8,128)(2,1)}, u32[]{:S(2)}, u32[]{:S(2)}) collective-permute-start(bf16[96,2048]{1,0:T(8,128)(2,1)} %get-tuple-element.471), channel_id=1, source_target_pairs={{0,2},{1,3},{2,0},{3,1},{4,6},{5,7},{6,4},{7,5},{8,10},{9,11},{10,... | collective-permute-start | bytes 1179656 | tf_op jit(solution)/shard_map/cond/branch_1_fun/ppermute | solution.py:30
  476.7 12.3 %collective-permute-start.11 = (bf16[96,2048]{1,0:T(8,128)(2,1)}, bf16[96,2048]{1,0:T(8,128)(2,1)}, u32[]{:S(2)}, u32[]{:S(2)}) collective-permute-start(bf16[96,2048]{1,0:T(8,128)(2,1)} %get-tuple-element.470), channel_id=1, source_target_pairs={{0,4},{1,5},{2,6},{3,7},{4,0},{5,1},{6,2},{7,3},{8,12},{9,13},{10,... | collective-permute-start | bytes 1179656 | tf_op jit(solution)/shard_map/cond/branch_1_fun/ppermute | solution.py:30
  476.7 18.8 %collective-permute-start.12 = (bf16[96,2048]{1,0:T(8,128)(2,1)}, bf16[96,2048]{1,0:T(8,128)(2,1)}, u32[]{:S(2)}, u32[]{:S(2)}) collective-permute-start(bf16[96,2048]{1,0:T(8,128)(2,1)} %get-tuple-element.469), channel_id=1, source_target_pairs={{0,2},{1,3},{2,0},{3,1},{4,6},{5,7},{6,4},{7,5},{8,10},{9,11},{10,... | collective-permute-start | bytes 1179656 | tf_op jit(solution)/shard_map/cond/branch_1_fun/ppermute | solution.py:30
  477.5 19.2 %collective-permute-start.13 = (bf16[96,2048]{1,0:T(8,128)(2,1)}, bf16[96,2048]{1,0:T(8,128)(2,1)}, u32[]{:S(2)}, u32[]{:S(2)}) collective-permute-start(bf16[96,2048]{1,0:T(8,128)(2,1)} %get-tuple-element.468), channel_id=1, source_target_pairs={{0,4},{1,5},{2,6},{3,7},{4,0},{5,1},{6,2},{7,3},{8,12},{9,13},{10,... | collective-permute-start | bytes 1179656 | tf_op jit(solution)/shard_map/cond/branch_1_fun/ppermute | solution.py:30
  497.4 5.0 collective-permute-start.16
  500.4 16.9 %collective-permute-start.19 = (bf16[96,2048]{1,0:T(8,128)(2,1)}, bf16[96,2048]{1,0:T(8,128)(2,1)}, u32[]{:S(2)}, u32[]{:S(2)}) collective-permute-start(bf16[96,2048]{1,0:T(8,128)(2,1)} %get-tuple-element.463), channel_id=1, source_target_pairs={{0,4},{1,5},{2,6},{3,7},{4,0},{5,1},{6,2},{7,3},{8,12},{9,13},{10,... | collective-permute-start | bytes 1179656 | tf_op jit(solution)/shard_map/cond/branch_1_fun/ppermute | solution.py:30
  501.9 15.4 %collective-permute-start.20 = (bf16[96,2048]{1,0:T(8,128)(2,1)S(1)}, bf16[96,2048]{1,0:T(8,128)(2,1)}, u32[]{:S(2)}, u32[]{:S(2)}) collective-permute-start(bf16[96,2048]{1,0:T(8,128)(2,1)S(1)} %get-tuple-element.462), channel_id=1, source_target_pairs={{0,2},{1,3},{2,0},{3,1},{4,6},{5,7},{6,4},{7,5},{8,10},{9,11},{10,... | collective-permute-start | bytes 1179656 | tf_op jit(solution)/shard_map/cond/branch_1_fun/ppermute | solution.py:30
  505.9 6.8 %collective-permute-start.17 = (f32[2,1792]{1,0:T(2,128)S(1)}, f32[2,1792]{1,0:T(2,128)S(1)}, u32[]{:S(2)}, u32[]{:S(2)}) collective-permute-start(f32[2,1792]{1,0:T(2,128)S(1)} %dynamic-slice_bitcast_fusion.2), channel_id=1, source_target_pairs={{0,2},{1,3},{2,0},{3,1},{4,6},{5,7},{6,4},{7,5},{8,10},{9,11},{10,... | collective-permute-start | bytes 43016 | tf_op jit(solution)/shard_map/cond/branch_1_fun/ppermute | solution.py:30
  510.0 9.7 %collective-permute-start.14 = (bf16[96,2048]{1,0:T(8,128)(2,1)}, bf16[96,2048]{1,0:T(8,128)(2,1)}, u32[]{:S(2)}, u32[]{:S(2)}) collective-permute-start(bf16[96,2048]{1,0:T(8,128)(2,1)} %get-tuple-element.466), channel_id=1, source_target_pairs={{0,4},{1,5},{2,6},{3,7},{4,0},{5,1},{6,2},{7,3},{8,12},{9,13},{10,... | collective-permute-start | bytes 1179656 | tf_op jit(solution)/shard_map/cond/branch_1_fun/ppermute | solution.py:30
  510.4 10.3 %collective-permute-start.15 = (bf16[96,2048]{1,0:T(8,128)(2,1)}, bf16[96,2048]{1,0:T(8,128)(2,1)}, u32[]{:S(2)}, u32[]{:S(2)}) collective-permute-start(bf16[96,2048]{1,0:T(8,128)(2,1)} %get-tuple-element.467), channel_id=1, source_target_pairs={{0,2},{1,3},{2,0},{3,1},{4,6},{5,7},{6,4},{7,5},{8,10},{9,11},{10,... | collective-permute-start | bytes 1179656 | tf_op jit(solution)/shard_map/cond/branch_1_fun/ppermute | solution.py:30
  514.0 1.8 collective-permute-start.18
  531.2 6.7 %collective-permute-start.51 = (f32[2,448]{1,0:T(2,128)S(1)}, f32[2,448]{1,0:T(2,128)S(1)}, u32[]{:S(2)}, u32[]{:S(2)}) collective-permute-start(f32[2,448]{1,0:T(2,128)S(1)} %dynamic-slice_bitcast_fusion.11), channel_id=1, source_target_pairs={{0,16},{8,24},{16,0},{24,8},{1,17},{9,25},{17,1},{25,9},{2,18},{10... | collective-permute-start | bytes 10760 | tf_op jit(solution)/shard_map/ppermute | solution.py:30
  534.4 16.1 %all-to-all-start.1 = ((bf16[8,64,768]{2,1,0:T(8,128)(2,1)}), bf16[8,64,768]{2,1,0:T(8,128)(2,1)S(1)}, u32[]{:S(2)}, u32[]{:S(2)}) async-start(bf16[8,64,768]{2,1,0:T(8,128)(2,1)} %bitcast.54), calls=%async_computation.4 | async-start | bytes 1572864 | tf_op jit(solution)/shard_map/all_to_all | solution.py:907
  538.0 4.6 collective-permute-start.52
  (65 other events, 652.7 us)
Sparse Core Ops, SparseCore 0:
  9.6 30.6 all-gather.8
  41.9 63.0 all-gather.10
  107.1 105.3 all-gather.14
  214.5 61.7 all-gather.12
  278.5 58.8 reduce-scatter.4
  339.6 102.2 reduce-scatter.6
  450.3 58.0 reduce-scatter.8
  510.6 27.2 reduce-scatter.10

commit v6 on v5

--- a/solution.py
+++ b/solution.py
@@ -287,7 +287,7 @@
     count = lax.axis_size("wide")
     total = x.shape[0]
     depth, columns = weight.shape
-    block = math.gcd(depth, 512)
+    block = math.gcd(depth, 1024)
     order = jnp.stack([lax.axis_index("wide") ^ m for m in range(first, count, 2)])
     vec = pl.BlockSpec((1, block), lambda j, order: (0, j))
     return pl.pallas_call(

time: 567 us -> 566 us (level)
  no operation moved by 1% of the time
where the time goes in v6:
time: 566 us; the launch traced here: 558 us
  waiting for transfers between devices  121 us (21%)
  matrix products  102 us (18%)
  Pallas kernels  96.7 us (17%)
  starting transfers between devices  67.2 us (12%)
  local copies, waits for them, and re-layouts  59.1 us (10%)
  other arithmetic  54.6 us (10%)
  blocking collectives  40 us (7%)
  between operations  15.8 us (3%)
    ppermute x53, waiting for transfers between devices, swap(): lax.ppermute(x, axis, [(i, i ^ bit) for i in range(lax.axis_size(axis))])  103 us
    dot_general x17, matrix products, dot(): return lax.dot_general(left, right, dims, preferred_element_type=F32)  102 us
    ppermute x53, starting transfers between devices, swap(): lax.ppermute(x, axis, [(i, i ^ bit) for i in range(lax.axis_size(axis))])  47.4 us
    pallas_call x1, Pallas kernels, attend(): pl.pallas_call(attend_kernel, grid=(pairs, total // block), in_specs=[pl....  33.8 us
    pallas_call x1, Pallas kernels, attend_back(): pl.pallas_call(attend_back_kernel, grid=(total // block,), in_specs=[whol...  32 us
    all_gather x2, blocking collectives, first_stage(): small = lax.all_gather(lax.all_gather(packed, 'rows'), 'wide')  22.2 us
    all_to_all x1, blocking collectives, shards(): lax.all_to_all(regroup(w_qkv, wide_n), 'wide', 0, 0, tiled=True)  17.8 us
    convert_element_type x8, other arithmetic, add_low(): return (left.astype(F32) + right.astype(F32)).astype(BF)  17 us
  transfers between devices with their start and end apart: 62, of which 31 were waited for; matrix products, arithmetic and copies ran while one was open for 37% of the time, Pallas kernels for 17%

profile of v6, /device:TPU:0, one launch (start us, length us, event | category | flops | bytes accessed | tf_op | source)
XLA Modules:
  0.0 557.9 jit_solution(9454212189504561852)
XLA Ops:
  9.5 17.8 %all_to_all.10 = bf16[8,64,768]{2,1,0:T(8,128)(2,1)} all-to-all(bf16[8,64,768]{2,1,0:T(8,128)(2,1)S(1)} %regroup.1), channel_id=1, replica_groups=mesh['rows'=4,'wide'=8] {'wide'}, dimensions={0} | all-to-all | bytes 1572864 | tf_op jit(solution)/shard_map/all_to_all | solution.py:656
  30.3 46.1 %conditional.7 = (bf16[768,2048]{1,0:T(8,128)(2,1)}, bf16[768,2048]{1,0:T(8,128)(2,1)}, f32[1,768]{1,0:T(1,128)S(1)}, f32[1,2048]{1,0:T(1,128)S(1)}, f32[1,2048]...) conditional(s32[]{:T(128)} %bitcast.31, () %tuple.83, ...), branch_computations={%region_0.0_spmd, %region_1.3_spmd} | conditional | flops 7882702 | bytes 32684328 | solution.py:639
  31.6 13.2 %all-gather.2 = bf16[4,1,640]{2,1,0:T(2,128)(2,1)S(1)} all-gather(bf16[1,1,640]{2,1,0:T(2,128)(2,1)S(1)} %reshape.238), channel_id=2, replica_groups=mesh['rows'=4,'wide'=8] {'rows'}, dimensions={0}, use_global_device_ids=true | all-gather | bytes 6400 | tf_op jit(solution)/shard_map/cond/branch_1_fun/all_gather | solution.py:670
  44.8 9.1 %all-gather.3 = bf16[8,4,640]{2,1,0:T(4,128)(2,1)S(1)} all-gather(bf16[1,4,640]{2,1,0:T(4,128)(2,1)S(1)} %bitcast.160), channel_id=3, replica_groups=mesh['rows'=4,'wide'=8] {'wide'}, dimensions={0}, use_global_device_ids=true | all-gather | bytes 46080 | tf_op jit(solution)/shard_map/cond/branch_1_fun/all_gather | solution.py:670
  63.3 4.0 collective-permute-done.6
  72.4 2.9 fusion.27
  80.9 16.0 %all-gather.13.cloned.1.call-start = ((), (), s32[]{:S(2)}) async-start(), calls=%async_computation.8 | async-start | bytes 3932160 | tf_op jit(solution)/shard_map/all_gather | solution.py:664
  100.6 4.4 all-gather.11.cloned.1.call-done.weight
  105.0 15.5 %project.1 = (bf16[1536,2048]{1,0:T(8,128)(2,1)}, bf16[1536,256]{1,0:T(8,128)(2,1)S(1)}, bf16[1536,256]{1,0:T(8,128)(2,1)S(1)}, bf16[1536,256]{1,0:T(8,128)(2,1)S(1)}, f32[1536,128]{1,0:T(8,128)}) custom-call(s32[8]{0:T(128)S(1)} %stack.65.order, bf16[768,2048]{1,0:T(8,128)(2,1)} %get-tuple-element.289.own_ref, ...), custom_call_target="tpu_custom_call" | custom-call | flops 16999999488 | bytes 1 | tf_op jit(solution)/shard_map/project/pallas_call | solution.py:229
  120.5 33.8 %attend.1 = (bf16[1536,256]{1,0:T(8,128)(2,1)S(1)}, f32[2,2,1536]{2,1,0:T(2,128)}) custom-call(s32[1,1536]{1,0:T(1,128)S(1)} %get-tuple-element.298.first, bf16[1536,256]{1,0:T(8,128)(2,1)S(1)} %get-tuple-element.301.q_ref, bf16[1536,256]{1,0:T(8,128)(2,1)S(1)} %get-tuple-element.302.k_ref, bf16[1536,256]{1,0:T(8,128)(2,1)S(1)} %get-tuple-element.303.v_ref), custom_call_target="tpu_custom_call" | custom-call | flops 38999998464 | bytes 1 | tf_op jit(solution)/shard_map/attend/pallas_call | solution.py:385
  156.4 2.3 copy.90
  162.3 3.2 add_convert_fusion.9
  171.0 6.7 %collective-permute-done.40 = bf16[96,2048]{1,0:T(8,128)(2,1)S(1)} collective-permute-done((bf16[96,2048]{1,0:T(8,128)(2,1)S(1)}, bf16[96,2048]{1,0:T(8,128)(2,1)S(1)}, u32[]{:S(2)}, u32[]{:S(2)}) %collective-permute-start.40) | collective-permute-done | bytes 393248 | tf_op jit(solution)/shard_map/ppermute | solution.py:30
  180.2 5.5 collective-permute-done.39
  185.7 4.2 collective-permute-done.41
  191.8 5.5 collective-permute-done.42
  206.6 12.1 %collective-permute-done.46 = bf16[192,2048]{1,0:T(8,128)(2,1)S(1)} collective-permute-done((bf16[192,2048]{1,0:T(8,128)(2,1)S(1)}, bf16[192,2048]{1,0:T(8,128)(2,1)S(1)}, u32[]{:S(2)}, u32[]{:S(2)}) %collective-permute-start.46) | collective-permute-done | bytes 786464 | tf_op jit(solution)/shard_map/ppermute | solution.py:30
  224.4 4.1 collective-permute-done.47
  230.9 35.4 %conditional.8 = (bf16[768,2048]{1,0:T(8,128)(2,1)}, f32[1408,768]{1,0:T(8,128)}, f32[1408,768]{1,0:T(8,128)}, bf16[704,768]{1,0:T(8,128)(2,1)}, bf16[704,768]{1,0:T(8,128)(2,1)}, /*index=5*/bf16[2048,704]{0,1:T(8,128)(2,1)}) conditional(s32[]{:T(128)} %bitcast.31, () %tuple.94, (bf16[768,2048]{1,0:T(8,128)(2,1)}, bf16[2048,1408]{1,0:T(8,128)(2,1)}, ...), branch_computations={%region_5.6_spmd, %region_6.7_spmd} | conditional | flops 13299810304 | bytes 103153824 | solution.py:639
  230.9 10.6 %fusion.49 = f32[1408,768]{1,0:T(8,128)} fusion(bf16[2048,1408]{1,0:T(8,128)(2,1)} %get-tuple-element.143, bf16[768,2048]{1,0:T(8,128)(2,1)} %get-tuple-element.142), kind=kOutput, calls=%fused_computation.198 | convolution fusion | flops 4429185024 | bytes 13238272 | tf_op jit(solution)/shard_map/cond/branch_1_fun/dot_general | solution.py:26
  241.5 4.0 fusion.2
  245.5 8.9 %fusion.50 = f32[1408,768]{1,0:T(8,128)} fusion(bf16[2048,1408]{1,0:T(8,128)(2,1)S(1)} %copy-done.51, bf16[768,2048]{1,0:T(8,128)(2,1)} %collective-permute-done.21), kind=kOutput, calls=%fused_computation.199 | convolution fusion | flops 4429185024 | bytes 13238272 | tf_op jit(solution)/shard_map/cond/branch_1_fun/dot_general | solution.py:26
  254.4 3.9 fusion.1
  258.3 7.6 %fusion = bf16[2048,704]{0,1:T(8,128)(2,1)} fusion(bf16[1536,2048]{1,0:T(8,128)(2,1)S(1)} %bitcast.155, bf16[704,768]{1,0:T(8,128)(2,1)} %fusion.1, bf16[704,768]{1,0:T(8,128)(2,1)} %fusion.2), kind=kOutput, calls=%fused_computation.1 | convolution fusion | flops 4434952192 | bytes 11337728 | tf_op jit(solution)/shard_map/cond/branch_1_fun/dot_general | solution.py:26
  266.3 4.6 copy.93
  271.0 5.4 all-gather.13.cloned.1.call-done
  276.3 42.4 %conditional.9 = (bf16[768,2048]{1,0:T(8,128)(2,1)}, bf16[1408,2048]{1,0:T(8,128)(2,1)}) conditional(s32[]{:T(128)} %bitcast.31, () %tuple.93, (bf16[2048,704]{1,0:T(8,128)(2,1)}, bf16[768,2048]{1,0:T(8,128)(2,1)}, f32[1408,768]{1,0:T(8,128)}, bf16[2048,1408]{1,0:T(8,128)(2,1)}, bf16[768,2048]{1,0:T(8,128)(2,1)}, /*index=5*/f32[1408,768]{1,0:T(8,128)}, ...), branch_computations={%region_7.8_spmd, %region_8.9_spmd} | conditional | flops 22210838528 | bytes 158728528 | solution.py:639
  276.3 7.5 %multiply_convert_fusion.1 = (bf16[704,768]{1,0:T(8,128)(2,1)S(1)}, bf16[704,768]{1,0:T(8,128)(2,1)S(1)}) fusion(f32[1408,768]{1,0:T(8,128)} %get-tuple-element.150, bf16[2048,704]{1,0:T(8,128)(2,1)} %get-tuple-element.145, bf16[768,2048]{1,0:T(8,128)(2,1)} %get-tuple-element.149), kind=kOutput, calls=%fused_computation.31 | convolution fusion | flops 2221621248 | bytes 12517376 | tf_op jit(solution)/shard_map/cond/branch_1_fun/dot_general | solution.py:26
  283.9 6.7 %convolution_convert_fusion.2 = bf16[768,2048]{1,0:T(8,128)(2,1)} fusion(bf16[2048,1408]{1,0:T(8,128)(2,1)S(1)} %copy-done.52, bf16[704,768]{1,0:T(8,128)(2,1)S(1)} %get-tuple-element.444, bf16[704,768]{1,0:T(8,128)(2,1)S(1)} %get-tuple-element.443), kind=kOutput, calls=%fused_computation.22 | convolution fusion | flops 4435083264 | bytes 11075584 | tf_op jit(solution)/shard_map/cond/branch_1_fun/dot_general | solution.py:26
  290.6 5.6 %multiply_convert_fusion.3 = (bf16[704,768]{1,0:T(8,128)(2,1)S(1)}, bf16[704,768]{1,0:T(8,128)(2,1)S(1)}) fusion(f32[1408,768]{1,0:T(8,128)} %get-tuple-element.147, bf16[2048,704]{1,0:T(8,128)(2,1)S(1)} %copy-done.53, bf16[768,2048]{1,0:T(8,128)(2,1)S(1)} %copy-done.34), kind=kOutput, calls=%fused_computation.34 | convolution fusion | flops 2221621248 | bytes 12517376 | tf_op jit(solution)/shard_map/cond/branch_1_fun/dot_general | solution.py:26
  296.3 5.4 convolution_convert_fusion.3
  301.7 13.6 %convolution_convert_fusion.1 = bf16[1408,2048]{1,0:T(8,128)(2,1)} fusion(bf16[768,2048]{1,0:T(8,128)(2,1)} %get-tuple-element.152, bf16[768,2048]{1,0:T(8,128)(2,1)} %get-tuple-element.151, bf16[704,768]{1,0:T(8,128)(2,1)S(1)} %copy-done.59, bf16[704,768]{1,0:T(8,128)(2,1)S(1)} %copy-done.57, bf16[704,768]{1,0:T(8,128)(2,1)} %copy-done.61, ...), kind=kOutput, calls=%fused_computation.10 | convolution fusion | flops 8891138048 | bytes 16384000 | tf_op jit(solution)/shard_map/cond/branch_1_fun/dot_general | solution.py:26
  315.3 3.0 add_convert_fusion
  318.8 43.2 %conditional.10 = (f32[192,2048]{1,0:T(8,128)S(1)}, f32[2048]{0:T(1024)S(1)}, f32[2048]{0:T(1024)}, bf16[768,2048]{1,0:T(8,128)(2,1)}, bf16[192,2048]{1,0:T(8,128)(2,1)}) conditional(s32[]{:T(128)} %bitcast.31, () %tuple.89, (bf16[192,2048]{1,0:T(8,128)(2,1)}, f32[192]{0:T(256)}, bf16[768,2048]{1,0:T(8,128)(2,1)}, f32[1,2048]{1,0:T(1,128)S(1)}, ...), branch_computations={%region_9.10_spmd, %region_10.16_spmd} | conditional | flops 4448842240 | bytes 79310488 | solution.py:639
  324.1 4.2 convolution_convert_fusion.4
  328.3 4.1 collective-permute-done.24
  335.7 4.8 collective-permute-done.23
  340.4 5.2 collective-permute-done.25
  348.9 4.2 convolution_convert_fusion.5
  359.0 3.1 add_convert_fusion.1
  362.1 28.8 %conditional.11 = (bf16[768,2048]{1,0:T(8,128)(2,1)}, f32[512,704]{0,1:T(8,128)}) conditional(s32[]{:T(128)} %bitcast.31, () %tuple.88, (bf16[192,2048]{1,0:T(8,128)(2,1)}, bf16[512,704]{1,0:T(8,128)(2,1)}) %tuple.98), branch_computations={%region_17.18_spmd, %region_18.19_spmd} | conditional | bytes 19464368 | solution.py:639
  365.1 2.5 copy.97
  369.7 8.9 %collective-permute-done.1 = bf16[192,2048]{1,0:T(8,128)(2,1)S(1)} collective-permute-done((bf16[192,2048]{1,0:T(8,128)(2,1)}, bf16[192,2048]{1,0:T(8,128)(2,1)S(1)}, u32[]{:S(2)}, u32[]{:S(2)}) %collective-permute-start.1) | collective-permute-done | bytes 786464 | tf_op jit(solution)/shard_map/cond/branch_1_fun/ppermute | solution.py:30
  384.5 2.6 collective-permute-done.2
  390.9 4.3 fusion.34
  395.3 3.7 convolution_convert_fusion.10
  398.9 51.1 %conditional.12 = (bf16[1536,768]{1,0:T(8,128)(2,1)}, bf16[2048,768]{0,1:T(8,128)(2,1)}, bf16[96,2048]{1,0:T(8,128)(2,1)}, bf16[96,2048]{1,0:T(8,128)(2,1)}, bf1...) conditional(s32[]{:T(128)} %bitcast.31, () %tuple.87, (bf16[768,2048]{1,0:T(8,128)(2,1)}, ...), branch_computations={%region_19.20_spmd, %region_20.21_spmd} | conditional | flops 49640488960 | bytes 30540804 | solution.py:639
  399.1 2.4 fusion.44
  405.5 3.0 convolution_convert_fusion.7
  408.8 32.0 %attend_back.1 = bf16[1536,768]{1,0:T(8,128)(2,1)} custom-call(s32[1,1536]{1,0:T(1,128)S(1)} %get-tuple-element.163.first, bf16[1536,256]{1,0:T(8,128)(2,1)} %get-tuple-element.164.q_ref, bf16[1536,256]{1,0:T(8,128)(2,1)} %get-tuple-element.165.k_ref, bf16[1536,256]{1,0:T(8,128)(2,1)} %get-tuple-element.166.v_ref, ...), custom_call_target="tpu_custom_call" | custom-call | flops 44000002048 | bytes 1 | tf_op jit(solution)/shard_map/cond/branch_1_fun/attend_back/pallas_call | solution.py:507
  440.8 9.2 %fusion.26 = bf16[2048,768]{0,1:T(8,128)(2,1)} fusion(bf16[1536,768]{1,0:T(8,128)(2,1)} %attend_back.1, bf16[1536,2048]{1,0:T(8,128)(2,1)} %get-tuple-element.175), kind=kOutput, calls=%fused_computation.60 | convolution fusion | flops 4833411072 | bytes 11796480 | tf_op jit(solution)/shard_map/cond/branch_1_fun/dot_general | solution.py:26
  451.1 4.6 fusion.33
  455.8 73.4 %conditional.13 = (f32[1,192,2048]{2,1,0:T(8,128)}, f32[4,448]{1,0:T(4,128)}, bf16[1,192,2048]{2,1,0:T(8,128)(2,1)}) conditional(s32[]{:T(128)} %bitcast.31, () %tuple.82, (f32[1536,128]{1,0:T(8,128)}, bf16[1536,768]{1,0:T(8,128)(2,1)}, bf16[768,2048]{1,0:T(8,128)(2,1)}, bf16[2048,768]{1,0:T(8,128)(2,1)}, bf16[768,2048]{1,0:T(8,128)(2,1)}, ...), branch_computations={%region_22.23_spmd, %region_23.26_spmd} | conditional | flops 14021644288 | bytes 79257176 | solution.py:639
  455.9 6.8 %unproject.3 = (bf16[768,2048]{1,0:T(8,128)(2,1)S(1)}, f32[1,2048]{1,0:T(1,128)S(1)}, f32[1,2048]{1,0:T(1,128)S(1)}, f32[1,768]{1,0:T(1,128)S(1)}) custom-call(s32[4]{0:T(128)S(1)} %get-tuple-element.473.order, bf16[1536,768]{1,0:T(8,128)(2,1)} %get-tuple-element.179.g_ref, bf16[768,2048]{1,0:T(8,128)(2,1)} %get-tuple-element.183.x_ref, ...), custom_call_target="tpu_custom_call" | custom-call | flops 7000000000 | bytes 1 | tf_op jit(solution)/shard_map/cond/branch_1_fun/unproject/pallas_call | solution.py:293
  462.8 6.8 %unproject.2 = (bf16[768,2048]{1,0:T(8,128)(2,1)S(1)}, f32[1,2048]{1,0:T(1,128)S(1)}, f32[1,2048]{1,0:T(1,128)S(1)}, f32[1,768]{1,0:T(1,128)S(1)}) custom-call(s32[4]{0:T(128)S(1)} %get-tuple-element.472.order, bf16[1536,768]{1,0:T(8,128)(2,1)} %get-tuple-element.179.g_ref, bf16[768,2048]{1,0:T(8,128)(2,1)} %get-tuple-element.180.x_ref, ...), custom_call_target="tpu_custom_call" | custom-call | flops 7000000000 | bytes 1 | tf_op jit(solution)/shard_map/cond/branch_1_fun/unproject/pallas_call | solution.py:293
  478.9 7.3 %collective-permute-done.10 = bf16[96,2048]{1,0:T(8,128)(2,1)} collective-permute-done((bf16[96,2048]{1,0:T(8,128)(2,1)}, bf16[96,2048]{1,0:T(8,128)(2,1)}, u32[]{:S(2)}, u32[]{:S(2)}) %collective-permute-start.10) | collective-permute-done | bytes 393248 | tf_op jit(solution)/shard_map/cond/branch_1_fun/ppermute | solution.py:30
  487.8 6.5 %collective-permute-done.12 = bf16[96,2048]{1,0:T(8,128)(2,1)} collective-permute-done((bf16[96,2048]{1,0:T(8,128)(2,1)}, bf16[96,2048]{1,0:T(8,128)(2,1)}, u32[]{:S(2)}, u32[]{:S(2)}) %collective-permute-start.12) | collective-permute-done | bytes 393248 | tf_op jit(solution)/shard_map/cond/branch_1_fun/ppermute | solution.py:30
  496.9 2.4 add_convert_fusion.5
  506.2 2.5 add_convert_fusion.8
  516.1 2.4 collective-permute-done.14
  526.3 2.9 add_bitcast_fusion
  531.0 2.3 copy.94
  533.3 3.5 all-to-all-start.1
  542.7 6.7 %all-to-all-done.1 = bf16[8,64,768]{2,1,0:T(8,128)(2,1)S(1)} async-done(((bf16[8,64,768]{2,1,0:T(8,128)(2,1)}), bf16[8,64,768]{2,1,0:T(8,128)(2,1)S(1)}, u32[]{:S(2)}, u32[]{:S(2)}) %all-to-all-start.1) | async-done | bytes 786464 | tf_op jit(solution)/shard_map/all_to_all | solution.py:907
  (378 shorter events, 144.7 us)
Async XLA Ops:
  7.2 93.4 %all-gather.9.cloned.1.call-start = ((), (), s32[]{:S(2)}) async-start(), calls=%async_computation.6 | async-start | bytes 1310720 | tf_op jit(solution)/shard_map/all_gather | solution.py:646
  7.9 97.0 %all-gather.11.cloned.1.call-start = ((), (), s32[]{:S(2)}) async-start(), calls=%async_computation.7 | async-start | bytes 3932160 | tf_op jit(solution)/shard_map/all_gather | solution.py:659
  27.3 203.6 %all-gather.15.cloned.1.call-start = ((), (), s32[]{:S(2)}) async-start(), calls=%async_computation.9 | async-start | bytes 7208960 | tf_op jit(solution)/shard_map/all_gather | solution.py:661
  30.3 47.0 %copy-start.7 = (bf16[1,192,2048]{2,1,0:T(8,128)(2,1)S(1)}, bf16[1,192,2048]{2,1,0:T(8,128)(2,1)}, u32[]{:S(2)}) copy-start(bf16[1,192,2048]{2,1,0:T(8,128)(2,1)} %param.39) | copy-start | bytes 2359300
  30.3 24.5 %collective-permute-start.4 = (bf16[192,2048]{1,0:T(8,128)(2,1)S(1)}, bf16[192,2048]{1,0:T(8,128)(2,1)}, u32[]{:S(2)}, u32[]{:S(2)}) collective-permute-start(bf16[192,2048]{1,0:T(8,128)(2,1)S(1)} %get-tuple-element.131), channel_id=1, source_target_pairs={{0,2},{1,3},{2,0},{3,1},{4,6},{5,7},{6,4},{7,5},{8,10},{9,11},{10,... | collective-permute-start | bytes 2359304 | tf_op jit(solution)/shard_map/cond/branch_1_fun/ppermute | solution.py:30
  30.9 23.9 %collective-permute-start.5 = (bf16[192,2048]{1,0:T(8,128)(2,1)S(1)}, bf16[192,2048]{1,0:T(8,128)(2,1)}, u32[]{:S(2)}, u32[]{:S(2)}) collective-permute-start(bf16[192,2048]{1,0:T(8,128)(2,1)S(1)} %get-tuple-element.131), channel_id=1, source_target_pairs={{0,4},{1,5},{2,6},{3,7},{4,0},{5,1},{6,2},{7,3},{8,12},{9,13},{10,... | collective-permute-start | bytes 2359304 | tf_op jit(solution)/shard_map/cond/branch_1_fun/ppermute | solution.py:30
  55.9 11.4 %collective-permute-start.6 = (bf16[96,2048]{1,0:T(8,128)(2,1)S(1)}, bf16[96,2048]{1,0:T(8,128)(2,1)S(1)}, u32[]{:S(2)}, u32[]{:S(2)}) collective-permute-start(bf16[96,2048]{1,0:T(8,128)(2,1)S(1)} %slice.146), channel_id=1, source_target_pairs={{0,2},{1,3},{2,0},{3,1},{4,6},{5,7},{6,4},{7,5},{8,10},{9,11},{10,... | collective-permute-start | bytes 1179656 | tf_op jit(solution)/shard_map/cond/branch_1_fun/ppermute | solution.py:30
  58.4 11.1 %collective-permute-start.7 = (bf16[96,2048]{1,0:T(8,128)(2,1)S(1)}, bf16[96,2048]{1,0:T(8,128)(2,1)S(1)}, u32[]{:S(2)}, u32[]{:S(2)}) collective-permute-start(bf16[96,2048]{1,0:T(8,128)(2,1)S(1)} %slice.147), channel_id=1, source_target_pairs={{0,4},{1,5},{2,6},{3,7},{4,0},{5,1},{6,2},{7,3},{8,12},{9,13},{10,... | collective-permute-start | bytes 1179656 | tf_op jit(solution)/shard_map/cond/branch_1_fun/ppermute | solution.py:30
  70.4 6.0 %collective-permute-start.8 = (bf16[768,2048]{1,0:T(8,128)(2,1)}, bf16[768,2048]{1,0:T(8,128)(2,1)}, u32[]{:S(2)}, u32[]{:S(2)}) collective-permute-start(bf16[768,2048]{1,0:T(8,128)(2,1)} %constant_dynamic-update-slice_fusion.5), channel_id=1, source_target_pairs={{0,1},{1,0},{2,3},{3,2},{4,5},{5,4},{6,7},{7,6},{8,9},{9,8},{10,11... | collective-permute-start | bytes 9437192 | tf_op jit(solution)/shard_map/cond/branch_1_fun/ppermute | solution.py:30
  76.4 44.1 %copy-start.44 = (s32[1,1536]{1,0:T(1,128)}, s32[1,1536]{1,0:T(1,128)S(1)}, u32[]{:S(2)}) copy-start(s32[1,1536]{1,0:T(1,128)S(1)} %get-tuple-element.298.first) | copy-start | bytes 18436
  77.3 21.4 %collective-permute-start.34 = (bf16[192,2048]{1,0:T(8,128)(2,1)S(1)}, bf16[192,2048]{1,0:T(8,128)(2,1)}, u32[]{:S(2)}, u32[]{:S(2)}) collective-permute-start(bf16[192,2048]{1,0:T(8,128)(2,1)S(1)} %bitcast.143), channel_id=1, source_target_pairs={{0,2},{1,3},{2,0},{3,1},{4,6},{5,7},{6,4},{7,5},{8,10},{9,11},{10,... | collective-permute-start | bytes 2359304 | tf_op jit(solution)/shard_map/ppermute | solution.py:30
  77.8 19.5 %collective-permute-start.35 = (bf16[192,2048]{1,0:T(8,128)(2,1)S(1)}, bf16[192,2048]{1,0:T(8,128)(2,1)S(1)}, u32[]{:S(2)}, u32[]{:S(2)}) collective-permute-start(bf16[192,2048]{1,0:T(8,128)(2,1)S(1)} %bitcast.144), channel_id=1, source_target_pairs={{0,4},{1,5},{2,6},{3,7},{4,0},{5,1},{6,2},{7,3},{8,12},{9,13},{10,... | collective-permute-start | bytes 2359304 | tf_op jit(solution)/shard_map/ppermute | solution.py:30
  80.9 195.5 %all-gather.13.cloned.1.call-start = ((), (), s32[]{:S(2)}) async-start(), calls=%async_computation.8 | async-start | bytes 3932160 | tf_op jit(solution)/shard_map/all_gather | solution.py:664
  97.4 56.9 %collective-permute-start.36 = (bf16[96,2048]{1,0:T(8,128)(2,1)S(1)}, bf16[96,2048]{1,0:T(8,128)(2,1)S(1)}, u32[]{:S(2)}, u32[]{:S(2)}) collective-permute-start(bf16[96,2048]{1,0:T(8,128)(2,1)S(1)} %slice.259), channel_id=1, source_target_pairs={{0,2},{1,3},{2,0},{3,1},{4,6},{5,7},{6,4},{7,5},{8,10},{9,11},{10,... | collective-permute-start | bytes 1179656 | tf_op jit(solution)/shard_map/ppermute | solution.py:30
  99.7 54.6 %collective-permute-start.37 = (bf16[96,2048]{1,0:T(8,128)(2,1)S(1)}, bf16[96,2048]{1,0:T(8,128)(2,1)S(1)}, u32[]{:S(2)}, u32[]{:S(2)}) collective-permute-start(bf16[96,2048]{1,0:T(8,128)(2,1)S(1)} %slice.260), channel_id=1, source_target_pairs={{0,4},{1,5},{2,6},{3,7},{4,0},{5,1},{6,2},{7,3},{8,12},{9,13},{10,... | collective-permute-start | bytes 1179656 | tf_op jit(solution)/shard_map/ppermute | solution.py:30
  156.3 6.0 %collective-permute-start.38 = (bf16[768,2048]{1,0:T(8,128)(2,1)S(1)}, bf16[768,2048]{1,0:T(8,128)(2,1)}, u32[]{:S(2)}, u32[]{:S(2)}) collective-permute-start(bf16[768,2048]{1,0:T(8,128)(2,1)S(1)} %convolution_convert_fusion.8), channel_id=1, source_target_pairs={{0,1},{1,0},{2,3},{3,2},{4,5},{5,4},{6,7},{7,6},{8,9},{9,8},{10,11... | collective-permute-start | bytes 9437192 | tf_op jit(solution)/shard_map/ppermute | solution.py:30
  158.7 203.4 %reduce-scatter.5.cloned.1.call-start = ((), (), s32[]{:S(2)}) async-start(), calls=%async_computation.10 | async-start | bytes 3932160 | tf_op jit(solution)/shard_map/reduce_scatter | solution.py:642
  165.7 12.0 %collective-permute-start.40 = (bf16[96,2048]{1,0:T(8,128)(2,1)S(1)}, bf16[96,2048]{1,0:T(8,128)(2,1)S(1)}, u32[]{:S(2)}, u32[]{:S(2)}) collective-permute-start(bf16[96,2048]{1,0:T(8,128)(2,1)S(1)} %get-tuple-element.486), channel_id=1, source_target_pairs={{0,2},{1,3},{2,0},{3,1},{4,6},{5,7},{6,4},{7,5},{8,10},{9,11},{10,... | collective-permute-start | bytes 1179656 | tf_op jit(solution)/shard_map/ppermute | solution.py:30
  168.8 16.9 %collective-permute-start.39 = (bf16[96,2048]{1,0:T(8,128)(2,1)S(1)}, bf16[96,2048]{1,0:T(8,128)(2,1)S(1)}, u32[]{:S(2)}, u32[]{:S(2)}) collective-permute-start(bf16[96,2048]{1,0:T(8,128)(2,1)S(1)} %get-tuple-element.483), channel_id=1, source_target_pairs={{0,2},{1,3},{2,0},{3,1},{4,6},{5,7},{6,4},{7,5},{8,10},{9,11},{10,... | collective-permute-start | bytes 1179656 | tf_op jit(solution)/shard_map/ppermute | solution.py:30
  169.4 16.3 %collective-permute-start.43 = (bf16[96,2048]{1,0:T(8,128)(2,1)S(1)}, bf16[96,2048]{1,0:T(8,128)(2,1)S(1)}, u32[]{:S(2)}, u32[]{:S(2)}) collective-permute-start(bf16[96,2048]{1,0:T(8,128)(2,1)S(1)} %get-tuple-element.484), channel_id=1, source_target_pairs={{0,4},{1,5},{2,6},{3,7},{4,0},{5,1},{6,2},{7,3},{8,12},{9,13},{10,... | collective-permute-start | bytes 1179656 | tf_op jit(solution)/shard_map/ppermute | solution.py:30
  177.8 12.1 %collective-permute-start.41 = (bf16[96,2048]{1,0:T(8,128)(2,1)S(1)}, bf16[96,2048]{1,0:T(8,128)(2,1)S(1)}, u32[]{:S(2)}, u32[]{:S(2)}) collective-permute-start(bf16[96,2048]{1,0:T(8,128)(2,1)S(1)} %add_convert_fusion.12), channel_id=1, source_target_pairs={{0,4},{1,5},{2,6},{3,7},{4,0},{5,1},{6,2},{7,3},{8,12},{9,13},{10,... | collective-permute-start | bytes 1179656 | tf_op jit(solution)/shard_map/ppermute | solution.py:30
  179.6 25.4 %collective-permute-start.49 = (bf16[768,2048]{1,0:T(8,128)(2,1)S(1)}, bf16[768,2048]{1,0:T(8,128)(2,1)S(1)}, u32[]{:S(2)}, u32[]{:S(2)}) collective-permute-start(bf16[768,2048]{1,0:T(8,128)(2,1)S(1)} %get-tuple-element.504), channel_id=1, source_target_pairs={{0,1},{1,0},{2,3},{3,2},{4,5},{5,4},{6,7},{7,6},{8,9},{9,8},{10,11... | collective-permute-start | bytes 9437192 | tf_op jit(solution)/shard_map/ppermute | solution.py:30
  179.7 17.5 %collective-permute-start.42 = (bf16[96,2048]{1,0:T(8,128)(2,1)S(1)}, bf16[96,2048]{1,0:T(8,128)(2,1)S(1)}, u32[]{:S(2)}, u32[]{:S(2)}) collective-permute-start(bf16[96,2048]{1,0:T(8,128)(2,1)S(1)} %get-tuple-element.485), channel_id=1, source_target_pairs={{0,4},{1,5},{2,6},{3,7},{4,0},{5,1},{6,2},{7,3},{8,12},{9,13},{10,... | collective-permute-start | bytes 1179656 | tf_op jit(solution)/shard_map/ppermute | solution.py:30
  190.2 9.1 %collective-permute-start.44 = (bf16[96,2048]{1,0:T(8,128)(2,1)S(1)}, bf16[96,2048]{1,0:T(8,128)(2,1)S(1)}, u32[]{:S(2)}, u32[]{:S(2)}) collective-permute-start(bf16[96,2048]{1,0:T(8,128)(2,1)S(1)} %get-tuple-element.482), channel_id=1, source_target_pairs={{0,2},{1,3},{2,0},{3,1},{4,6},{5,7},{6,4},{7,5},{8,10},{9,11},{10,... | collective-permute-start | bytes 1179656 | tf_op jit(solution)/shard_map/ppermute | solution.py:30
  202.1 16.7 %collective-permute-start.46 = (bf16[192,2048]{1,0:T(8,128)(2,1)S(1)}, bf16[192,2048]{1,0:T(8,128)(2,1)S(1)}, u32[]{:S(2)}, u32[]{:S(2)}) collective-permute-start(bf16[192,2048]{1,0:T(8,128)(2,1)S(1)} %get-tuple-element.437), channel_id=1, source_target_pairs={{0,4},{1,5},{2,6},{3,7},{4,0},{5,1},{6,2},{7,3},{8,12},{9,13},{10,... | collective-permute-start | bytes 2359304 | tf_op jit(solution)/shard_map/ppermute | solution.py:30
  203.6 18.6 %collective-permute-start.45 = (bf16[192,2048]{1,0:T(8,128)(2,1)S(1)}, bf16[192,2048]{1,0:T(8,128)(2,1)S(1)}, u32[]{:S(2)}, u32[]{:S(2)}) collective-permute-start(bf16[192,2048]{1,0:T(8,128)(2,1)S(1)} %get-tuple-element.437), channel_id=1, source_target_pairs={{0,2},{1,3},{2,0},{3,1},{4,6},{5,7},{6,4},{7,5},{8,10},{9,11},{10,... | collective-permute-start | bytes 2359304 | tf_op jit(solution)/shard_map/ppermute | solution.py:30
  218.7 9.7 %collective-permute-start.47 = (bf16[96,2048]{1,0:T(8,128)(2,1)S(1)}, bf16[96,2048]{1,0:T(8,128)(2,1)S(1)}, u32[]{:S(2)}, u32[]{:S(2)}) collective-permute-start(bf16[96,2048]{1,0:T(8,128)(2,1)S(1)} %slice.269), channel_id=1, source_target_pairs={{0,2},{1,3},{2,0},{3,1},{4,6},{5,7},{6,4},{7,5},{8,10},{9,11},{10,... | collective-permute-start | bytes 1179656 | tf_op jit(solution)/shard_map/ppermute | solution.py:30
  222.3 7.8 %collective-permute-start.48 = (bf16[96,2048]{1,0:T(8,128)(2,1)S(1)}, bf16[96,2048]{1,0:T(8,128)(2,1)S(1)}, u32[]{:S(2)}, u32[]{:S(2)}) collective-permute-start(bf16[96,2048]{1,0:T(8,128)(2,1)S(1)} %slice.270), channel_id=1, source_target_pairs={{0,4},{1,5},{2,6},{3,7},{4,0},{5,1},{6,2},{7,3},{8,12},{9,13},{10,... | collective-permute-start | bytes 1179656 | tf_op jit(solution)/shard_map/ppermute | solution.py:30
  230.9 14.6 %collective-permute-start.21 = (bf16[768,2048]{1,0:T(8,128)(2,1)}, bf16[768,2048]{1,0:T(8,128)(2,1)}, u32[]{:S(2)}, u32[]{:S(2)}) collective-permute-start(bf16[768,2048]{1,0:T(8,128)(2,1)} %get-tuple-element.142), channel_id=1, source_target_pairs={{0,1},{1,0},{2,3},{3,2},{4,5},{5,4},{6,7},{7,6},{8,9},{9,8},{10,11... | collective-permute-start | bytes 9437192 | tf_op jit(solution)/shard_map/cond/branch_1_fun/ppermute | solution.py:30
  270.9 179.2 %reduce-scatter.7.cloned.1.call-start = ((), (), s32[]{:S(2)}) async-start(), calls=%async_computation.11 | async-start | bytes 7208960 | tf_op jit(solution)/shard_map/reduce_scatter | solution.py:642
  290.6 24.7 %collective-permute-start.22 = (bf16[768,2048]{1,0:T(8,128)(2,1)}, bf16[768,2048]{1,0:T(8,128)(2,1)S(1)}, u32[]{:S(2)}, u32[]{:S(2)}) collective-permute-start(bf16[768,2048]{1,0:T(8,128)(2,1)} %convolution_convert_fusion.2), channel_id=1, source_target_pairs={{0,1},{1,0},{2,3},{3,2},{4,5},{5,4},{6,7},{7,6},{8,9},{9,8},{10,11... | collective-permute-start | bytes 9437192 | tf_op jit(solution)/shard_map/cond/branch_1_fun/ppermute | solution.py:30
  318.8 210.4 %reduce-scatter.9.cloned.1.call-start = ((), (), s32[]{:S(2)}) async-start(), calls=%async_computation.12 | async-start | bytes 3932160 | tf_op jit(solution)/shard_map/reduce_scatter | solution.py:642
  320.5 12.0 %collective-permute-start.24 = (bf16[96,2048]{1,0:T(8,128)(2,1)S(1)}, bf16[96,2048]{1,0:T(8,128)(2,1)S(1)}, u32[]{:S(2)}, u32[]{:S(2)}) collective-permute-start(bf16[96,2048]{1,0:T(8,128)(2,1)S(1)} %get-tuple-element.478), channel_id=1, source_target_pairs={{0,2},{1,3},{2,0},{3,1},{4,6},{5,7},{6,4},{7,5},{8,10},{9,11},{10,... | collective-permute-start | bytes 1179656 | tf_op jit(solution)/shard_map/cond/branch_1_fun/ppermute | solution.py:30
  322.0 18.4 %collective-permute-start.23 = (bf16[96,2048]{1,0:T(8,128)(2,1)S(1)}, bf16[96,2048]{1,0:T(8,128)(2,1)S(1)}, u32[]{:S(2)}, u32[]{:S(2)}) collective-permute-start(bf16[96,2048]{1,0:T(8,128)(2,1)S(1)} %get-tuple-element.475), channel_id=1, source_target_pairs={{0,2},{1,3},{2,0},{3,1},{4,6},{5,7},{6,4},{7,5},{8,10},{9,11},{10,... | collective-permute-start | bytes 1179656 | tf_op jit(solution)/shard_map/cond/branch_1_fun/ppermute | solution.py:30
  322.6 17.9 %collective-permute-start.27 = (bf16[96,2048]{1,0:T(8,128)(2,1)S(1)}, bf16[96,2048]{1,0:T(8,128)(2,1)S(1)}, u32[]{:S(2)}, u32[]{:S(2)}) collective-permute-start(bf16[96,2048]{1,0:T(8,128)(2,1)S(1)} %get-tuple-element.476), channel_id=1, source_target_pairs={{0,4},{1,5},{2,6},{3,7},{4,0},{5,1},{6,2},{7,3},{8,12},{9,13},{10,... | collective-permute-start | bytes 1179656 | tf_op jit(solution)/shard_map/cond/branch_1_fun/ppermute | solution.py:30
  328.3 30.7 %collective-permute-start.29 = (bf16[768,2048]{1,0:T(8,128)(2,1)S(1)}, bf16[768,2048]{1,0:T(8,128)(2,1)S(1)}, u32[]{:S(2)}, u32[]{:S(2)}) collective-permute-start(bf16[768,2048]{1,0:T(8,128)(2,1)S(1)} %convolution_convert_fusion.4), channel_id=1, source_target_pairs={{0,1},{1,0},{2,3},{3,2},{4,5},{5,4},{6,7},{7,6},{8,9},{9,8},{10,11... | collective-permute-start | bytes 9437192 | tf_op jit(solution)/shard_map/cond/branch_1_fun/ppermute | solution.py:30
  333.6 12.1 %collective-permute-start.25 = (bf16[96,2048]{1,0:T(8,128)(2,1)S(1)}, bf16[96,2048]{1,0:T(8,128)(2,1)S(1)}, u32[]{:S(2)}, u32[]{:S(2)}) collective-permute-start(bf16[96,2048]{1,0:T(8,128)(2,1)S(1)} %add_convert_fusion.3), channel_id=1, source_target_pairs={{0,4},{1,5},{2,6},{3,7},{4,0},{5,1},{6,2},{7,3},{8,12},{9,13},{10,... | collective-permute-start | bytes 1179656 | tf_op jit(solution)/shard_map/cond/branch_1_fun/ppermute | solution.py:30
  335.1 18.0 %collective-permute-start.26 = (bf16[96,2048]{1,0:T(8,128)(2,1)S(1)}, bf16[96,2048]{1,0:T(8,128)(2,1)S(1)}, u32[]{:S(2)}, u32[]{:S(2)}) collective-permute-start(bf16[96,2048]{1,0:T(8,128)(2,1)S(1)} %get-tuple-element.477), channel_id=1, source_target_pairs={{0,4},{1,5},{2,6},{3,7},{4,0},{5,1},{6,2},{7,3},{8,12},{9,13},{10,... | collective-permute-start | bytes 1179656 | tf_op jit(solution)/shard_map/cond/branch_1_fun/ppermute | solution.py:30
  347.3 7.8 %collective-permute-start.28 = (bf16[96,2048]{1,0:T(8,128)(2,1)S(1)}, bf16[96,2048]{1,0:T(8,128)(2,1)S(1)}, u32[]{:S(2)}, u32[]{:S(2)}) collective-permute-start(bf16[96,2048]{1,0:T(8,128)(2,1)S(1)} %get-tuple-element.474), channel_id=1, source_target_pairs={{0,2},{1,3},{2,0},{3,1},{4,6},{5,7},{6,4},{7,5},{8,10},{9,11},{10,... | collective-permute-start | bytes 1179656 | tf_op jit(solution)/shard_map/cond/branch_1_fun/ppermute | solution.py:30
  362.1 16.4 %collective-permute-start.1 = (bf16[192,2048]{1,0:T(8,128)(2,1)}, bf16[192,2048]{1,0:T(8,128)(2,1)S(1)}, u32[]{:S(2)}, u32[]{:S(2)}) collective-permute-start(bf16[192,2048]{1,0:T(8,128)(2,1)} %get-tuple-element.161), channel_id=1, source_target_pairs={{0,4},{1,5},{2,6},{3,7},{4,0},{5,1},{6,2},{7,3},{8,12},{9,13},{10,... | collective-permute-start | bytes 2359304 | tf_op jit(solution)/shard_map/cond/branch_1_fun/ppermute | solution.py:30
  363.6 18.6 %collective-permute-start = (bf16[192,2048]{1,0:T(8,128)(2,1)}, bf16[192,2048]{1,0:T(8,128)(2,1)S(1)}, u32[]{:S(2)}, u32[]{:S(2)}) collective-permute-start(bf16[192,2048]{1,0:T(8,128)(2,1)} %get-tuple-element.161), channel_id=1, source_target_pairs={{0,2},{1,3},{2,0},{3,1},{4,6},{5,7},{6,4},{7,5},{8,10},{9,11},{10,... | collective-permute-start | bytes 2359304 | tf_op jit(solution)/shard_map/cond/branch_1_fun/ppermute | solution.py:30
  378.6 8.6 %collective-permute-start.2 = (bf16[96,2048]{1,0:T(8,128)(2,1)S(1)}, bf16[96,2048]{1,0:T(8,128)(2,1)S(1)}, u32[]{:S(2)}, u32[]{:S(2)}) collective-permute-start(bf16[96,2048]{1,0:T(8,128)(2,1)S(1)} %slice.245), channel_id=1, source_target_pairs={{0,2},{1,3},{2,0},{3,1},{4,6},{5,7},{6,4},{7,5},{8,10},{9,11},{10,... | collective-permute-start | bytes 1179656 | tf_op jit(solution)/shard_map/cond/branch_1_fun/ppermute | solution.py:30
  382.2 7.8 %collective-permute-start.3 = (bf16[96,2048]{1,0:T(8,128)(2,1)S(1)}, bf16[96,2048]{1,0:T(8,128)(2,1)S(1)}, u32[]{:S(2)}, u32[]{:S(2)}) collective-permute-start(bf16[96,2048]{1,0:T(8,128)(2,1)S(1)} %slice.246), channel_id=1, source_target_pairs={{0,4},{1,5},{2,6},{3,7},{4,0},{5,1},{6,2},{7,3},{8,12},{9,13},{10,... | collective-permute-start | bytes 1179656 | tf_op jit(solution)/shard_map/cond/branch_1_fun/ppermute | solution.py:30
  390.9 8.0 %collective-permute-start.50 = (bf16[768,2048]{1,0:T(8,128)(2,1)}, bf16[768,2048]{1,0:T(8,128)(2,1)}, u32[]{:S(2)}, u32[]{:S(2)}) collective-permute-start(bf16[768,2048]{1,0:T(8,128)(2,1)} %get-tuple-element.316), channel_id=1, source_target_pairs={{0,1},{1,0},{2,3},{3,2},{4,5},{5,4},{6,7},{7,6},{8,9},{9,8},{10,11... | collective-permute-start | bytes 9437192 | tf_op jit(solution)/shard_map/ppermute | solution.py:30
  401.5 48.5 %collective-permute-start.30 = (bf16[96,2048]{1,0:T(8,128)(2,1)}, bf16[96,2048]{1,0:T(8,128)(2,1)}, u32[]{:S(2)}, u32[]{:S(2)}) collective-permute-start(bf16[96,2048]{1,0:T(8,128)(2,1)} %get-tuple-element.448), channel_id=1, source_target_pairs={{0,2},{1,3},{2,0},{3,1},{4,6},{5,7},{6,4},{7,5},{8,10},{9,11},{10,... | collective-permute-start | bytes 1179656 | tf_op jit(solution)/shard_map/cond/branch_1_fun/ppermute | solution.py:30
  403.0 47.1 %collective-permute-start.31 = (bf16[96,2048]{1,0:T(8,128)(2,1)}, bf16[96,2048]{1,0:T(8,128)(2,1)}, u32[]{:S(2)}, u32[]{:S(2)}) collective-permute-start(bf16[96,2048]{1,0:T(8,128)(2,1)} %get-tuple-element.447), channel_id=1, source_target_pairs={{0,4},{1,5},{2,6},{3,7},{4,0},{5,1},{6,2},{7,3},{8,12},{9,13},{10,... | collective-permute-start | bytes 1179656 | tf_op jit(solution)/shard_map/cond/branch_1_fun/ppermute | solution.py:30
  403.0 47.1 %collective-permute-start.32 = (bf16[96,2048]{1,0:T(8,128)(2,1)}, bf16[96,2048]{1,0:T(8,128)(2,1)}, u32[]{:S(2)}, u32[]{:S(2)}) collective-permute-start(bf16[96,2048]{1,0:T(8,128)(2,1)} %get-tuple-element.446), channel_id=1, source_target_pairs={{0,2},{1,3},{2,0},{3,1},{4,6},{5,7},{6,4},{7,5},{8,10},{9,11},{10,... | collective-permute-start | bytes 1179656 | tf_op jit(solution)/shard_map/cond/branch_1_fun/ppermute | solution.py:30
  403.8 46.2 %collective-permute-start.33 = (bf16[96,2048]{1,0:T(8,128)(2,1)S(1)}, bf16[96,2048]{1,0:T(8,128)(2,1)}, u32[]{:S(2)}, u32[]{:S(2)}) collective-permute-start(bf16[96,2048]{1,0:T(8,128)(2,1)S(1)} %get-tuple-element.445), channel_id=1, source_target_pairs={{0,4},{1,5},{2,6},{3,7},{4,0},{5,1},{6,2},{7,3},{8,12},{9,13},{10,... | collective-permute-start | bytes 1179656 | tf_op jit(solution)/shard_map/cond/branch_1_fun/ppermute | solution.py:30
  450.2 89.6 %reduce-scatter.11.cloned.1.call-start = ((), (), s32[]{:S(2)}) async-start(), calls=%async_computation.13 | async-start | bytes 1310720 | tf_op jit(solution)/shard_map/reduce_scatter | solution.py:642
  462.7 6.9 %collective-permute-start.9 = (bf16[768,2048]{1,0:T(8,128)(2,1)S(1)}, bf16[768,2048]{1,0:T(8,128)(2,1)S(1)}, u32[]{:S(2)}, u32[]{:S(2)}) collective-permute-start(bf16[768,2048]{1,0:T(8,128)(2,1)S(1)} %get-tuple-element.184), channel_id=1, source_target_pairs={{0,1},{1,0},{2,3},{3,2},{4,5},{5,4},{6,7},{7,6},{8,9},{9,8},{10,11... | collective-permute-start | bytes 9437192 | tf_op jit(solution)/shard_map/cond/branch_1_fun/ppermute | solution.py:30
  474.0 12.2 %collective-permute-start.10 = (bf16[96,2048]{1,0:T(8,128)(2,1)}, bf16[96,2048]{1,0:T(8,128)(2,1)}, u32[]{:S(2)}, u32[]{:S(2)}) collective-permute-start(bf16[96,2048]{1,0:T(8,128)(2,1)} %get-tuple-element.471), channel_id=1, source_target_pairs={{0,2},{1,3},{2,0},{3,1},{4,6},{5,7},{6,4},{7,5},{8,10},{9,11},{10,... | collective-permute-start | bytes 1179656 | tf_op jit(solution)/shard_map/cond/branch_1_fun/ppermute | solution.py:30
  475.5 12.3 %collective-permute-start.11 = (bf16[96,2048]{1,0:T(8,128)(2,1)}, bf16[96,2048]{1,0:T(8,128)(2,1)}, u32[]{:S(2)}, u32[]{:S(2)}) collective-permute-start(bf16[96,2048]{1,0:T(8,128)(2,1)} %get-tuple-element.470), channel_id=1, source_target_pairs={{0,4},{1,5},{2,6},{3,7},{4,0},{5,1},{6,2},{7,3},{8,12},{9,13},{10,... | collective-permute-start | bytes 1179656 | tf_op jit(solution)/shard_map/cond/branch_1_fun/ppermute | solution.py:30
  475.5 18.8 %collective-permute-start.12 = (bf16[96,2048]{1,0:T(8,128)(2,1)}, bf16[96,2048]{1,0:T(8,128)(2,1)}, u32[]{:S(2)}, u32[]{:S(2)}) collective-permute-start(bf16[96,2048]{1,0:T(8,128)(2,1)} %get-tuple-element.469), channel_id=1, source_target_pairs={{0,2},{1,3},{2,0},{3,1},{4,6},{5,7},{6,4},{7,5},{8,10},{9,11},{10,... | collective-permute-start | bytes 1179656 | tf_op jit(solution)/shard_map/cond/branch_1_fun/ppermute | solution.py:30
  476.4 19.1 %collective-permute-start.13 = (bf16[96,2048]{1,0:T(8,128)(2,1)}, bf16[96,2048]{1,0:T(8,128)(2,1)}, u32[]{:S(2)}, u32[]{:S(2)}) collective-permute-start(bf16[96,2048]{1,0:T(8,128)(2,1)} %get-tuple-element.468), channel_id=1, source_target_pairs={{0,4},{1,5},{2,6},{3,7},{4,0},{5,1},{6,2},{7,3},{8,12},{9,13},{10,... | collective-permute-start | bytes 1179656 | tf_op jit(solution)/shard_map/cond/branch_1_fun/ppermute | solution.py:30
  496.3 5.0 collective-permute-start.16
  499.2 16.8 %collective-permute-start.19 = (bf16[96,2048]{1,0:T(8,128)(2,1)}, bf16[96,2048]{1,0:T(8,128)(2,1)}, u32[]{:S(2)}, u32[]{:S(2)}) collective-permute-start(bf16[96,2048]{1,0:T(8,128)(2,1)} %get-tuple-element.463), channel_id=1, source_target_pairs={{0,4},{1,5},{2,6},{3,7},{4,0},{5,1},{6,2},{7,3},{8,12},{9,13},{10,... | collective-permute-start | bytes 1179656 | tf_op jit(solution)/shard_map/cond/branch_1_fun/ppermute | solution.py:30
  500.7 15.3 %collective-permute-start.20 = (bf16[96,2048]{1,0:T(8,128)(2,1)S(1)}, bf16[96,2048]{1,0:T(8,128)(2,1)}, u32[]{:S(2)}, u32[]{:S(2)}) collective-permute-start(bf16[96,2048]{1,0:T(8,128)(2,1)S(1)} %get-tuple-element.462), channel_id=1, source_target_pairs={{0,2},{1,3},{2,0},{3,1},{4,6},{5,7},{6,4},{7,5},{8,10},{9,11},{10,... | collective-permute-start | bytes 1179656 | tf_op jit(solution)/shard_map/cond/branch_1_fun/ppermute | solution.py:30
  504.7 6.7 %collective-permute-start.17 = (f32[2,1792]{1,0:T(2,128)S(1)}, f32[2,1792]{1,0:T(2,128)S(1)}, u32[]{:S(2)}, u32[]{:S(2)}) collective-permute-start(f32[2,1792]{1,0:T(2,128)S(1)} %dynamic-slice_bitcast_fusion.2), channel_id=1, source_target_pairs={{0,2},{1,3},{2,0},{3,1},{4,6},{5,7},{6,4},{7,5},{8,10},{9,11},{10,... | collective-permute-start | bytes 43016 | tf_op jit(solution)/shard_map/cond/branch_1_fun/ppermute | solution.py:30
  508.7 9.7 %collective-permute-start.14 = (bf16[96,2048]{1,0:T(8,128)(2,1)}, bf16[96,2048]{1,0:T(8,128)(2,1)}, u32[]{:S(2)}, u32[]{:S(2)}) collective-permute-start(bf16[96,2048]{1,0:T(8,128)(2,1)} %get-tuple-element.466), channel_id=1, source_target_pairs={{0,4},{1,5},{2,6},{3,7},{4,0},{5,1},{6,2},{7,3},{8,12},{9,13},{10,... | collective-permute-start | bytes 1179656 | tf_op jit(solution)/shard_map/cond/branch_1_fun/ppermute | solution.py:30
  509.3 10.2 %collective-permute-start.15 = (bf16[96,2048]{1,0:T(8,128)(2,1)}, bf16[96,2048]{1,0:T(8,128)(2,1)}, u32[]{:S(2)}, u32[]{:S(2)}) collective-permute-start(bf16[96,2048]{1,0:T(8,128)(2,1)} %get-tuple-element.467), channel_id=1, source_target_pairs={{0,2},{1,3},{2,0},{3,1},{4,6},{5,7},{6,4},{7,5},{8,10},{9,11},{10,... | collective-permute-start | bytes 1179656 | tf_op jit(solution)/shard_map/cond/branch_1_fun/ppermute | solution.py:30
  512.8 1.8 collective-permute-start.18
  530.0 6.9 %collective-permute-start.51 = (f32[2,448]{1,0:T(2,128)S(1)}, f32[2,448]{1,0:T(2,128)S(1)}, u32[]{:S(2)}, u32[]{:S(2)}) collective-permute-start(f32[2,448]{1,0:T(2,128)S(1)} %dynamic-slice_bitcast_fusion.11), channel_id=1, source_target_pairs={{0,16},{8,24},{16,0},{24,8},{1,17},{9,25},{17,1},{25,9},{2,18},{10... | collective-permute-start | bytes 10760 | tf_op jit(solution)/shard_map/ppermute | solution.py:30
  533.3 16.1 %all-to-all-start.1 = ((bf16[8,64,768]{2,1,0:T(8,128)(2,1)}), bf16[8,64,768]{2,1,0:T(8,128)(2,1)S(1)}, u32[]{:S(2)}, u32[]{:S(2)}) async-start(bf16[8,64,768]{2,1,0:T(8,128)(2,1)} %bitcast.54), calls=%async_computation.4 | async-start | bytes 1572864 | tf_op jit(solution)/shard_map/all_to_all | solution.py:907
  536.9 4.6 collective-permute-start.52
  (65 other events, 652.3 us)
Sparse Core Ops, SparseCore 0:
  9.6 30.6 all-gather.8
  41.9 63.0 all-gather.10
  107.1 105.3 all-gather.14
  214.5 61.7 all-gather.12
  278.5 58.8 reduce-scatter.4
  339.6 102.2 reduce-scatter.6
  450.3 58.0 reduce-scatter.8
  510.6 27.2 reduce-scatter.10
